TPU v7x, 512 devices: a whole 4x8x8 slice. The times are simulated.
512 devices in a mesh: gx: 32 (over x, z), gy: 16 (over y, core).
Axes of the slice: x: 4, y: 8, z: 8, core: 2. Of those that a mesh axis runs over, the one named last changes fastest.
Arguments:
- forcing: float32 [256, 128, 256], P('gx', 'gy'), may hold values from -5 to 5
- coefficient: float32 [256, 128, 256], P('gx', 'gy'), may hold values from 0.2 to 5
Outputs:
- correction: float32 [256, 128, 256], P('gx', 'gy')
- residual: float32 [256, 128, 256], P('gx', 'gy')
All inputs are finite; a program needn't handle non-finite values.
Results may differ from a plain program's by a relative error of at most 0.0003.
Values sent between devices are 32-bit elements; how exact they have to be, the bound alone decides.
No kernel may reach another device: no remote copies, remote signals or barrier semaphores. Data moves between devices by JAX's collectives and lax.ppermute only.
A program may use at most 64 MiB of HBM per device.

v0:
```python
from functools import partial

import jax
import jax.numpy as jnp
from jax import lax
from jax.sharding import PartitionSpec as P

LEVELS = 4
SWEEPS = 2
COARSE_STEPS = 8


smooth_low = 0.4
coarse_low = 0.02
upper_bound = 2.0


def passed_along(value, axis, steps):
    count = lax.axis_size(axis)
    leading, last = (max(0, -steps), min(count, count - steps))
    return lax.ppermute(value, axis, [(source, source + steps) for source in range(leading, last)])


def swapped(block, axis, bit):
    count = lax.axis_size(axis)
    route = []
    for low in range(count):
        high = low | 1 << bit
        if high != low and high < count:
            route += [(low, high), (high, low)]
    return lax.ppermute(block, axis, route)


def faces_of(grid_values, stride_now):
    received = []
    for outgoing, offset in ((grid_values[-1:], stride_now), (grid_values[:1], -stride_now)):
        received.append(passed_along(outgoing, "gx", offset))
    below_x, above_x = received
    received = []
    for outgoing, offset in ((grid_values[:, -1:], stride_now), (grid_values[:, :1], -stride_now)):
        received.append(passed_along(outgoing, "gy", offset))
    below_y, above_y = received
    zero_z = jnp.zeros_like(grid_values[:, :, :1])
    return (
        jnp.concatenate([below_x, grid_values[:-1]], 0),
        jnp.concatenate([grid_values[1:], above_x], 0),
        jnp.concatenate([below_y, grid_values[:, :-1]], 1),
        jnp.concatenate([grid_values[:, 1:], above_y], 1),
        jnp.concatenate([zero_z, grid_values[:, :, :-1]], 2),
        jnp.concatenate([grid_values[:, :, 1:], zero_z], 2),
    )


def build_operator(coefficient, stride_now):
    weights = tuple(
        (0.5 * (coefficient + near_coeff) for near_coeff in faces_of(coefficient, stride_now))
    )
    summed = weights[0] + weights[1] + weights[2] + weights[3] + weights[4] + weights[5]
    return (weights, 1.0 / summed)


def apply_operator(grid_values, weights, stride_now):
    summed = jnp.zeros_like(grid_values)
    for weight, near_value in zip(weights, faces_of(grid_values, stride_now)):
        summed = summed + weight * (grid_values - near_value)
    return summed


def chebyshev(forcing, initial, sweeps_count, low_end, keep_last, operate, inverse):
    center = 0.5 * (upper_bound + low_end)
    radius = 0.5 * (upper_bound - low_end)
    sigma_value = center / radius
    ratio_now = 1.0 / sigma_value
    if initial is None:
        solution = jnp.zeros_like(forcing)
        residual = forcing
    else:
        solution = initial
        residual = forcing - operate(initial)
    direction = None
    for sweep_index in range(sweeps_count):
        if sweep_index == 0:
            direction = inverse * residual / center
        else:
            ratio_next = 1.0 / (2.0 * sigma_value - ratio_now)
            direction = ratio_next * ratio_now * direction + 2.0 * ratio_next / radius * (
                inverse * residual
            )
            ratio_now = ratio_next
        solution = solution + direction
        if keep_last or sweep_index + 1 < sweeps_count:
            residual = residual - operate(direction)
    return (solution, residual)


def coarsen(grid_values):
    size_x, size_y, size_z = grid_values.shape
    return grid_values.reshape(size_x // 2, 2, size_y // 2, 2, size_z // 2, 2).sum(axis=(1, 3, 5))


def refine(grid_values):
    return jnp.repeat(jnp.repeat(jnp.repeat(grid_values, 2, axis=0), 2, axis=1), 2, axis=2)


def fold_pair(stacked, bit_index):
    partner = swapped(stacked, "gx", bit_index)
    upper_half = lax.axis_index("gx") >> bit_index & 1
    lead_block = jnp.where(upper_half == 1, partner, stacked)
    tail_block = jnp.where(upper_half == 1, stacked, partner)
    joined = jnp.concatenate([lead_block, tail_block], 1)
    partner = swapped(joined, "gy", bit_index)
    upper_half = lax.axis_index("gy") >> bit_index & 1
    lead_block = jnp.where(upper_half == 1, partner, joined)
    tail_block = jnp.where(upper_half == 1, joined, partner)
    return jnp.concatenate([lead_block, tail_block], 2)


def own_part(coarse, bit_index):
    half_x = coarse.shape[0] // 2
    half_y = coarse.shape[1] // 2
    start_x = (lax.axis_index("gx") >> bit_index & 1) * half_x
    start_y = (lax.axis_index("gy") >> bit_index & 1) * half_y
    zero_index = jnp.zeros((), jnp.int32)
    return lax.dynamic_slice(
        coarse, (start_x, start_y, zero_index), (half_x, half_y, coarse.shape[2])
    )


def body(forcing, coefficient):
    right_sides = [forcing]
    coeffs = [coefficient]
    strides = [1]
    operators = []
    solutions = []
    stacked = None
    for level_index in range(LEVELS - 1):
        stride_now = strides[level_index]
        weights, inverse = build_operator(coeffs[level_index], stride_now)
        operators.append((weights, inverse))
        solution, residual = chebyshev(
            right_sides[level_index],
            None,
            SWEEPS,
            smooth_low,
            True,
            partial(apply_operator, weights=weights, stride_now=stride_now),
            inverse,
        )
        solutions.append(solution)
        stacked = jnp.stack([0.5 * coarsen(residual), 0.125 * coarsen(coeffs[level_index])])
        if level_index + 1 < LEVELS - 1:
            if level_index >= 1:
                stacked = fold_pair(stacked, level_index - 1)
            right_sides.append(stacked[0])
            coeffs.append(stacked[1])
            strides.append(1 << level_index)
    folded = fold_pair(stacked, LEVELS - 3)
    weights, inverse = build_operator(folded[1], 1 << LEVELS - 2)
    coarse, unused_residual = chebyshev(
        folded[0],
        None,
        COARSE_STEPS,
        coarse_low,
        False,
        partial(apply_operator, weights=weights, stride_now=1 << LEVELS - 2),
        inverse,
    )
    estimate = own_part(coarse, LEVELS - 3)
    residual = forcing
    for level_index in reversed(range(LEVELS - 1)):
        initial = solutions[level_index] + refine(estimate)
        weights, inverse = operators[level_index]
        estimate, residual = chebyshev(
            right_sides[level_index],
            initial,
            SWEEPS,
            smooth_low,
            level_index == 0,
            partial(apply_operator, weights=weights, stride_now=strides[level_index]),
            inverse,
        )
        if level_index >= 2:
            estimate = own_part(estimate, level_index - 2)
    return (estimate, residual)


def solution(mesh):
    in_specs = (P("gx", "gy", None), P("gx", "gy", None))
    out_specs = (P("gx", "gy", None), P("gx", "gy", None))
    return jax.shard_map(body, mesh=mesh, in_specs=in_specs, out_specs=out_specs, check_vma=False)
```

profile of v0, /device:TPU:34, one launch (start us, length us, event | category | flops | bytes accessed | tf_op | source)
XLA Modules:
  0.0 473.2 jit_solution(5100980044752089269)
XLA Ops:
  3.5 4.9 %collective-permute-start.3 = (f32[8,1,256]{2,0,1:T(8,128)S(1)}, f32[8,1,256]{2,0,1:T(8,128)S(1)}, u32[]{:S(2)}, u32[]{:S(2)}) collective-permute-start(f32[8,1,256]{2,0,1:T(8,128)S(1)} %copy.371), channel_id=1, source_target_pairs={{1,0},{2,1},{3,2},{4,3},{5,4},{6,5},{7,6},{8,7},{9,8},{10,9},{11,1... | collective-permute-start | bytes 24584 | tf_op jit(solution)/shard_map/ppermute | solution.py:21
  9.1 4.3 collective-permute-start
  13.4 8.7 %collective-permute-start.1 = (f32[1,8,256]{2,1,0:T(8,128)S(1)}, f32[1,8,256]{2,1,0:T(8,128)S(1)}, u32[]{:S(2)}, u32[]{:S(2)}) collective-permute-start(f32[1,8,256]{2,1,0:T(8,128)S(1)} %get-tuple-element.124), channel_id=1, source_target_pairs={{16,0},{32,16},{48,32},{64,48},{80,64},{96,80},{112,96},{128,112},... | collective-permute-start | bytes 24584 | tf_op jit(solution)/shard_map/ppermute | solution.py:21
  22.1 6.3 %reshape.90 = f32[4,2,4,2,128,2]{5,4,3,2,1,0:T(8,128)} reshape(f32[8,8,256]{2,1,0:T(8,128)} %param.3) | data formatting | bytes 131072 | tf_op jit(solution)/shard_map/reshape | solution.py:98
  28.4 2.5 reduce_sum.54
  36.0 4.9 %collective-permute-start.7 = (f32[8,1,256]{2,0,1:T(8,128)S(1)}, f32[8,1,256]{2,0,1:T(8,128)S(1)}, u32[]{:S(2)}, u32[]{:S(2)}) collective-permute-start(f32[8,1,256]{2,0,1:T(8,128)S(1)} %copy.345), channel_id=1, source_target_pairs={{1,0},{2,1},{3,2},{4,3},{5,4},{6,5},{7,6},{8,7},{9,8},{10,9},{11,1... | collective-permute-start | bytes 24584 | tf_op jit(solution)/shard_map/ppermute | solution.py:21
  42.8 6.0 %collective-permute-start.5 = (f32[1,8,256]{2,1,0:T(8,128)S(1)}, f32[1,8,256]{2,1,0:T(8,128)S(1)}, u32[]{:S(2)}, u32[]{:S(2)}) collective-permute-start(f32[1,8,256]{2,1,0:T(8,128)S(1)} %get-tuple-element.114), channel_id=1, source_target_pairs={{16,0},{32,16},{48,32},{64,48},{80,64},{96,80},{112,96},{128,112},... | collective-permute-start | bytes 24584 | tf_op jit(solution)/shard_map/ppermute | solution.py:21
  52.3 4.9 %collective-permute-start.15 = (f32[8,1,256]{2,0,1:T(8,128)S(1)}, f32[8,1,256]{2,0,1:T(8,128)S(1)}, u32[]{:S(2)}, u32[]{:S(2)}) collective-permute-start(f32[8,1,256]{2,0,1:T(8,128)S(1)} %copy.349), channel_id=1, source_target_pairs={{1,0},{2,1},{3,2},{4,3},{5,4},{6,5},{7,6},{8,7},{9,8},{10,9},{11,1... | collective-permute-start | bytes 24584 | tf_op jit(solution)/shard_map/ppermute | solution.py:21
  59.1 6.3 %collective-permute-start.13 = (f32[1,8,256]{2,1,0:T(8,128)S(1)}, f32[1,8,256]{2,1,0:T(8,128)S(1)}, u32[]{:S(2)}, u32[]{:S(2)}) collective-permute-start(f32[1,8,256]{2,1,0:T(8,128)S(1)} %get-tuple-element.111), channel_id=1, source_target_pairs={{16,0},{32,16},{48,32},{64,48},{80,64},{96,80},{112,96},{128,112},... | collective-permute-start | bytes 24584 | tf_op jit(solution)/shard_map/ppermute | solution.py:21
  69.4 6.0 %collective-permute-start.9 = (f32[1,4,128]{2,1,0:T(4,128)S(1)}, f32[1,4,128]{2,1,0:T(4,128)S(1)}, u32[]{:S(2)}, u32[]{:S(2)}) collective-permute-start(f32[1,4,128]{2,1,0:T(4,128)S(1)} %get-tuple-element.316), channel_id=1, source_target_pairs={{16,0},{32,16},{48,32},{64,48},{80,64},{96,80},{112,96},{128,112},... | collective-permute-start | bytes 6152 | tf_op jit(solution)/shard_map/ppermute | solution.py:21
  75.5 5.5 %reshape.91 = f32[4,2,4,2,128,2]{5,4,3,2,1,0:T(8,128)} reshape(f32[8,8,256]{2,1,0:T(8,128)S(1)} %fusion.20) | data formatting | bytes 131072 | tf_op jit(solution)/shard_map/reshape | solution.py:98
  81.1 2.5 reduce_sum.55
  85.8 6.0 %collective-permute-start.17 = (f32[1,4,128]{2,1,0:T(4,128)S(1)}, f32[1,4,128]{2,1,0:T(4,128)S(1)}, u32[]{:S(2)}, u32[]{:S(2)}) collective-permute-start(f32[1,4,128]{2,1,0:T(4,128)S(1)} %get-tuple-element.306), channel_id=1, source_target_pairs={{16,0},{32,16},{48,32},{64,48},{80,64},{96,80},{112,96},{128,112},... | collective-permute-start | bytes 6152 | tf_op jit(solution)/shard_map/ppermute | solution.py:21
  93.7 4.9 %collective-permute-start.19 = (f32[4,1,128]{2,1,0:T(1,128)S(1)}, f32[4,1,128]{2,1,0:T(1,128)S(1)}, u32[]{:S(2)}, u32[]{:S(2)}) collective-permute-start(f32[4,1,128]{2,1,0:T(1,128)S(1)} %get-tuple-element.310), channel_id=1, source_target_pairs={{1,0},{2,1},{3,2},{4,3},{5,4},{6,5},{7,6},{8,7},{9,8},{10,9},{11,1... | collective-permute-start | bytes 6152 | tf_op jit(solution)/shard_map/ppermute | solution.py:21
  102.0 6.0 %collective-permute-start.21 = (f32[1,4,128]{2,1,0:T(4,128)S(1)}, f32[1,4,128]{2,1,0:T(4,128)S(1)}, u32[]{:S(2)}, u32[]{:S(2)}) collective-permute-start(f32[1,4,128]{2,1,0:T(4,128)S(1)} %get-tuple-element.303), channel_id=1, source_target_pairs={{16,0},{32,16},{48,32},{64,48},{80,64},{96,80},{112,96},{128,112},... | collective-permute-start | bytes 6152 | tf_op jit(solution)/shard_map/ppermute | solution.py:21
  109.9 4.9 %collective-permute-start.23 = (f32[4,1,128]{2,1,0:T(1,128)S(1)}, f32[4,1,128]{2,1,0:T(1,128)S(1)}, u32[]{:S(2)}, u32[]{:S(2)}) collective-permute-start(f32[4,1,128]{2,1,0:T(1,128)S(1)} %get-tuple-element.299), channel_id=1, source_target_pairs={{1,0},{2,1},{3,2},{4,3},{5,4},{6,5},{7,6},{8,7},{9,8},{10,9},{11,1... | collective-permute-start | bytes 6152 | tf_op jit(solution)/shard_map/ppermute | solution.py:21
  118.7 3.6 collective-permute-done.24
  127.7 5.1 %collective-permute-start.29 = (f32[4,1,64]{2,1,0:T(1,128)S(1)}, f32[4,1,64]{2,1,0:T(1,128)S(1)}, u32[]{:S(2)}, u32[]{:S(2)}) collective-permute-start(f32[4,1,64]{2,1,0:T(1,128)S(1)} %get-tuple-element.291), channel_id=1, source_target_pairs={{2,0},{3,1},{4,2},{5,3},{6,4},{7,5},{8,6},{9,7},{10,8},{11,9},{12,... | collective-permute-start | bytes 3080 | tf_op jit(solution)/shard_map/ppermute | solution.py:21
  134.8 6.9 %collective-permute-start.27 = (f32[1,4,64]{2,1,0:T(4,128)S(1)}, f32[1,4,64]{2,1,0:T(4,128)S(1)}, u32[]{:S(2)}, u32[]{:S(2)}) collective-permute-start(f32[1,4,64]{2,1,0:T(4,128)S(1)} %get-tuple-element.140), channel_id=1, source_target_pairs={{32,0},{48,16},{64,32},{80,48},{96,64},{112,80},{128,96},{144,112}... | collective-permute-start | bytes 3080 | tf_op jit(solution)/shard_map/ppermute | solution.py:21
  145.1 7.2 %collective-permute-start.31 = (f32[1,4,64]{2,1,0:T(4,128)S(1)}, f32[1,4,64]{2,1,0:T(4,128)S(1)}, u32[]{:S(2)}, u32[]{:S(2)}) collective-permute-start(f32[1,4,64]{2,1,0:T(4,128)S(1)} %get-tuple-element.278), channel_id=1, source_target_pairs={{32,0},{48,16},{64,32},{80,48},{96,64},{112,80},{128,96},{144,112}... | collective-permute-start | bytes 3080 | tf_op jit(solution)/shard_map/ppermute | solution.py:21
  154.3 5.1 %collective-permute-start.33 = (f32[4,1,64]{2,1,0:T(1,128)S(1)}, f32[4,1,64]{2,1,0:T(1,128)S(1)}, u32[]{:S(2)}, u32[]{:S(2)}) collective-permute-start(f32[4,1,64]{2,1,0:T(1,128)S(1)} %get-tuple-element.282), channel_id=1, source_target_pairs={{2,0},{3,1},{4,2},{5,3},{6,4},{7,5},{8,6},{9,7},{10,8},{11,9},{12,... | collective-permute-start | bytes 3080 | tf_op jit(solution)/shard_map/ppermute | solution.py:21
  162.8 6.9 %collective-permute-start.35 = (f32[1,4,64]{2,1,0:T(4,128)S(1)}, f32[1,4,64]{2,1,0:T(4,128)S(1)}, u32[]{:S(2)}, u32[]{:S(2)}) collective-permute-start(f32[1,4,64]{2,1,0:T(4,128)S(1)} %get-tuple-element.275), channel_id=1, source_target_pairs={{32,0},{48,16},{64,32},{80,48},{96,64},{112,80},{128,96},{144,112}... | collective-permute-start | bytes 3080 | tf_op jit(solution)/shard_map/ppermute | solution.py:21
  171.7 5.4 %collective-permute-start.37 = (f32[4,1,64]{2,1,0:T(1,128)S(1)}, f32[4,1,64]{2,1,0:T(1,128)S(1)}, u32[]{:S(2)}, u32[]{:S(2)}) collective-permute-start(f32[4,1,64]{2,1,0:T(1,128)S(1)} %get-tuple-element.271), channel_id=1, source_target_pairs={{2,0},{3,1},{4,2},{5,3},{6,4},{7,5},{8,6},{9,7},{10,8},{11,9},{12,... | collective-permute-start | bytes 3080 | tf_op jit(solution)/shard_map/ppermute | solution.py:21
  180.8 4.5 collective-permute-done.38
  187.2 3.6 collective-permute-done.39
  190.9 3.4 collective-permute-start.40
  194.3 7.2 %collective-permute-start.41 = (f32[1,4,32]{2,1,0:T(4,128)S(1)}, f32[1,4,32]{2,1,0:T(4,128)S(1)}, u32[]{:S(2)}, u32[]{:S(2)}) collective-permute-start(f32[1,4,32]{2,1,0:T(4,128)S(1)} %get-tuple-element.134), channel_id=1, source_target_pairs={{64,0},{80,16},{96,32},{112,48},{128,64},{144,80},{160,96},{176,11... | collective-permute-start | bytes 1544 | tf_op jit(solution)/shard_map/ppermute | solution.py:21
  203.5 6.0 %collective-permute-start.43 = (f32[4,1,32]{2,1,0:T(1,128)S(1)}, f32[4,1,32]{2,1,0:T(1,128)S(1)}, u32[]{:S(2)}, u32[]{:S(2)}) collective-permute-start(f32[4,1,32]{2,1,0:T(1,128)S(1)} %get-tuple-element.263), channel_id=1, source_target_pairs={{4,0},{5,1},{6,2},{7,3},{8,4},{9,5},{10,6},{11,7},{12,8},{13,9},{1... | collective-permute-start | bytes 1544 | tf_op jit(solution)/shard_map/ppermute | solution.py:21
  211.0 2.5 collective-permute-start.44
  213.5 8.1 %collective-permute-start.45 = (f32[1,4,32]{2,1,0:T(4,128)S(1)}, f32[1,4,32]{2,1,0:T(4,128)S(1)}, u32[]{:S(2)}, u32[]{:S(2)}) collective-permute-start(f32[1,4,32]{2,1,0:T(4,128)S(1)} %get-tuple-element.250), channel_id=1, source_target_pairs={{64,0},{80,16},{96,32},{112,48},{128,64},{144,80},{160,96},{176,11... | collective-permute-start | bytes 1544 | tf_op jit(solution)/shard_map/ppermute | solution.py:21
  223.6 6.3 %collective-permute-start.47 = (f32[4,1,32]{2,1,0:T(1,128)S(1)}, f32[4,1,32]{2,1,0:T(1,128)S(1)}, u32[]{:S(2)}, u32[]{:S(2)}) collective-permute-start(f32[4,1,32]{2,1,0:T(1,128)S(1)} %get-tuple-element.254), channel_id=1, source_target_pairs={{4,0},{5,1},{6,2},{7,3},{8,4},{9,5},{10,6},{11,7},{12,8},{13,9},{1... | collective-permute-start | bytes 1544 | tf_op jit(solution)/shard_map/ppermute | solution.py:21
  231.4 1.9 collective-permute-start.48
  233.4 8.7 %collective-permute-start.49 = (f32[1,4,32]{2,1,0:T(4,128)S(1)}, f32[1,4,32]{2,1,0:T(4,128)S(1)}, u32[]{:S(2)}, u32[]{:S(2)}) collective-permute-start(f32[1,4,32]{2,1,0:T(4,128)S(1)} %get-tuple-element.240), channel_id=1, source_target_pairs={{64,0},{80,16},{96,32},{112,48},{128,64},{144,80},{160,96},{176,11... | collective-permute-start | bytes 1544 | tf_op jit(solution)/shard_map/ppermute | solution.py:21
  244.0 6.3 %collective-permute-start.51 = (f32[4,1,32]{2,1,0:T(1,128)S(1)}, f32[4,1,32]{2,1,0:T(1,128)S(1)}, u32[]{:S(2)}, u32[]{:S(2)}) collective-permute-start(f32[4,1,32]{2,1,0:T(1,128)S(1)} %get-tuple-element.244), channel_id=1, source_target_pairs={{4,0},{5,1},{6,2},{7,3},{8,4},{9,5},{10,6},{11,7},{12,8},{13,9},{1... | collective-permute-start | bytes 1544 | tf_op jit(solution)/shard_map/ppermute | solution.py:21
  251.8 1.9 collective-permute-start.52
  253.7 8.7 %collective-permute-start.53 = (f32[1,4,32]{2,1,0:T(4,128)S(1)}, f32[1,4,32]{2,1,0:T(4,128)S(1)}, u32[]{:S(2)}, u32[]{:S(2)}) collective-permute-start(f32[1,4,32]{2,1,0:T(4,128)S(1)} %get-tuple-element.230), channel_id=1, source_target_pairs={{64,0},{80,16},{96,32},{112,48},{128,64},{144,80},{160,96},{176,11... | collective-permute-start | bytes 1544 | tf_op jit(solution)/shard_map/ppermute | solution.py:21
  264.3 6.3 %collective-permute-start.55 = (f32[4,1,32]{2,1,0:T(1,128)S(1)}, f32[4,1,32]{2,1,0:T(1,128)S(1)}, u32[]{:S(2)}, u32[]{:S(2)}) collective-permute-start(f32[4,1,32]{2,1,0:T(1,128)S(1)} %get-tuple-element.234), channel_id=1, source_target_pairs={{4,0},{5,1},{6,2},{7,3},{8,4},{9,5},{10,6},{11,7},{12,8},{13,9},{1... | collective-permute-start | bytes 1544 | tf_op jit(solution)/shard_map/ppermute | solution.py:21
  272.1 1.9 collective-permute-start.56
  274.1 8.7 %collective-permute-start.57 = (f32[1,4,32]{2,1,0:T(4,128)S(1)}, f32[1,4,32]{2,1,0:T(4,128)S(1)}, u32[]{:S(2)}, u32[]{:S(2)}) collective-permute-start(f32[1,4,32]{2,1,0:T(4,128)S(1)} %get-tuple-element.220), channel_id=1, source_target_pairs={{64,0},{80,16},{96,32},{112,48},{128,64},{144,80},{160,96},{176,11... | collective-permute-start | bytes 1544 | tf_op jit(solution)/shard_map/ppermute | solution.py:21
  284.7 6.3 %collective-permute-start.59 = (f32[4,1,32]{2,1,0:T(1,128)S(1)}, f32[4,1,32]{2,1,0:T(1,128)S(1)}, u32[]{:S(2)}, u32[]{:S(2)}) collective-permute-start(f32[4,1,32]{2,1,0:T(1,128)S(1)} %get-tuple-element.224), channel_id=1, source_target_pairs={{4,0},{5,1},{6,2},{7,3},{8,4},{9,5},{10,6},{11,7},{12,8},{13,9},{1... | collective-permute-start | bytes 1544 | tf_op jit(solution)/shard_map/ppermute | solution.py:21
  292.5 1.9 collective-permute-start.60
  294.4 8.7 %collective-permute-start.61 = (f32[1,4,32]{2,1,0:T(4,128)S(1)}, f32[1,4,32]{2,1,0:T(4,128)S(1)}, u32[]{:S(2)}, u32[]{:S(2)}) collective-permute-start(f32[1,4,32]{2,1,0:T(4,128)S(1)} %get-tuple-element.210), channel_id=1, source_target_pairs={{64,0},{80,16},{96,32},{112,48},{128,64},{144,80},{160,96},{176,11... | collective-permute-start | bytes 1544 | tf_op jit(solution)/shard_map/ppermute | solution.py:21
  305.1 6.3 %collective-permute-start.63 = (f32[4,1,32]{2,1,0:T(1,128)S(1)}, f32[4,1,32]{2,1,0:T(1,128)S(1)}, u32[]{:S(2)}, u32[]{:S(2)}) collective-permute-start(f32[4,1,32]{2,1,0:T(1,128)S(1)} %get-tuple-element.214), channel_id=1, source_target_pairs={{4,0},{5,1},{6,2},{7,3},{8,4},{9,5},{10,6},{11,7},{12,8},{13,9},{1... | collective-permute-start | bytes 1544 | tf_op jit(solution)/shard_map/ppermute | solution.py:21
  312.8 1.9 collective-permute-start.64
  314.8 8.7 %collective-permute-start.65 = (f32[1,4,32]{2,1,0:T(4,128)S(1)}, f32[1,4,32]{2,1,0:T(4,128)S(1)}, u32[]{:S(2)}, u32[]{:S(2)}) collective-permute-start(f32[1,4,32]{2,1,0:T(4,128)S(1)} %get-tuple-element.200), channel_id=1, source_target_pairs={{64,0},{80,16},{96,32},{112,48},{128,64},{144,80},{160,96},{176,11... | collective-permute-start | bytes 1544 | tf_op jit(solution)/shard_map/ppermute | solution.py:21
  325.4 6.3 %collective-permute-start.67 = (f32[4,1,32]{2,1,0:T(1,128)S(1)}, f32[4,1,32]{2,1,0:T(1,128)S(1)}, u32[]{:S(2)}, u32[]{:S(2)}) collective-permute-start(f32[4,1,32]{2,1,0:T(1,128)S(1)} %get-tuple-element.204), channel_id=1, source_target_pairs={{4,0},{5,1},{6,2},{7,3},{8,4},{9,5},{10,6},{11,7},{12,8},{13,9},{1... | collective-permute-start | bytes 1544 | tf_op jit(solution)/shard_map/ppermute | solution.py:21
  333.2 1.9 collective-permute-start.68
  335.2 8.7 %collective-permute-start.69 = (f32[1,4,32]{2,1,0:T(4,128)S(1)}, f32[1,4,32]{2,1,0:T(4,128)S(1)}, u32[]{:S(2)}, u32[]{:S(2)}) collective-permute-start(f32[1,4,32]{2,1,0:T(4,128)S(1)} %get-tuple-element.197), channel_id=1, source_target_pairs={{64,0},{80,16},{96,32},{112,48},{128,64},{144,80},{160,96},{176,11... | collective-permute-start | bytes 1544 | tf_op jit(solution)/shard_map/ppermute | solution.py:21
  345.8 6.3 %collective-permute-start.71 = (f32[4,1,32]{2,1,0:T(1,128)S(1)}, f32[4,1,32]{2,1,0:T(1,128)S(1)}, u32[]{:S(2)}, u32[]{:S(2)}) collective-permute-start(f32[4,1,32]{2,1,0:T(1,128)S(1)} %get-tuple-element.193), channel_id=1, source_target_pairs={{4,0},{5,1},{6,2},{7,3},{8,4},{9,5},{10,6},{11,7},{12,8},{13,9},{1... | collective-permute-start | bytes 1544 | tf_op jit(solution)/shard_map/ppermute | solution.py:21
  355.8 6.9 %collective-permute-start.73 = (f32[1,4,64]{2,1,0:T(4,128)S(1)}, f32[1,4,64]{2,1,0:T(4,128)S(1)}, u32[]{:S(2)}, u32[]{:S(2)}) collective-permute-start(f32[1,4,64]{2,1,0:T(4,128)S(1)} %get-tuple-element.178), channel_id=1, source_target_pairs={{32,0},{48,16},{64,32},{80,48},{96,64},{112,80},{128,96},{144,112}... | collective-permute-start | bytes 3080 | tf_op jit(solution)/shard_map/ppermute | solution.py:21
  362.7 2.7 collective-permute-start.74
  365.5 4.8 %collective-permute-start.75 = (f32[4,1,64]{2,1,0:T(1,128)S(1)}, f32[4,1,64]{2,1,0:T(1,128)S(1)}, u32[]{:S(2)}, u32[]{:S(2)}) collective-permute-start(f32[4,1,64]{2,1,0:T(1,128)S(1)} %get-tuple-element.182), channel_id=1, source_target_pairs={{2,0},{3,1},{4,2},{5,3},{6,4},{7,5},{8,6},{9,7},{10,8},{11,9},{12,... | collective-permute-start | bytes 3080 | tf_op jit(solution)/shard_map/ppermute | solution.py:21
  373.7 6.9 %collective-permute-start.77 = (f32[1,4,64]{2,1,0:T(4,128)S(1)}, f32[1,4,64]{2,1,0:T(4,128)S(1)}, u32[]{:S(2)}, u32[]{:S(2)}) collective-permute-start(f32[1,4,64]{2,1,0:T(4,128)S(1)} %get-tuple-element.175), channel_id=1, source_target_pairs={{32,0},{48,16},{64,32},{80,48},{96,64},{112,80},{128,96},{144,112}... | collective-permute-start | bytes 3080 | tf_op jit(solution)/shard_map/ppermute | solution.py:21
  382.6 5.6 %collective-permute-start.79 = (f32[4,1,64]{2,1,0:T(1,128)S(1)}, f32[4,1,64]{2,1,0:T(1,128)S(1)}, u32[]{:S(2)}, u32[]{:S(2)}) collective-permute-start(f32[4,1,64]{2,1,0:T(1,128)S(1)} %get-tuple-element.171), channel_id=1, source_target_pairs={{2,0},{3,1},{4,2},{5,3},{6,4},{7,5},{8,6},{9,7},{10,8},{11,9},{12,... | collective-permute-start | bytes 3080 | tf_op jit(solution)/shard_map/ppermute | solution.py:21
  391.7 6.0 %collective-permute-start.81 = (f32[1,4,128]{2,1,0:T(4,128)S(1)}, f32[1,4,128]{2,1,0:T(4,128)S(1)}, u32[]{:S(2)}, u32[]{:S(2)}) collective-permute-start(f32[1,4,128]{2,1,0:T(4,128)S(1)} %get-tuple-element.156), channel_id=1, source_target_pairs={{16,0},{32,16},{48,32},{64,48},{80,64},{96,80},{112,96},{128,112},... | collective-permute-start | bytes 6152 | tf_op jit(solution)/shard_map/ppermute | solution.py:21
  399.7 4.9 %collective-permute-start.83 = (f32[4,1,128]{2,1,0:T(1,128)S(1)}, f32[4,1,128]{2,1,0:T(1,128)S(1)}, u32[]{:S(2)}, u32[]{:S(2)}) collective-permute-start(f32[4,1,128]{2,1,0:T(1,128)S(1)} %get-tuple-element.160), channel_id=1, source_target_pairs={{1,0},{2,1},{3,2},{4,3},{5,4},{6,5},{7,6},{8,7},{9,8},{10,9},{11,1... | collective-permute-start | bytes 6152 | tf_op jit(solution)/shard_map/ppermute | solution.py:21
  408.0 6.0 %collective-permute-start.85 = (f32[1,4,128]{2,1,0:T(4,128)S(1)}, f32[1,4,128]{2,1,0:T(4,128)S(1)}, u32[]{:S(2)}, u32[]{:S(2)}) collective-permute-start(f32[1,4,128]{2,1,0:T(4,128)S(1)} %get-tuple-element.146), channel_id=1, source_target_pairs={{16,0},{32,16},{48,32},{64,48},{80,64},{96,80},{112,96},{128,112},... | collective-permute-start | bytes 6152 | tf_op jit(solution)/shard_map/ppermute | solution.py:21
  415.9 4.9 %collective-permute-start.87 = (f32[4,1,128]{2,1,0:T(1,128)S(1)}, f32[4,1,128]{2,1,0:T(1,128)S(1)}, u32[]{:S(2)}, u32[]{:S(2)}) collective-permute-start(f32[4,1,128]{2,1,0:T(1,128)S(1)} %get-tuple-element.150), channel_id=1, source_target_pairs={{1,0},{2,1},{3,2},{4,3},{5,4},{6,5},{7,6},{8,7},{9,8},{10,9},{11,1... | collective-permute-start | bytes 6152 | tf_op jit(solution)/shard_map/ppermute | solution.py:21
  425.0 4.9 %collective-permute-start.91 = (f32[8,1,256]{2,0,1:T(8,128)S(1)}, f32[8,1,256]{2,0,1:T(8,128)S(1)}, u32[]{:S(2)}, u32[]{:S(2)}) collective-permute-start(f32[8,1,256]{2,0,1:T(8,128)S(1)} %copy.360), channel_id=1, source_target_pairs={{1,0},{2,1},{3,2},{4,3},{5,4},{6,5},{7,6},{8,7},{9,8},{10,9},{11,1... | collective-permute-start | bytes 24584 | tf_op jit(solution)/shard_map/ppermute | solution.py:21
  431.8 6.0 %collective-permute-start.89 = (f32[1,8,256]{2,1,0:T(8,128)S(1)}, f32[1,8,256]{2,1,0:T(8,128)S(1)}, u32[]{:S(2)}, u32[]{:S(2)}) collective-permute-start(f32[1,8,256]{2,1,0:T(8,128)S(1)} %get-tuple-element.94), channel_id=1, source_target_pairs={{16,0},{32,16},{48,32},{64,48},{80,64},{96,80},{112,96},{128,112},... | collective-permute-start | bytes 24584 | tf_op jit(solution)/shard_map/ppermute | solution.py:21
  441.4 4.9 %collective-permute-start.95 = (f32[8,1,256]{2,0,1:T(8,128)S(1)}, f32[8,1,256]{2,0,1:T(8,128)S(1)}, u32[]{:S(2)}, u32[]{:S(2)}) collective-permute-start(f32[8,1,256]{2,0,1:T(8,128)S(1)} %copy.364), channel_id=1, source_target_pairs={{1,0},{2,1},{3,2},{4,3},{5,4},{6,5},{7,6},{8,7},{9,8},{10,9},{11,1... | collective-permute-start | bytes 24584 | tf_op jit(solution)/shard_map/ppermute | solution.py:21
  448.1 6.3 %collective-permute-start.93 = (f32[1,8,256]{2,1,0:T(8,128)S(1)}, f32[1,8,256]{2,1,0:T(8,128)S(1)}, u32[]{:S(2)}, u32[]{:S(2)}) collective-permute-start(f32[1,8,256]{2,1,0:T(8,128)S(1)} %get-tuple-element.84), channel_id=1, source_target_pairs={{16,0},{32,16},{48,32},{64,48},{80,64},{96,80},{112,96},{128,112},... | collective-permute-start | bytes 24584 | tf_op jit(solution)/shard_map/ppermute | solution.py:21
  458.0 4.9 %collective-permute-start.99 = (f32[8,1,256]{2,0,1:T(8,128)S(1)}, f32[8,1,256]{2,0,1:T(8,128)S(1)}, u32[]{:S(2)}, u32[]{:S(2)}) collective-permute-start(f32[8,1,256]{2,0,1:T(8,128)S(1)} %copy.368), channel_id=1, source_target_pairs={{1,0},{2,1},{3,2},{4,3},{5,4},{6,5},{7,6},{8,7},{9,8},{10,9},{11,1... | collective-permute-start | bytes 24584 | tf_op jit(solution)/shard_map/ppermute | solution.py:21
  464.8 6.3 %collective-permute-start.97 = (f32[1,8,256]{2,1,0:T(8,128)S(1)}, f32[1,8,256]{2,1,0:T(8,128)S(1)}, u32[]{:S(2)}, u32[]{:S(2)}) collective-permute-start(f32[1,8,256]{2,1,0:T(8,128)S(1)} %get-tuple-element.81), channel_id=1, source_target_pairs={{16,0},{32,16},{48,32},{64,48},{80,64},{96,80},{112,96},{128,112},... | collective-permute-start | bytes 24584 | tf_op jit(solution)/shard_map/ppermute | solution.py:21
  (356 shorter events, 120.1 us)
Async XLA Ops:
  1.6 32.1 %collective-permute-start.2 = (f32[8,1,256]{2,0,1:T(8,128)S(1)}, f32[8,1,256]{2,0,1:T(8,128)S(1)}, u32[]{:S(2)}, u32[]{:S(2)}) collective-permute-start(f32[8,1,256]{2,0,1:T(8,128)S(1)} %copy.370), channel_id=1, source_target_pairs={{0,1},{1,2},{2,3},{3,4},{4,5},{5,6},{6,7},{7,8},{8,9},{9,10},{10,1... | collective-permute-start | bytes 24584 | tf_op jit(solution)/shard_map/ppermute | solution.py:21
  3.5 30.2 %collective-permute-start.3 = (f32[8,1,256]{2,0,1:T(8,128)S(1)}, f32[8,1,256]{2,0,1:T(8,128)S(1)}, u32[]{:S(2)}, u32[]{:S(2)}) collective-permute-start(f32[8,1,256]{2,0,1:T(8,128)S(1)} %copy.371), channel_id=1, source_target_pairs={{1,0},{2,1},{3,2},{4,3},{5,4},{6,5},{7,6},{8,7},{9,8},{10,9},{11,1... | collective-permute-start | bytes 24584 | tf_op jit(solution)/shard_map/ppermute | solution.py:21
  9.1 24.6 %collective-permute-start = (f32[1,8,256]{2,1,0:T(8,128)S(1)}, f32[1,8,256]{2,1,0:T(8,128)S(1)}, u32[]{:S(2)}, u32[]{:S(2)}) collective-permute-start(f32[1,8,256]{2,1,0:T(8,128)S(1)} %get-tuple-element.123), channel_id=1, source_target_pairs={{0,16},{16,32},{32,48},{48,64},{64,80},{80,96},{96,112},{112,128},... | collective-permute-start | bytes 24584 | tf_op jit(solution)/shard_map/ppermute | solution.py:21
  13.4 20.4 %collective-permute-start.1 = (f32[1,8,256]{2,1,0:T(8,128)S(1)}, f32[1,8,256]{2,1,0:T(8,128)S(1)}, u32[]{:S(2)}, u32[]{:S(2)}) collective-permute-start(f32[1,8,256]{2,1,0:T(8,128)S(1)} %get-tuple-element.124), channel_id=1, source_target_pairs={{16,0},{32,16},{48,32},{64,48},{80,64},{96,80},{112,96},{128,112},... | collective-permute-start | bytes 24584 | tf_op jit(solution)/shard_map/ppermute | solution.py:21
  30.9 52.7 %collective-permute-start.10 = (f32[4,1,128]{2,1,0:T(1,128)S(1)}, f32[4,1,128]{2,1,0:T(1,128)S(1)}, u32[]{:S(2)}, u32[]{:S(2)}) collective-permute-start(f32[4,1,128]{2,1,0:T(1,128)S(1)} %get-tuple-element.324), channel_id=1, source_target_pairs={{0,1},{1,2},{2,3},{3,4},{4,5},{5,6},{6,7},{7,8},{8,9},{9,10},{10,1... | collective-permute-start | bytes 6152 | tf_op jit(solution)/shard_map/ppermute | solution.py:21
  34.0 14.8 %collective-permute-start.6 = (f32[8,1,256]{2,0,1:T(8,128)S(1)}, f32[8,1,256]{2,0,1:T(8,128)S(1)}, u32[]{:S(2)}, u32[]{:S(2)}) collective-permute-start(f32[8,1,256]{2,0,1:T(8,128)S(1)} %copy.343), channel_id=1, source_target_pairs={{0,1},{1,2},{2,3},{3,4},{4,5},{5,6},{6,7},{7,8},{8,9},{9,10},{10,1... | collective-permute-start | bytes 24584 | tf_op jit(solution)/shard_map/ppermute | solution.py:21
  36.0 12.9 %collective-permute-start.7 = (f32[8,1,256]{2,0,1:T(8,128)S(1)}, f32[8,1,256]{2,0,1:T(8,128)S(1)}, u32[]{:S(2)}, u32[]{:S(2)}) collective-permute-start(f32[8,1,256]{2,0,1:T(8,128)S(1)} %copy.345), channel_id=1, source_target_pairs={{1,0},{2,1},{3,2},{4,3},{5,4},{6,5},{7,6},{8,7},{9,8},{10,9},{11,1... | collective-permute-start | bytes 24584 | tf_op jit(solution)/shard_map/ppermute | solution.py:21
  50.4 15.1 %collective-permute-start.14 = (f32[8,1,256]{2,0,1:T(8,128)S(1)}, f32[8,1,256]{2,0,1:T(8,128)S(1)}, u32[]{:S(2)}, u32[]{:S(2)}) collective-permute-start(f32[8,1,256]{2,0,1:T(8,128)S(1)} %copy.347), channel_id=1, source_target_pairs={{0,1},{1,2},{2,3},{3,4},{4,5},{5,6},{6,7},{7,8},{8,9},{9,10},{10,1... | collective-permute-start | bytes 24584 | tf_op jit(solution)/shard_map/ppermute | solution.py:21
  52.3 15.1 %collective-permute-start.15 = (f32[8,1,256]{2,0,1:T(8,128)S(1)}, f32[8,1,256]{2,0,1:T(8,128)S(1)}, u32[]{:S(2)}, u32[]{:S(2)}) collective-permute-start(f32[8,1,256]{2,0,1:T(8,128)S(1)} %copy.349), channel_id=1, source_target_pairs={{1,0},{2,1},{3,2},{4,3},{5,4},{6,5},{7,6},{8,7},{9,8},{10,9},{11,1... | collective-permute-start | bytes 24584 | tf_op jit(solution)/shard_map/ppermute | solution.py:21
  57.2 12.2 %collective-permute-start.12 = (f32[1,8,256]{2,1,0:T(8,128)S(1)}, f32[1,8,256]{2,1,0:T(8,128)S(1)}, u32[]{:S(2)}, u32[]{:S(2)}) collective-permute-start(f32[1,8,256]{2,1,0:T(8,128)S(1)} %get-tuple-element.112), channel_id=1, source_target_pairs={{0,16},{16,32},{32,48},{48,64},{64,80},{80,96},{96,112},{112,128},... | collective-permute-start | bytes 24584 | tf_op jit(solution)/shard_map/ppermute | solution.py:21
  59.1 16.3 %collective-permute-start.13 = (f32[1,8,256]{2,1,0:T(8,128)S(1)}, f32[1,8,256]{2,1,0:T(8,128)S(1)}, u32[]{:S(2)}, u32[]{:S(2)}) collective-permute-start(f32[1,8,256]{2,1,0:T(8,128)S(1)} %get-tuple-element.111), channel_id=1, source_target_pairs={{16,0},{32,16},{48,32},{64,48},{80,64},{96,80},{112,96},{128,112},... | collective-permute-start | bytes 24584 | tf_op jit(solution)/shard_map/ppermute | solution.py:21
  65.5 18.2 %collective-permute-start.11 = (f32[4,1,128]{2,1,0:T(1,128)S(1)}, f32[4,1,128]{2,1,0:T(1,128)S(1)}, u32[]{:S(2)}, u32[]{:S(2)}) collective-permute-start(f32[4,1,128]{2,1,0:T(1,128)S(1)} %get-tuple-element.323), channel_id=1, source_target_pairs={{1,0},{2,1},{3,2},{4,3},{5,4},{6,5},{7,6},{8,7},{9,8},{10,9},{11,1... | collective-permute-start | bytes 6152 | tf_op jit(solution)/shard_map/ppermute | solution.py:21
  67.4 16.2 %collective-permute-start.8 = (f32[1,4,128]{2,1,0:T(4,128)S(1)}, f32[1,4,128]{2,1,0:T(4,128)S(1)}, u32[]{:S(2)}, u32[]{:S(2)}) collective-permute-start(f32[1,4,128]{2,1,0:T(4,128)S(1)} %get-tuple-element.315), channel_id=1, source_target_pairs={{0,16},{16,32},{32,48},{48,64},{64,80},{80,96},{96,112},{112,128},... | collective-permute-start | bytes 6152 | tf_op jit(solution)/shard_map/ppermute | solution.py:21
  69.4 14.3 %collective-permute-start.9 = (f32[1,4,128]{2,1,0:T(4,128)S(1)}, f32[1,4,128]{2,1,0:T(4,128)S(1)}, u32[]{:S(2)}, u32[]{:S(2)}) collective-permute-start(f32[1,4,128]{2,1,0:T(4,128)S(1)} %get-tuple-element.316), channel_id=1, source_target_pairs={{16,0},{32,16},{48,32},{64,48},{80,64},{96,80},{112,96},{128,112},... | collective-permute-start | bytes 6152 | tf_op jit(solution)/shard_map/ppermute | solution.py:21
  83.8 14.8 %collective-permute-start.16 = (f32[1,4,128]{2,1,0:T(4,128)S(1)}, f32[1,4,128]{2,1,0:T(4,128)S(1)}, u32[]{:S(2)}, u32[]{:S(2)}) collective-permute-start(f32[1,4,128]{2,1,0:T(4,128)S(1)} %get-tuple-element.305), channel_id=1, source_target_pairs={{0,16},{16,32},{32,48},{48,64},{64,80},{80,96},{96,112},{112,128},... | collective-permute-start | bytes 6152 | tf_op jit(solution)/shard_map/ppermute | solution.py:21
  85.8 12.9 %collective-permute-start.17 = (f32[1,4,128]{2,1,0:T(4,128)S(1)}, f32[1,4,128]{2,1,0:T(4,128)S(1)}, u32[]{:S(2)}, u32[]{:S(2)}) collective-permute-start(f32[1,4,128]{2,1,0:T(4,128)S(1)} %get-tuple-element.306), channel_id=1, source_target_pairs={{16,0},{32,16},{48,32},{64,48},{80,64},{96,80},{112,96},{128,112},... | collective-permute-start | bytes 6152 | tf_op jit(solution)/shard_map/ppermute | solution.py:21
  100.1 14.8 %collective-permute-start.20 = (f32[1,4,128]{2,1,0:T(4,128)S(1)}, f32[1,4,128]{2,1,0:T(4,128)S(1)}, u32[]{:S(2)}, u32[]{:S(2)}) collective-permute-start(f32[1,4,128]{2,1,0:T(4,128)S(1)} %get-tuple-element.304), channel_id=1, source_target_pairs={{0,16},{16,32},{32,48},{48,64},{64,80},{80,96},{96,112},{112,128},... | collective-permute-start | bytes 6152 | tf_op jit(solution)/shard_map/ppermute | solution.py:21
  102.0 12.9 %collective-permute-start.21 = (f32[1,4,128]{2,1,0:T(4,128)S(1)}, f32[1,4,128]{2,1,0:T(4,128)S(1)}, u32[]{:S(2)}, u32[]{:S(2)}) collective-permute-start(f32[1,4,128]{2,1,0:T(4,128)S(1)} %get-tuple-element.303), channel_id=1, source_target_pairs={{16,0},{32,16},{48,32},{64,48},{80,64},{96,80},{112,96},{128,112},... | collective-permute-start | bytes 6152 | tf_op jit(solution)/shard_map/ppermute | solution.py:21
  125.8 16.1 %collective-permute-start.28 = (f32[4,1,64]{2,1,0:T(1,128)S(1)}, f32[4,1,64]{2,1,0:T(1,128)S(1)}, u32[]{:S(2)}, u32[]{:S(2)}) collective-permute-start(f32[4,1,64]{2,1,0:T(1,128)S(1)} %get-tuple-element.292), channel_id=1, source_target_pairs={{0,2},{1,3},{2,4},{3,5},{4,6},{5,7},{6,8},{7,9},{8,10},{9,11},{10,... | collective-permute-start | bytes 3080 | tf_op jit(solution)/shard_map/ppermute | solution.py:21
  127.7 14.2 %collective-permute-start.29 = (f32[4,1,64]{2,1,0:T(1,128)S(1)}, f32[4,1,64]{2,1,0:T(1,128)S(1)}, u32[]{:S(2)}, u32[]{:S(2)}) collective-permute-start(f32[4,1,64]{2,1,0:T(1,128)S(1)} %get-tuple-element.291), channel_id=1, source_target_pairs={{2,0},{3,1},{4,2},{5,3},{6,4},{7,5},{8,6},{9,7},{10,8},{11,9},{12,... | collective-permute-start | bytes 3080 | tf_op jit(solution)/shard_map/ppermute | solution.py:21
  132.9 9.0 %collective-permute-start.26 = (f32[1,4,64]{2,1,0:T(4,128)S(1)}, f32[1,4,64]{2,1,0:T(4,128)S(1)}, u32[]{:S(2)}, u32[]{:S(2)}) collective-permute-start(f32[1,4,64]{2,1,0:T(4,128)S(1)} %get-tuple-element.139), channel_id=1, source_target_pairs={{0,32},{16,48},{32,64},{48,80},{64,96},{80,112},{96,128},{112,144}... | collective-permute-start | bytes 3080 | tf_op jit(solution)/shard_map/ppermute | solution.py:21
  143.2 16.2 %collective-permute-start.30 = (f32[1,4,64]{2,1,0:T(4,128)S(1)}, f32[1,4,64]{2,1,0:T(4,128)S(1)}, u32[]{:S(2)}, u32[]{:S(2)}) collective-permute-start(f32[1,4,64]{2,1,0:T(4,128)S(1)} %get-tuple-element.277), channel_id=1, source_target_pairs={{0,32},{16,48},{32,64},{48,80},{64,96},{80,112},{96,128},{112,144}... | collective-permute-start | bytes 3080 | tf_op jit(solution)/shard_map/ppermute | solution.py:21
  145.1 14.3 %collective-permute-start.31 = (f32[1,4,64]{2,1,0:T(4,128)S(1)}, f32[1,4,64]{2,1,0:T(4,128)S(1)}, u32[]{:S(2)}, u32[]{:S(2)}) collective-permute-start(f32[1,4,64]{2,1,0:T(4,128)S(1)} %get-tuple-element.278), channel_id=1, source_target_pairs={{32,0},{48,16},{64,32},{80,48},{96,64},{112,80},{128,96},{144,112}... | collective-permute-start | bytes 3080 | tf_op jit(solution)/shard_map/ppermute | solution.py:21
  160.9 16.2 %collective-permute-start.34 = (f32[1,4,64]{2,1,0:T(4,128)S(1)}, f32[1,4,64]{2,1,0:T(4,128)S(1)}, u32[]{:S(2)}, u32[]{:S(2)}) collective-permute-start(f32[1,4,64]{2,1,0:T(4,128)S(1)} %get-tuple-element.276), channel_id=1, source_target_pairs={{0,32},{16,48},{32,64},{48,80},{64,96},{80,112},{96,128},{112,144}... | collective-permute-start | bytes 3080 | tf_op jit(solution)/shard_map/ppermute | solution.py:21
  162.8 14.3 %collective-permute-start.35 = (f32[1,4,64]{2,1,0:T(4,128)S(1)}, f32[1,4,64]{2,1,0:T(4,128)S(1)}, u32[]{:S(2)}, u32[]{:S(2)}) collective-permute-start(f32[1,4,64]{2,1,0:T(4,128)S(1)} %get-tuple-element.275), channel_id=1, source_target_pairs={{32,0},{48,16},{64,32},{80,48},{96,64},{112,80},{128,96},{144,112}... | collective-permute-start | bytes 3080 | tf_op jit(solution)/shard_map/ppermute | solution.py:21
  190.9 18.7 %collective-permute-start.40 = (f32[1,4,32]{2,1,0:T(4,128)S(1)}, f32[1,4,32]{2,1,0:T(4,128)S(1)}, u32[]{:S(2)}, u32[]{:S(2)}) collective-permute-start(f32[1,4,32]{2,1,0:T(4,128)S(1)} %get-tuple-element.133), channel_id=1, source_target_pairs={{0,64},{16,80},{32,96},{48,112},{64,128},{80,144},{96,160},{112,17... | collective-permute-start | bytes 1544 | tf_op jit(solution)/shard_map/ppermute | solution.py:21
  194.3 15.3 %collective-permute-start.41 = (f32[1,4,32]{2,1,0:T(4,128)S(1)}, f32[1,4,32]{2,1,0:T(4,128)S(1)}, u32[]{:S(2)}, u32[]{:S(2)}) collective-permute-start(f32[1,4,32]{2,1,0:T(4,128)S(1)} %get-tuple-element.134), channel_id=1, source_target_pairs={{64,0},{80,16},{96,32},{112,48},{128,64},{144,80},{160,96},{176,11... | collective-permute-start | bytes 1544 | tf_op jit(solution)/shard_map/ppermute | solution.py:21
  211.0 18.9 %collective-permute-start.44 = (f32[1,4,32]{2,1,0:T(4,128)S(1)}, f32[1,4,32]{2,1,0:T(4,128)S(1)}, u32[]{:S(2)}, u32[]{:S(2)}) collective-permute-start(f32[1,4,32]{2,1,0:T(4,128)S(1)} %get-tuple-element.249), channel_id=1, source_target_pairs={{0,64},{16,80},{32,96},{48,112},{64,128},{80,144},{96,160},{112,17... | collective-permute-start | bytes 1544 | tf_op jit(solution)/shard_map/ppermute | solution.py:21
  213.5 16.4 %collective-permute-start.45 = (f32[1,4,32]{2,1,0:T(4,128)S(1)}, f32[1,4,32]{2,1,0:T(4,128)S(1)}, u32[]{:S(2)}, u32[]{:S(2)}) collective-permute-start(f32[1,4,32]{2,1,0:T(4,128)S(1)} %get-tuple-element.250), channel_id=1, source_target_pairs={{64,0},{80,16},{96,32},{112,48},{128,64},{144,80},{160,96},{176,11... | collective-permute-start | bytes 1544 | tf_op jit(solution)/shard_map/ppermute | solution.py:21
  221.7 8.3 %collective-permute-start.46 = (f32[4,1,32]{2,1,0:T(1,128)S(1)}, f32[4,1,32]{2,1,0:T(1,128)S(1)}, u32[]{:S(2)}, u32[]{:S(2)}) collective-permute-start(f32[4,1,32]{2,1,0:T(1,128)S(1)} %get-tuple-element.253), channel_id=1, source_target_pairs={{0,4},{1,5},{2,6},{3,7},{4,8},{5,9},{6,10},{7,11},{8,12},{9,13},{1... | collective-permute-start | bytes 1544 | tf_op jit(solution)/shard_map/ppermute | solution.py:21
  231.4 18.9 %collective-permute-start.48 = (f32[1,4,32]{2,1,0:T(4,128)S(1)}, f32[1,4,32]{2,1,0:T(4,128)S(1)}, u32[]{:S(2)}, u32[]{:S(2)}) collective-permute-start(f32[1,4,32]{2,1,0:T(4,128)S(1)} %get-tuple-element.239), channel_id=1, source_target_pairs={{0,64},{16,80},{32,96},{48,112},{64,128},{80,144},{96,160},{112,17... | collective-permute-start | bytes 1544 | tf_op jit(solution)/shard_map/ppermute | solution.py:21
  233.4 17.0 %collective-permute-start.49 = (f32[1,4,32]{2,1,0:T(4,128)S(1)}, f32[1,4,32]{2,1,0:T(4,128)S(1)}, u32[]{:S(2)}, u32[]{:S(2)}) collective-permute-start(f32[1,4,32]{2,1,0:T(4,128)S(1)} %get-tuple-element.240), channel_id=1, source_target_pairs={{64,0},{80,16},{96,32},{112,48},{128,64},{144,80},{160,96},{176,11... | collective-permute-start | bytes 1544 | tf_op jit(solution)/shard_map/ppermute | solution.py:21
  242.1 8.3 %collective-permute-start.50 = (f32[4,1,32]{2,1,0:T(1,128)S(1)}, f32[4,1,32]{2,1,0:T(1,128)S(1)}, u32[]{:S(2)}, u32[]{:S(2)}) collective-permute-start(f32[4,1,32]{2,1,0:T(1,128)S(1)} %get-tuple-element.243), channel_id=1, source_target_pairs={{0,4},{1,5},{2,6},{3,7},{4,8},{5,9},{6,10},{7,11},{8,12},{9,13},{1... | collective-permute-start | bytes 1544 | tf_op jit(solution)/shard_map/ppermute | solution.py:21
  251.8 18.9 %collective-permute-start.52 = (f32[1,4,32]{2,1,0:T(4,128)S(1)}, f32[1,4,32]{2,1,0:T(4,128)S(1)}, u32[]{:S(2)}, u32[]{:S(2)}) collective-permute-start(f32[1,4,32]{2,1,0:T(4,128)S(1)} %get-tuple-element.229), channel_id=1, source_target_pairs={{0,64},{16,80},{32,96},{48,112},{64,128},{80,144},{96,160},{112,17... | collective-permute-start | bytes 1544 | tf_op jit(solution)/shard_map/ppermute | solution.py:21
  253.7 17.0 %collective-permute-start.53 = (f32[1,4,32]{2,1,0:T(4,128)S(1)}, f32[1,4,32]{2,1,0:T(4,128)S(1)}, u32[]{:S(2)}, u32[]{:S(2)}) collective-permute-start(f32[1,4,32]{2,1,0:T(4,128)S(1)} %get-tuple-element.230), channel_id=1, source_target_pairs={{64,0},{80,16},{96,32},{112,48},{128,64},{144,80},{160,96},{176,11... | collective-permute-start | bytes 1544 | tf_op jit(solution)/shard_map/ppermute | solution.py:21
  262.4 8.3 %collective-permute-start.54 = (f32[4,1,32]{2,1,0:T(1,128)S(1)}, f32[4,1,32]{2,1,0:T(1,128)S(1)}, u32[]{:S(2)}, u32[]{:S(2)}) collective-permute-start(f32[4,1,32]{2,1,0:T(1,128)S(1)} %get-tuple-element.233), channel_id=1, source_target_pairs={{0,4},{1,5},{2,6},{3,7},{4,8},{5,9},{6,10},{7,11},{8,12},{9,13},{1... | collective-permute-start | bytes 1544 | tf_op jit(solution)/shard_map/ppermute | solution.py:21
  272.1 18.9 %collective-permute-start.56 = (f32[1,4,32]{2,1,0:T(4,128)S(1)}, f32[1,4,32]{2,1,0:T(4,128)S(1)}, u32[]{:S(2)}, u32[]{:S(2)}) collective-permute-start(f32[1,4,32]{2,1,0:T(4,128)S(1)} %get-tuple-element.219), channel_id=1, source_target_pairs={{0,64},{16,80},{32,96},{48,112},{64,128},{80,144},{96,160},{112,17... | collective-permute-start | bytes 1544 | tf_op jit(solution)/shard_map/ppermute | solution.py:21
  274.1 17.0 %collective-permute-start.57 = (f32[1,4,32]{2,1,0:T(4,128)S(1)}, f32[1,4,32]{2,1,0:T(4,128)S(1)}, u32[]{:S(2)}, u32[]{:S(2)}) collective-permute-start(f32[1,4,32]{2,1,0:T(4,128)S(1)} %get-tuple-element.220), channel_id=1, source_target_pairs={{64,0},{80,16},{96,32},{112,48},{128,64},{144,80},{160,96},{176,11... | collective-permute-start | bytes 1544 | tf_op jit(solution)/shard_map/ppermute | solution.py:21
  282.8 8.3 %collective-permute-start.58 = (f32[4,1,32]{2,1,0:T(1,128)S(1)}, f32[4,1,32]{2,1,0:T(1,128)S(1)}, u32[]{:S(2)}, u32[]{:S(2)}) collective-permute-start(f32[4,1,32]{2,1,0:T(1,128)S(1)} %get-tuple-element.223), channel_id=1, source_target_pairs={{0,4},{1,5},{2,6},{3,7},{4,8},{5,9},{6,10},{7,11},{8,12},{9,13},{1... | collective-permute-start | bytes 1544 | tf_op jit(solution)/shard_map/ppermute | solution.py:21
  292.5 18.9 %collective-permute-start.60 = (f32[1,4,32]{2,1,0:T(4,128)S(1)}, f32[1,4,32]{2,1,0:T(4,128)S(1)}, u32[]{:S(2)}, u32[]{:S(2)}) collective-permute-start(f32[1,4,32]{2,1,0:T(4,128)S(1)} %get-tuple-element.209), channel_id=1, source_target_pairs={{0,64},{16,80},{32,96},{48,112},{64,128},{80,144},{96,160},{112,17... | collective-permute-start | bytes 1544 | tf_op jit(solution)/shard_map/ppermute | solution.py:21
  294.4 17.0 %collective-permute-start.61 = (f32[1,4,32]{2,1,0:T(4,128)S(1)}, f32[1,4,32]{2,1,0:T(4,128)S(1)}, u32[]{:S(2)}, u32[]{:S(2)}) collective-permute-start(f32[1,4,32]{2,1,0:T(4,128)S(1)} %get-tuple-element.210), channel_id=1, source_target_pairs={{64,0},{80,16},{96,32},{112,48},{128,64},{144,80},{160,96},{176,11... | collective-permute-start | bytes 1544 | tf_op jit(solution)/shard_map/ppermute | solution.py:21
  303.1 8.3 %collective-permute-start.62 = (f32[4,1,32]{2,1,0:T(1,128)S(1)}, f32[4,1,32]{2,1,0:T(1,128)S(1)}, u32[]{:S(2)}, u32[]{:S(2)}) collective-permute-start(f32[4,1,32]{2,1,0:T(1,128)S(1)} %get-tuple-element.213), channel_id=1, source_target_pairs={{0,4},{1,5},{2,6},{3,7},{4,8},{5,9},{6,10},{7,11},{8,12},{9,13},{1... | collective-permute-start | bytes 1544 | tf_op jit(solution)/shard_map/ppermute | solution.py:21
  312.8 18.9 %collective-permute-start.64 = (f32[1,4,32]{2,1,0:T(4,128)S(1)}, f32[1,4,32]{2,1,0:T(4,128)S(1)}, u32[]{:S(2)}, u32[]{:S(2)}) collective-permute-start(f32[1,4,32]{2,1,0:T(4,128)S(1)} %get-tuple-element.199), channel_id=1, source_target_pairs={{0,64},{16,80},{32,96},{48,112},{64,128},{80,144},{96,160},{112,17... | collective-permute-start | bytes 1544 | tf_op jit(solution)/shard_map/ppermute | solution.py:21
  314.8 17.0 %collective-permute-start.65 = (f32[1,4,32]{2,1,0:T(4,128)S(1)}, f32[1,4,32]{2,1,0:T(4,128)S(1)}, u32[]{:S(2)}, u32[]{:S(2)}) collective-permute-start(f32[1,4,32]{2,1,0:T(4,128)S(1)} %get-tuple-element.200), channel_id=1, source_target_pairs={{64,0},{80,16},{96,32},{112,48},{128,64},{144,80},{160,96},{176,11... | collective-permute-start | bytes 1544 | tf_op jit(solution)/shard_map/ppermute | solution.py:21
  323.5 8.3 %collective-permute-start.66 = (f32[4,1,32]{2,1,0:T(1,128)S(1)}, f32[4,1,32]{2,1,0:T(1,128)S(1)}, u32[]{:S(2)}, u32[]{:S(2)}) collective-permute-start(f32[4,1,32]{2,1,0:T(1,128)S(1)} %get-tuple-element.203), channel_id=1, source_target_pairs={{0,4},{1,5},{2,6},{3,7},{4,8},{5,9},{6,10},{7,11},{8,12},{9,13},{1... | collective-permute-start | bytes 1544 | tf_op jit(solution)/shard_map/ppermute | solution.py:21
  333.2 18.9 %collective-permute-start.68 = (f32[1,4,32]{2,1,0:T(4,128)S(1)}, f32[1,4,32]{2,1,0:T(4,128)S(1)}, u32[]{:S(2)}, u32[]{:S(2)}) collective-permute-start(f32[1,4,32]{2,1,0:T(4,128)S(1)} %get-tuple-element.198), channel_id=1, source_target_pairs={{0,64},{16,80},{32,96},{48,112},{64,128},{80,144},{96,160},{112,17... | collective-permute-start | bytes 1544 | tf_op jit(solution)/shard_map/ppermute | solution.py:21
  335.2 17.0 %collective-permute-start.69 = (f32[1,4,32]{2,1,0:T(4,128)S(1)}, f32[1,4,32]{2,1,0:T(4,128)S(1)}, u32[]{:S(2)}, u32[]{:S(2)}) collective-permute-start(f32[1,4,32]{2,1,0:T(4,128)S(1)} %get-tuple-element.197), channel_id=1, source_target_pairs={{64,0},{80,16},{96,32},{112,48},{128,64},{144,80},{160,96},{176,11... | collective-permute-start | bytes 1544 | tf_op jit(solution)/shard_map/ppermute | solution.py:21
  343.9 8.3 %collective-permute-start.70 = (f32[4,1,32]{2,1,0:T(1,128)S(1)}, f32[4,1,32]{2,1,0:T(1,128)S(1)}, u32[]{:S(2)}, u32[]{:S(2)}) collective-permute-start(f32[4,1,32]{2,1,0:T(1,128)S(1)} %get-tuple-element.194), channel_id=1, source_target_pairs={{0,4},{1,5},{2,6},{3,7},{4,8},{5,9},{6,10},{7,11},{8,12},{9,13},{1... | collective-permute-start | bytes 1544 | tf_op jit(solution)/shard_map/ppermute | solution.py:21
  353.9 16.5 %collective-permute-start.72 = (f32[1,4,64]{2,1,0:T(4,128)S(1)}, f32[1,4,64]{2,1,0:T(4,128)S(1)}, u32[]{:S(2)}, u32[]{:S(2)}) collective-permute-start(f32[1,4,64]{2,1,0:T(4,128)S(1)} %get-tuple-element.177), channel_id=1, source_target_pairs={{0,32},{16,48},{32,64},{48,80},{64,96},{80,112},{96,128},{112,144}... | collective-permute-start | bytes 3080 | tf_op jit(solution)/shard_map/ppermute | solution.py:21
  355.8 14.6 %collective-permute-start.73 = (f32[1,4,64]{2,1,0:T(4,128)S(1)}, f32[1,4,64]{2,1,0:T(4,128)S(1)}, u32[]{:S(2)}, u32[]{:S(2)}) collective-permute-start(f32[1,4,64]{2,1,0:T(4,128)S(1)} %get-tuple-element.178), channel_id=1, source_target_pairs={{32,0},{48,16},{64,32},{80,48},{96,64},{112,80},{128,96},{144,112}... | collective-permute-start | bytes 3080 | tf_op jit(solution)/shard_map/ppermute | solution.py:21
  371.8 16.4 %collective-permute-start.76 = (f32[1,4,64]{2,1,0:T(4,128)S(1)}, f32[1,4,64]{2,1,0:T(4,128)S(1)}, u32[]{:S(2)}, u32[]{:S(2)}) collective-permute-start(f32[1,4,64]{2,1,0:T(4,128)S(1)} %get-tuple-element.176), channel_id=1, source_target_pairs={{0,32},{16,48},{32,64},{48,80},{64,96},{80,112},{96,128},{112,144}... | collective-permute-start | bytes 3080 | tf_op jit(solution)/shard_map/ppermute | solution.py:21
  373.7 14.5 %collective-permute-start.77 = (f32[1,4,64]{2,1,0:T(4,128)S(1)}, f32[1,4,64]{2,1,0:T(4,128)S(1)}, u32[]{:S(2)}, u32[]{:S(2)}) collective-permute-start(f32[1,4,64]{2,1,0:T(4,128)S(1)} %get-tuple-element.175), channel_id=1, source_target_pairs={{32,0},{48,16},{64,32},{80,48},{96,64},{112,80},{128,96},{144,112}... | collective-permute-start | bytes 3080 | tf_op jit(solution)/shard_map/ppermute | solution.py:21
  389.8 14.8 %collective-permute-start.80 = (f32[1,4,128]{2,1,0:T(4,128)S(1)}, f32[1,4,128]{2,1,0:T(4,128)S(1)}, u32[]{:S(2)}, u32[]{:S(2)}) collective-permute-start(f32[1,4,128]{2,1,0:T(4,128)S(1)} %get-tuple-element.155), channel_id=1, source_target_pairs={{0,16},{16,32},{32,48},{48,64},{64,80},{80,96},{96,112},{112,128},... | collective-permute-start | bytes 6152 | tf_op jit(solution)/shard_map/ppermute | solution.py:21
  391.7 12.9 %collective-permute-start.81 = (f32[1,4,128]{2,1,0:T(4,128)S(1)}, f32[1,4,128]{2,1,0:T(4,128)S(1)}, u32[]{:S(2)}, u32[]{:S(2)}) collective-permute-start(f32[1,4,128]{2,1,0:T(4,128)S(1)} %get-tuple-element.156), channel_id=1, source_target_pairs={{16,0},{32,16},{48,32},{64,48},{80,64},{96,80},{112,96},{128,112},... | collective-permute-start | bytes 6152 | tf_op jit(solution)/shard_map/ppermute | solution.py:21
  406.0 14.8 %collective-permute-start.84 = (f32[1,4,128]{2,1,0:T(4,128)S(1)}, f32[1,4,128]{2,1,0:T(4,128)S(1)}, u32[]{:S(2)}, u32[]{:S(2)}) collective-permute-start(f32[1,4,128]{2,1,0:T(4,128)S(1)} %get-tuple-element.145), channel_id=1, source_target_pairs={{0,16},{16,32},{32,48},{48,64},{64,80},{80,96},{96,112},{112,128},... | collective-permute-start | bytes 6152 | tf_op jit(solution)/shard_map/ppermute | solution.py:21
  408.0 12.9 %collective-permute-start.85 = (f32[1,4,128]{2,1,0:T(4,128)S(1)}, f32[1,4,128]{2,1,0:T(4,128)S(1)}, u32[]{:S(2)}, u32[]{:S(2)}) collective-permute-start(f32[1,4,128]{2,1,0:T(4,128)S(1)} %get-tuple-element.146), channel_id=1, source_target_pairs={{16,0},{32,16},{48,32},{64,48},{80,64},{96,80},{112,96},{128,112},... | collective-permute-start | bytes 6152 | tf_op jit(solution)/shard_map/ppermute | solution.py:21
  423.1 14.8 %collective-permute-start.90 = (f32[8,1,256]{2,0,1:T(8,128)S(1)}, f32[8,1,256]{2,0,1:T(8,128)S(1)}, u32[]{:S(2)}, u32[]{:S(2)}) collective-permute-start(f32[8,1,256]{2,0,1:T(8,128)S(1)} %copy.358), channel_id=1, source_target_pairs={{0,1},{1,2},{2,3},{3,4},{4,5},{5,6},{6,7},{7,8},{8,9},{9,10},{10,1... | collective-permute-start | bytes 24584 | tf_op jit(solution)/shard_map/ppermute | solution.py:21
  425.0 12.9 %collective-permute-start.91 = (f32[8,1,256]{2,0,1:T(8,128)S(1)}, f32[8,1,256]{2,0,1:T(8,128)S(1)}, u32[]{:S(2)}, u32[]{:S(2)}) collective-permute-start(f32[8,1,256]{2,0,1:T(8,128)S(1)} %copy.360), channel_id=1, source_target_pairs={{1,0},{2,1},{3,2},{4,3},{5,4},{6,5},{7,6},{8,7},{9,8},{10,9},{11,1... | collective-permute-start | bytes 24584 | tf_op jit(solution)/shard_map/ppermute | solution.py:21
  439.4 15.1 %collective-permute-start.94 = (f32[8,1,256]{2,0,1:T(8,128)S(1)}, f32[8,1,256]{2,0,1:T(8,128)S(1)}, u32[]{:S(2)}, u32[]{:S(2)}) collective-permute-start(f32[8,1,256]{2,0,1:T(8,128)S(1)} %copy.362), channel_id=1, source_target_pairs={{0,1},{1,2},{2,3},{3,4},{4,5},{5,6},{6,7},{7,8},{8,9},{9,10},{10,1... | collective-permute-start | bytes 24584 | tf_op jit(solution)/shard_map/ppermute | solution.py:21
  441.4 13.1 %collective-permute-start.95 = (f32[8,1,256]{2,0,1:T(8,128)S(1)}, f32[8,1,256]{2,0,1:T(8,128)S(1)}, u32[]{:S(2)}, u32[]{:S(2)}) collective-permute-start(f32[8,1,256]{2,0,1:T(8,128)S(1)} %copy.364), channel_id=1, source_target_pairs={{1,0},{2,1},{3,2},{4,3},{5,4},{6,5},{7,6},{8,7},{9,8},{10,9},{11,1... | collective-permute-start | bytes 24584 | tf_op jit(solution)/shard_map/ppermute | solution.py:21
  446.2 8.3 %collective-permute-start.92 = (f32[1,8,256]{2,1,0:T(8,128)S(1)}, f32[1,8,256]{2,1,0:T(8,128)S(1)}, u32[]{:S(2)}, u32[]{:S(2)}) collective-permute-start(f32[1,8,256]{2,1,0:T(8,128)S(1)} %get-tuple-element.83), channel_id=1, source_target_pairs={{0,16},{16,32},{32,48},{48,64},{64,80},{80,96},{96,112},{112,128},... | collective-permute-start | bytes 24584 | tf_op jit(solution)/shard_map/ppermute | solution.py:21
  456.1 15.7 %collective-permute-start.98 = (f32[8,1,256]{2,0,1:T(8,128)S(1)}, f32[8,1,256]{2,0,1:T(8,128)S(1)}, u32[]{:S(2)}, u32[]{:S(2)}) collective-permute-start(f32[8,1,256]{2,0,1:T(8,128)S(1)} %copy.366), channel_id=1, source_target_pairs={{0,1},{1,2},{2,3},{3,4},{4,5},{5,6},{6,7},{7,8},{8,9},{9,10},{10,1... | collective-permute-start | bytes 24584 | tf_op jit(solution)/shard_map/ppermute | solution.py:21
  458.0 13.8 %collective-permute-start.99 = (f32[8,1,256]{2,0,1:T(8,128)S(1)}, f32[8,1,256]{2,0,1:T(8,128)S(1)}, u32[]{:S(2)}, u32[]{:S(2)}) collective-permute-start(f32[8,1,256]{2,0,1:T(8,128)S(1)} %copy.368), channel_id=1, source_target_pairs={{1,0},{2,1},{3,2},{4,3},{5,4},{6,5},{7,6},{8,7},{9,8},{10,9},{11,1... | collective-permute-start | bytes 24584 | tf_op jit(solution)/shard_map/ppermute | solution.py:21
  462.9 9.0 %collective-permute-start.96 = (f32[1,8,256]{2,1,0:T(8,128)S(1)}, f32[1,8,256]{2,1,0:T(8,128)S(1)}, u32[]{:S(2)}, u32[]{:S(2)}) collective-permute-start(f32[1,8,256]{2,1,0:T(8,128)S(1)} %get-tuple-element.82), channel_id=1, source_target_pairs={{0,16},{16,32},{32,48},{48,64},{64,80},{80,96},{96,112},{112,128},... | collective-permute-start | bytes 24584 | tf_op jit(solution)/shard_map/ppermute | solution.py:21
  (38 other events, 290.7 us)
where the time goes:
time: 477 us; the launch traced here: 473 us
  starting transfers between devices  404 us (85%)
  waiting for transfers between devices  38.2 us (8%)
  local copies, waits for them, and re-layouts  18.7 us (4%)
  other arithmetic  9.17 us (2%)
    ppermute x96, starting transfers between devices, passed_along(): lax.ppermute(value, axis, [(source, source + steps) for source in range(l...  396 us
    ppermute x96, waiting for transfers between devices, passed_along(): lax.ppermute(value, axis, [(source, source + steps) for source in range(l...  25.4 us
    ppermute x4, waiting for transfers between devices, swapped(): return lax.ppermute(block, axis, route)  12.8 us
    reshape x4, local copies, waits for them, and re-layouts, coarsen(): grid_values.reshape(size_x // 2, 2, size_y // 2, 2, size_z // 2, 2)  12.5 us
  transfers between devices with their start and end apart: 100, of which 25 were waited for; matrix products, arithmetic and copies ran while one was open for 4% of the time, Pallas kernels for 0%

commit v1 on v0

v1 whole, which is shorter than its diff:
```python
import jax
import jax.numpy as jnp
from jax import lax
from jax.experimental import pallas as pl
from jax.experimental.pallas import tpu as pltpu
from jax.sharding import PartitionSpec as P

INTERPRET = False
COARSE_STEPS = 8
F32 = jnp.float32
HIGHEST = lax.Precision.HIGHEST
VMEM_LIMIT = 56 * 1024 * 1024


def step_factors(low_end, steps):
    center, radius = 0.5 * (2.0 + low_end), 0.5 * (2.0 - low_end)
    sigma = center / radius
    ratio = 1.0 / sigma
    factors = [(0.0, 1.0 / center)]
    for _ in range(steps - 1):
        ratio_next = 1.0 / (2.0 * sigma - ratio)
        factors.append((ratio_next * ratio, 2.0 * ratio_next / radius))
        ratio = ratio_next
    return factors


(_, FIRST), (KEEP, ADD) = step_factors(0.4, 2)
COARSE_FACTORS = step_factors(0.02, COARSE_STEPS)


def iota(shape, dim):
    return lax.broadcasted_iota(jnp.int32, shape, dim)


def shifted(value, step, axis):
    return pltpu.roll(value, (-step) % value.shape[axis], axis)


def dot(a, b):
    return jnp.dot(a, b, precision=HIGHEST, preferred_element_type=F32)


def ones_where(condition):
    return jnp.where(condition, 1.0, 0.0).astype(F32)


def planes(first, last, step):
    def one(index, carry):
        step(index)
        return carry

    lax.fori_loop(first, last, one, 0)


def near(ref, index):
    plane = ref[index]
    return (ref[index - 1], ref[index + 1], shifted(plane, -1, 0), shifted(plane, 1, 0),
            shifted(plane, -1, 1), shifted(plane, 1, 1))


def near_inside(ref, index):
    x_low, x_high, y_low, y_high, z_low, z_high = near(ref, index)
    lane = iota(z_low.shape, 1)
    z_low = jnp.where(lane == 0, 0.0, z_low)
    z_high = jnp.where(lane == z_low.shape[1] - 1, 0.0, z_high)
    return x_low, x_high, y_low, y_high, z_low, z_high


def coupling(center, around, masked):
    total = 6.0 * center
    for value in around:
        total = total + value
    half_inverse = jnp.where(center > 0.0, 1.0 / jnp.where(center > 0.0, total, 1.0), 0.0)
    couplings = []
    for number, value in enumerate(around):
        c = (center + value) * half_inverse
        couplings.append(jnp.where(value > 0.0, c, 0.0) if number in masked else c)
    return couplings, 2.0 * half_inverse, 0.5 * total


def spread(c_ref, c_index, around):
    total = c_ref[0, c_index] * around[0]
    for number in range(1, 6):
        total = total + c_ref[number, c_index] * around[number]
    return total


def fine_kernel(low_ref, own_ref, high_ref, gather_ref, share_ref, x0_ref,
                k0, c0, diag0, g0, d0, e0, sums, zsums, k1, f1, c1, diag1, g1, d1, e1, out):
    def join(index):
        k0[index] = jnp.concatenate([low_ref[index], own_ref[index], high_ref[index]], 0)

    planes(0, 22, join)

    def setup(index):
        couplings, inverse, diagonal = coupling(k0[index + 1], near_inside(k0, index + 1), (4, 5))
        for number in range(6):
            c0[number, index] = couplings[number]
        diag0[index] = diagonal
        force = jnp.concatenate([low_ref[index + 22], own_ref[index + 22], high_ref[index + 22]], 0)
        scaled = inverse * force
        g0[index] = scaled
        d0[index] = FIRST * scaled

    planes(0, 20, setup)

    def second(index):
        scaled = g0[index] - d0[index] + spread(c0, index, near(d0, index))
        g0[index] = scaled
        e0[index] = KEEP * d0[index] + ADD * scaled

    planes(1, 19, second)

    def guess(index):
        total = d0[index + 3] + e0[index + 3]
        x0_ref[index] = shifted(total, 4, 0)[0:16]

    planes(0, 14, guess)

    def left(index):
        return diag0[index] * (g0[index] - e0[index] + spread(c0, index, near(e0, index)))

    def pair(index):
        sums[index] = 0.5 * (left(2 * index + 2) + left(2 * index + 3))

    planes(0, 8, pair)

    def pair_k(index):
        sums[index + 8] = 0.125 * (k0[2 * index + 1] + k0[2 * index + 2])

    planes(0, 10, pair_k)
    fold = ones_where(iota((256, 128), 0) // 2 == iota((256, 128), 1))
    zsums[...] = dot(sums[...].reshape(18 * 24, 256), fold).reshape(18, 24, 128)

    k1[...] = jnp.zeros_like(k1)
    f1[...] = jnp.zeros_like(f1)

    def halve(index):
        rows = zsums[index, pl.ds(0, 12, stride=2), :] + zsums[index, pl.ds(1, 12, stride=2), :]

        @pl.when(index < 8)
        def _():
            f1[index, 2:14, :] = rows

        @pl.when(index >= 8)
        def _():
            k1[index - 8, 2:14, :] = rows

    planes(0, 18, halve)

    def share(index):
        share_ref[index] = k1[index + 1, 4:12, :]
        share_ref[index + 8] = f1[index, 4:12, :]

    planes(0, 8, share)

    def setup1(index):
        couplings, inverse, diagonal = coupling(k1[index + 1], near_inside(k1, index + 1), (4, 5))
        for number in range(6):
            c1[number, index] = couplings[number]
        diag1[index] = diagonal
        scaled = inverse * f1[index]
        g1[index] = scaled
        d1[index] = FIRST * scaled

    planes(0, 8, setup1)

    def second1(index):
        scaled = g1[index] - d1[index] + spread(c1, index, near(d1, index))
        g1[index] = scaled
        e1[index] = KEEP * d1[index] + ADD * scaled

    planes(1, 7, second1)

    def left1(index):
        return diag1[index] * (g1[index] - e1[index] + spread(c1, index, near(e1, index)))

    for half in range(2):
        out[half] = 0.5 * (left1(2 * half + 2) + left1(2 * half + 3))
        out[half + 2] = 0.125 * (k1[2 * half + 3] + k1[2 * half + 4])
    row, lane = iota((128, 256), 0), iota((128, 256), 1)
    fold = ones_where((lane == row // 2) | (lane == 192 + row // 2))
    folded = dot(out[...].reshape(64, 128), fold).reshape(4, 16, 256)
    for number in range(4):
        gather_ref[number:number + 1, :] = (folded[number, 6:7, 0:128] + folded[number, 7:8, 0:128]
                                            + folded[number, 8:9, 128:256] + folded[number, 9:10, 128:256])


def near2(ref, index):
    plane = ref[index]
    swapped = shifted(plane, 64, 1)
    first = iota(plane.shape, 1) < 64
    y_low = jnp.where(first, shifted(swapped, -1, 0), swapped)
    y_high = jnp.where(first, swapped, shifted(swapped, 1, 0))
    return ref[index - 1], ref[index + 1], y_low, y_high, shifted(plane, -1, 1), shifted(plane, 1, 1)


def near2_inside(ref, index):
    x_low, x_high, y_low, y_high, z_low, z_high = near2(ref, index)
    lane, row, rows = iota(z_low.shape, 1), iota(z_low.shape, 0), z_low.shape[0]
    y_low = jnp.where((row == 0) & (lane < 64), 0.0, y_low)
    y_high = jnp.where((row == rows - 1) & (lane >= 64), 0.0, y_high)
    z_low = jnp.where(lane % 64 == 0, 0.0, z_low)
    z_high = jnp.where(lane % 64 == 63, 0.0, z_high)
    return x_low, x_high, y_low, y_high, z_low, z_high


def near3(values, index, count):
    plane = values[index]
    x_low = values[index - 1] if index else shifted(values[count - 1], -32, 1)
    x_high = values[index + 1] if index + 1 < count else shifted(values[0], 32, 1)
    return (x_low, x_high, shifted(plane, -1, 0), shifted(plane, 1, 0),
            shifted(plane, -1, 1), shifted(plane, 1, 1))


def near3_inside(values, index, count):
    x_low, x_high, y_low, y_high, z_low, z_high = near3(values, index, count)
    lane, row, rows = iota(z_low.shape, 1), iota(z_low.shape, 0), z_low.shape[0]
    if index == 0:
        x_low = jnp.where(lane < 32, 0.0, x_low)
    if index == count - 1:
        x_high = jnp.where(lane >= 96, 0.0, x_high)
    y_low = jnp.where(row == 0, 0.0, y_low)
    y_high = jnp.where(row == rows - 1, 0.0, y_high)
    z_low = jnp.where(lane % 32 == 0, 0.0, z_low)
    z_high = jnp.where(lane % 32 == 31, 0.0, z_high)
    return x_low, x_high, y_low, y_high, z_low, z_high


def make_coarse_kernel(count_x, count_y):
    planes2, rows, count3 = 2 * count_x, count_y, count_x // 4

    def coarse_kernel(place_ref, data_ref, near_ref,
                      k2, c2, diag2, g2, d2, e2, sums, c3, h3, e3, x0, u0, u1):
        for ref in (k2, g2, d2, e2):
            for end in range(4):
                ref[end] = jnp.zeros((rows, 128), F32)
                ref[planes2 + 4 + end] = jnp.zeros((rows, 128), F32)
        for number in range(6):
            for end in range(4):
                c2[number, end] = jnp.zeros((rows, 128), F32)
                c2[number, planes2 + 4 + end] = jnp.zeros((rows, 128), F32)

        def load(index):
            for half in range(2):
                start = index * (4 * rows) + half
                k2[2 * index + half + 4] = data_ref[pl.ds(start + 2, rows, stride=4), :]
                e2[2 * index + half + 4] = data_ref[pl.ds(start, rows, stride=4), :]

        planes(0, count_x, load)

        def setup(index):
            couplings, inverse, diagonal = coupling(k2[index], near2_inside(k2, index), (2, 3, 4, 5))
            for number in range(6):
                c2[number, index] = couplings[number]
            diag2[index] = diagonal
            scaled = inverse * e2[index]
            g2[index] = scaled
            d2[index] = FIRST * scaled

        planes(4, planes2 + 4, setup)

        def second(index):
            scaled = g2[index] - d2[index] + spread(c2, index, near2(d2, index))
            u0[index] = scaled
            e2[index] = KEEP * d2[index] + ADD * scaled

        planes(4, planes2 + 4, second)

        def left(index):
            return diag2[index] * (u0[index] - e2[index] + spread(c2, index, near2(e2, index)))

        def pair(index):
            sums[index] = 0.5 * (left(2 * index + 4) + left(2 * index + 5))
            sums[index + count_x] = 0.125 * (k2[2 * index + 4] + k2[2 * index + 5])

        planes(0, count_x, pair)

        f3 = jnp.zeros((count3 * rows, 128), F32)
        k3 = jnp.zeros((count3 * rows, 128), F32)
        row, lane = iota((128, 128), 0), iota((128, 128), 1)
        for quarter in range(4):
            fold = ones_where(lane == 32 * quarter + (row % 64) // 2)
            part = sums[pl.ds(quarter * count3, count3)].reshape(count3 * rows, 128)
            f3 = f3 + dot(part, fold)
            part = sums[pl.ds(count_x + quarter * count3, count3)].reshape(count3 * rows, 128)
            k3 = k3 + dot(part, fold)
        f3 = f3.reshape(count3, rows, 128)
        k3 = k3.reshape(count3, rows, 128)

        g3, d3, total = [], [], []
        for index in range(count3):
            around = near3_inside([k3[i] for i in range(count3)], index, count3)
            couplings, inverse, _ = coupling(k3[index], around, (0, 1, 2, 3, 4, 5))
            for number in range(6):
                c3[number, index] = couplings[number]
            scaled = inverse * f3[index]
            g3.append(scaled)
            d3.append(COARSE_FACTORS[0][1] * scaled)
            total.append(d3[-1])
        for keep, add in COARSE_FACTORS[1:]:
            d3_new = []
            for index in range(count3):
                g3[index] = g3[index] - d3[index] + spread(c3, index, near3(d3, index, count3))
                d3_new.append(keep * d3[index] + add * g3[index])
                total[index] = total[index] + d3_new[-1]
            d3 = d3_new
        for index in range(count3):
            e3[index] = total[index]

        at_x, at_y = place_ref[0], place_ref[1]
        base = 2 * at_x
        parts = []
        for number in range(5):
            x3 = at_x - 2 + number
            inside = (x3 >= 0) & (x3 < count_x)
            safe = jnp.clip(x3, 0, count_x - 1)
            plane = pltpu.roll(e3[safe % count3], (128 - 32 * (safe // count3)) % 128, 1)
            parts.append(jnp.where(inside, plane, 0.0))
        unfold = ones_where((row < 32) & ((lane % 64) // 2 == row))
        up = dot(jnp.concatenate(parts, 0), unfold).reshape(5, rows, 128)
        for index in range(10):
            x0[index] = d2[base + index] + e2[base + index] + up[index // 2]
        for index in range(1, 9):
            u0[index] = g2[base + index] - x0[index] + spread(c2, base + index, near2(x0, index))
        for index in range(1, 9):
            u1[index] = FIRST * u0[index]
        for index in range(2, 8):
            scaled = u0[index] - u1[index] + spread(c2, base + index, near2(u1, index))
            x0[index] = x0[index] + (1.0 + KEEP) * u1[index] + ADD * scaled

        widen = ones_where((iota((128, 256), 0) == 64 * (iota((128, 256), 1) // 128) + (iota((128, 256), 1) % 128) // 2))
        wide = dot(x0[2:8].reshape(6 * rows, 128), widen)
        target, source = iota((16, rows), 0), iota((16, rows), 1)
        inside = (target >= 2) & (target < 14) & (source == at_y - 1 + (target - 2) // 4)
        first = ones_where(inside & ((target - 2) % 4 < 2))
        other = ones_where(inside & ((target - 2) % 4 >= 2))
        for index in range(6):
            block = wide[index * rows:(index + 1) * rows]
            near_ref[index] = dot(first, block[:, 0:128]) + dot(other, block[:, 128:256])

    return coarse_kernel


def post_kernel(near_ref, low1_ref, own1_ref, high1_ref, low_ref, own_ref, high_ref, x0_ref,
                correction_ref, residual_ref,
                k1, c1, g1, d1, h1, x1, wide, k0, c0, diag0, g0, y0, d0, h0):
    def join(ref_index):
        row = iota((8, 128), 0)
        middle = shifted(own1_ref[ref_index], 4, 0)
        return jnp.concatenate([jnp.where(row < 6, low1_ref[ref_index], middle),
                                jnp.where(row < 2, middle, high1_ref[ref_index])], 0)

    def load(index):
        k1[index] = join(index)

    planes(0, 16, load)

    def setup1(index):
        couplings, inverse, _ = coupling(k1[index], near_inside(k1, index), (4, 5))
        for number in range(6):
            c1[number, index] = couplings[number]
        scaled = inverse * join(index + 16)
        g1[index] = scaled
        d1[index] = FIRST * scaled

    planes(1, 15, setup1)

    def guess1(index):
        scaled = g1[index] - d1[index] + spread(c1, index, near(d1, index))
        x1[index] = (1.0 + KEEP) * d1[index] + ADD * scaled + near_ref[index // 2 - 1]

    planes(2, 14, guess1)

    def first1(index):
        scaled = g1[index] - x1[index] + spread(c1, index, near(x1, index))
        h1[index] = scaled
        d1[index] = FIRST * scaled

    planes(3, 13, first1)

    def second1(index):
        scaled = h1[index] - d1[index] + spread(c1, index, near(d1, index))
        value = x1[index] + (1.0 + KEEP) * d1[index] + ADD * scaled
        wide[index - 4, pl.ds(0, 8, stride=2), :] = value[4:12]
        wide[index - 4, pl.ds(1, 8, stride=2), :] = value[4:12]

    planes(4, 12, second1)
    unfold = ones_where(iota((128, 256), 0) == iota((128, 256), 1) // 2)
    up = dot(wide[...].reshape(128, 128), unfold).reshape(8, 16, 256)

    for index in range(1, 15):
        y0[index] = x0_ref[index - 1] + up[index // 2]

    def cut(ref_index):
        both = jnp.concatenate([low_ref[ref_index], own_ref[ref_index], high_ref[ref_index]], 0)
        return shifted(both, 4, 0)[0:16]

    def load0(index):
        k0[index] = cut(index + 3)

    planes(1, 15, load0)

    def setup0(index):
        couplings, inverse, diagonal = coupling(k0[index], near_inside(k0, index), (4, 5))
        for number in range(6):
            c0[number, index] = couplings[number]
        diag0[index] = diagonal
        scaled = inverse * cut(index + 24) - y0[index] + spread(c0, index, near(y0, index))
        g0[index] = scaled
        d0[index] = FIRST * scaled

    planes(2, 14, setup0)

    def second0(index):
        scaled = g0[index] - d0[index] + spread(c0, index, near(d0, index))
        g0[index] = scaled
        h0[index] = KEEP * d0[index] + ADD * scaled

    planes(3, 13, second0)

    def last0(index):
        value = y0[index] + d0[index] + h0[index]
        correction_ref[index - 4] = value[4:12]
        scaled = g0[index] - h0[index] + spread(c0, index, near(h0, index))
        residual_ref[index - 4] = (diag0[index] * scaled)[4:12]

    planes(4, 12, last0)


def call(kernel, shapes, scratch, *operands, scalars=0):
    specs = [pl.BlockSpec(memory_space=pltpu.SMEM)] * scalars
    specs += [pl.BlockSpec(memory_space=pltpu.VMEM)] * (len(operands) - scalars)
    return pl.pallas_call(
        kernel,
        out_shape=[jax.ShapeDtypeStruct(shape, F32) for shape in shapes],
        in_specs=specs,
        out_specs=[pl.BlockSpec(memory_space=pltpu.VMEM)] * len(shapes),
        scratch_shapes=[pltpu.VMEM(shape, F32) for shape in scratch],
        compiler_params=pltpu.CompilerParams(vmem_limit_bytes=VMEM_LIMIT),
        interpret=INTERPRET,
    )(*operands)


def both_sides(value, axis):
    count = lax.axis_size(axis)
    low = lax.ppermute(value, axis, [(i, i + 1) for i in range(count - 1)])
    high = lax.ppermute(value, axis, [(i + 1, i) for i in range(count - 1)])
    return low, high


def body(forcing, coefficient):
    count_x, count_y = lax.axis_size("gx"), lax.axis_size("gy")
    block = jnp.concatenate([coefficient, forcing], 0)
    low, high = both_sides(block, "gx")
    own = jnp.concatenate([low[1:8], coefficient, high[0:7], low[10:16], forcing, high[8:14]], 0)
    low, high = both_sides(own, "gy")

    full, full1 = (24, 256), (16, 128)
    payload, share, guess = call(
        fine_kernel,
        [(4, 128), (16, 8, 128), (14, 16, 256)],
        [(22, *full), (6, 20, *full)] + [(20, *full)] * 4 + [(18, *full), (18, 24, 128)]
        + [(10, *full1), (8, *full1), (6, 8, *full1)] + [(8, *full1)] * 4 + [(4, *full1)],
        low, own, high)

    copies = jnp.broadcast_to(payload[None], (count_x * count_y, *payload.shape))
    everything = lax.all_to_all(copies, ("gx", "gy"), 0, 0).reshape(-1, 128)

    low1, high1 = both_sides(share, "gx")
    own1 = jnp.concatenate([low1[0:6], share[2:6], high1[2:8], low1[8:14], share[10:14], high1[10:16]], 0)
    low1, high1 = both_sides(own1, "gy")

    place = jnp.stack([lax.axis_index("gx"), lax.axis_index("gy")]).astype(jnp.int32)
    padded = 2 * count_x + 8
    plane2 = (count_y, 128)
    near_e, = call(
        make_coarse_kernel(count_x, count_y),
        [(6, 16, 128)],
        [(padded, *plane2), (6, padded, *plane2)] + [(padded, *plane2)] * 4
        + [(2 * count_x, *plane2), (6, count_x // 4, *plane2)] + [(count_x // 4, *plane2)] * 2
        + [(10, *plane2), (padded, *plane2), (10, *plane2)],
        place, everything, scalars=1)

    half = (16, 256)
    correction, residual = call(
        post_kernel,
        [forcing.shape, forcing.shape],
        [(16, *full1), (6, 16, *full1)] + [(16, *full1)] * 4 + [(8, *full1)]
        + [(16, *half), (6, 16, *half)] + [(16, *half)] * 5,
        near_e, low1, own1, high1, low, own, high, guess)
    return correction, residual


def solution(mesh):
    spec = P("gx", "gy", None)
    return jax.shard_map(body, mesh=mesh, in_specs=(spec, spec), out_specs=(spec, spec), check_vma=False)
```

time: 477 us -> 122 us (0.26)
  the two profiles are of different devices: /device:TPU:34 before, /device:TPU:1 now
where the time goes in v1:
time: 122 us; the launch traced here: 120 us
  starting transfers between devices  44.6 us (37%)
  Pallas kernels  36 us (30%)
  waiting for transfers between devices  32.7 us (27%)
  local copies, waits for them, and re-layouts  5.22 us (4%)
    pallas_call x3, Pallas kernels, call(): pl.pallas_call(kernel, out_shape=[jax.ShapeDtypeStruct(shape, F32) for sh...  36 us
    all_to_all x1, starting transfers between devices, body(): everything = lax.all_to_all(copies, ('gx', 'gy'), 0, 0).reshape(-1, 128)  20.4 us
    ppermute x4, starting transfers between devices, both_sides(): low = lax.ppermute(value, axis, [(i, i + 1) for i in range(count - 1)])  17.8 us
    ppermute x4, waiting for transfers between devices, both_sides(): low = lax.ppermute(value, axis, [(i, i + 1) for i in range(count - 1)])  15.1 us
    ppermute x4, waiting for transfers between devices, both_sides(): high = lax.ppermute(value, axis, [(i + 1, i) for i in range(count - 1)])  12.8 us
    ppermute x4, starting transfers between devices, both_sides(): high = lax.ppermute(value, axis, [(i + 1, i) for i in range(count - 1)])  6.43 us
    all_to_all x1, waiting for transfers between devices, body(): everything = lax.all_to_all(copies, ('gx', 'gy'), 0, 0).reshape(-1, 128)  4.72 us
    unnamed x31, local copies, waits for them, and re-layouts  3.39 us
  transfers between devices with their start and end apart: 9, of which 7 were waited for; matrix products, arithmetic and copies ran while one was open for 1% of the time, Pallas kernels for 15%

profile of v1, /device:TPU:1, one launch (start us, length us, event | category | flops | bytes accessed | tf_op | source)
XLA Modules:
  0.0 119.8 jit_solution(18351340490535214946)
XLA Ops:
  0.6 0.0 copy-start.5
  0.6 0.9 constant_dynamic-update-slice_fusion.1
  1.5 0.0 copy-done.5
  1.5 0.0 copy-start.4
  1.5 5.0 %collective-permute-start = (f32[16,8,256]{2,1,0:T(8,128)S(1)}, f32[16,8,256]{2,1,0:T(8,128)S(1)}, u32[]{:S(2)}, u32[]{:S(2)}) collective-permute-start(f32[16,8,256]{2,1,0:T(8,128)S(1)} %constant_dynamic-update-slice_fusion), channel_id=1, source_target_pairs={{0,16},{16,32},{32,48},{48,64},{64,80},{80,96},{96,112},{112,128},... | collective-permute-start | bytes 393224 | tf_op jit(solution)/shard_map/ppermute | solution.py:447
  6.5 1.3 %collective-permute-start.1 = (f32[16,8,256]{2,1,0:T(8,128)S(1)}, f32[16,8,256]{2,1,0:T(8,128)S(1)}, u32[]{:S(2)}, u32[]{:S(2)}) collective-permute-start(f32[16,8,256]{2,1,0:T(8,128)S(1)} %constant_dynamic-update-slice_fusion), channel_id=1, source_target_pairs={{16,0},{32,16},{48,32},{64,48},{80,64},{96,80},{112,96},{128,112},... | collective-permute-start | bytes 393224 | tf_op jit(solution)/shard_map/ppermute | solution.py:448
  7.8 0.6 collective-permute-done
  8.4 0.0 copy-done.4
  8.5 4.4 %collective-permute-done.1 = f32[16,8,256]{2,1,0:T(8,128)S(1)} collective-permute-done((f32[16,8,256]{2,1,0:T(8,128)S(1)}, f32[16,8,256]{2,1,0:T(8,128)S(1)}, u32[]{:S(2)}, u32[]{:S(2)}) %collective-permute-start.1) | collective-permute-done | bytes 131104 | tf_op jit(solution)/shard_map/ppermute | solution.py:448
  12.9 0.0 copy-start.1
  12.9 5.2 %collective-permute-start.2 = (f32[42,8,256]{2,1,0:T(8,128)S(1)}, f32[42,8,256]{2,1,0:T(8,128)S(1)}, u32[]{:S(2)}, u32[]{:S(2)}) collective-permute-start(f32[42,8,256]{2,1,0:T(8,128)S(1)} %slice_dynamic-update-slice_fusion.2.own_ref), channel_id=1, source_target_pairs={{0,1},{1,2},{2,3},{3,4},{4,5},{5,6},{6,7},{7,8},{8,9},{9,10},{10,1... | collective-permute-start | bytes 1032200 | tf_op jit(solution)/shard_map/ppermute | solution.py:447
  18.1 1.9 %collective-permute-start.3 = (f32[42,8,256]{2,1,0:T(8,128)S(1)}, f32[42,8,256]{2,1,0:T(8,128)S(1)}, u32[]{:S(2)}, u32[]{:S(2)}) collective-permute-start(f32[42,8,256]{2,1,0:T(8,128)S(1)} %slice_dynamic-update-slice_fusion.2.own_ref), channel_id=1, source_target_pairs={{1,0},{2,1},{3,2},{4,3},{5,4},{6,5},{7,6},{8,7},{9,8},{10,9},{11,1... | collective-permute-start | bytes 1032200 | tf_op jit(solution)/shard_map/ppermute | solution.py:448
  20.0 2.2 %collective-permute-done.2.low_ref = f32[42,8,256]{2,1,0:T(8,128)S(1)} collective-permute-done((f32[42,8,256]{2,1,0:T(8,128)S(1)}, f32[42,8,256]{2,1,0:T(8,128)S(1)}, u32[]{:S(2)}, u32[]{:S(2)}) %collective-permute-start.2) | collective-permute-done | bytes 344096 | tf_op jit(solution)/shard_map/ppermute | solution.py:447
  22.3 0.0 copy-start.2
  22.3 4.4 %collective-permute-done.3.high_ref = f32[42,8,256]{2,1,0:T(8,128)S(1)} collective-permute-done((f32[42,8,256]{2,1,0:T(8,128)S(1)}, f32[42,8,256]{2,1,0:T(8,128)S(1)}, u32[]{:S(2)}, u32[]{:S(2)}) %collective-permute-start.3) | collective-permute-done | bytes 344096 | tf_op jit(solution)/shard_map/ppermute | solution.py:448
  26.7 0.0 copy-done.1
  26.7 0.0 copy-done.2
  26.7 0.0 copy-start.3
  26.7 0.8 copy-done.3
  27.5 8.8 %shard_map.41 = (f32[4,128]{1,0:T(4,128)}, f32[16,8,128]{2,1,0:T(8,128)}, f32[14,16,256]{2,1,0:T(8,128)}) custom-call(f32[42,8,256]{2,1,0:T(8,128)} %copy-done.2, f32[42,8,256]{2,1,0:T(8,128)} %copy-done.1, f32[42,8,256]{2,1,0:T(8,128)} %copy-done.3), custom_call_target="tpu_custom_call" | custom-call | tf_op jit(solution)/shard_map/pallas_call | solution.py:434
  36.3 1.8 %broadcast_in_dim.2 = f32[512,4,128]{2,1,0:T(4,128)} broadcast(f32[4,128]{1,0:T(4,128)} %get-tuple-element.5), dimensions={1,2} | broadcast | bytes 1050624 | tf_op jit(solution)/shard_map/broadcast_in_dim | solution.py:467
  38.1 0.0 copy-start.9
  38.1 20.4 %all-to-all-start = ((f32[512,4,128]{2,1,0:T(4,128)}), f32[512,4,128]{2,1,0:T(4,128)S(1)}, u32[]{:S(2)}, u32[]{:S(2)}) async-start(f32[512,4,128]{2,1,0:T(4,128)} %broadcast_in_dim.2), calls=%async_computation | async-start | bytes 2097152 | tf_op jit(solution)/shard_map/all_to_all | solution.py:468
  58.4 0.0 copy-done.9
  58.5 3.7 %collective-permute-start.4 = (f32[16,8,128]{2,1,0:T(8,128)S(1)}, f32[16,8,128]{2,1,0:T(8,128)S(1)}, u32[]{:S(2)}, u32[]{:S(2)}) collective-permute-start(f32[16,8,128]{2,1,0:T(8,128)S(1)} %copy-done.9), channel_id=1, source_target_pairs={{0,16},{16,32},{32,48},{48,64},{64,80},{80,96},{96,112},{112,128},... | collective-permute-start | bytes 196616 | tf_op jit(solution)/shard_map/ppermute | solution.py:447
  62.1 1.3 %collective-permute-start.5 = (f32[16,8,128]{2,1,0:T(8,128)S(1)}, f32[16,8,128]{2,1,0:T(8,128)S(1)}, u32[]{:S(2)}, u32[]{:S(2)}) collective-permute-start(f32[16,8,128]{2,1,0:T(8,128)S(1)} %copy-done.9), channel_id=1, source_target_pairs={{16,0},{32,16},{48,32},{64,48},{80,64},{96,80},{112,96},{128,112},... | collective-permute-start | bytes 196616 | tf_op jit(solution)/shard_map/ppermute | solution.py:448
  63.4 12.3 %collective-permute-done.4 = f32[16,8,128]{2,1,0:T(8,128)S(1)} collective-permute-done((f32[16,8,128]{2,1,0:T(8,128)S(1)}, f32[16,8,128]{2,1,0:T(8,128)S(1)}, u32[]{:S(2)}, u32[]{:S(2)}) %collective-permute-start.4) | collective-permute-done | bytes 65568 | tf_op jit(solution)/shard_map/ppermute | solution.py:447
  75.7 4.0 %collective-permute-done.5 = f32[16,8,128]{2,1,0:T(8,128)S(1)} collective-permute-done((f32[16,8,128]{2,1,0:T(8,128)S(1)}, f32[16,8,128]{2,1,0:T(8,128)S(1)}, u32[]{:S(2)}, u32[]{:S(2)}) %collective-permute-start.5) | collective-permute-done | bytes 65568 | tf_op jit(solution)/shard_map/ppermute | solution.py:448
  79.8 0.0 copy-start.6
  79.8 4.0 %collective-permute-start.6 = (f32[32,8,128]{2,1,0:T(8,128)S(1)}, f32[32,8,128]{2,1,0:T(8,128)S(1)}, u32[]{:S(2)}, u32[]{:S(2)}) collective-permute-start(f32[32,8,128]{2,1,0:T(8,128)S(1)} %constant_dynamic-update-slice_fusion.4.own1_ref), channel_id=1, source_target_pairs={{0,1},{1,2},{2,3},{3,4},{4,5},{5,6},{6,7},{7,8},{8,9},{9,10},{10,1... | collective-permute-start | bytes 393224 | tf_op jit(solution)/shard_map/ppermute | solution.py:447
  83.7 1.9 %collective-permute-start.7 = (f32[32,8,128]{2,1,0:T(8,128)S(1)}, f32[32,8,128]{2,1,0:T(8,128)S(1)}, u32[]{:S(2)}, u32[]{:S(2)}) collective-permute-start(f32[32,8,128]{2,1,0:T(8,128)S(1)} %constant_dynamic-update-slice_fusion.4.own1_ref), channel_id=1, source_target_pairs={{1,0},{2,1},{3,2},{4,3},{5,4},{6,5},{7,6},{8,7},{9,8},{10,9},{11,1... | collective-permute-start | bytes 393224 | tf_op jit(solution)/shard_map/ppermute | solution.py:448
  85.7 0.6 pad_add_fusion.place_ref
  86.2 4.7 %all-to-all-done = f32[512,4,128]{2,1,0:T(4,128)S(1)} async-done(((f32[512,4,128]{2,1,0:T(4,128)}), f32[512,4,128]{2,1,0:T(4,128)S(1)}, u32[]{:S(2)}, u32[]{:S(2)}) %all-to-all-start) | async-done | bytes 1048608 | tf_op jit(solution)/shard_map/all_to_all | solution.py:468
  91.0 0.0 copy-start
  91.0 1.0 copy-done
  92.0 18.4 %shard_map.42.near_ref = f32[6,16,128]{2,1,0:T(8,128)} custom-call(s32[2]{0:T(128)} %pad_add_fusion.place_ref, f32[2048,128]{1,0:T(8,128)} %bitcast.3), custom_call_target="tpu_custom_call" | custom-call | tf_op jit(solution)/shard_map/pallas_call | solution.py:434
  110.3 0.0 copy-done.6
  110.3 0.0 collective-permute-done.6.low1_ref
  110.3 0.0 copy-start.7
  110.3 0.0 collective-permute-done.7.high1_ref
  110.4 0.0 copy-start.8
  110.4 0.6 copy-done.7
  111.0 0.1 copy-done.8
  111.0 8.8 %shard_map.43 = (f32[8,8,256]{2,1,0:T(8,128)}, f32[8,8,256]{2,1,0:T(8,128)}) custom-call(f32[6,16,128]{2,1,0:T(8,128)} %shard_map.42.near_ref, f32[32,8,128]{2,1,0:T(8,128)} %copy-done.7, f32[32,8,128]{2,1,0:T(8,128)} %copy-done.6, f32[32,8,128]{2,1,0:T(8,128)} %copy-done.8, f32[42,8,256]{2,1,0:T(8,128)} %copy-done.2, f32[42,8,256]{2,1,0:T(8,128)} %copy-done.1, ...), custom_call_target="tpu_custom_call" | custom-call | tf_op jit(solution)/shard_map/pallas_call | solution.py:434
  (13 shorter events, 0.1 us)
Async XLA Ops:
  0.6 0.9 copy-start.5
  1.5 6.9 %copy-start.4 = (f32[8,8,256]{2,1,0:T(8,128)S(1)}, f32[8,8,256]{2,1,0:T(8,128)}, u32[]{:S(2)}) copy-start(f32[8,8,256]{2,1,0:T(8,128)} %param.3) | copy-start | bytes 196612
  1.5 6.9 %collective-permute-start = (f32[16,8,256]{2,1,0:T(8,128)S(1)}, f32[16,8,256]{2,1,0:T(8,128)S(1)}, u32[]{:S(2)}, u32[]{:S(2)}) collective-permute-start(f32[16,8,256]{2,1,0:T(8,128)S(1)} %constant_dynamic-update-slice_fusion), channel_id=1, source_target_pairs={{0,16},{16,32},{32,48},{48,64},{64,80},{80,96},{96,112},{112,128},... | collective-permute-start | bytes 393224 | tf_op jit(solution)/shard_map/ppermute | solution.py:447
  6.5 6.3 %collective-permute-start.1 = (f32[16,8,256]{2,1,0:T(8,128)S(1)}, f32[16,8,256]{2,1,0:T(8,128)S(1)}, u32[]{:S(2)}, u32[]{:S(2)}) collective-permute-start(f32[16,8,256]{2,1,0:T(8,128)S(1)} %constant_dynamic-update-slice_fusion), channel_id=1, source_target_pairs={{16,0},{32,16},{48,32},{64,48},{80,64},{96,80},{112,96},{128,112},... | collective-permute-start | bytes 393224 | tf_op jit(solution)/shard_map/ppermute | solution.py:448
  12.9 13.8 %copy-start.1 = (f32[42,8,256]{2,1,0:T(8,128)}, f32[42,8,256]{2,1,0:T(8,128)S(1)}, u32[]{:S(2)}) copy-start(f32[42,8,256]{2,1,0:T(8,128)S(1)} %slice_dynamic-update-slice_fusion.2.own_ref) | copy-start | bytes 1032196
  12.9 9.4 %collective-permute-start.2 = (f32[42,8,256]{2,1,0:T(8,128)S(1)}, f32[42,8,256]{2,1,0:T(8,128)S(1)}, u32[]{:S(2)}, u32[]{:S(2)}) collective-permute-start(f32[42,8,256]{2,1,0:T(8,128)S(1)} %slice_dynamic-update-slice_fusion.2.own_ref), channel_id=1, source_target_pairs={{0,1},{1,2},{2,3},{3,4},{4,5},{5,6},{6,7},{7,8},{8,9},{9,10},{10,1... | collective-permute-start | bytes 1032200 | tf_op jit(solution)/shard_map/ppermute | solution.py:447
  18.1 8.6 %collective-permute-start.3 = (f32[42,8,256]{2,1,0:T(8,128)S(1)}, f32[42,8,256]{2,1,0:T(8,128)S(1)}, u32[]{:S(2)}, u32[]{:S(2)}) collective-permute-start(f32[42,8,256]{2,1,0:T(8,128)S(1)} %slice_dynamic-update-slice_fusion.2.own_ref), channel_id=1, source_target_pairs={{1,0},{2,1},{3,2},{4,3},{5,4},{6,5},{7,6},{8,7},{9,8},{10,9},{11,1... | collective-permute-start | bytes 1032200 | tf_op jit(solution)/shard_map/ppermute | solution.py:448
  22.3 4.4 %copy-start.2 = (f32[42,8,256]{2,1,0:T(8,128)}, f32[42,8,256]{2,1,0:T(8,128)S(1)}, u32[]{:S(2)}) copy-start(f32[42,8,256]{2,1,0:T(8,128)S(1)} %collective-permute-done.2.low_ref) | copy-start | bytes 1032196
  26.7 0.8 copy-start.3
  38.1 20.4 %copy-start.9 = (f32[16,8,128]{2,1,0:T(8,128)S(1)}, f32[16,8,128]{2,1,0:T(8,128)}, u32[]{:S(2)}) copy-start(f32[16,8,128]{2,1,0:T(8,128)} %get-tuple-element.6) | copy-start | bytes 196612
  38.1 52.9 %all-to-all-start = ((f32[512,4,128]{2,1,0:T(4,128)}), f32[512,4,128]{2,1,0:T(4,128)S(1)}, u32[]{:S(2)}, u32[]{:S(2)}) async-start(f32[512,4,128]{2,1,0:T(4,128)} %broadcast_in_dim.2), calls=%async_computation | async-start | bytes 2097152 | tf_op jit(solution)/shard_map/all_to_all | solution.py:468
  58.5 17.3 %collective-permute-start.4 = (f32[16,8,128]{2,1,0:T(8,128)S(1)}, f32[16,8,128]{2,1,0:T(8,128)S(1)}, u32[]{:S(2)}, u32[]{:S(2)}) collective-permute-start(f32[16,8,128]{2,1,0:T(8,128)S(1)} %copy-done.9), channel_id=1, source_target_pairs={{0,16},{16,32},{32,48},{48,64},{64,80},{80,96},{96,112},{112,128},... | collective-permute-start | bytes 196616 | tf_op jit(solution)/shard_map/ppermute | solution.py:447
  62.1 17.6 %collective-permute-start.5 = (f32[16,8,128]{2,1,0:T(8,128)S(1)}, f32[16,8,128]{2,1,0:T(8,128)S(1)}, u32[]{:S(2)}, u32[]{:S(2)}) collective-permute-start(f32[16,8,128]{2,1,0:T(8,128)S(1)} %copy-done.9), channel_id=1, source_target_pairs={{16,0},{32,16},{48,32},{64,48},{80,64},{96,80},{112,96},{128,112},... | collective-permute-start | bytes 196616 | tf_op jit(solution)/shard_map/ppermute | solution.py:448
  79.8 30.6 %copy-start.6 = (f32[32,8,128]{2,1,0:T(8,128)}, f32[32,8,128]{2,1,0:T(8,128)S(1)}, u32[]{:S(2)}) copy-start(f32[32,8,128]{2,1,0:T(8,128)S(1)} %constant_dynamic-update-slice_fusion.4.own1_ref) | copy-start | bytes 393220
  79.8 30.6 %collective-permute-start.6 = (f32[32,8,128]{2,1,0:T(8,128)S(1)}, f32[32,8,128]{2,1,0:T(8,128)S(1)}, u32[]{:S(2)}, u32[]{:S(2)}) collective-permute-start(f32[32,8,128]{2,1,0:T(8,128)S(1)} %constant_dynamic-update-slice_fusion.4.own1_ref), channel_id=1, source_target_pairs={{0,1},{1,2},{2,3},{3,4},{4,5},{5,6},{6,7},{7,8},{8,9},{9,10},{10,1... | collective-permute-start | bytes 393224 | tf_op jit(solution)/shard_map/ppermute | solution.py:447
  83.7 26.6 %collective-permute-start.7 = (f32[32,8,128]{2,1,0:T(8,128)S(1)}, f32[32,8,128]{2,1,0:T(8,128)S(1)}, u32[]{:S(2)}, u32[]{:S(2)}) collective-permute-start(f32[32,8,128]{2,1,0:T(8,128)S(1)} %constant_dynamic-update-slice_fusion.4.own1_ref), channel_id=1, source_target_pairs={{1,0},{2,1},{3,2},{4,3},{5,4},{6,5},{7,6},{8,7},{9,8},{10,9},{11,1... | collective-permute-start | bytes 393224 | tf_op jit(solution)/shard_map/ppermute | solution.py:448
  91.0 1.0 copy-start
  110.3 0.6 copy-start.7
  110.4 0.7 copy-start.8

commit v2 on v0

v2 whole, which is shorter than its diff:
```python
import math

import jax
import jax.numpy as jnp
from jax import lax
from jax.experimental import pallas as pl
from jax.experimental.pallas import tpu as pltpu
from jax.sharding import PartitionSpec as P

INTERPRET = False
COARSE_STEPS = 8
F32 = jnp.float32
HIGHEST = lax.Precision.HIGHEST
MIB = 1024 * 1024


def step_factors(low_end, steps):
    center, radius = 0.5 * (2.0 + low_end), 0.5 * (2.0 - low_end)
    sigma = center / radius
    ratio = 1.0 / sigma
    factors = [(0.0, 1.0 / center)]
    for _ in range(steps - 1):
        ratio_next = 1.0 / (2.0 * sigma - ratio)
        factors.append((ratio_next * ratio, 2.0 * ratio_next / radius))
        ratio = ratio_next
    return factors


(_, FIRST), (KEEP, ADD) = step_factors(0.4, 2)
COARSE_FACTORS = step_factors(0.02, COARSE_STEPS)


def iota(shape, dim):
    return lax.broadcasted_iota(jnp.int32, shape, dim)


def shifted(value, step, axis):
    return pltpu.roll(value, (-step) % value.shape[axis], axis)


def dot(a, b):
    return jnp.dot(a, b, precision=HIGHEST, preferred_element_type=F32)


def ones_where(condition):
    return jnp.where(condition, 1.0, 0.0).astype(F32)


def blocks(first, last, size, step):
    count = (last - first) // size
    assert first + count * size == last
    if count == 1:
        step(first)
        return

    def one(number, carry):
        step(first + number * size)
        return carry

    lax.fori_loop(0, count, one, 0)


def near(ref, start, size):
    here = ref[pl.ds(start, size)]
    return (ref[pl.ds(start - 1, size)], ref[pl.ds(start + 1, size)],
            shifted(here, -1, 1), shifted(here, 1, 1), shifted(here, -1, 2), shifted(here, 1, 2))


def near_inside(ref, start, size):
    x_low, x_high, y_low, y_high, z_low, z_high = near(ref, start, size)
    lane = iota(z_low.shape, 2)
    z_low = jnp.where(lane == 0, 0.0, z_low)
    z_high = jnp.where(lane == z_low.shape[2] - 1, 0.0, z_high)
    return x_low, x_high, y_low, y_high, z_low, z_high


def coupling(center, around, masked):
    total = 6.0 * center
    for value in around:
        total = total + value
    inside = center > 0.0
    half_inverse = jnp.where(inside, 1.0 / jnp.where(inside, total, 1.0), 0.0)
    couplings = []
    for number, value in enumerate(around):
        c = (center + value) * half_inverse
        couplings.append(jnp.where(value > 0.0, c, 0.0) if number in masked else c)
    return couplings, 2.0 * half_inverse, 0.5 * total


def pick(c_ref, number, where):
    return c_ref.at[number][where] if where else c_ref[number]


def spread(c_ref, where, around):
    total = pick(c_ref, 0, where) * around[0]
    for number in range(1, 6):
        total = total + pick(c_ref, number, where) * around[number]
    return total


def fine_kernel(low_ref, own_ref, high_ref, copies_ref, share_ref,
                k0, c0, diag0, g0, d0, e0, sums, zsums, k1, f1, c1, diag1, g1, d1, e1, out):
    for index in range(22):
        k0[index, 0:8] = low_ref[index]
        k0[index, 8:16] = own_ref[index]
        k0[index, 16:24] = high_ref[index]

    def setup(start):
        at = pl.ds(start, 2)
        couplings, inverse, diagonal = coupling(k0[pl.ds(start + 1, 2)], near_inside(k0, start + 1, 2), (4, 5))
        for number in range(6):
            c0.at[number][at] = couplings[number]
        diag0[at] = diagonal
        force = pl.ds(start + 22, 2)
        scaled = inverse * jnp.concatenate([low_ref[force], own_ref[force], high_ref[force]], 1)
        g0[at] = scaled
        d0[at] = FIRST * scaled

    blocks(0, 20, 2, setup)

    def second(start):
        at = pl.ds(start, 2)
        here = d0[at]
        scaled = g0[at] - here + spread(c0, (at,), near(d0, start, 2))
        g0[at] = scaled
        e0[at] = KEEP * here + ADD * scaled

    blocks(1, 19, 2, second)

    def left(start):
        at = pl.ds(start, 2)
        rest = diag0[at] * (g0[at] - e0[at] + spread(c0, (at,), near(e0, start, 2)))
        sums[start // 2 - 1] = 0.5 * (rest[0] + rest[1])

    blocks(2, 18, 2, left)
    for index in range(10):
        sums[index + 8] = 0.125 * (k0[2 * index + 1] + k0[2 * index + 2])
    fold = ones_where(iota((256, 128), 0) // 2 == iota((256, 128), 1))
    zsums[...] = dot(sums[...].reshape(18 * 24, 256), fold).reshape(18, 24, 128)

    k1[...] = jnp.zeros_like(k1)
    f1[...] = jnp.zeros_like(f1)
    rows = zsums[:, pl.ds(0, 12, stride=2), :] + zsums[:, pl.ds(1, 12, stride=2), :]
    f1[:, 2:14, :] = rows[0:8]
    k1[:, 2:14, :] = rows[8:18]
    share_ref[0:8] = k1[1:9, 4:12, :]
    share_ref[8:16] = f1[:, 4:12, :]

    def setup1(start):
        at = pl.ds(start, 4)
        couplings, inverse, diagonal = coupling(k1[pl.ds(start + 1, 4)], near_inside(k1, start + 1, 4), (4, 5))
        for number in range(6):
            c1.at[number][at] = couplings[number]
        diag1[at] = diagonal
        scaled = inverse * f1[at]
        g1[at] = scaled
        d1[at] = FIRST * scaled

    blocks(0, 8, 4, setup1)
    at = pl.ds(1, 6)
    scaled = g1[at] - d1[at] + spread(c1, (at,), near(d1, 1, 6))
    g1[at] = scaled
    e1[at] = KEEP * d1[at] + ADD * scaled
    at = pl.ds(2, 4)
    rest = diag1[at] * (g1[at] - e1[at] + spread(c1, (at,), near(e1, 2, 4)))
    for half in range(2):
        out[half] = 0.5 * (rest[2 * half] + rest[2 * half + 1])
        out[half + 2] = 0.125 * (k1[2 * half + 3] + k1[2 * half + 4])
    row, lane = iota((128, 256), 0), iota((128, 256), 1)
    fold = ones_where((lane == row // 2) | (lane == 192 + row // 2))
    folded = dot(out[...].reshape(64, 128), fold).reshape(4, 16, 256)
    lines = [folded[number, 6:7, 0:128] + folded[number, 7:8, 0:128]
             + folded[number, 8:9, 128:256] + folded[number, 9:10, 128:256] for number in range(4)]
    payload = jnp.concatenate(lines, 0)

    def copy(start):
        copies_ref[pl.ds(start, 8)] = jnp.broadcast_to(payload[None], (8, 4, 128))

    blocks(0, copies_ref.shape[0], 8, copy)


def near2(ref, start, size):
    here = ref[pl.ds(start, size)]
    below, above = ref[pl.ds(start - 1, size)], ref[pl.ds(start + 1, size)]
    z_low, z_high = shifted(here, -1, 3), shifted(here, 1, 3)
    turned = shifted(here, 64, 3)
    turned0, turned1 = turned[:, 0:1], turned[:, 1:2]
    first = iota(turned0.shape, 3) < 64
    y_high = [jnp.where(first, turned0, turned1), jnp.where(first, turned1, shifted(turned0, 1, 2))]
    y_low = [jnp.where(first, shifted(turned1, -1, 2), turned0), jnp.where(first, turned0, turned1)]
    return below, above, jnp.concatenate(y_low, 1), jnp.concatenate(y_high, 1), z_low, z_high


def near2_inside(ref, start, size):
    x_low, x_high, y_low, y_high, z_low, z_high = near2(ref, start, size)
    core, row, lane = (iota(z_low.shape, dim) for dim in (1, 2, 3))
    last = z_low.shape[2] - 1
    y_low = jnp.where((core == 0) & (row == 0) & (lane < 64), 0.0, y_low)
    y_high = jnp.where((core == 1) & (row == last) & (lane >= 64), 0.0, y_high)
    z_low = jnp.where(lane % 64 == 0, 0.0, z_low)
    z_high = jnp.where(lane % 64 == 63, 0.0, z_high)
    return x_low, x_high, y_low, y_high, z_low, z_high


def near3(value):
    count = value.shape[0]
    before, after = shifted(value[count - 1:], -32, 3), shifted(value[0:1], 32, 3)
    x_low = jnp.concatenate([before, value[:count - 1]], 0) if count > 1 else before
    x_high = jnp.concatenate([value[1:], after], 0) if count > 1 else after
    core0, core1 = value[:, 0:1], value[:, 1:2]
    y_low = jnp.concatenate([shifted(core1, -1, 2), core0], 1)
    y_high = jnp.concatenate([core1, shifted(core0, 1, 2)], 1)
    return x_low, x_high, y_low, y_high, shifted(value, -1, 3), shifted(value, 1, 3)


def near3_inside(value):
    x_low, x_high, y_low, y_high, z_low, z_high = near3(value)
    plane, core, row, lane = (iota(value.shape, dim) for dim in range(4))
    count, rows = value.shape[0], value.shape[2]
    x_low = jnp.where((plane == 0) & (lane < 32), 0.0, x_low)
    x_high = jnp.where((plane == count - 1) & (lane >= 96), 0.0, x_high)
    y_low = jnp.where((core == 0) & (row == 0), 0.0, y_low)
    y_high = jnp.where((core == 1) & (row == rows - 1), 0.0, y_high)
    z_low = jnp.where(lane % 32 == 0, 0.0, z_low)
    z_high = jnp.where(lane % 32 == 31, 0.0, z_high)
    return x_low, x_high, y_low, y_high, z_low, z_high


def make_coarse_kernel(count_x, count_y):
    planes2, rows, count3 = 2 * count_x, count_y // 2, count_x // 4
    size = 8
    line = (2, rows, 128)

    def coarse_kernel(place_ref, mine_ref, other_ref, near_ref,
                      k2, c2, diag2, g2, d2, e2, h2, sums, c3, e3, x0):
        at_x, at_y = place_ref[0], place_ref[1]
        zero = jnp.zeros((4, *line), F32)
        for ends in (pl.ds(0, 4), pl.ds(planes2 + 4, 4)):
            for ref in (k2, g2, d2, e2):
                ref[ends] = zero
            for number in range(6):
                c2.at[number][ends] = zero

        core = at_y % 2

        def load(index):
            for half in range(2):
                start = index * (4 * rows) + half
                to = 2 * index + half + 4
                for ref, side in ((mine_ref, core), (other_ref, 1 - core)):
                    k2[to, side] = ref[pl.ds(start + 2, rows, stride=4), :]
                    e2[to, side] = ref[pl.ds(start, rows, stride=4), :]

        def load_some(start):
            for index in range(4):
                load(start + index)

        blocks(0, count_x, 4, load_some)

        def setup(start):
            at = pl.ds(start, size)
            couplings, inverse, diagonal = coupling(k2[at], near2_inside(k2, start, size), (2, 3, 4, 5))
            for number in range(6):
                c2.at[number][at] = couplings[number]
            diag2[at] = diagonal
            scaled = inverse * e2[at]
            g2[at] = scaled
            d2[at] = FIRST * scaled

        blocks(4, planes2 + 4, size, setup)

        def second(start):
            at = pl.ds(start, size)
            here = d2[at]
            scaled = g2[at] - here + spread(c2, (at,), near2(d2, start, size))
            h2[at] = scaled
            e2[at] = KEEP * here + ADD * scaled

        blocks(4, planes2 + 4, size, second)

        def left(start):
            at = pl.ds(start, size)
            rest = diag2[at] * (h2[at] - e2[at] + spread(c2, (at,), near2(e2, start, size)))
            rest = rest.reshape(size // 2, 2, *line)
            here = k2[at].reshape(size // 2, 2, *line)
            to = (start - 4) // 2
            sums[pl.ds(to, size // 2)] = 0.5 * (rest[:, 0] + rest[:, 1])
            sums[pl.ds(to + count_x, size // 2)] = 0.125 * (here[:, 0] + here[:, 1])

        blocks(4, planes2 + 4, size, left)

        flat = count3 * 2 * rows
        f3 = jnp.zeros((flat, 128), F32)
        k3 = jnp.zeros((flat, 128), F32)
        row, lane = iota((128, 128), 0), iota((128, 128), 1)
        for quarter in range(4):
            fold = ones_where(lane == 32 * quarter + (row % 64) // 2)
            f3 = f3 + dot(sums[pl.ds(quarter * count3, count3)].reshape(flat, 128), fold)
            k3 = k3 + dot(sums[pl.ds(count_x + quarter * count3, count3)].reshape(flat, 128), fold)
        f3 = f3.reshape(count3, *line)
        k3 = k3.reshape(count3, *line)
        couplings, inverse, _ = coupling(k3, near3_inside(k3), (0, 1, 2, 3, 4, 5))
        for number in range(6):
            c3[number] = couplings[number]
        scaled = inverse * f3
        step = COARSE_FACTORS[0][1] * scaled
        total = step
        for keep, add in COARSE_FACTORS[1:]:
            scaled = scaled - step + spread(c3, (), near3(step))
            step = keep * step + add * scaled
            total = total + step
        e3[...] = total

        base = 2 * at_x
        parts = []
        for number in range(5):
            x3 = at_x - 2 + number
            inside = (x3 >= 0) & (x3 < count_x)
            safe = jnp.clip(x3, 0, count_x - 1)
            plane = pltpu.roll(e3[safe % count3].reshape(2 * rows, 128), (128 - 32 * (safe // count3)) % 128, 1)
            parts.append(jnp.where(inside, plane, 0.0))
        unfold = ones_where((row < 32) & ((lane % 64) // 2 == row))
        up = dot(jnp.concatenate(parts, 0), unfold).reshape(5, *line)
        local = pl.ds(base, 10)
        twice = jnp.stack([up, up], 1).reshape(10, *line)
        x0[...] = d2[local] + e2[local] + twice
        inner = pl.ds(base + 1, 8)
        scaled = g2[inner] - x0[1:9] + spread(c2, (inner,), near2(x0, 1, 8))
        h2[0:8] = scaled
        d2[0:8] = FIRST * scaled
        inner = pl.ds(base + 2, 6)
        here = d2[1:7]
        scaled = h2[1:7] - here + spread(c2, (inner,), near2(d2, 1, 6))
        found = x0[2:8] + (1.0 + KEEP) * here + ADD * scaled

        row, lane = iota((128, 256), 0), iota((128, 256), 1)
        widen = ones_where(row == 64 * (lane // 128) + (lane % 128) // 2)
        wide = dot(found.reshape(6 * 2 * rows, 128), widen)
        target, source = iota((16, 2 * rows), 0), iota((16, 2 * rows), 1)
        source = 2 * (source % rows) + source // rows
        inside = (target >= 2) & (target < 14) & (source == at_y - 1 + (target - 2) // 4)
        first = ones_where(inside & ((target - 2) % 4 < 2))
        other = ones_where(inside & ((target - 2) % 4 >= 2))
        for index in range(6):
            block = wide[index * 2 * rows:(index + 1) * 2 * rows]
            near_ref[index] = dot(first, block[:, 0:128]) + dot(other, block[:, 128:256])

    return coarse_kernel


def prepare_kernel(low1_ref, own1_ref, high1_ref, low_ref, own_ref, high_ref,
                   c1, g1, x1, c0, diag0, g0, x0, k1, d1, k0, d0, all0):
    def join(start, size):
        at = pl.ds(start, size)
        row = iota((size, 8, 128), 1)
        middle = shifted(own1_ref[at], 4, 1)
        return jnp.concatenate([jnp.where(row < 6, low1_ref[at], middle),
                                jnp.where(row < 2, middle, high1_ref[at])], 1)

    k1[0:8] = join(0, 8)
    k1[8:16] = join(8, 8)

    def setup1(start):
        at = pl.ds(start, 7)
        couplings, inverse, _ = coupling(k1[at], near_inside(k1, start, 7), (4, 5))
        for number in range(6):
            c1.at[number][at] = couplings[number]
        scaled = inverse * join(start + 16, 7)
        g1[at] = scaled
        d1[at] = FIRST * scaled

    blocks(1, 15, 7, setup1)

    def guess1(start):
        at = pl.ds(start, 6)
        here = d1[at]
        scaled = g1[at] - here + spread(c1, (at,), near(d1, start, 6))
        x1[at] = (1.0 + KEEP) * here + ADD * scaled

    blocks(2, 14, 6, guess1)

    def load0(start):
        at = pl.ds(start + 2, 2)
        k0[pl.ds(start, 2)] = jnp.concatenate([low_ref[at], own_ref[at], high_ref[at]], 1)

    blocks(0, 18, 2, load0)

    def setup0(start):
        def cut(value):
            return shifted(value, 4, 1)[:, 0:16]

        at = pl.ds(start, 2)
        couplings, inverse, diagonal = coupling(k0[pl.ds(start + 1, 2)], near_inside(k0, start + 1, 2), (4, 5))
        for number in range(6):
            c0.at[number][at] = cut(couplings[number])
        diag0[at] = cut(diagonal)
        force = pl.ds(start + 24, 2)
        scaled = cut(inverse * jnp.concatenate([low_ref[force], own_ref[force], high_ref[force]], 1))
        g0[at] = scaled
        d0[at] = FIRST * scaled

    blocks(0, 16, 2, setup0)

    def guess0(start):
        at = pl.ds(start, 2)
        here = d0[at]
        scaled = g0[at] - here + spread(c0, (at,), near(d0, start, 2))
        x0[at] = (1.0 + KEEP) * here + ADD * scaled

    blocks(1, 15, 2, guess0)


def post_kernel(near_ref, c1, g1, x1, c0, diag0, g0, x0, correction_ref, residual_ref,
                y1, d1, h1, wide, y0, d0, h0, v0):
    up = near_ref[...]
    y1[2:14] = x1[2:14] + jnp.stack([up, up], 1).reshape(12, 16, 128)
    scaled = g1[3:13] - y1[3:13] + spread(c1, (pl.ds(3, 10),), near(y1, 3, 10))
    h1[3:13] = scaled
    d1[3:13] = FIRST * scaled
    here = d1[4:12]
    scaled = h1[4:12] - here + spread(c1, (pl.ds(4, 8),), near(d1, 4, 8))
    found = y1[4:12] + (1.0 + KEEP) * here + ADD * scaled
    wide[:, pl.ds(0, 8, stride=2), :] = found[:, 4:12]
    wide[:, pl.ds(1, 8, stride=2), :] = found[:, 4:12]
    unfold = ones_where(iota((128, 256), 0) == iota((128, 256), 1) // 2)
    up = dot(wide[...].reshape(128, 128), unfold).reshape(8, 16, 256)

    for index in range(1, 15):
        y0[index] = x0[index] + up[index // 2]

    def first0(start):
        at = pl.ds(start, 3)
        scaled = g0[at] - y0[at] + spread(c0, (at,), near(y0, start, 3))
        h0[at] = scaled
        d0[at] = FIRST * scaled

    blocks(2, 14, 3, first0)

    def second0(start):
        at = pl.ds(start, 2)
        here = d0[at]
        scaled = h0[at] - here + spread(c0, (at,), near(d0, start, 2))
        h0[at] = scaled
        v0[at] = KEEP * here + ADD * scaled

    blocks(3, 13, 2, second0)

    def last0(start):
        at, to = pl.ds(start, 2), pl.ds(start - 4, 2)
        here = v0[at]
        correction_ref[to] = (y0[at] + d0[at] + here)[:, 4:12]
        scaled = h0[at] - here + spread(c0, (at,), near(v0, start, 2))
        residual_ref[to] = (diag0[at] * scaled)[:, 4:12]

    blocks(4, 12, 2, last0)


def call(kernel, limit, shapes, scratch, *operands, scalars=0):
    specs = [pl.BlockSpec(memory_space=pltpu.SMEM)] * scalars
    specs += [pl.BlockSpec(memory_space=pltpu.VMEM)] * (len(operands) - scalars)
    return pl.pallas_call(
        kernel,
        out_shape=[jax.ShapeDtypeStruct(shape, F32) for shape in shapes],
        in_specs=specs,
        out_specs=[pl.BlockSpec(memory_space=pltpu.VMEM)] * len(shapes),
        scratch_shapes=[pltpu.VMEM(shape, F32) for shape in scratch],
        compiler_params=pltpu.CompilerParams(vmem_limit_bytes=limit * MIB),
        interpret=INTERPRET,
    )(*operands)


def both_sides(value, axes):
    count = math.prod(lax.axis_size(axis) for axis in axes)
    low = lax.ppermute(value, axes, [(i, i + 1) for i in range(count - 1)])
    high = lax.ppermute(value, axes, [(i + 1, i) for i in range(count - 1)])
    return low, high


def body(forcing, coefficient):
    count_x, chips = lax.axis_size("gx"), lax.axis_size("chip")
    count_y = 2 * chips
    block = jnp.concatenate([coefficient, forcing], 0)
    low, high = both_sides(block, ("gx",))
    own = jnp.concatenate([low[1:8], coefficient, high[0:7], low[10:16], forcing, high[8:14]], 0)
    low, high = both_sides(own, ("chip", "core"))

    full, half, full1 = (24, 256), (16, 256), (16, 128)
    copies, share = call(
        fine_kernel, 16,
        [(count_x * chips, 4, 128), (16, 8, 128)],
        [(22, *full), (6, 20, *full)] + [(20, *full)] * 4 + [(18, *full), (18, 24, 128)]
        + [(10, *full1), (8, *full1), (6, 8, *full1)] + [(8, *full1)] * 4 + [(4, *full1)],
        low, own, high)

    mine = lax.all_to_all(copies, ("gx", "chip"), 0, 0).reshape(-1, 128)
    other = lax.ppermute(mine, "core", [(0, 1), (1, 0)])

    low1, high1 = both_sides(share, ("gx",))
    own1 = jnp.concatenate([low1[0:6], share[2:6], high1[2:8], low1[8:14], share[10:14], high1[10:16]], 0)
    low1, high1 = both_sides(own1, ("chip", "core"))
    prepared = call(
        prepare_kernel, 16,
        [(6, 16, *full1)] + [(16, *full1)] * 2 + [(6, 16, *half)] + [(16, *half)] * 3,
        [(16, *full1)] * 2 + [(18, *full), (16, *half), (1, *full)],
        low1, own1, high1, low, own, high)

    place = jnp.stack([lax.axis_index("gx"), lax.axis_index(("chip", "core"))]).astype(jnp.int32)
    plane2 = (2, count_y // 2, 128)
    padded = (2 * count_x + 8, *plane2)
    near_e, = call(
        make_coarse_kernel(count_x, count_y), 20,
        [(6, 16, 128)],
        [padded, (6, *padded)] + [padded] * 5
        + [(2 * count_x, *plane2), (6, count_x // 4, *plane2), (count_x // 4, *plane2), (10, *plane2)],
        place, mine, other, scalars=1)

    correction, residual = call(
        post_kernel, 16,
        [forcing.shape, forcing.shape],
        [(16, *full1)] * 3 + [(8, *full1)] + [(16, *half)] * 4,
        near_e, *prepared)
    return correction, residual


def solution(mesh):
    shape = (mesh.shape["gx"], mesh.shape["gy"] // 2, 2)
    mesh = jax.sharding.Mesh(mesh.devices.reshape(shape), ("gx", "chip", "core"))
    spec = P("gx", ("chip", "core"), None)
    return jax.shard_map(body, mesh=mesh, in_specs=(spec, spec), out_specs=(spec, spec), check_vma=False)
```

time: 477 us -> 94.2 us (0.20)
  the two profiles are of different devices: /device:TPU:34 before, /device:TPU:1 now
where the time goes in v2:
time: 94.2 us; the launch traced here: 93.6 us
  starting transfers between devices  49.8 us (53%)
  waiting for transfers between devices  23.1 us (25%)
  Pallas kernels  16.5 us (18%)
  local copies, waits for them, and re-layouts  3.42 us (4%)
    all_to_all x1, starting transfers between devices, body(): mine = lax.all_to_all(copies, ('gx', 'chip'), 0, 0).reshape(-1, 128)  20.3 us
    pallas_call x4, Pallas kernels, call(): pl.pallas_call(kernel, out_shape=[jax.ShapeDtypeStruct(shape, F32) for sh...  16.5 us
    ppermute x4, starting transfers between devices, both_sides(): low = lax.ppermute(value, axes, [(i, i + 1) for i in range(count - 1)])  12 us
    ppermute x4, waiting for transfers between devices, both_sides(): low = lax.ppermute(value, axes, [(i, i + 1) for i in range(count - 1)])  10.6 us
    ppermute x4, starting transfers between devices, both_sides(): high = lax.ppermute(value, axes, [(i + 1, i) for i in range(count - 1)])  10.3 us
    ppermute x4, waiting for transfers between devices, both_sides(): high = lax.ppermute(value, axes, [(i + 1, i) for i in range(count - 1)])  9.85 us
    ppermute x1, starting transfers between devices, body(): other = lax.ppermute(mine, 'core', [(0, 1), (1, 0)])  7.22 us
    all_to_all x1, waiting for transfers between devices, body(): mine = lax.all_to_all(copies, ('gx', 'chip'), 0, 0).reshape(-1, 128)  2.65 us
  transfers between devices with their start and end apart: 10, of which 9 were waited for; matrix products, arithmetic and copies ran while one was open for 1% of the time, Pallas kernels for 3%

profile of v2, /device:TPU:1, one launch (start us, length us, event | category | flops | bytes accessed | tf_op | source)
XLA Modules:
  0.0 93.6 jit_solution(14450017951367438027)
XLA Ops:
  0.6 0.8 constant_dynamic-update-slice_fusion.1
  1.5 0.8 constant_dynamic-update-slice_fusion
  2.3 4.8 %collective-permute-start = (f32[16,8,256]{2,1,0:T(8,128)S(1)}, f32[16,8,256]{2,1,0:T(8,128)S(1)}, u32[]{:S(2)}, u32[]{:S(2)}) collective-permute-start(f32[16,8,256]{2,1,0:T(8,128)S(1)} %constant_dynamic-update-slice_fusion), channel_id=1, source_target_pairs={{0,16},{16,32},{32,48},{48,64},{64,80},{80,96},{96,112},{112,128},... | collective-permute-start | bytes 393224 | tf_op jit(solution)/shard_map/ppermute | solution.py:474
  7.1 1.3 %collective-permute-start.1 = (f32[16,8,256]{2,1,0:T(8,128)S(1)}, f32[16,8,256]{2,1,0:T(8,128)S(1)}, u32[]{:S(2)}, u32[]{:S(2)}) collective-permute-start(f32[16,8,256]{2,1,0:T(8,128)S(1)} %constant_dynamic-update-slice_fusion), channel_id=1, source_target_pairs={{16,0},{32,16},{48,32},{64,48},{80,64},{96,80},{112,96},{128,112},... | collective-permute-start | bytes 393224 | tf_op jit(solution)/shard_map/ppermute | solution.py:475
  8.4 0.6 collective-permute-done
  9.1 0.8 constant_dynamic-update-slice_fusion.3
  9.9 3.6 %collective-permute-done.1 = f32[16,8,256]{2,1,0:T(8,128)S(1)} collective-permute-done((f32[16,8,256]{2,1,0:T(8,128)S(1)}, f32[16,8,256]{2,1,0:T(8,128)S(1)}, u32[]{:S(2)}, u32[]{:S(2)}) %collective-permute-start.1) | collective-permute-done | bytes 131104 | tf_op jit(solution)/shard_map/ppermute | solution.py:475
  13.5 0.8 constant_dynamic-update-slice_fusion.2
  14.4 5.8 %collective-permute-start.3 = (f32[42,8,256]{2,1,0:T(8,128)S(1)}, f32[42,8,256]{2,1,0:T(8,128)S(1)}, u32[]{:S(2)}, u32[]{:S(2)}) collective-permute-start(f32[42,8,256]{2,1,0:T(8,128)S(1)} %slice_dynamic-update-slice_fusion.2.own_ref), channel_id=1, source_target_pairs={{1,0},{2,1},{3,2},{4,3},{5,4},{6,5},{7,6},{8,7},{9,8},{10,9},{11,1... | collective-permute-start | bytes 1032200 | tf_op jit(solution)/shard_map/ppermute | solution.py:475
  20.1 1.9 %collective-permute-start.2 = (f32[42,8,256]{2,1,0:T(8,128)S(1)}, f32[42,8,256]{2,1,0:T(8,128)S(1)}, u32[]{:S(2)}, u32[]{:S(2)}) collective-permute-start(f32[42,8,256]{2,1,0:T(8,128)S(1)} %slice_dynamic-update-slice_fusion.2.own_ref), channel_id=1, source_target_pairs={{0,1},{1,2},{2,3},{3,4},{4,5},{5,6},{6,7},{7,8},{8,9},{9,10},{10,1... | collective-permute-start | bytes 1032200 | tf_op jit(solution)/shard_map/ppermute | solution.py:474
  22.1 2.4 %collective-permute-done.3.high_ref = f32[42,8,256]{2,1,0:T(8,128)S(1)} collective-permute-done((f32[42,8,256]{2,1,0:T(8,128)S(1)}, f32[42,8,256]{2,1,0:T(8,128)S(1)}, u32[]{:S(2)}, u32[]{:S(2)}) %collective-permute-start.3) | collective-permute-done | bytes 344096 | tf_op jit(solution)/shard_map/ppermute | solution.py:475
  24.5 1.8 %collective-permute-done.2.low_ref = f32[42,8,256]{2,1,0:T(8,128)S(1)} collective-permute-done((f32[42,8,256]{2,1,0:T(8,128)S(1)}, f32[42,8,256]{2,1,0:T(8,128)S(1)}, u32[]{:S(2)}, u32[]{:S(2)}) %collective-permute-start.2) | collective-permute-done | bytes 344096 | tf_op jit(solution)/shard_map/ppermute | solution.py:474
  26.2 5.3 %shard_map.41 = (f32[256,4,128]{2,1,0:T(4,128)}, f32[16,8,128]{2,1,0:T(8,128)S(1)}) custom-call(f32[42,8,256]{2,1,0:T(8,128)S(1)} %collective-permute-done.2.low_ref, f32[42,8,256]{2,1,0:T(8,128)S(1)} %slice_dynamic-update-slice_fusion.2.own_ref, f32[42,8,256]{2,1,0:T(8,128)S(1)} %collective-permute-done.3.high_ref), custom_call_target="tpu_custom_call" | custom-call | tf_op jit(solution)/shard_map/pallas_call | solution.py:461
  31.5 20.3 %all-to-all-start = ((f32[256,4,128]{2,1,0:T(4,128)}), f32[256,4,128]{2,1,0:T(4,128)S(1)}, u32[]{:S(2)}, u32[]{:S(2)}) async-start(f32[256,4,128]{2,1,0:T(4,128)} %get-tuple-element.11), calls=%async_computation | async-start | bytes 1048576 | tf_op jit(solution)/shard_map/all_to_all | solution.py:495
  51.8 1.6 %collective-permute-start.5 = (f32[16,8,128]{2,1,0:T(8,128)S(1)}, f32[16,8,128]{2,1,0:T(8,128)S(1)}, u32[]{:S(2)}, u32[]{:S(2)}) collective-permute-start(f32[16,8,128]{2,1,0:T(8,128)S(1)} %get-tuple-element.12), channel_id=1, source_target_pairs={{0,16},{16,32},{32,48},{48,64},{64,80},{80,96},{96,112},{112,128},... | collective-permute-start | bytes 196616 | tf_op jit(solution)/shard_map/ppermute | solution.py:474
  53.4 1.3 %collective-permute-start.6 = (f32[16,8,128]{2,1,0:T(8,128)S(1)}, f32[16,8,128]{2,1,0:T(8,128)S(1)}, u32[]{:S(2)}, u32[]{:S(2)}) collective-permute-start(f32[16,8,128]{2,1,0:T(8,128)S(1)} %get-tuple-element.12), channel_id=1, source_target_pairs={{16,0},{32,16},{48,32},{64,48},{80,64},{96,80},{112,96},{128,112},... | collective-permute-start | bytes 196616 | tf_op jit(solution)/shard_map/ppermute | solution.py:475
  54.7 7.0 %collective-permute-done.5 = f32[16,8,128]{2,1,0:T(8,128)S(1)} collective-permute-done((f32[16,8,128]{2,1,0:T(8,128)S(1)}, f32[16,8,128]{2,1,0:T(8,128)S(1)}, u32[]{:S(2)}, u32[]{:S(2)}) %collective-permute-start.5) | collective-permute-done | bytes 65568 | tf_op jit(solution)/shard_map/ppermute | solution.py:474
  61.7 3.2 %collective-permute-done.6 = f32[16,8,128]{2,1,0:T(8,128)S(1)} collective-permute-done((f32[16,8,128]{2,1,0:T(8,128)S(1)}, f32[16,8,128]{2,1,0:T(8,128)S(1)}, u32[]{:S(2)}, u32[]{:S(2)}) %collective-permute-start.6) | collective-permute-done | bytes 65568 | tf_op jit(solution)/shard_map/ppermute | solution.py:475
  65.0 2.6 %all-to-all-done = f32[256,4,128]{2,1,0:T(4,128)S(1)} async-done(((f32[256,4,128]{2,1,0:T(4,128)}), f32[256,4,128]{2,1,0:T(4,128)S(1)}, u32[]{:S(2)}, u32[]{:S(2)}) %all-to-all-start) | async-done | bytes 524320 | tf_op jit(solution)/shard_map/all_to_all | solution.py:495
  67.6 7.2 %collective-permute-start.4 = (f32[1024,128]{1,0:T(8,128)S(1)}, f32[1024,128]{1,0:T(8,128)S(1)}, u32[]{:S(2)}, u32[]{:S(2)}) collective-permute-start(f32[1024,128]{1,0:T(8,128)S(1)} %bitcast.3), channel_id=1, source_target_pairs={{0,1},{1,0},{2,3},{3,2},{4,5},{5,4},{6,7},{7,6},{8,9},{9,8},{10,11... | collective-permute-start | bytes 1572872 | tf_op jit(solution)/shard_map/ppermute | solution.py:496
  74.9 1.9 %collective-permute-start.8 = (f32[32,8,128]{2,1,0:T(8,128)S(1)}, f32[32,8,128]{2,1,0:T(8,128)S(1)}, u32[]{:S(2)}, u32[]{:S(2)}) collective-permute-start(f32[32,8,128]{2,1,0:T(8,128)S(1)} %constant_dynamic-update-slice_fusion.4.own1_ref), channel_id=1, source_target_pairs={{1,0},{2,1},{3,2},{4,3},{5,4},{6,5},{7,6},{8,7},{9,8},{10,9},{11,1... | collective-permute-start | bytes 393224 | tf_op jit(solution)/shard_map/ppermute | solution.py:475
  76.8 3.6 %collective-permute-start.7 = (f32[32,8,128]{2,1,0:T(8,128)S(1)}, f32[32,8,128]{2,1,0:T(8,128)S(1)}, u32[]{:S(2)}, u32[]{:S(2)}) collective-permute-start(f32[32,8,128]{2,1,0:T(8,128)S(1)} %constant_dynamic-update-slice_fusion.4.own1_ref), channel_id=1, source_target_pairs={{0,1},{1,2},{2,3},{3,4},{4,5},{5,6},{6,7},{7,8},{8,9},{9,10},{10,1... | collective-permute-start | bytes 393224 | tf_op jit(solution)/shard_map/ppermute | solution.py:474
  80.5 0.1 pad_add_fusion.place_ref
  80.5 0.6 collective-permute-done.8.high1_ref
  81.2 1.2 %collective-permute-done.7.low1_ref = f32[32,8,128]{2,1,0:T(8,128)S(1)} collective-permute-done((f32[32,8,128]{2,1,0:T(8,128)S(1)}, f32[32,8,128]{2,1,0:T(8,128)S(1)}, u32[]{:S(2)}, u32[]{:S(2)}) %collective-permute-start.7) | collective-permute-done | bytes 131104 | tf_op jit(solution)/shard_map/ppermute | solution.py:474
  82.4 2.4 %shard_map.43 = (f32[6,16,16,128]{3,2,1,0:T(8,128)S(1)}, f32[16,16,128]{2,1,0:T(8,128)S(1)}, f32[16,16,128]{2,1,0:T(8,128)S(1)}, f32[6,16,16,256]{3,2,1,0:T(8,12...) custom-call(f32[32,8,128]{2,1,0:T(8,128)S(1)} %collective-permute-done.7.low1_ref, ...), custom_call_target="tpu_custom_call" | custom-call | tf_op jit(solution)/shard_map/pallas_call | solution.py:461
  84.8 0.0 collective-permute-done.4.other_ref
  84.8 6.4 %shard_map.42.near_ref = f32[6,16,128]{2,1,0:T(8,128)S(1)} custom-call(s32[2]{0:T(128)S(1)} %pad_add_fusion.place_ref, f32[1024,128]{1,0:T(8,128)S(1)} %bitcast.4, f32[1024,128]{1,0:T(8,128)S(1)} %collective-permute-done.4.other_ref), custom_call_target="tpu_custom_call" | custom-call | tf_op jit(solution)/shard_map/pallas_call | solution.py:461
  91.2 2.3 %shard_map.44 = (f32[8,8,256]{2,1,0:T(8,128)}, f32[8,8,256]{2,1,0:T(8,128)}) custom-call(f32[6,16,128]{2,1,0:T(8,128)S(1)} %shard_map.42.near_ref, f32[6,16,16,128]{3,2,1,0:T(8,128)S(1)} %get-tuple-element.13.c1, f32[16,16,128]{2,1,0:T(8,128)S(1)} %get-tuple-element.14.g1, f32[16,16,128]{2,1,0:T(8,128)S(1)} %get-tuple-element.15.x1, ...), custom_call_target="tpu_custom_call" | custom-call | tf_op jit(solution)/shard_map/pallas_call | solution.py:461
  (10 shorter events, 0.0 us)
Async XLA Ops:
  2.3 6.8 %collective-permute-start = (f32[16,8,256]{2,1,0:T(8,128)S(1)}, f32[16,8,256]{2,1,0:T(8,128)S(1)}, u32[]{:S(2)}, u32[]{:S(2)}) collective-permute-start(f32[16,8,256]{2,1,0:T(8,128)S(1)} %constant_dynamic-update-slice_fusion), channel_id=1, source_target_pairs={{0,16},{16,32},{32,48},{48,64},{64,80},{80,96},{96,112},{112,128},... | collective-permute-start | bytes 393224 | tf_op jit(solution)/shard_map/ppermute | solution.py:474
  7.1 6.3 %collective-permute-start.1 = (f32[16,8,256]{2,1,0:T(8,128)S(1)}, f32[16,8,256]{2,1,0:T(8,128)S(1)}, u32[]{:S(2)}, u32[]{:S(2)}) collective-permute-start(f32[16,8,256]{2,1,0:T(8,128)S(1)} %constant_dynamic-update-slice_fusion), channel_id=1, source_target_pairs={{16,0},{32,16},{48,32},{64,48},{80,64},{96,80},{112,96},{128,112},... | collective-permute-start | bytes 393224 | tf_op jit(solution)/shard_map/ppermute | solution.py:475
  14.4 10.1 %collective-permute-start.3 = (f32[42,8,256]{2,1,0:T(8,128)S(1)}, f32[42,8,256]{2,1,0:T(8,128)S(1)}, u32[]{:S(2)}, u32[]{:S(2)}) collective-permute-start(f32[42,8,256]{2,1,0:T(8,128)S(1)} %slice_dynamic-update-slice_fusion.2.own_ref), channel_id=1, source_target_pairs={{1,0},{2,1},{3,2},{4,3},{5,4},{6,5},{7,6},{8,7},{9,8},{10,9},{11,1... | collective-permute-start | bytes 1032200 | tf_op jit(solution)/shard_map/ppermute | solution.py:475
  20.1 6.1 %collective-permute-start.2 = (f32[42,8,256]{2,1,0:T(8,128)S(1)}, f32[42,8,256]{2,1,0:T(8,128)S(1)}, u32[]{:S(2)}, u32[]{:S(2)}) collective-permute-start(f32[42,8,256]{2,1,0:T(8,128)S(1)} %slice_dynamic-update-slice_fusion.2.own_ref), channel_id=1, source_target_pairs={{0,1},{1,2},{2,3},{3,4},{4,5},{5,6},{6,7},{7,8},{8,9},{9,10},{10,1... | collective-permute-start | bytes 1032200 | tf_op jit(solution)/shard_map/ppermute | solution.py:474
  31.5 36.1 %all-to-all-start = ((f32[256,4,128]{2,1,0:T(4,128)}), f32[256,4,128]{2,1,0:T(4,128)S(1)}, u32[]{:S(2)}, u32[]{:S(2)}) async-start(f32[256,4,128]{2,1,0:T(4,128)} %get-tuple-element.11), calls=%async_computation | async-start | bytes 1048576 | tf_op jit(solution)/shard_map/all_to_all | solution.py:495
  51.8 9.9 %collective-permute-start.5 = (f32[16,8,128]{2,1,0:T(8,128)S(1)}, f32[16,8,128]{2,1,0:T(8,128)S(1)}, u32[]{:S(2)}, u32[]{:S(2)}) collective-permute-start(f32[16,8,128]{2,1,0:T(8,128)S(1)} %get-tuple-element.12), channel_id=1, source_target_pairs={{0,16},{16,32},{32,48},{48,64},{64,80},{80,96},{96,112},{112,128},... | collective-permute-start | bytes 196616 | tf_op jit(solution)/shard_map/ppermute | solution.py:474
  53.4 11.5 %collective-permute-start.6 = (f32[16,8,128]{2,1,0:T(8,128)S(1)}, f32[16,8,128]{2,1,0:T(8,128)S(1)}, u32[]{:S(2)}, u32[]{:S(2)}) collective-permute-start(f32[16,8,128]{2,1,0:T(8,128)S(1)} %get-tuple-element.12), channel_id=1, source_target_pairs={{16,0},{32,16},{48,32},{64,48},{80,64},{96,80},{112,96},{128,112},... | collective-permute-start | bytes 196616 | tf_op jit(solution)/shard_map/ppermute | solution.py:475
  67.6 17.2 %collective-permute-start.4 = (f32[1024,128]{1,0:T(8,128)S(1)}, f32[1024,128]{1,0:T(8,128)S(1)}, u32[]{:S(2)}, u32[]{:S(2)}) collective-permute-start(f32[1024,128]{1,0:T(8,128)S(1)} %bitcast.3), channel_id=1, source_target_pairs={{0,1},{1,0},{2,3},{3,2},{4,5},{5,4},{6,7},{7,6},{8,9},{9,8},{10,11... | collective-permute-start | bytes 1572872 | tf_op jit(solution)/shard_map/ppermute | solution.py:496
  74.9 6.3 %collective-permute-start.8 = (f32[32,8,128]{2,1,0:T(8,128)S(1)}, f32[32,8,128]{2,1,0:T(8,128)S(1)}, u32[]{:S(2)}, u32[]{:S(2)}) collective-permute-start(f32[32,8,128]{2,1,0:T(8,128)S(1)} %constant_dynamic-update-slice_fusion.4.own1_ref), channel_id=1, source_target_pairs={{1,0},{2,1},{3,2},{4,3},{5,4},{6,5},{7,6},{8,7},{9,8},{10,9},{11,1... | collective-permute-start | bytes 393224 | tf_op jit(solution)/shard_map/ppermute | solution.py:475
  76.8 5.6 %collective-permute-start.7 = (f32[32,8,128]{2,1,0:T(8,128)S(1)}, f32[32,8,128]{2,1,0:T(8,128)S(1)}, u32[]{:S(2)}, u32[]{:S(2)}) collective-permute-start(f32[32,8,128]{2,1,0:T(8,128)S(1)} %constant_dynamic-update-slice_fusion.4.own1_ref), channel_id=1, source_target_pairs={{0,1},{1,2},{2,3},{3,4},{4,5},{5,6},{6,7},{7,8},{8,9},{9,10},{10,1... | collective-permute-start | bytes 393224 | tf_op jit(solution)/shard_map/ppermute | solution.py:474

commit v3 on v2

--- a/solution.py
+++ b/solution.py
@@ -98,12 +98,71 @@
     return total
 
 
-def fine_kernel(low_ref, own_ref, high_ref, copies_ref, share_ref,
-                k0, c0, diag0, g0, d0, e0, sums, zsums, k1, f1, c1, diag1, g1, d1, e1, out):
-    for index in range(22):
-        k0[index, 0:8] = low_ref[index]
-        k0[index, 8:16] = own_ref[index]
-        k0[index, 16:24] = high_ref[index]
+PAIRS = ([("k", dx, 7 - dx) for dx in (1, 2, 3)], [("f", dx, 6 - dx) for dx in (1, 2, 3)])
+Y_TILES = 28
+
+
+def pack_x_kernel(k_ref, f_ref, up_ref, down_ref):
+    up_ref[0:7] = k_ref[1:8]
+    up_ref[7:13] = f_ref[2:8]
+    down_ref[0:7] = k_ref[0:7]
+    down_ref[7:13] = f_ref[0:6]
+
+
+def pair_tiles():
+    tile = 16
+    for pairs in PAIRS:
+        for side in ("low", "high"):
+            for name, dx, far in pairs:
+                yield tile, name, side, dx, far
+                tile += 1
+
+
+def halo_plane(name, side, dx, low_ref, high_ref):
+    reach = 7 if name == "k" else 6
+    base = 0 if name == "k" else 7
+    return low_ref[base + reach - dx] if side == "low" else high_ref[base + dx - 1]
+
+
+def pack_y_kernel(k_ref, f_ref, low_ref, high_ref, up_ref, down_ref):
+    for ref in (up_ref, down_ref):
+        ref[0:8] = k_ref[...]
+        ref[8:16] = f_ref[...]
+    row = iota((8, k_ref.shape[2]), 0)
+    for tile, name, side, dx, far in pair_tiles():
+        near_plane = halo_plane(name, side, dx, low_ref, high_ref)
+        far_plane = halo_plane(name, side, far, low_ref, high_ref)
+        up_ref[tile] = jnp.where(row < dx, shifted(far_plane, 8 - dx, 0), near_plane)
+        down_ref[tile] = jnp.where(row >= 8 - dx, shifted(far_plane, dx - 8, 0), near_plane)
+
+
+def unpack(k_ref, f_ref, x_low_ref, x_high_ref, y_low_ref, y_high_ref, k0, f0):
+    for to, base, reach, name, ref in ((k0, 0, 7, "k", k_ref), (f0, 8, 6, "f", f_ref)):
+        to[reach:reach + 8, 0:8] = y_low_ref[base:base + 8]
+        to[reach:reach + 8, 8:16] = ref[...]
+        to[reach:reach + 8, 16:24] = y_high_ref[base:base + 8]
+        first = 0 if name == "k" else 7
+        to[0:reach, 8:16] = x_low_ref[first:first + reach]
+        to[reach + 8:2 * reach + 8, 8:16] = x_high_ref[first:first + reach]
+        for plane in (0, 2 * reach + 7):
+            to[plane, 0:8] = jnp.zeros(ref.shape[1:], F32)
+            to[plane, 16:24] = jnp.zeros(ref.shape[1:], F32)
+    for tile, name, side, dx, far in pair_tiles():
+        to, reach = (k0, 7) if name == "k" else (f0, 6)
+        near_plane = reach - dx if side == "low" else reach + 7 + dx
+        far_plane = reach - far if side == "low" else reach + 7 + far
+        below, above = y_low_ref[tile], y_high_ref[tile]
+        to[near_plane, 0:8] = below
+        to[near_plane, 16:24] = above
+        if far != dx:
+            to[far_plane, 0:8] = shifted(below, dx - 8, 0)
+            to[far_plane, 16:24] = shifted(above, 8 - dx, 0)
+
+
+def fine_kernel(k_ref, f_ref, x_low_ref, x_high_ref, y_low_ref, y_high_ref,
+                k0, f0, k1, f1, up_ref, down_ref,
+                c0, diag0, g0, d0, e0, sums, zsums):
+    unpack(k_ref, f_ref, x_low_ref, x_high_ref, y_low_ref, y_high_ref, k0, f0)
 
     def setup(start):
         at = pl.ds(start, 2)
@@ -111,8 +170,7 @@
         for number in range(6):
             c0.at[number][at] = couplings[number]
         diag0[at] = diagonal
-        force = pl.ds(start + 22, 2)
-        scaled = inverse * jnp.concatenate([low_ref[force], own_ref[force], high_ref[force]], 1)
+        scaled = inverse * f0[at]
         g0[at] = scaled
         d0[at] = FIRST * scaled
 
@@ -143,9 +201,13 @@
     rows = zsums[:, pl.ds(0, 12, stride=2), :] + zsums[:, pl.ds(1, 12, stride=2), :]
     f1[:, 2:14, :] = rows[0:8]
     k1[:, 2:14, :] = rows[8:18]
-    share_ref[0:8] = k1[1:9, 4:12, :]
-    share_ref[8:16] = f1[:, 4:12, :]
-
+    up_ref[0:6] = k1[1:7, 4:12, :]
+    up_ref[6:11] = f1[1:6, 4:12, :]
+    down_ref[0:6] = k1[3:9, 4:12, :]
+    down_ref[6:11] = f1[2:7, 4:12, :]
+
+
+def next_kernel(k1, f1, copies_ref, c1, diag1, g1, d1, e1, out):
     def setup1(start):
         at = pl.ds(start, 4)
         couplings, inverse, diagonal = coupling(k1[pl.ds(start + 1, 4)], near_inside(k1, start + 1, 4), (4, 5))
@@ -348,24 +410,36 @@
     return coarse_kernel
 
 
-def prepare_kernel(low1_ref, own1_ref, high1_ref, low_ref, own_ref, high_ref,
-                   c1, g1, x1, c0, diag0, g0, x0, k1, d1, k0, d0, all0):
-    def join(start, size):
-        at = pl.ds(start, size)
-        row = iota((size, 8, 128), 1)
-        middle = shifted(own1_ref[at], 4, 1)
-        return jnp.concatenate([jnp.where(row < 6, low1_ref[at], middle),
-                                jnp.where(row < 2, middle, high1_ref[at])], 1)
-
-    k1[0:8] = join(0, 8)
-    k1[8:16] = join(8, 8)
+def pack_share_kernel(k1, f1, low_ref, high_ref, out_ref):
+    out_ref[0:5] = low_ref[1:6]
+    out_ref[5:9] = k1[3:7, 4:12, :]
+    out_ref[9:14] = high_ref[0:5]
+    out_ref[14:18] = low_ref[7:11]
+    out_ref[18:22] = f1[2:6, 4:12, :]
+    out_ref[22:26] = high_ref[6:10]
+
+
+def prepare_kernel(x_low_ref, x_high_ref, y_low_ref, own_ref, y_high_ref, k_ref, f_ref,
+                   c1, g1, x1, c0, diag0, g0, x0, k1, f1, d1, d0):
+    row = iota((8, 128), 0)
+
+    def join(low, middle, high):
+        middle = shifted(middle, 4, 1)
+        return jnp.concatenate([jnp.where(row < 6, low, middle), jnp.where(row < 2, middle, high)], 1)
+
+    zero = jnp.zeros((1, 8, 128), F32)
+    k1[1:15] = join(y_low_ref[0:14], own_ref[0:14], y_high_ref[0:14])
+    f1[2:14] = join(y_low_ref[14:26], own_ref[14:26], y_high_ref[14:26])
+    for to, plane, tile in ((k1, 0, x_low_ref[0:1]), (k1, 15, x_high_ref[5:6]),
+                            (f1, 1, x_low_ref[6:7]), (f1, 14, x_high_ref[10:11])):
+        to[plane:plane + 1] = join(zero, tile, zero)
 
     def setup1(start):
         at = pl.ds(start, 7)
         couplings, inverse, _ = coupling(k1[at], near_inside(k1, start, 7), (4, 5))
         for number in range(6):
             c1.at[number][at] = couplings[number]
-        scaled = inverse * join(start + 16, 7)
+        scaled = inverse * f1[at]
         g1[at] = scaled
         d1[at] = FIRST * scaled
 
@@ -379,23 +453,16 @@
 
     blocks(2, 14, 6, guess1)
 
-    def load0(start):
-        at = pl.ds(start + 2, 2)
-        k0[pl.ds(start, 2)] = jnp.concatenate([low_ref[at], own_ref[at], high_ref[at]], 1)
-
-    blocks(0, 18, 2, load0)
-
     def setup0(start):
         def cut(value):
             return shifted(value, 4, 1)[:, 0:16]
 
         at = pl.ds(start, 2)
-        couplings, inverse, diagonal = coupling(k0[pl.ds(start + 1, 2)], near_inside(k0, start + 1, 2), (4, 5))
+        couplings, inverse, diagonal = coupling(k_ref[pl.ds(start + 3, 2)], near_inside(k_ref, start + 3, 2), (4, 5))
         for number in range(6):
             c0.at[number][at] = cut(couplings[number])
         diag0[at] = cut(diagonal)
-        force = pl.ds(start + 24, 2)
-        scaled = cut(inverse * jnp.concatenate([low_ref[force], own_ref[force], high_ref[force]], 1))
+        scaled = cut(inverse * f_ref[pl.ds(start + 2, 2)])
         g0[at] = scaled
         d0[at] = FIRST * scaled
 
@@ -455,7 +522,7 @@
     blocks(4, 12, 2, last0)
 
 
-def call(kernel, limit, shapes, scratch, *operands, scalars=0):
+def call(kernel, limit, shapes, scratch, *operands, scalars=0, flops=0):
     specs = [pl.BlockSpec(memory_space=pltpu.SMEM)] * scalars
     specs += [pl.BlockSpec(memory_space=pltpu.VMEM)] * (len(operands) - scalars)
     return pl.pallas_call(
@@ -465,44 +532,51 @@
         out_specs=[pl.BlockSpec(memory_space=pltpu.VMEM)] * len(shapes),
         scratch_shapes=[pltpu.VMEM(shape, F32) for shape in scratch],
         compiler_params=pltpu.CompilerParams(vmem_limit_bytes=limit * MIB),
+        cost_estimate=pl.CostEstimate(flops=flops, bytes_accessed=0, transcendentals=0) if flops else None,
         interpret=INTERPRET,
     )(*operands)
 
 
-def both_sides(value, axes):
+def both_sides(up, down, axes):
     count = math.prod(lax.axis_size(axis) for axis in axes)
-    low = lax.ppermute(value, axes, [(i, i + 1) for i in range(count - 1)])
-    high = lax.ppermute(value, axes, [(i + 1, i) for i in range(count - 1)])
+    low = lax.ppermute(up, axes, [(i, i + 1) for i in range(count - 1)])
+    high = lax.ppermute(down, axes, [(i + 1, i) for i in range(count - 1)])
     return low, high
 
 
-def body(forcing, coefficient):
+def body(f, k):
     count_x, chips = lax.axis_size("gx"), lax.axis_size("chip")
     count_y = 2 * chips
-    block = jnp.concatenate([coefficient, forcing], 0)
-    low, high = both_sides(block, ("gx",))
-    own = jnp.concatenate([low[1:8], coefficient, high[0:7], low[10:16], forcing, high[8:14]], 0)
-    low, high = both_sides(own, ("chip", "core"))
-
-    full, half, full1 = (24, 256), (16, 256), (16, 128)
-    copies, share = call(
+    along_x, along_y = ("gx",), ("chip", "core")
+    tile, full, half = f.shape[1:], (24, 256), (16, 256)
+    tile1, full1 = (8, 128), (16, 128)
+    up, down = call(pack_x_kernel, 4, [(13, *tile)] * 2, [], k, f)
+    x_low, x_high = both_sides(up, down, along_x)
+    up, down = call(pack_y_kernel, 4, [(Y_TILES, *tile)] * 2, [], k, f, x_low, x_high)
+    y_low, y_high = both_sides(up, down, along_y)
+
+    k0, f0, k1, f1, up, down = call(
         fine_kernel, 16,
-        [(count_x * chips, 4, 128), (16, 8, 128)],
-        [(22, *full), (6, 20, *full)] + [(20, *full)] * 4 + [(18, *full), (18, 24, 128)]
-        + [(10, *full1), (8, *full1), (6, 8, *full1)] + [(8, *full1)] * 4 + [(4, *full1)],
-        low, own, high)
+        [(22, *full), (20, *full), (10, *full1), (8, *full1), (11, *tile1), (11, *tile1)],
+        [(6, 20, *full)] + [(20, *full)] * 4 + [(18, *full), (18, 24, 128)],
+        k, f, x_low, x_high, y_low, y_high)
+    x_low, x_high = both_sides(up, down, along_x)
+    copies, = call(
+        next_kernel, 8,
+        [(count_x * chips, 4, 128)],
+        [(6, 8, *full1)] + [(8, *full1)] * 4 + [(4, *full1)],
+        k1, f1, flops=1500000000)
 
     mine = lax.all_to_all(copies, ("gx", "chip"), 0, 0).reshape(-1, 128)
     other = lax.ppermute(mine, "core", [(0, 1), (1, 0)])
 
-    low1, high1 = both_sides(share, ("gx",))
-    own1 = jnp.concatenate([low1[0:6], share[2:6], high1[2:8], low1[8:14], share[10:14], high1[10:16]], 0)
-    low1, high1 = both_sides(own1, ("chip", "core"))
+    own, = call(pack_share_kernel, 4, [(26, *tile1)], [], k1, f1, x_low, x_high)
+    y_low, y_high = both_sides(own, own, along_y)
     prepared = call(
         prepare_kernel, 16,
         [(6, 16, *full1)] + [(16, *full1)] * 2 + [(6, 16, *half)] + [(16, *half)] * 3,
-        [(16, *full1)] * 2 + [(18, *full), (16, *half), (1, *full)],
-        low1, own1, high1, low, own, high)
+        [(16, *full1)] * 3 + [(16, *half)],
+        x_low, x_high, y_low, own, y_high, k0, f0, flops=2500000000)
 
     place = jnp.stack([lax.axis_index("gx"), lax.axis_index(("chip", "core"))]).astype(jnp.int32)
     plane2 = (2, count_y // 2, 128)
@@ -512,11 +586,11 @@
         [(6, 16, 128)],
         [padded, (6, *padded)] + [padded] * 5
         + [(2 * count_x, *plane2), (6, count_x // 4, *plane2), (count_x // 4, *plane2), (10, *plane2)],
-        place, mine, other, scalars=1)
+        place, mine, other, scalars=1, flops=6000000000)
 
     correction, residual = call(
         post_kernel, 16,
-        [forcing.shape, forcing.shape],
+        [f.shape, f.shape],
         [(16, *full1)] * 3 + [(8, *full1)] + [(16, *half)] * 4,
         near_e, *prepared)
     return correction, residual

time: 94.2 us -> 104 us (1.10)
  blocking collectives: 0 us -> 41.4 us
  starting transfers between devices: 49.8 us -> 27.3 us
  waiting for transfers between devices: 23.1 us -> 15.1 us
    all_to_all x0 -> x1, blocking collectives: none -> 41.4 us  [body(): mine = lax.all_to_all(copies, ('gx', 'chip'), 0, 0).reshape(-1, 128)]
    all_to_all x1 -> x0, starting transfers between devices: 20.3 us -> none  [body(): mine = lax.all_to_all(copies, ('gx', 'chip'), 0, 0).reshape(-1, 128)]
    ppermute x8, waiting for transfers between devices: 20.4 us -> 15.1 us  [the longest x4 12.6 us: both_sides(): high = lax.ppermute(down, axes, [(i + 1, i) for i in range(count - 1)])]
    ppermute x1, starting transfers between devices: 7.22 us -> 3.41 us  [body(): other = lax.ppermute(mine, 'core', [(0, 1), (1, 0)])]
    all_to_all x1 -> x0, waiting for transfers between devices: 2.65 us -> none  [body(): mine = lax.all_to_all(copies, ('gx', 'chip'), 0, 0).reshape(-1, 128)]
    ppermute x8, starting transfers between devices: 22.3 us -> 23.9 us  [the longest x4 15.9 us: both_sides(): low = lax.ppermute(up, axes, [(i, i + 1) for i in range(count - 1)])]
    pallas_call x4 -> x8, Pallas kernels: 16.5 us -> 15.6 us  [call(): pl.pallas_call(kernel, out_shape=[jax.ShapeDtypeStruct(shape, F32) for sh...]
    unnamed x11 -> x8, local copies, waits for them, and re-layouts: 2.57 us -> 3.35 us
  transfers between devices with their start and end apart: 10 -> 9, of which waited for: 9 -> 7; matrix products, arithmetic and copies ran while one was open for 1% -> 0% of each run, Pallas kernels for 3% -> 2%
where the time goes in v3:
time: 104 us
  blocking collectives  41.4 us (40%)
  starting transfers between devices  27.3 us (26%)
  Pallas kernels  15.6 us (15%)
  waiting for transfers between devices  15.1 us (15%)
  local copies, waits for them, and re-layouts  3.35 us (3%)
    all_to_all x1, blocking collectives, body(): mine = lax.all_to_all(copies, ('gx', 'chip'), 0, 0).reshape(-1, 128)  41.4 us
    ppermute x4, starting transfers between devices, both_sides(): low = lax.ppermute(up, axes, [(i, i + 1) for i in range(count - 1)])  15.9 us
    pallas_call x8, Pallas kernels, call(): pl.pallas_call(kernel, out_shape=[jax.ShapeDtypeStruct(shape, F32) for sh...  15.6 us
    ppermute x4, waiting for transfers between devices, both_sides(): high = lax.ppermute(down, axes, [(i + 1, i) for i in range(count - 1)])  12.6 us
    ppermute x4, starting transfers between devices, both_sides(): high = lax.ppermute(down, axes, [(i + 1, i) for i in range(count - 1)])  8.08 us
    ppermute x1, starting transfers between devices, body(): other = lax.ppermute(mine, 'core', [(0, 1), (1, 0)])  3.41 us
    unnamed x8, local copies, waits for them, and re-layouts  3.35 us
    ppermute x4, waiting for transfers between devices, both_sides(): low = lax.ppermute(up, axes, [(i, i + 1) for i in range(count - 1)])  2.43 us
  transfers between devices with their start and end apart: 9, of which 7 were waited for; matrix products, arithmetic and copies ran while one was open for 0% of the time, Pallas kernels for 2%

profile of v3, /device:TPU:1, one launch (start us, length us, event | category | flops | bytes accessed | tf_op | source)
XLA Modules:
  0.0 103.6 jit_solution(9309731287302032788)
XLA Ops:
  0.6 0.0 copy-start
  0.6 0.8 copy-done
  1.5 0.0 copy-start.2
  1.5 0.8 copy-done.2
  2.3 4.8 %collective-permute-start = (f32[13,8,256]{2,1,0:T(8,128)S(1)}, f32[13,8,256]{2,1,0:T(8,128)S(1)}, u32[]{:S(2)}, u32[]{:S(2)}) collective-permute-start(f32[13,8,256]{2,1,0:T(8,128)S(1)} %get-tuple-element.19), channel_id=1, source_target_pairs={{0,16},{16,32},{32,48},{48,64},{64,80},{80,96},{96,112},{112,128},... | collective-permute-start | bytes 319496 | tf_op jit(solution)/shard_map/ppermute | solution.py:542
  7.2 1.3 %collective-permute-start.1 = (f32[13,8,256]{2,1,0:T(8,128)S(1)}, f32[13,8,256]{2,1,0:T(8,128)S(1)}, u32[]{:S(2)}, u32[]{:S(2)}) collective-permute-start(f32[13,8,256]{2,1,0:T(8,128)S(1)} %get-tuple-element.20), channel_id=1, source_target_pairs={{16,0},{32,16},{48,32},{64,48},{80,64},{96,80},{112,96},{128,112},... | collective-permute-start | bytes 319496 | tf_op jit(solution)/shard_map/ppermute | solution.py:543
  8.5 0.4 collective-permute-done.low_ref.x_low_ref
  8.9 4.4 %collective-permute-done.1.high_ref.x_high_ref = f32[13,8,256]{2,1,0:T(8,128)S(1)} collective-permute-done((f32[13,8,256]{2,1,0:T(8,128)S(1)}, f32[13,8,256]{2,1,0:T(8,128)S(1)}, u32[]{:S(2)}, u32[]{:S(2)}) %collective-permute-start.1) | collective-permute-done | bytes 106528 | tf_op jit(solution)/shard_map/ppermute | solution.py:543
  13.3 4.9 %collective-permute-start.2 = (f32[28,8,256]{2,1,0:T(8,128)S(1)}, f32[28,8,256]{2,1,0:T(8,128)S(1)}, u32[]{:S(2)}, u32[]{:S(2)}) collective-permute-start(f32[28,8,256]{2,1,0:T(8,128)S(1)} %get-tuple-element.21), channel_id=1, source_target_pairs={{0,1},{1,2},{2,3},{3,4},{4,5},{5,6},{6,7},{7,8},{8,9},{9,10},{10,1... | collective-permute-start | bytes 688136 | tf_op jit(solution)/shard_map/ppermute | solution.py:542
  18.2 2.1 %collective-permute-start.3 = (f32[28,8,256]{2,1,0:T(8,128)S(1)}, f32[28,8,256]{2,1,0:T(8,128)S(1)}, u32[]{:S(2)}, u32[]{:S(2)}) collective-permute-start(f32[28,8,256]{2,1,0:T(8,128)S(1)} %get-tuple-element.22), channel_id=1, source_target_pairs={{1,0},{2,1},{3,2},{4,3},{5,4},{6,5},{7,6},{8,7},{9,8},{10,9},{11,1... | collective-permute-start | bytes 688136 | tf_op jit(solution)/shard_map/ppermute | solution.py:543
  20.4 0.8 collective-permute-done.2.y_low_ref
  21.2 4.4 %collective-permute-done.3.y_high_ref = f32[28,8,256]{2,1,0:T(8,128)S(1)} collective-permute-done((f32[28,8,256]{2,1,0:T(8,128)S(1)}, f32[28,8,256]{2,1,0:T(8,128)S(1)}, u32[]{:S(2)}, u32[]{:S(2)}) %collective-permute-start.3) | collective-permute-done | bytes 229408 | tf_op jit(solution)/shard_map/ppermute | solution.py:543
  25.6 0.0 copy-start.1
  25.6 0.8 copy-done.1
  26.4 0.0 copy-start.3
  26.4 0.8 copy-done.3
  27.2 3.7 %shard_map.43 = (f32[22,24,256]{2,1,0:T(8,128)S(1)}, f32[20,24,256]{2,1,0:T(8,128)S(1)}, f32[10,16,128]{2,1,0:T(8,128)S(1)}, f32[8,16,128]{2,1,0:T(8,128)S(1)}, ...) custom-call(f32[8,8,256]{2,1,0:T(8,128)S(1)} %copy-done.1, f32[8,8,256]{2,1,0:T(8,128)S(1)} %copy-done.3, ...), custom_call_target="tpu_custom_call" | custom-call | tf_op jit(solution)/shard_map/pallas_call | solution.py:528
  30.9 0.7 shard_map.44
  31.7 41.4 %all_to_all.5 = f32[256,4,128]{2,1,0:T(4,128)S(1)} all-to-all(f32[256,4,128]{2,1,0:T(4,128)S(1)} %shard_map.44), channel_id=1, replica_groups=mesh['gx'=32,'chip'=8,'core'=2] {'gx','chip'}, dimensions={0} | all-to-all | bytes 1048576 | tf_op jit(solution)/shard_map/all_to_all | solution.py:570
  73.1 3.4 %collective-permute-start.4 = (f32[1024,128]{1,0:T(8,128)S(1)}, f32[1024,128]{1,0:T(8,128)S(1)}, u32[]{:S(2)}, u32[]{:S(2)}) collective-permute-start(f32[1024,128]{1,0:T(8,128)S(1)} %bitcast.3), channel_id=1, source_target_pairs={{0,1},{1,0},{2,3},{3,2},{4,5},{5,4},{6,7},{7,6},{8,9},{9,8},{10,11... | collective-permute-start | bytes 1572872 | tf_op jit(solution)/shard_map/ppermute | solution.py:571
  76.5 3.9 %collective-permute-start.5 = (f32[11,8,128]{2,1,0:T(8,128)S(1)}, f32[11,8,128]{2,1,0:T(8,128)S(1)}, u32[]{:S(2)}, u32[]{:S(2)}) collective-permute-start(f32[11,8,128]{2,1,0:T(8,128)S(1)} %get-tuple-element.25), channel_id=1, source_target_pairs={{0,16},{16,32},{32,48},{48,64},{64,80},{80,96},{96,112},{112,128},... | collective-permute-start | bytes 135176 | tf_op jit(solution)/shard_map/ppermute | solution.py:542
  80.4 1.3 %collective-permute-start.6 = (f32[11,8,128]{2,1,0:T(8,128)S(1)}, f32[11,8,128]{2,1,0:T(8,128)S(1)}, u32[]{:S(2)}, u32[]{:S(2)}) collective-permute-start(f32[11,8,128]{2,1,0:T(8,128)S(1)} %get-tuple-element.26), channel_id=1, source_target_pairs={{16,0},{32,16},{48,32},{64,48},{80,64},{96,80},{112,96},{128,112},... | collective-permute-start | bytes 135176 | tf_op jit(solution)/shard_map/ppermute | solution.py:543
  81.7 0.0 collective-permute-done.5.low_ref.x_low_ref
  81.7 3.5 %collective-permute-done.6.high_ref.x_high_ref = f32[11,8,128]{2,1,0:T(8,128)S(1)} collective-permute-done((f32[11,8,128]{2,1,0:T(8,128)S(1)}, f32[11,8,128]{2,1,0:T(8,128)S(1)}, u32[]{:S(2)}, u32[]{:S(2)}) %collective-permute-start.6) | collective-permute-done | bytes 45088 | tf_op jit(solution)/shard_map/ppermute | solution.py:543
  85.2 3.4 %collective-permute-start.8 = (f32[26,8,128]{2,1,0:T(8,128)S(1)}, f32[26,8,128]{2,1,0:T(8,128)S(1)}, u32[]{:S(2)}, u32[]{:S(2)}) collective-permute-start(f32[26,8,128]{2,1,0:T(8,128)S(1)} %shard_map.46.own_ref), channel_id=1, source_target_pairs={{1,0},{2,1},{3,2},{4,3},{5,4},{6,5},{7,6},{8,7},{9,8},{10,9},{11,1... | collective-permute-start | bytes 319496 | tf_op jit(solution)/shard_map/ppermute | solution.py:543
  88.5 2.2 %collective-permute-start.7 = (f32[26,8,128]{2,1,0:T(8,128)S(1)}, f32[26,8,128]{2,1,0:T(8,128)S(1)}, u32[]{:S(2)}, u32[]{:S(2)}) collective-permute-start(f32[26,8,128]{2,1,0:T(8,128)S(1)} %shard_map.46.own_ref), channel_id=1, source_target_pairs={{0,1},{1,2},{2,3},{3,4},{4,5},{5,6},{6,7},{7,8},{8,9},{9,10},{10,1... | collective-permute-start | bytes 319496 | tf_op jit(solution)/shard_map/ppermute | solution.py:542
  90.8 0.1 pad_add_fusion.place_ref
  90.8 0.4 collective-permute-done.8.y_high_ref
  91.2 1.2 %collective-permute-done.7.y_low_ref = f32[26,8,128]{2,1,0:T(8,128)S(1)} collective-permute-done((f32[26,8,128]{2,1,0:T(8,128)S(1)}, f32[26,8,128]{2,1,0:T(8,128)S(1)}, u32[]{:S(2)}, u32[]{:S(2)}) %collective-permute-start.7) | collective-permute-done | bytes 106528 | tf_op jit(solution)/shard_map/ppermute | solution.py:542
  92.5 2.4 %shard_map.47 = (f32[6,16,16,128]{3,2,1,0:T(8,128)S(1)}, f32[16,16,128]{2,1,0:T(8,128)S(1)}, f32[16,16,128]{2,1,0:T(8,128)S(1)}, f32[6,16,16,256]{3,2,1,0:T(8,12...) custom-call(f32[11,8,128]{2,1,0:T(8,128)S(1)} %collective-permute-done.5.low_ref.x_low_re, ...), custom_call_target="tpu_custom_call" | custom-call | flops 2500000000 | tf_op jit(solution)/shard_map/pallas_call | solution.py:528
  94.8 0.0 collective-permute-done.4.other_ref
  94.9 6.4 %shard_map.45.near_ref = f32[6,16,128]{2,1,0:T(8,128)S(1)} custom-call(s32[2]{0:T(128)S(1)} %pad_add_fusion.place_ref, f32[1024,128]{1,0:T(8,128)S(1)} %bitcast.4, f32[1024,128]{1,0:T(8,128)S(1)} %collective-permute-done.4.other_ref), custom_call_target="tpu_custom_call" | custom-call | flops 6000000000 | tf_op jit(solution)/shard_map/pallas_call | solution.py:528
  101.3 2.3 %shard_map.48 = (f32[8,8,256]{2,1,0:T(8,128)}, f32[8,8,256]{2,1,0:T(8,128)}) custom-call(f32[6,16,128]{2,1,0:T(8,128)S(1)} %shard_map.45.near_ref, f32[6,16,16,128]{3,2,1,0:T(8,128)S(1)} %get-tuple-element.29.c1, f32[16,16,128]{2,1,0:T(8,128)S(1)} %get-tuple-element.30.g1, f32[16,16,128]{2,1,0:T(8,128)S(1)} %get-tuple-element.31.x1, ...), custom_call_target="tpu_custom_call" | custom-call | tf_op jit(solution)/shard_map/pallas_call | solution.py:528
  (3 shorter events, 0.1 us)
Async XLA Ops:
  0.6 0.8 copy-start
  1.5 0.8 copy-start.2
  2.3 6.5 %collective-permute-start = (f32[13,8,256]{2,1,0:T(8,128)S(1)}, f32[13,8,256]{2,1,0:T(8,128)S(1)}, u32[]{:S(2)}, u32[]{:S(2)}) collective-permute-start(f32[13,8,256]{2,1,0:T(8,128)S(1)} %get-tuple-element.19), channel_id=1, source_target_pairs={{0,16},{16,32},{32,48},{48,64},{64,80},{80,96},{96,112},{112,128},... | collective-permute-start | bytes 319496 | tf_op jit(solution)/shard_map/ppermute | solution.py:542
  7.2 6.1 %collective-permute-start.1 = (f32[13,8,256]{2,1,0:T(8,128)S(1)}, f32[13,8,256]{2,1,0:T(8,128)S(1)}, u32[]{:S(2)}, u32[]{:S(2)}) collective-permute-start(f32[13,8,256]{2,1,0:T(8,128)S(1)} %get-tuple-element.20), channel_id=1, source_target_pairs={{16,0},{32,16},{48,32},{64,48},{80,64},{96,80},{112,96},{128,112},... | collective-permute-start | bytes 319496 | tf_op jit(solution)/shard_map/ppermute | solution.py:543
  13.3 7.9 %collective-permute-start.2 = (f32[28,8,256]{2,1,0:T(8,128)S(1)}, f32[28,8,256]{2,1,0:T(8,128)S(1)}, u32[]{:S(2)}, u32[]{:S(2)}) collective-permute-start(f32[28,8,256]{2,1,0:T(8,128)S(1)} %get-tuple-element.21), channel_id=1, source_target_pairs={{0,1},{1,2},{2,3},{3,4},{4,5},{5,6},{6,7},{7,8},{8,9},{9,10},{10,1... | collective-permute-start | bytes 688136 | tf_op jit(solution)/shard_map/ppermute | solution.py:542
  18.2 7.3 %collective-permute-start.3 = (f32[28,8,256]{2,1,0:T(8,128)S(1)}, f32[28,8,256]{2,1,0:T(8,128)S(1)}, u32[]{:S(2)}, u32[]{:S(2)}) collective-permute-start(f32[28,8,256]{2,1,0:T(8,128)S(1)} %get-tuple-element.22), channel_id=1, source_target_pairs={{1,0},{2,1},{3,2},{4,3},{5,4},{6,5},{7,6},{8,7},{9,8},{10,9},{11,1... | collective-permute-start | bytes 688136 | tf_op jit(solution)/shard_map/ppermute | solution.py:543
  25.6 0.8 copy-start.1
  26.4 0.8 copy-start.3
  73.1 21.8 %collective-permute-start.4 = (f32[1024,128]{1,0:T(8,128)S(1)}, f32[1024,128]{1,0:T(8,128)S(1)}, u32[]{:S(2)}, u32[]{:S(2)}) collective-permute-start(f32[1024,128]{1,0:T(8,128)S(1)} %bitcast.3), channel_id=1, source_target_pairs={{0,1},{1,0},{2,3},{3,2},{4,5},{5,4},{6,7},{7,6},{8,9},{9,8},{10,11... | collective-permute-start | bytes 1572872 | tf_op jit(solution)/shard_map/ppermute | solution.py:571
  76.5 5.2 %collective-permute-start.5 = (f32[11,8,128]{2,1,0:T(8,128)S(1)}, f32[11,8,128]{2,1,0:T(8,128)S(1)}, u32[]{:S(2)}, u32[]{:S(2)}) collective-permute-start(f32[11,8,128]{2,1,0:T(8,128)S(1)} %get-tuple-element.25), channel_id=1, source_target_pairs={{0,16},{16,32},{32,48},{48,64},{64,80},{80,96},{96,112},{112,128},... | collective-permute-start | bytes 135176 | tf_op jit(solution)/shard_map/ppermute | solution.py:542
  80.4 4.8 %collective-permute-start.6 = (f32[11,8,128]{2,1,0:T(8,128)S(1)}, f32[11,8,128]{2,1,0:T(8,128)S(1)}, u32[]{:S(2)}, u32[]{:S(2)}) collective-permute-start(f32[11,8,128]{2,1,0:T(8,128)S(1)} %get-tuple-element.26), channel_id=1, source_target_pairs={{16,0},{32,16},{48,32},{64,48},{80,64},{96,80},{112,96},{128,112},... | collective-permute-start | bytes 135176 | tf_op jit(solution)/shard_map/ppermute | solution.py:543
  85.2 6.0 %collective-permute-start.8 = (f32[26,8,128]{2,1,0:T(8,128)S(1)}, f32[26,8,128]{2,1,0:T(8,128)S(1)}, u32[]{:S(2)}, u32[]{:S(2)}) collective-permute-start(f32[26,8,128]{2,1,0:T(8,128)S(1)} %shard_map.46.own_ref), channel_id=1, source_target_pairs={{1,0},{2,1},{3,2},{4,3},{5,4},{6,5},{7,6},{8,7},{9,8},{10,9},{11,1... | collective-permute-start | bytes 319496 | tf_op jit(solution)/shard_map/ppermute | solution.py:543
  88.5 3.9 %collective-permute-start.7 = (f32[26,8,128]{2,1,0:T(8,128)S(1)}, f32[26,8,128]{2,1,0:T(8,128)S(1)}, u32[]{:S(2)}, u32[]{:S(2)}) collective-permute-start(f32[26,8,128]{2,1,0:T(8,128)S(1)} %shard_map.46.own_ref), channel_id=1, source_target_pairs={{0,1},{1,2},{2,3},{3,4},{4,5},{5,6},{6,7},{7,8},{8,9},{9,10},{10,1... | collective-permute-start | bytes 319496 | tf_op jit(solution)/shard_map/ppermute | solution.py:542

commit v4 on v3

--- a/solution.py
+++ b/solution.py
@@ -102,11 +102,15 @@
 Y_TILES = 28
 
 
-def pack_x_kernel(k_ref, f_ref, up_ref, down_ref):
-    up_ref[0:7] = k_ref[1:8]
-    up_ref[7:13] = f_ref[2:8]
-    down_ref[0:7] = k_ref[0:7]
-    down_ref[7:13] = f_ref[0:6]
+def pack_x_kernel(k_ref, f_ref, up_ref, down_ref, own_ref, done):
+    pieces = ((k_ref, 1, up_ref, 0, 7), (f_ref, 2, up_ref, 7, 6), (k_ref, 0, down_ref, 0, 7), (f_ref, 0, down_ref, 7, 6),
+              (k_ref, 0, own_ref, 0, 8), (f_ref, 0, own_ref, 8, 8))
+    copies = [pltpu.make_async_copy(ref.at[pl.ds(first, size)], to.at[pl.ds(place, size)], done.at[number])
+              for number, (ref, first, to, place, size) in enumerate(pieces)]
+    for copy in copies:
+        copy.start()
+    for copy in copies:
+        copy.wait()
 
 
 def pair_tiles():
@@ -124,11 +128,10 @@
     return low_ref[base + reach - dx] if side == "low" else high_ref[base + dx - 1]
 
 
-def pack_y_kernel(k_ref, f_ref, low_ref, high_ref, up_ref, down_ref):
+def pack_y_kernel(own_ref, low_ref, high_ref, up_ref, down_ref):
     for ref in (up_ref, down_ref):
-        ref[0:8] = k_ref[...]
-        ref[8:16] = f_ref[...]
-    row = iota((8, k_ref.shape[2]), 0)
+        ref[0:16] = own_ref[...]
+    row = iota((8, own_ref.shape[2]), 0)
     for tile, name, side, dx, far in pair_tiles():
         near_plane = halo_plane(name, side, dx, low_ref, high_ref)
         far_plane = halo_plane(name, side, far, low_ref, high_ref)
@@ -136,17 +139,17 @@
         down_ref[tile] = jnp.where(row >= 8 - dx, shifted(far_plane, dx - 8, 0), near_plane)
 
 
-def unpack(k_ref, f_ref, x_low_ref, x_high_ref, y_low_ref, y_high_ref, k0, f0):
-    for to, base, reach, name, ref in ((k0, 0, 7, "k", k_ref), (f0, 8, 6, "f", f_ref)):
+def unpack(own_ref, x_low_ref, x_high_ref, y_low_ref, y_high_ref, k0, f0):
+    for to, base, reach, name in ((k0, 0, 7, "k"), (f0, 8, 6, "f")):
         to[reach:reach + 8, 0:8] = y_low_ref[base:base + 8]
-        to[reach:reach + 8, 8:16] = ref[...]
+        to[reach:reach + 8, 8:16] = own_ref[base:base + 8]
         to[reach:reach + 8, 16:24] = y_high_ref[base:base + 8]
         first = 0 if name == "k" else 7
         to[0:reach, 8:16] = x_low_ref[first:first + reach]
         to[reach + 8:2 * reach + 8, 8:16] = x_high_ref[first:first + reach]
         for plane in (0, 2 * reach + 7):
-            to[plane, 0:8] = jnp.zeros(ref.shape[1:], F32)
-            to[plane, 16:24] = jnp.zeros(ref.shape[1:], F32)
+            to[plane, 0:8] = jnp.zeros(own_ref.shape[1:], F32)
+            to[plane, 16:24] = jnp.zeros(own_ref.shape[1:], F32)
     for tile, name, side, dx, far in pair_tiles():
         to, reach = (k0, 7) if name == "k" else (f0, 6)
         near_plane = reach - dx if side == "low" else reach + 7 + dx
@@ -159,10 +162,10 @@
             to[far_plane, 16:24] = shifted(above, 8 - dx, 0)
 
 
-def fine_kernel(k_ref, f_ref, x_low_ref, x_high_ref, y_low_ref, y_high_ref,
+def fine_kernel(own_ref, x_low_ref, x_high_ref, y_low_ref, y_high_ref,
                 k0, f0, k1, f1, up_ref, down_ref,
                 c0, diag0, g0, d0, e0, sums, zsums):
-    unpack(k_ref, f_ref, x_low_ref, x_high_ref, y_low_ref, y_high_ref, k0, f0)
+    unpack(own_ref, x_low_ref, x_high_ref, y_low_ref, y_high_ref, k0, f0)
 
     def setup(start):
         at = pl.ds(start, 2)
@@ -419,8 +422,38 @@
     out_ref[22:26] = high_ref[6:10]
 
 
-def prepare_kernel(x_low_ref, x_high_ref, y_low_ref, own_ref, y_high_ref, k_ref, f_ref,
-                   c1, g1, x1, c0, diag0, g0, x0, k1, f1, d1, d0):
+def prepare_kernel(k_ref, f_ref, c0, diag0, g0, x0, d0):
+    def setup0(start):
+        def cut(value):
+            return shifted(value, 4, 1)[:, 0:16]
+
+        at = pl.ds(start, 2)
+        couplings, inverse, diagonal = coupling(k_ref[pl.ds(start + 3, 2)], near_inside(k_ref, start + 3, 2), (4, 5))
+        for number in range(6):
+            c0.at[number][at] = cut(couplings[number])
+        diag0[at] = cut(diagonal)
+        scaled = cut(inverse * f_ref[pl.ds(start + 2, 2)])
+        g0[at] = scaled
+        d0[at] = FIRST * scaled
+
+    blocks(0, 16, 2, setup0)
+
+    def guess0(start):
+        at = pl.ds(start, 2)
+        here = d0[at]
+        scaled = g0[at] - here + spread(c0, (at,), near(d0, start, 2))
+        x0[at] = (1.0 + KEEP) * here + ADD * scaled
+
+    blocks(1, 15, 2, guess0)
+
+
+def gate_kernel(*refs):
+    pass
+
+
+def post_kernel(near_ref, x_low_ref, x_high_ref, y_low_ref, own_ref, y_high_ref, c0, diag0, g0, x0,
+                correction_ref, residual_ref,
+                k1, f1, c1, g1, x1, y1, d1, h1, wide, y0, d0, h0, v0):
     row = iota((8, 128), 0)
 
     def join(low, middle, high):
@@ -453,32 +486,6 @@
 
     blocks(2, 14, 6, guess1)
 
-    def setup0(start):
-        def cut(value):
-            return shifted(value, 4, 1)[:, 0:16]
-
-        at = pl.ds(start, 2)
-        couplings, inverse, diagonal = coupling(k_ref[pl.ds(start + 3, 2)], near_inside(k_ref, start + 3, 2), (4, 5))
-        for number in range(6):
-            c0.at[number][at] = cut(couplings[number])
-        diag0[at] = cut(diagonal)
-        scaled = cut(inverse * f_ref[pl.ds(start + 2, 2)])
-        g0[at] = scaled
-        d0[at] = FIRST * scaled
-
-    blocks(0, 16, 2, setup0)
-
-    def guess0(start):
-        at = pl.ds(start, 2)
-        here = d0[at]
-        scaled = g0[at] - here + spread(c0, (at,), near(d0, start, 2))
-        x0[at] = (1.0 + KEEP) * here + ADD * scaled
-
-    blocks(1, 15, 2, guess0)
-
-
-def post_kernel(near_ref, c1, g1, x1, c0, diag0, g0, x0, correction_ref, residual_ref,
-                y1, d1, h1, wide, y0, d0, h0, v0):
     up = near_ref[...]
     y1[2:14] = x1[2:14] + jnp.stack([up, up], 1).reshape(12, 16, 128)
     scaled = g1[3:13] - y1[3:13] + spread(c1, (pl.ds(3, 10),), near(y1, 3, 10))
@@ -550,33 +557,50 @@
     along_x, along_y = ("gx",), ("chip", "core")
     tile, full, half = f.shape[1:], (24, 256), (16, 256)
     tile1, full1 = (8, 128), (16, 128)
-    up, down = call(pack_x_kernel, 4, [(13, *tile)] * 2, [], k, f)
+    up, down, own = pl.pallas_call(
+        pack_x_kernel,
+        out_shape=[jax.ShapeDtypeStruct((planes, *tile), F32) for planes in (13, 13, 16)],
+        in_specs=[pl.BlockSpec(memory_space=pltpu.HBM)] * 2,
+        out_specs=[pl.BlockSpec(memory_space=pltpu.VMEM)] * 3,
+        scratch_shapes=[pltpu.SemaphoreType.DMA((6,))],
+        compiler_params=pltpu.CompilerParams(vmem_limit_bytes=4 * MIB),
+        interpret=INTERPRET,
+    )(k, f)
     x_low, x_high = both_sides(up, down, along_x)
-    up, down = call(pack_y_kernel, 4, [(Y_TILES, *tile)] * 2, [], k, f, x_low, x_high)
+    up, down = call(pack_y_kernel, 4, [(Y_TILES, *tile)] * 2, [], own, x_low, x_high)
     y_low, y_high = both_sides(up, down, along_y)
 
     k0, f0, k1, f1, up, down = call(
         fine_kernel, 16,
         [(22, *full), (20, *full), (10, *full1), (8, *full1), (11, *tile1), (11, *tile1)],
         [(6, 20, *full)] + [(20, *full)] * 4 + [(18, *full), (18, 24, 128)],
-        k, f, x_low, x_high, y_low, y_high)
+        own, x_low, x_high, y_low, y_high)
     x_low, x_high = both_sides(up, down, along_x)
     copies, = call(
         next_kernel, 8,
         [(count_x * chips, 4, 128)],
         [(6, 8, *full1)] + [(8, *full1)] * 4 + [(4, *full1)],
-        k1, f1, flops=1500000000)
+        k1, f1)
+
+    prepared = call(
+        prepare_kernel, 16,
+        [(6, 16, *half)] + [(16, *half)] * 3,
+        [(16, *half)],
+        k0, f0)
 
     mine = lax.all_to_all(copies, ("gx", "chip"), 0, 0).reshape(-1, 128)
+    mine = pl.pallas_call(
+        gate_kernel,
+        out_shape=jax.ShapeDtypeStruct(mine.shape, F32),
+        in_specs=[pl.BlockSpec(memory_space=pl.ANY)] * 4,
+        out_specs=pl.BlockSpec(memory_space=pl.ANY),
+        input_output_aliases={0: 0},
+        interpret=INTERPRET,
+    )(mine, x_low, x_high, prepared[0])
     other = lax.ppermute(mine, "core", [(0, 1), (1, 0)])
 
     own, = call(pack_share_kernel, 4, [(26, *tile1)], [], k1, f1, x_low, x_high)
     y_low, y_high = both_sides(own, own, along_y)
-    prepared = call(
-        prepare_kernel, 16,
-        [(6, 16, *full1)] + [(16, *full1)] * 2 + [(6, 16, *half)] + [(16, *half)] * 3,
-        [(16, *full1)] * 3 + [(16, *half)],
-        x_low, x_high, y_low, own, y_high, k0, f0, flops=2500000000)
 
     place = jnp.stack([lax.axis_index("gx"), lax.axis_index(("chip", "core"))]).astype(jnp.int32)
     plane2 = (2, count_y // 2, 128)
@@ -591,8 +615,8 @@
     correction, residual = call(
         post_kernel, 16,
         [f.shape, f.shape],
-        [(16, *full1)] * 3 + [(8, *full1)] + [(16, *half)] * 4,
-        near_e, *prepared)
+        [(16, *full1)] * 2 + [(6, 16, *full1)] + [(16, *full1)] * 5 + [(8, *full1)] + [(16, *half)] * 4,
+        near_e, x_low, x_high, y_low, own, y_high, *prepared)
     return correction, residual
 
 

time: 104 us -> 94.2 us (0.906)
  blocking collectives: 41.4 us -> 0 us
  starting transfers between devices: 27.3 us -> 45.9 us
  waiting for transfers between devices: 15.1 us -> 23.7 us
  local copies, waits for them, and re-layouts: 3.35 us -> 6.28 us
  Pallas kernels: 15.6 us -> 16.8 us
    all_to_all x1 -> x0, blocking collectives: 41.4 us -> none  [body(): mine = lax.all_to_all(copies, ('gx', 'chip'), 0, 0).reshape(-1, 128)]
    all_to_all x0 -> x1, starting transfers between devices: none -> 22 us  [body(): mine = lax.all_to_all(copies, ('gx', 'chip'), 0, 0).reshape(-1, 128)]
    all_to_all x0 -> x1, waiting for transfers between devices: none -> 7.21 us  [body(): mine = lax.all_to_all(copies, ('gx', 'chip'), 0, 0).reshape(-1, 128)]
    unnamed x8 -> x24, local copies, waits for them, and re-layouts: 3.35 us -> 6.28 us
    ppermute x4, waiting for transfers between devices: 12.6 us -> 15.2 us  [both_sides(): high = lax.ppermute(down, axes, [(i + 1, i) for i in range(count - 1)])]
    ppermute x4, starting transfers between devices: 15.9 us -> 13.7 us  [both_sides(): low = lax.ppermute(up, axes, [(i, i + 1) for i in range(count - 1)])]
    ppermute x4, starting transfers between devices: 8.08 us -> 6.83 us  [both_sides(): high = lax.ppermute(down, axes, [(i + 1, i) for i in range(count - 1)])]
    ppermute x4, waiting for transfers between devices: 2.43 us -> 1.27 us  [both_sides(): low = lax.ppermute(up, axes, [(i, i + 1) for i in range(count - 1)])]
  transfers between devices with their start and end apart: 9 -> 10, of which waited for: 7 -> 7; matrix products, arithmetic and copies ran while one was open for 0% -> 0% of each run, Pallas kernels for 2% -> 9%
where the time goes in v4:
time: 94.2 us; the launch traced here: 93.5 us
  starting transfers between devices  45.9 us (49%)
  waiting for transfers between devices  23.7 us (25%)
  Pallas kernels  16.8 us (18%)
  local copies, waits for them, and re-layouts  6.28 us (7%)
    all_to_all x1, starting transfers between devices, body(): mine = lax.all_to_all(copies, ('gx', 'chip'), 0, 0).reshape(-1, 128)  22 us
    pallas_call x7, Pallas kernels, call(): pl.pallas_call(kernel, out_shape=[jax.ShapeDtypeStruct(shape, F32) for sh...  16.3 us
    ppermute x4, waiting for transfers between devices, both_sides(): high = lax.ppermute(down, axes, [(i + 1, i) for i in range(count - 1)])  15.2 us
    ppermute x4, starting transfers between devices, both_sides(): low = lax.ppermute(up, axes, [(i, i + 1) for i in range(count - 1)])  13.7 us
    all_to_all x1, waiting for transfers between devices, body(): mine = lax.all_to_all(copies, ('gx', 'chip'), 0, 0).reshape(-1, 128)  7.21 us
    ppermute x4, starting transfers between devices, both_sides(): high = lax.ppermute(down, axes, [(i + 1, i) for i in range(count - 1)])  6.83 us
    unnamed x24, local copies, waits for them, and re-layouts  6.28 us
    ppermute x1, starting transfers between devices, body(): other = lax.ppermute(mine, 'core', [(0, 1), (1, 0)])  3.4 us
  transfers between devices with their start and end apart: 10, of which 7 were waited for; matrix products, arithmetic and copies ran while one was open for 0% of the time, Pallas kernels for 9%

profile of v4, /device:TPU:1, one launch (start us, length us, event | category | flops | bytes accessed | tf_op | source)
XLA Modules:
  0.0 93.5 jit_solution(7729702518662213445)
XLA Ops:
  0.6 0.0 copy-start.10
  0.6 0.8 copy-done.10
  1.5 0.0 copy-start.11
  1.5 0.8 copy-done.11
  2.3 0.5 shard_map.41
  2.8 4.8 %collective-permute-start = (f32[13,8,256]{2,1,0:T(8,128)S(1)}, f32[13,8,256]{2,1,0:T(8,128)S(1)}, u32[]{:S(2)}, u32[]{:S(2)}) collective-permute-start(f32[13,8,256]{2,1,0:T(8,128)S(1)} %get-tuple-element.18), channel_id=1, source_target_pairs={{0,16},{16,32},{32,48},{48,64},{64,80},{80,96},{96,112},{112,128},... | collective-permute-start | bytes 319496 | tf_op jit(solution)/shard_map/ppermute | solution.py:549
  7.6 1.3 %collective-permute-start.1 = (f32[13,8,256]{2,1,0:T(8,128)S(1)}, f32[13,8,256]{2,1,0:T(8,128)S(1)}, u32[]{:S(2)}, u32[]{:S(2)}) collective-permute-start(f32[13,8,256]{2,1,0:T(8,128)S(1)} %get-tuple-element.19), channel_id=1, source_target_pairs={{16,0},{32,16},{48,32},{64,48},{80,64},{96,80},{112,96},{128,112},... | collective-permute-start | bytes 319496 | tf_op jit(solution)/shard_map/ppermute | solution.py:550
  8.9 0.4 collective-permute-done.low_ref.x_low_ref
  9.3 4.4 %collective-permute-done.1.high_ref.x_high_ref = f32[13,8,256]{2,1,0:T(8,128)S(1)} collective-permute-done((f32[13,8,256]{2,1,0:T(8,128)S(1)}, f32[13,8,256]{2,1,0:T(8,128)S(1)}, u32[]{:S(2)}, u32[]{:S(2)}) %collective-permute-start.1) | collective-permute-done | bytes 106528 | tf_op jit(solution)/shard_map/ppermute | solution.py:550
  13.8 4.9 %collective-permute-start.2 = (f32[28,8,256]{2,1,0:T(8,128)S(1)}, f32[28,8,256]{2,1,0:T(8,128)S(1)}, u32[]{:S(2)}, u32[]{:S(2)}) collective-permute-start(f32[28,8,256]{2,1,0:T(8,128)S(1)} %get-tuple-element.20), channel_id=1, source_target_pairs={{0,1},{1,2},{2,3},{3,4},{4,5},{5,6},{6,7},{7,8},{8,9},{9,10},{10,1... | collective-permute-start | bytes 688136 | tf_op jit(solution)/shard_map/ppermute | solution.py:549
  18.7 2.1 %collective-permute-start.3 = (f32[28,8,256]{2,1,0:T(8,128)S(1)}, f32[28,8,256]{2,1,0:T(8,128)S(1)}, u32[]{:S(2)}, u32[]{:S(2)}) collective-permute-start(f32[28,8,256]{2,1,0:T(8,128)S(1)} %get-tuple-element.21), channel_id=1, source_target_pairs={{1,0},{2,1},{3,2},{4,3},{5,4},{6,5},{7,6},{8,7},{9,8},{10,9},{11,1... | collective-permute-start | bytes 688136 | tf_op jit(solution)/shard_map/ppermute | solution.py:550
  20.8 0.8 collective-permute-done.2.y_low_ref
  21.6 4.4 %collective-permute-done.3.y_high_ref = f32[28,8,256]{2,1,0:T(8,128)S(1)} collective-permute-done((f32[28,8,256]{2,1,0:T(8,128)S(1)}, f32[28,8,256]{2,1,0:T(8,128)S(1)}, u32[]{:S(2)}, u32[]{:S(2)}) %collective-permute-start.3) | collective-permute-done | bytes 229408 | tf_op jit(solution)/shard_map/ppermute | solution.py:550
  26.0 3.7 %shard_map.43 = (f32[22,24,256]{2,1,0:T(8,128)S(1)}, f32[20,24,256]{2,1,0:T(8,128)S(1)}, f32[10,16,128]{2,1,0:T(8,128)S(1)}, f32[8,16,128]{2,1,0:T(8,128)S(1)}, ...) custom-call(f32[16,8,256]{2,1,0:T(8,128)S(1)} %get-tuple-element.17.own_ref, ...), custom_call_target="tpu_custom_call" | custom-call | tf_op jit(solution)/shard_map/pallas_call | solution.py:535
  29.7 1.5 %shard_map.44 = f32[256,4,128]{2,1,0:T(4,128)} custom-call(f32[10,16,128]{2,1,0:T(8,128)S(1)} %get-tuple-element.22.k1, f32[8,16,128]{2,1,0:T(8,128)S(1)} %get-tuple-element.23.f1), custom_call_target="tpu_custom_call" | custom-call | tf_op jit(solution)/shard_map/pallas_call | solution.py:535
  31.2 22.0 %all-to-all-start = ((f32[256,4,128]{2,1,0:T(4,128)}), f32[256,4,128]{2,1,0:T(4,128)S(1)}, u32[]{:S(2)}, u32[]{:S(2)}) async-start(f32[256,4,128]{2,1,0:T(4,128)} %shard_map.44), calls=%async_computation | async-start | bytes 1048576 | tf_op jit(solution)/shard_map/all_to_all | solution.py:591
  53.2 1.6 %collective-permute-start.4 = (f32[11,8,128]{2,1,0:T(8,128)S(1)}, f32[11,8,128]{2,1,0:T(8,128)S(1)}, u32[]{:S(2)}, u32[]{:S(2)}) collective-permute-start(f32[11,8,128]{2,1,0:T(8,128)S(1)} %get-tuple-element.24), channel_id=1, source_target_pairs={{0,16},{16,32},{32,48},{48,64},{64,80},{80,96},{96,112},{112,128},... | collective-permute-start | bytes 135176 | tf_op jit(solution)/shard_map/ppermute | solution.py:549
  54.8 1.3 %collective-permute-start.5 = (f32[11,8,128]{2,1,0:T(8,128)S(1)}, f32[11,8,128]{2,1,0:T(8,128)S(1)}, u32[]{:S(2)}, u32[]{:S(2)}) collective-permute-start(f32[11,8,128]{2,1,0:T(8,128)S(1)} %get-tuple-element.25), channel_id=1, source_target_pairs={{16,0},{32,16},{48,32},{64,48},{80,64},{96,80},{112,96},{128,112},... | collective-permute-start | bytes 135176 | tf_op jit(solution)/shard_map/ppermute | solution.py:550
  56.1 1.9 %shard_map.45 = (f32[6,16,16,256]{3,2,1,0:T(8,128)S(1)}, f32[16,16,256]{2,1,0:T(8,128)S(1)}, f32[16,16,256]{2,1,0:T(8,128)S(1)}, f32[16,16,256]{2,1,0:T(8,128)S(1)}) custom-call(f32[22,24,256]{2,1,0:T(8,128)S(1)} %get-tuple-element.26.k_ref, f32[20,24,256]{2,1,0:T(8,128)S(1)} %get-tuple-element.27.f_ref), custom_call_target="tpu_custom_call" | custom-call | tf_op jit(solution)/shard_map/pallas_call | solution.py:535
  58.0 0.0 copy-start
  58.0 1.2 %copy-done = f32[6,16,16,256]{3,2,1,0:T(8,128)} copy-done((f32[6,16,16,256]{3,2,1,0:T(8,128)}, f32[6,16,16,256]{3,2,1,0:T(8,128)S(1)}, u32[]{:S(2)}) %copy-start) | copy-done | bytes 1572888
  59.1 0.1 collective-permute-done.4.refs_1_.low_ref.x_low_ref
  59.2 0.0 copy-start.4
  59.2 6.4 %collective-permute-done.5.refs_2_.high_ref.x_high_ref = f32[11,8,128]{2,1,0:T(8,128)S(1)} collective-permute-done((f32[11,8,128]{2,1,0:T(8,128)S(1)}, f32[11,8,128]{2,1,0:T(8,128)S(1)}, u32[]{:S(2)}, u32[]{:S(2)}) %collective-permute-start.5) | collective-permute-done | bytes 45088 | tf_op jit(solution)/shard_map/ppermute | solution.py:550
  65.6 0.0 copy-start.7
  65.6 7.2 %all-to-all-done = f32[256,4,128]{2,1,0:T(4,128)S(1)} async-done(((f32[256,4,128]{2,1,0:T(4,128)}), f32[256,4,128]{2,1,0:T(4,128)S(1)}, u32[]{:S(2)}, u32[]{:S(2)}) %all-to-all-start) | async-done | bytes 524320 | tf_op jit(solution)/shard_map/all_to_all | solution.py:591
  72.8 0.0 copy-start.2
  72.8 0.0 copy-done.4
  72.8 0.0 copy-done.7
  72.8 0.8 copy-done.2
  73.6 3.4 %collective-permute-start.6 = (f32[1024,128]{1,0:T(8,128)}, f32[1024,128]{1,0:T(8,128)S(1)}, u32[]{:S(2)}, u32[]{:S(2)}) collective-permute-start(f32[1024,128]{1,0:T(8,128)} %shard_map.46.mine_ref), channel_id=1, source_target_pairs={{0,1},{1,0},{2,3},{3,2},{4,5},{5,4},{6,7},{7,6},{8,9},{9,8},{10,11... | collective-permute-start | bytes 1572872 | tf_op jit(solution)/shard_map/ppermute | solution.py:600
  77.0 0.1 pad_add_fusion.place_ref
  77.1 0.0 copy-start.5
  77.1 0.8 copy-done.5
  77.9 0.0 copy-start.8
  77.9 0.8 copy-done.8
  78.7 0.0 copy-start.6
  78.7 0.0 copy-start.9
  78.7 0.0 copy-start.1
  78.7 2.4 %collective-permute-start.7 = (f32[26,8,128]{2,1,0:T(8,128)S(1)}, f32[26,8,128]{2,1,0:T(8,128)S(1)}, u32[]{:S(2)}, u32[]{:S(2)}) collective-permute-start(f32[26,8,128]{2,1,0:T(8,128)S(1)} %shard_map.48.own_ref), channel_id=1, source_target_pairs={{0,1},{1,2},{2,3},{3,4},{4,5},{5,6},{6,7},{7,8},{8,9},{9,10},{10,1... | collective-permute-start | bytes 319496 | tf_op jit(solution)/shard_map/ppermute | solution.py:549
  81.1 2.1 %collective-permute-start.8 = (f32[26,8,128]{2,1,0:T(8,128)S(1)}, f32[26,8,128]{2,1,0:T(8,128)S(1)}, u32[]{:S(2)}, u32[]{:S(2)}) collective-permute-start(f32[26,8,128]{2,1,0:T(8,128)S(1)} %shard_map.48.own_ref), channel_id=1, source_target_pairs={{1,0},{2,1},{3,2},{4,3},{5,4},{6,5},{7,6},{8,7},{9,8},{10,9},{11,1... | collective-permute-start | bytes 319496 | tf_op jit(solution)/shard_map/ppermute | solution.py:550
  83.2 0.0 collective-permute-done.6.other_ref
  83.2 0.0 copy-start.3
  83.2 1.0 %copy-done.3 = f32[1024,128]{1,0:T(8,128)S(1)} copy-done((f32[1024,128]{1,0:T(8,128)S(1)}, f32[1024,128]{1,0:T(8,128)}, u32[]{:S(2)}) %copy-start.3) | copy-done | bytes 524312
  84.2 6.4 %shard_map.47.near_ref = f32[6,16,128]{2,1,0:T(8,128)S(1)} custom-call(s32[2]{0:T(128)S(1)} %pad_add_fusion.place_ref, f32[1024,128]{1,0:T(8,128)S(1)} %copy-done.3, f32[1024,128]{1,0:T(8,128)S(1)} %collective-permute-done.6.other_ref), custom_call_target="tpu_custom_call" | custom-call | flops 6000000000 | tf_op jit(solution)/shard_map/pallas_call | solution.py:535
  90.7 0.0 collective-permute-done.7.y_low_ref
  90.7 0.0 collective-permute-done.8.y_high_ref
  90.7 0.0 copy-done.6
  90.7 0.0 copy-done.9
  90.7 0.0 copy-done.1
  90.7 2.8 %shard_map.49 = (f32[8,8,256]{2,1,0:T(8,128)}, f32[8,8,256]{2,1,0:T(8,128)}) custom-call(f32[6,16,128]{2,1,0:T(8,128)S(1)} %shard_map.47.near_ref, f32[11,8,128]{2,1,0:T(8,128)S(1)} %copy-done.6, f32[11,8,128]{2,1,0:T(8,128)S(1)} %copy-done.9, f32[26,8,128]{2,1,0:T(8,128)S(1)} %collective-permute-done.7.y_low_ref, f32[26,8,128]{2,1,0:T(8,128)S(1)} %shard_map.48.own_ref, ...), custom_call_target="tpu_custom_call" | custom-call | tf_op jit(solution)/shard_map/pallas_call | solution.py:535
  (3 shorter events, 0.0 us)
Async XLA Ops:
  0.6 0.8 copy-start.10
  1.5 0.8 copy-start.11
  2.8 6.5 %collective-permute-start = (f32[13,8,256]{2,1,0:T(8,128)S(1)}, f32[13,8,256]{2,1,0:T(8,128)S(1)}, u32[]{:S(2)}, u32[]{:S(2)}) collective-permute-start(f32[13,8,256]{2,1,0:T(8,128)S(1)} %get-tuple-element.18), channel_id=1, source_target_pairs={{0,16},{16,32},{32,48},{48,64},{64,80},{80,96},{96,112},{112,128},... | collective-permute-start | bytes 319496 | tf_op jit(solution)/shard_map/ppermute | solution.py:549
  7.6 6.1 %collective-permute-start.1 = (f32[13,8,256]{2,1,0:T(8,128)S(1)}, f32[13,8,256]{2,1,0:T(8,128)S(1)}, u32[]{:S(2)}, u32[]{:S(2)}) collective-permute-start(f32[13,8,256]{2,1,0:T(8,128)S(1)} %get-tuple-element.19), channel_id=1, source_target_pairs={{16,0},{32,16},{48,32},{64,48},{80,64},{96,80},{112,96},{128,112},... | collective-permute-start | bytes 319496 | tf_op jit(solution)/shard_map/ppermute | solution.py:550
  13.8 7.9 %collective-permute-start.2 = (f32[28,8,256]{2,1,0:T(8,128)S(1)}, f32[28,8,256]{2,1,0:T(8,128)S(1)}, u32[]{:S(2)}, u32[]{:S(2)}) collective-permute-start(f32[28,8,256]{2,1,0:T(8,128)S(1)} %get-tuple-element.20), channel_id=1, source_target_pairs={{0,1},{1,2},{2,3},{3,4},{4,5},{5,6},{6,7},{7,8},{8,9},{9,10},{10,1... | collective-permute-start | bytes 688136 | tf_op jit(solution)/shard_map/ppermute | solution.py:549
  18.7 7.3 %collective-permute-start.3 = (f32[28,8,256]{2,1,0:T(8,128)S(1)}, f32[28,8,256]{2,1,0:T(8,128)S(1)}, u32[]{:S(2)}, u32[]{:S(2)}) collective-permute-start(f32[28,8,256]{2,1,0:T(8,128)S(1)} %get-tuple-element.21), channel_id=1, source_target_pairs={{1,0},{2,1},{3,2},{4,3},{5,4},{6,5},{7,6},{8,7},{9,8},{10,9},{11,1... | collective-permute-start | bytes 688136 | tf_op jit(solution)/shard_map/ppermute | solution.py:550
  31.2 41.6 %all-to-all-start = ((f32[256,4,128]{2,1,0:T(4,128)}), f32[256,4,128]{2,1,0:T(4,128)S(1)}, u32[]{:S(2)}, u32[]{:S(2)}) async-start(f32[256,4,128]{2,1,0:T(4,128)} %shard_map.44), calls=%async_computation | async-start | bytes 1048576 | tf_op jit(solution)/shard_map/all_to_all | solution.py:591
  53.2 6.0 %collective-permute-start.4 = (f32[11,8,128]{2,1,0:T(8,128)S(1)}, f32[11,8,128]{2,1,0:T(8,128)S(1)}, u32[]{:S(2)}, u32[]{:S(2)}) collective-permute-start(f32[11,8,128]{2,1,0:T(8,128)S(1)} %get-tuple-element.24), channel_id=1, source_target_pairs={{0,16},{16,32},{32,48},{48,64},{64,80},{80,96},{96,112},{112,128},... | collective-permute-start | bytes 135176 | tf_op jit(solution)/shard_map/ppermute | solution.py:549
  54.8 10.8 %collective-permute-start.5 = (f32[11,8,128]{2,1,0:T(8,128)S(1)}, f32[11,8,128]{2,1,0:T(8,128)S(1)}, u32[]{:S(2)}, u32[]{:S(2)}) collective-permute-start(f32[11,8,128]{2,1,0:T(8,128)S(1)} %get-tuple-element.25), channel_id=1, source_target_pairs={{16,0},{32,16},{48,32},{64,48},{80,64},{96,80},{112,96},{128,112},... | collective-permute-start | bytes 135176 | tf_op jit(solution)/shard_map/ppermute | solution.py:550
  58.0 1.2 %copy-start = (f32[6,16,16,256]{3,2,1,0:T(8,128)}, f32[6,16,16,256]{3,2,1,0:T(8,128)S(1)}, u32[]{:S(2)}) copy-start(f32[6,16,16,256]{3,2,1,0:T(8,128)S(1)} %get-tuple-element.28.refs_3_.c0) | copy-start | bytes 4718596
  59.2 13.6 %copy-start.4 = (f32[11,8,128]{2,1,0:T(8,128)}, f32[11,8,128]{2,1,0:T(8,128)S(1)}, u32[]{:S(2)}) copy-start(f32[11,8,128]{2,1,0:T(8,128)S(1)} %collective-permute-done.4.refs_1_.low_ref.x_low_ref) | copy-start | bytes 135172
  65.6 7.2 %copy-start.7 = (f32[11,8,128]{2,1,0:T(8,128)}, f32[11,8,128]{2,1,0:T(8,128)S(1)}, u32[]{:S(2)}) copy-start(f32[11,8,128]{2,1,0:T(8,128)S(1)} %collective-permute-done.5.refs_2_.high_ref.x_high_ref) | copy-start | bytes 135172
  72.8 0.8 copy-start.2
  73.6 9.6 %collective-permute-start.6 = (f32[1024,128]{1,0:T(8,128)}, f32[1024,128]{1,0:T(8,128)S(1)}, u32[]{:S(2)}, u32[]{:S(2)}) collective-permute-start(f32[1024,128]{1,0:T(8,128)} %shard_map.46.mine_ref), channel_id=1, source_target_pairs={{0,1},{1,0},{2,3},{3,2},{4,5},{5,4},{6,7},{7,6},{8,9},{9,8},{10,11... | collective-permute-start | bytes 1572872 | tf_op jit(solution)/shard_map/ppermute | solution.py:600
  77.1 0.8 copy-start.5
  77.9 0.8 copy-start.8
  78.7 12.0 %copy-start.6 = (f32[11,8,128]{2,1,0:T(8,128)S(1)}, f32[11,8,128]{2,1,0:T(8,128)}, u32[]{:S(2)}) copy-start(f32[11,8,128]{2,1,0:T(8,128)} %copy-done.4) | copy-start | bytes 135172
  78.7 12.0 %copy-start.9 = (f32[11,8,128]{2,1,0:T(8,128)S(1)}, f32[11,8,128]{2,1,0:T(8,128)}, u32[]{:S(2)}) copy-start(f32[11,8,128]{2,1,0:T(8,128)} %copy-done.7) | copy-start | bytes 135172
  78.7 12.0 %copy-start.1 = (f32[6,16,16,256]{3,2,1,0:T(8,128)S(1)}, f32[6,16,16,256]{3,2,1,0:T(8,128)}, u32[]{:S(2)}) copy-start(f32[6,16,16,256]{3,2,1,0:T(8,128)} %copy-done) | copy-start | bytes 4718596
  78.7 12.0 %collective-permute-start.7 = (f32[26,8,128]{2,1,0:T(8,128)S(1)}, f32[26,8,128]{2,1,0:T(8,128)S(1)}, u32[]{:S(2)}, u32[]{:S(2)}) collective-permute-start(f32[26,8,128]{2,1,0:T(8,128)S(1)} %shard_map.48.own_ref), channel_id=1, source_target_pairs={{0,1},{1,2},{2,3},{3,4},{4,5},{5,6},{6,7},{7,8},{8,9},{9,10},{10,1... | collective-permute-start | bytes 319496 | tf_op jit(solution)/shard_map/ppermute | solution.py:549
  81.1 9.6 %collective-permute-start.8 = (f32[26,8,128]{2,1,0:T(8,128)S(1)}, f32[26,8,128]{2,1,0:T(8,128)S(1)}, u32[]{:S(2)}, u32[]{:S(2)}) collective-permute-start(f32[26,8,128]{2,1,0:T(8,128)S(1)} %shard_map.48.own_ref), channel_id=1, source_target_pairs={{1,0},{2,1},{3,2},{4,3},{5,4},{6,5},{7,6},{8,7},{9,8},{10,9},{11,1... | collective-permute-start | bytes 319496 | tf_op jit(solution)/shard_map/ppermute | solution.py:550
  83.2 1.0 %copy-start.3 = (f32[1024,128]{1,0:T(8,128)S(1)}, f32[1024,128]{1,0:T(8,128)}, u32[]{:S(2)}) copy-start(f32[1024,128]{1,0:T(8,128)} %shard_map.46.mine_ref) | copy-start | bytes 1572868

commit v5 on v4

--- a/solution.py
+++ b/solution.py
@@ -163,7 +163,7 @@
 
 
 def fine_kernel(own_ref, x_low_ref, x_high_ref, y_low_ref, y_high_ref,
-                k0, f0, k1, f1, up_ref, down_ref,
+                k0, f0, k1, f1, up_ref, down_ref, side_ref,
                 c0, diag0, g0, d0, e0, sums, zsums):
     unpack(own_ref, x_low_ref, x_high_ref, y_low_ref, y_high_ref, k0, f0)
 
@@ -208,6 +208,8 @@
     up_ref[6:11] = f1[1:6, 4:12, :]
     down_ref[0:6] = k1[3:9, 4:12, :]
     down_ref[6:11] = f1[2:7, 4:12, :]
+    side_ref[0:10] = k1[:, 4:12, :]
+    side_ref[10:18] = f1[:, 4:12, :]
 
 
 def next_kernel(k1, f1, copies_ref, c1, diag1, g1, d1, e1, out):
@@ -413,15 +415,6 @@
     return coarse_kernel
 
 
-def pack_share_kernel(k1, f1, low_ref, high_ref, out_ref):
-    out_ref[0:5] = low_ref[1:6]
-    out_ref[5:9] = k1[3:7, 4:12, :]
-    out_ref[9:14] = high_ref[0:5]
-    out_ref[14:18] = low_ref[7:11]
-    out_ref[18:22] = f1[2:6, 4:12, :]
-    out_ref[22:26] = high_ref[6:10]
-
-
 def prepare_kernel(k_ref, f_ref, c0, diag0, g0, x0, d0):
     def setup0(start):
         def cut(value):
@@ -451,7 +444,7 @@
     pass
 
 
-def post_kernel(near_ref, x_low_ref, x_high_ref, y_low_ref, own_ref, y_high_ref, c0, diag0, g0, x0,
+def post_kernel(near_ref, k_ref, f_ref, x_low_ref, x_high_ref, y_low_ref, y_high_ref, c0, diag0, g0, x0,
                 correction_ref, residual_ref,
                 k1, f1, c1, g1, x1, y1, d1, h1, wide, y0, d0, h0, v0):
     row = iota((8, 128), 0)
@@ -460,12 +453,18 @@
         middle = shifted(middle, 4, 1)
         return jnp.concatenate([jnp.where(row < 6, low, middle), jnp.where(row < 2, middle, high)], 1)
 
-    zero = jnp.zeros((1, 8, 128), F32)
-    k1[1:15] = join(y_low_ref[0:14], own_ref[0:14], y_high_ref[0:14])
-    f1[2:14] = join(y_low_ref[14:26], own_ref[14:26], y_high_ref[14:26])
-    for to, plane, tile in ((k1, 0, x_low_ref[0:1]), (k1, 15, x_high_ref[5:6]),
-                            (f1, 1, x_low_ref[6:7]), (f1, 14, x_high_ref[10:11])):
-        to[plane:plane + 1] = join(zero, tile, zero)
+    def alone(tiles):
+        tiles = shifted(tiles, 4, 1)
+        return jnp.concatenate([tiles, tiles], 1)
+
+    middle = jnp.concatenate([x_low_ref[3:6], k_ref[3:7, 4:12, :], x_high_ref[0:3]], 0)
+    k1[0:3] = alone(x_low_ref[0:3])
+    k1[3:13] = join(y_low_ref[0:10], middle, y_high_ref[0:10])
+    k1[13:16] = alone(x_high_ref[3:6])
+    middle = jnp.concatenate([x_low_ref[9:11], f_ref[2:6, 4:12, :], x_high_ref[6:8]], 0)
+    f1[1:4] = alone(x_low_ref[6:9])
+    f1[4:12] = join(y_low_ref[10:18], middle, y_high_ref[10:18])
+    f1[12:15] = alone(x_high_ref[8:11])
 
     def setup1(start):
         at = pl.ds(start, 7)
@@ -561,21 +560,22 @@
         pack_x_kernel,
         out_shape=[jax.ShapeDtypeStruct((planes, *tile), F32) for planes in (13, 13, 16)],
         in_specs=[pl.BlockSpec(memory_space=pltpu.HBM)] * 2,
-        out_specs=[pl.BlockSpec(memory_space=pltpu.VMEM)] * 3,
+        out_specs=[pl.BlockSpec(memory_space=pltpu.HBM)] * 3,
         scratch_shapes=[pltpu.SemaphoreType.DMA((6,))],
-        compiler_params=pltpu.CompilerParams(vmem_limit_bytes=4 * MIB),
+        compiler_params=pltpu.CompilerParams(vmem_limit_bytes=60 * MIB),
         interpret=INTERPRET,
     )(k, f)
     x_low, x_high = both_sides(up, down, along_x)
-    up, down = call(pack_y_kernel, 4, [(Y_TILES, *tile)] * 2, [], own, x_low, x_high)
-    y_low, y_high = both_sides(up, down, along_y)
-
-    k0, f0, k1, f1, up, down = call(
+    packed, down = call(pack_y_kernel, 4, [(Y_TILES, *tile)] * 2, [], own, x_low, x_high)
+    y_low, y_high = both_sides(packed, down, along_y)
+
+    k0, f0, k1, f1, up, down, side = call(
         fine_kernel, 16,
-        [(22, *full), (20, *full), (10, *full1), (8, *full1), (11, *tile1), (11, *tile1)],
+        [(22, *full), (20, *full), (10, *full1), (8, *full1), (11, *tile1), (11, *tile1), (18, *tile1)],
         [(6, 20, *full)] + [(20, *full)] * 4 + [(18, *full), (18, 24, 128)],
-        own, x_low, x_high, y_low, y_high)
+        packed, x_low, x_high, y_low, y_high)
     x_low, x_high = both_sides(up, down, along_x)
+    y_low, y_high = both_sides(side, side, along_y)
     copies, = call(
         next_kernel, 8,
         [(count_x * chips, 4, 128)],
@@ -589,18 +589,17 @@
         k0, f0)
 
     mine = lax.all_to_all(copies, ("gx", "chip"), 0, 0).reshape(-1, 128)
+    waited = (mine, x_low, x_high, y_low, y_high, prepared[0])
     mine = pl.pallas_call(
         gate_kernel,
         out_shape=jax.ShapeDtypeStruct(mine.shape, F32),
-        in_specs=[pl.BlockSpec(memory_space=pl.ANY)] * 4,
-        out_specs=pl.BlockSpec(memory_space=pl.ANY),
+        in_specs=[pl.BlockSpec(memory_space=pltpu.VMEM)] * len(waited),
+        out_specs=pl.BlockSpec(memory_space=pltpu.VMEM),
         input_output_aliases={0: 0},
+        compiler_params=pltpu.CompilerParams(vmem_limit_bytes=4 * MIB),
         interpret=INTERPRET,
-    )(mine, x_low, x_high, prepared[0])
+    )(*waited)
     other = lax.ppermute(mine, "core", [(0, 1), (1, 0)])
-
-    own, = call(pack_share_kernel, 4, [(26, *tile1)], [], k1, f1, x_low, x_high)
-    y_low, y_high = both_sides(own, own, along_y)
 
     place = jnp.stack([lax.axis_index("gx"), lax.axis_index(("chip", "core"))]).astype(jnp.int32)
     plane2 = (2, count_y // 2, 128)
@@ -616,7 +615,7 @@
         post_kernel, 16,
         [f.shape, f.shape],
         [(16, *full1)] * 2 + [(6, 16, *full1)] + [(16, *full1)] * 5 + [(8, *full1)] + [(16, *half)] * 4,
-        near_e, x_low, x_high, y_low, own, y_high, *prepared)
+        near_e, k1, f1, x_low, x_high, y_low, y_high, *prepared)
     return correction, residual
 
 

time: 94.2 us -> 98.7 us (1.048)
  Pallas kernels: 16.8 us -> 28.5 us
  waiting for transfers between devices: 23.7 us -> 19.2 us
  local copies, waits for them, and re-layouts: 6.28 us -> 3.02 us
    pallas_call x1, Pallas kernels: 0.47 us -> 11.6 us  [body(): pl.pallas_call(pack_x_kernel, out_shape=[jax.ShapeDtypeStruct((planes, *t...]
    ppermute x4, waiting for transfers between devices: 15.2 us -> 10.1 us  [both_sides(): high = lax.ppermute(down, axes, [(i + 1, i) for i in range(count - 1)])]
    unnamed x24 -> x14, local copies, waits for them, and re-layouts: 6.28 us -> 3.02 us
    ppermute x1, waiting for transfers between devices: 0.01 us -> 1.43 us  [body(): other = lax.ppermute(mine, 'core', [(0, 1), (1, 0)])]
    all_to_all x1, waiting for transfers between devices: 7.21 us -> 6.21 us  [body(): mine = lax.all_to_all(copies, ('gx', 'chip'), 0, 0).reshape(-1, 128)]
    pallas_call x7 -> x6, Pallas kernels: 16.3 us -> 16.9 us  [call(): pl.pallas_call(kernel, out_shape=[jax.ShapeDtypeStruct(shape, F32) for sh...]
  transfers between devices with their start and end apart: 10 -> 10, of which waited for: 7 -> 7; matrix products, arithmetic and copies ran while one was open for 0% -> 0% of each run, Pallas kernels for 9% -> 2%
where the time goes in v5:
time: 98.7 us; the launch traced here: 98.3 us
  starting transfers between devices  46.7 us (47%)
  Pallas kernels  28.5 us (29%)
  waiting for transfers between devices  19.2 us (19%)
  local copies, waits for them, and re-layouts  3.02 us (3%)
    all_to_all x1, starting transfers between devices, body(): mine = lax.all_to_all(copies, ('gx', 'chip'), 0, 0).reshape(-1, 128)  22 us
    pallas_call x6, Pallas kernels, call(): pl.pallas_call(kernel, out_shape=[jax.ShapeDtypeStruct(shape, F32) for sh...  16.9 us
    ppermute x4, starting transfers between devices, both_sides(): low = lax.ppermute(up, axes, [(i, i + 1) for i in range(count - 1)])  14.1 us
    pallas_call x1, Pallas kernels, body(): pl.pallas_call(pack_x_kernel, out_shape=[jax.ShapeDtypeStruct((planes, *t...  11.6 us
    ppermute x4, waiting for transfers between devices, both_sides(): high = lax.ppermute(down, axes, [(i + 1, i) for i in range(count - 1)])  10.1 us
    ppermute x4, starting transfers between devices, both_sides(): high = lax.ppermute(down, axes, [(i + 1, i) for i in range(count - 1)])  7.14 us
    all_to_all x1, waiting for transfers between devices, body(): mine = lax.all_to_all(copies, ('gx', 'chip'), 0, 0).reshape(-1, 128)  6.21 us
    ppermute x1, starting transfers between devices, body(): other = lax.ppermute(mine, 'core', [(0, 1), (1, 0)])  3.53 us
  transfers between devices with their start and end apart: 10, of which 7 were waited for; matrix products, arithmetic and copies ran while one was open for 0% of the time, Pallas kernels for 2%

profile of v5, /device:TPU:1, one launch (start us, length us, event | category | flops | bytes accessed | tf_op | source)
XLA Modules:
  0.0 98.3 jit_solution(7072069626198523731)
XLA Ops:
  0.6 11.6 %shard_map.41 = (f32[13,8,256]{2,1,0:T(8,128)}, f32[13,8,256]{2,1,0:T(8,128)}, f32[16,8,256]{2,1,0:T(8,128)}) custom-call(f32[8,8,256]{2,1,0:T(8,128)} %k_ref.1, f32[8,8,256]{2,1,0:T(8,128)} %f_ref.1), custom_call_target="tpu_custom_call" | custom-call | tf_op jit(solution)/shard_map/pallas_call | solution.py:559
  12.2 4.8 %collective-permute-start = (f32[13,8,256]{2,1,0:T(8,128)}, f32[13,8,256]{2,1,0:T(8,128)S(1)}, u32[]{:S(2)}, u32[]{:S(2)}) collective-permute-start(f32[13,8,256]{2,1,0:T(8,128)} %get-tuple-element.19), channel_id=1, source_target_pairs={{0,16},{16,32},{32,48},{48,64},{64,80},{80,96},{96,112},{112,128},... | collective-permute-start | bytes 319496 | tf_op jit(solution)/shard_map/ppermute | solution.py:548
  17.1 1.3 %collective-permute-start.1 = (f32[13,8,256]{2,1,0:T(8,128)}, f32[13,8,256]{2,1,0:T(8,128)S(1)}, u32[]{:S(2)}, u32[]{:S(2)}) collective-permute-start(f32[13,8,256]{2,1,0:T(8,128)} %get-tuple-element.20), channel_id=1, source_target_pairs={{16,0},{32,16},{48,32},{64,48},{80,64},{96,80},{112,96},{128,112},... | collective-permute-start | bytes 319496 | tf_op jit(solution)/shard_map/ppermute | solution.py:549
  18.4 0.7 collective-permute-done.low_ref.x_low_ref
  19.1 4.3 %collective-permute-done.1.high_ref.x_high_ref = f32[13,8,256]{2,1,0:T(8,128)S(1)} collective-permute-done((f32[13,8,256]{2,1,0:T(8,128)}, f32[13,8,256]{2,1,0:T(8,128)S(1)}, u32[]{:S(2)}, u32[]{:S(2)}) %collective-permute-start.1) | collective-permute-done | bytes 106528 | tf_op jit(solution)/shard_map/ppermute | solution.py:549
  23.4 0.0 copy-start.6
  23.4 0.9 copy-done.6
  24.3 4.9 %collective-permute-start.2 = (f32[28,8,256]{2,1,0:T(8,128)S(1)}, f32[28,8,256]{2,1,0:T(8,128)S(1)}, u32[]{:S(2)}, u32[]{:S(2)}) collective-permute-start(f32[28,8,256]{2,1,0:T(8,128)S(1)} %get-tuple-element.21.own_ref), channel_id=1, source_target_pairs={{0,1},{1,2},{2,3},{3,4},{4,5},{5,6},{6,7},{7,8},{8,9},{9,10},{10,1... | collective-permute-start | bytes 688136 | tf_op jit(solution)/shard_map/ppermute | solution.py:548
  29.2 2.1 %collective-permute-start.3 = (f32[28,8,256]{2,1,0:T(8,128)S(1)}, f32[28,8,256]{2,1,0:T(8,128)S(1)}, u32[]{:S(2)}, u32[]{:S(2)}) collective-permute-start(f32[28,8,256]{2,1,0:T(8,128)S(1)} %get-tuple-element.22), channel_id=1, source_target_pairs={{1,0},{2,1},{3,2},{4,3},{5,4},{6,5},{7,6},{8,7},{9,8},{10,9},{11,1... | collective-permute-start | bytes 688136 | tf_op jit(solution)/shard_map/ppermute | solution.py:549
  31.4 0.8 collective-permute-done.2.y_low_ref
  32.2 4.4 %collective-permute-done.3.y_high_ref = f32[28,8,256]{2,1,0:T(8,128)S(1)} collective-permute-done((f32[28,8,256]{2,1,0:T(8,128)S(1)}, f32[28,8,256]{2,1,0:T(8,128)S(1)}, u32[]{:S(2)}, u32[]{:S(2)}) %collective-permute-start.3) | collective-permute-done | bytes 229408 | tf_op jit(solution)/shard_map/ppermute | solution.py:549
  36.6 4.3 %shard_map.43 = (f32[22,24,256]{2,1,0:T(8,128)S(1)}, f32[20,24,256]{2,1,0:T(8,128)S(1)}, f32[10,16,128]{2,1,0:T(8,128)S(1)}, f32[8,16,128]{2,1,0:T(8,128)S(1)}, ...) custom-call(f32[28,8,256]{2,1,0:T(8,128)S(1)} %get-tuple-element.21.own_ref, ...), custom_call_target="tpu_custom_call" | custom-call | tf_op jit(solution)/shard_map/pallas_call | solution.py:534
  40.9 1.5 %shard_map.44 = f32[256,4,128]{2,1,0:T(4,128)} custom-call(f32[10,16,128]{2,1,0:T(8,128)S(1)} %get-tuple-element.23.k1.k_ref, f32[8,16,128]{2,1,0:T(8,128)S(1)} %get-tuple-element.24.f1.f_ref), custom_call_target="tpu_custom_call" | custom-call | tf_op jit(solution)/shard_map/pallas_call | solution.py:534
  42.4 22.0 %all-to-all-start = ((f32[256,4,128]{2,1,0:T(4,128)}), f32[256,4,128]{2,1,0:T(4,128)S(1)}, u32[]{:S(2)}, u32[]{:S(2)}) async-start(f32[256,4,128]{2,1,0:T(4,128)} %shard_map.44), calls=%async_computation | async-start | bytes 1048576 | tf_op jit(solution)/shard_map/all_to_all | solution.py:591
  64.4 1.9 %collective-permute-start.6 = (f32[18,8,128]{2,1,0:T(8,128)}, f32[18,8,128]{2,1,0:T(8,128)S(1)}, u32[]{:S(2)}, u32[]{:S(2)}) collective-permute-start(f32[18,8,128]{2,1,0:T(8,128)} %get-tuple-element.27), channel_id=1, source_target_pairs={{0,1},{1,2},{2,3},{3,4},{4,5},{5,6},{6,7},{7,8},{8,9},{9,10},{10,1... | collective-permute-start | bytes 221192 | tf_op jit(solution)/shard_map/ppermute | solution.py:548
  66.3 2.4 %collective-permute-start.7 = (f32[18,8,128]{2,1,0:T(8,128)}, f32[18,8,128]{2,1,0:T(8,128)S(1)}, u32[]{:S(2)}, u32[]{:S(2)}) collective-permute-start(f32[18,8,128]{2,1,0:T(8,128)} %get-tuple-element.27), channel_id=1, source_target_pairs={{1,0},{2,1},{3,2},{4,3},{5,4},{6,5},{7,6},{8,7},{9,8},{10,9},{11,1... | collective-permute-start | bytes 221192 | tf_op jit(solution)/shard_map/ppermute | solution.py:549
  68.7 2.4 %collective-permute-start.4 = (f32[11,8,128]{2,1,0:T(8,128)}, f32[11,8,128]{2,1,0:T(8,128)S(1)}, u32[]{:S(2)}, u32[]{:S(2)}) collective-permute-start(f32[11,8,128]{2,1,0:T(8,128)} %get-tuple-element.25), channel_id=1, source_target_pairs={{0,16},{16,32},{32,48},{48,64},{64,80},{80,96},{96,112},{112,128},... | collective-permute-start | bytes 135176 | tf_op jit(solution)/shard_map/ppermute | solution.py:548
  71.1 1.3 %collective-permute-start.5 = (f32[11,8,128]{2,1,0:T(8,128)}, f32[11,8,128]{2,1,0:T(8,128)S(1)}, u32[]{:S(2)}, u32[]{:S(2)}) collective-permute-start(f32[11,8,128]{2,1,0:T(8,128)} %get-tuple-element.26), channel_id=1, source_target_pairs={{16,0},{32,16},{48,32},{64,48},{80,64},{96,80},{112,96},{128,112},... | collective-permute-start | bytes 135176 | tf_op jit(solution)/shard_map/ppermute | solution.py:549
  72.4 1.9 %shard_map.45 = (f32[6,16,16,256]{3,2,1,0:T(8,128)S(1)}, f32[16,16,256]{2,1,0:T(8,128)S(1)}, f32[16,16,256]{2,1,0:T(8,128)S(1)}, f32[16,16,256]{2,1,0:T(8,128)S(1)}) custom-call(f32[22,24,256]{2,1,0:T(8,128)S(1)} %get-tuple-element.28.k_ref, f32[20,24,256]{2,1,0:T(8,128)S(1)} %get-tuple-element.29.f_ref), custom_call_target="tpu_custom_call" | custom-call | tf_op jit(solution)/shard_map/pallas_call | solution.py:534
  74.3 0.0 copy-start
  74.3 0.7 copy-done
  75.0 0.0 copy-start.2
  75.0 0.7 copy-done.2
  75.7 0.0 copy-start.4
  75.7 0.7 copy-done.4
  76.4 0.0 collective-permute-done.4.refs_1_.x_low_ref
  76.4 1.4 %collective-permute-done.5.refs_2_.x_high_ref = f32[11,8,128]{2,1,0:T(8,128)S(1)} collective-permute-done((f32[11,8,128]{2,1,0:T(8,128)}, f32[11,8,128]{2,1,0:T(8,128)S(1)}, u32[]{:S(2)}, u32[]{:S(2)}) %collective-permute-start.5) | collective-permute-done | bytes 45088 | tf_op jit(solution)/shard_map/ppermute | solution.py:549
  77.8 0.0 collective-permute-done.6.refs_3_.y_low_ref
  77.8 0.0 collective-permute-done.7.refs_4_.y_high_ref
  77.8 6.2 %all-to-all-done = f32[256,4,128]{2,1,0:T(4,128)S(1)} async-done(((f32[256,4,128]{2,1,0:T(4,128)}), f32[256,4,128]{2,1,0:T(4,128)S(1)}, u32[]{:S(2)}, u32[]{:S(2)}) %all-to-all-start) | async-done | bytes 524320 | tf_op jit(solution)/shard_map/all_to_all | solution.py:591
  84.0 3.5 %collective-permute-start.8 = (f32[1024,128]{1,0:T(8,128)S(1)}, f32[1024,128]{1,0:T(8,128)S(1)}, u32[]{:S(2)}, u32[]{:S(2)}) collective-permute-start(f32[1024,128]{1,0:T(8,128)S(1)} %shard_map.46.mine_ref), channel_id=1, source_target_pairs={{0,1},{1,0},{2,3},{3,2},{4,5},{5,4},{6,7},{7,6},{8,9},{9,8},{10,11... | collective-permute-start | bytes 1572872 | tf_op jit(solution)/shard_map/ppermute | solution.py:602
  87.5 0.1 pad_add_fusion.place_ref
  87.6 0.0 copy-start.1
  87.6 0.0 copy-start.3
  87.6 0.0 copy-start.5
  87.6 1.4 %collective-permute-done.8.other_ref = f32[1024,128]{1,0:T(8,128)S(1)} collective-permute-done((f32[1024,128]{1,0:T(8,128)S(1)}, f32[1024,128]{1,0:T(8,128)S(1)}, u32[]{:S(2)}, u32[]{:S(2)}) %collective-permute-start.8) | collective-permute-done | bytes 524320 | tf_op jit(solution)/shard_map/ppermute | solution.py:602
  89.1 6.4 %shard_map.47.near_ref = f32[6,16,128]{2,1,0:T(8,128)S(1)} custom-call(s32[2]{0:T(128)S(1)} %pad_add_fusion.place_ref, f32[1024,128]{1,0:T(8,128)S(1)} %shard_map.46.mine_ref, f32[1024,128]{1,0:T(8,128)S(1)} %collective-permute-done.8.other_ref), custom_call_target="tpu_custom_call" | custom-call | flops 6000000000 | tf_op jit(solution)/shard_map/pallas_call | solution.py:534
  95.5 0.0 copy-done.1
  95.5 0.0 copy-done.3
  95.5 0.0 copy-done.5
  95.5 2.8 %shard_map.48 = (f32[8,8,256]{2,1,0:T(8,128)}, f32[8,8,256]{2,1,0:T(8,128)}) custom-call(f32[6,16,128]{2,1,0:T(8,128)S(1)} %shard_map.47.near_ref, f32[10,16,128]{2,1,0:T(8,128)S(1)} %get-tuple-element.23.k1.k_ref, f32[8,16,128]{2,1,0:T(8,128)S(1)} %get-tuple-element.24.f1.f_ref, f32[11,8,128]{2,1,0:T(8,128)S(1)} %collective-permute-done.4.refs_1_.x_low_ref, ...), custom_call_target="tpu_custom_call" | custom-call | tf_op jit(solution)/shard_map/pallas_call | solution.py:534
  (2 shorter events, 0.0 us)
Async XLA Ops:
  12.2 6.8 %collective-permute-start = (f32[13,8,256]{2,1,0:T(8,128)}, f32[13,8,256]{2,1,0:T(8,128)S(1)}, u32[]{:S(2)}, u32[]{:S(2)}) collective-permute-start(f32[13,8,256]{2,1,0:T(8,128)} %get-tuple-element.19), channel_id=1, source_target_pairs={{0,16},{16,32},{32,48},{48,64},{64,80},{80,96},{96,112},{112,128},... | collective-permute-start | bytes 319496 | tf_op jit(solution)/shard_map/ppermute | solution.py:548
  17.1 6.3 %collective-permute-start.1 = (f32[13,8,256]{2,1,0:T(8,128)}, f32[13,8,256]{2,1,0:T(8,128)S(1)}, u32[]{:S(2)}, u32[]{:S(2)}) collective-permute-start(f32[13,8,256]{2,1,0:T(8,128)} %get-tuple-element.20), channel_id=1, source_target_pairs={{16,0},{32,16},{48,32},{64,48},{80,64},{96,80},{112,96},{128,112},... | collective-permute-start | bytes 319496 | tf_op jit(solution)/shard_map/ppermute | solution.py:549
  23.4 0.9 copy-start.6
  24.3 7.9 %collective-permute-start.2 = (f32[28,8,256]{2,1,0:T(8,128)S(1)}, f32[28,8,256]{2,1,0:T(8,128)S(1)}, u32[]{:S(2)}, u32[]{:S(2)}) collective-permute-start(f32[28,8,256]{2,1,0:T(8,128)S(1)} %get-tuple-element.21.own_ref), channel_id=1, source_target_pairs={{0,1},{1,2},{2,3},{3,4},{4,5},{5,6},{6,7},{7,8},{8,9},{9,10},{10,1... | collective-permute-start | bytes 688136 | tf_op jit(solution)/shard_map/ppermute | solution.py:548
  29.2 7.3 %collective-permute-start.3 = (f32[28,8,256]{2,1,0:T(8,128)S(1)}, f32[28,8,256]{2,1,0:T(8,128)S(1)}, u32[]{:S(2)}, u32[]{:S(2)}) collective-permute-start(f32[28,8,256]{2,1,0:T(8,128)S(1)} %get-tuple-element.22), channel_id=1, source_target_pairs={{1,0},{2,1},{3,2},{4,3},{5,4},{6,5},{7,6},{8,7},{9,8},{10,9},{11,1... | collective-permute-start | bytes 688136 | tf_op jit(solution)/shard_map/ppermute | solution.py:549
  42.4 41.6 %all-to-all-start = ((f32[256,4,128]{2,1,0:T(4,128)}), f32[256,4,128]{2,1,0:T(4,128)S(1)}, u32[]{:S(2)}, u32[]{:S(2)}) async-start(f32[256,4,128]{2,1,0:T(4,128)} %shard_map.44), calls=%async_computation | async-start | bytes 1048576 | tf_op jit(solution)/shard_map/all_to_all | solution.py:591
  64.4 13.4 %collective-permute-start.6 = (f32[18,8,128]{2,1,0:T(8,128)}, f32[18,8,128]{2,1,0:T(8,128)S(1)}, u32[]{:S(2)}, u32[]{:S(2)}) collective-permute-start(f32[18,8,128]{2,1,0:T(8,128)} %get-tuple-element.27), channel_id=1, source_target_pairs={{0,1},{1,2},{2,3},{3,4},{4,5},{5,6},{6,7},{7,8},{8,9},{9,10},{10,1... | collective-permute-start | bytes 221192 | tf_op jit(solution)/shard_map/ppermute | solution.py:548
  66.3 11.5 %collective-permute-start.7 = (f32[18,8,128]{2,1,0:T(8,128)}, f32[18,8,128]{2,1,0:T(8,128)S(1)}, u32[]{:S(2)}, u32[]{:S(2)}) collective-permute-start(f32[18,8,128]{2,1,0:T(8,128)} %get-tuple-element.27), channel_id=1, source_target_pairs={{1,0},{2,1},{3,2},{4,3},{5,4},{6,5},{7,6},{8,7},{9,8},{10,9},{11,1... | collective-permute-start | bytes 221192 | tf_op jit(solution)/shard_map/ppermute | solution.py:549
  68.7 7.7 %collective-permute-start.4 = (f32[11,8,128]{2,1,0:T(8,128)}, f32[11,8,128]{2,1,0:T(8,128)S(1)}, u32[]{:S(2)}, u32[]{:S(2)}) collective-permute-start(f32[11,8,128]{2,1,0:T(8,128)} %get-tuple-element.25), channel_id=1, source_target_pairs={{0,16},{16,32},{32,48},{48,64},{64,80},{80,96},{96,112},{112,128},... | collective-permute-start | bytes 135176 | tf_op jit(solution)/shard_map/ppermute | solution.py:548
  71.1 6.7 %collective-permute-start.5 = (f32[11,8,128]{2,1,0:T(8,128)}, f32[11,8,128]{2,1,0:T(8,128)S(1)}, u32[]{:S(2)}, u32[]{:S(2)}) collective-permute-start(f32[11,8,128]{2,1,0:T(8,128)} %get-tuple-element.26), channel_id=1, source_target_pairs={{16,0},{32,16},{48,32},{64,48},{80,64},{96,80},{112,96},{128,112},... | collective-permute-start | bytes 135176 | tf_op jit(solution)/shard_map/ppermute | solution.py:549
  74.3 0.7 copy-start
  75.0 0.7 copy-start.2
  75.7 0.7 copy-start.4
  84.0 5.0 %collective-permute-start.8 = (f32[1024,128]{1,0:T(8,128)S(1)}, f32[1024,128]{1,0:T(8,128)S(1)}, u32[]{:S(2)}, u32[]{:S(2)}) collective-permute-start(f32[1024,128]{1,0:T(8,128)S(1)} %shard_map.46.mine_ref), channel_id=1, source_target_pairs={{0,1},{1,0},{2,3},{3,2},{4,5},{5,4},{6,7},{7,6},{8,9},{9,8},{10,11... | collective-permute-start | bytes 1572872 | tf_op jit(solution)/shard_map/ppermute | solution.py:602
  87.6 7.9 %copy-start.1 = (f32[16,16,256]{2,1,0:T(8,128)S(1)}, f32[16,16,256]{2,1,0:T(8,128)}, u32[]{:S(2)}) copy-start(f32[16,16,256]{2,1,0:T(8,128)} %copy-done) | copy-start | bytes 786436
  87.6 7.9 %copy-start.3 = (f32[16,16,256]{2,1,0:T(8,128)S(1)}, f32[16,16,256]{2,1,0:T(8,128)}, u32[]{:S(2)}) copy-start(f32[16,16,256]{2,1,0:T(8,128)} %copy-done.2) | copy-start | bytes 786436
  87.6 7.9 %copy-start.5 = (f32[16,16,256]{2,1,0:T(8,128)S(1)}, f32[16,16,256]{2,1,0:T(8,128)}, u32[]{:S(2)}) copy-start(f32[16,16,256]{2,1,0:T(8,128)} %copy-done.4) | copy-start | bytes 786436

commit v6 on v5

--- a/solution.py
+++ b/solution.py
@@ -10,7 +10,6 @@
 INTERPRET = False
 COARSE_STEPS = 8
 F32 = jnp.float32
-HIGHEST = lax.Precision.HIGHEST
 MIB = 1024 * 1024
 
 
@@ -38,12 +37,29 @@
     return pltpu.roll(value, (-step) % value.shape[axis], axis)
 
 
-def dot(a, b):
-    return jnp.dot(a, b, precision=HIGHEST, preferred_element_type=F32)
+def parts_of(value):
+    parts = []
+    for _ in range(3):
+        part = value.astype(jnp.bfloat16)
+        parts.append(part)
+        value = value - part.astype(F32)
+    return parts
 
 
 def ones_where(condition):
-    return jnp.where(condition, 1.0, 0.0).astype(F32)
+    return jnp.where(condition, 1.0, 0.0).astype(jnp.bfloat16)
+
+
+def dot(a, ones):
+    rows = a.shape[0]
+    out = jnp.dot(jnp.concatenate(parts_of(a), 0), ones, preferred_element_type=F32)
+    return out[0:rows] + out[rows:2 * rows] + out[2 * rows:]
+
+
+def dot_left(ones, a):
+    columns = a.shape[1]
+    out = jnp.dot(ones, jnp.concatenate(parts_of(a), 1), preferred_element_type=F32)
+    return out[:, 0:columns] + out[:, columns:2 * columns] + out[:, 2 * columns:]
 
 
 def blocks(first, last, size, step):
@@ -128,22 +144,32 @@
     return low_ref[base + reach - dx] if side == "low" else high_ref[base + dx - 1]
 
 
-def pack_y_kernel(own_ref, low_ref, high_ref, up_ref, down_ref):
-    for ref in (up_ref, down_ref):
+def pack_y_kernel(core_ref, own_ref, low_ref, high_ref, sibling_ref, next_ref):
+    first_core = core_ref[0] == 0
+    for ref in (sibling_ref, next_ref):
         ref[0:16] = own_ref[...]
     row = iota((8, own_ref.shape[2]), 0)
     for tile, name, side, dx, far in pair_tiles():
         near_plane = halo_plane(name, side, dx, low_ref, high_ref)
         far_plane = halo_plane(name, side, far, low_ref, high_ref)
-        up_ref[tile] = jnp.where(row < dx, shifted(far_plane, 8 - dx, 0), near_plane)
-        down_ref[tile] = jnp.where(row >= 8 - dx, shifted(far_plane, dx - 8, 0), near_plane)
-
-
-def unpack(own_ref, x_low_ref, x_high_ref, y_low_ref, y_high_ref, k0, f0):
+        up = jnp.where(row < dx, shifted(far_plane, 8 - dx, 0), near_plane)
+        down = jnp.where(row >= 8 - dx, shifted(far_plane, dx - 8, 0), near_plane)
+        sibling_ref[tile] = jnp.where(first_core, up, down)
+        next_ref[tile] = jnp.where(first_core, down, up)
+
+
+def unpack(first_core, own_ref, x_low_ref, x_high_ref, sibling_ref, next_ref, k0, f0):
+    def below(tiles):
+        return jnp.where(first_core, next_ref[tiles], sibling_ref[tiles])
+
+    def above(tiles):
+        return jnp.where(first_core, sibling_ref[tiles], next_ref[tiles])
+
     for to, base, reach, name in ((k0, 0, 7, "k"), (f0, 8, 6, "f")):
-        to[reach:reach + 8, 0:8] = y_low_ref[base:base + 8]
-        to[reach:reach + 8, 8:16] = own_ref[base:base + 8]
-        to[reach:reach + 8, 16:24] = y_high_ref[base:base + 8]
+        tiles = pl.ds(base, 8)
+        to[reach:reach + 8, 0:8] = below(tiles)
+        to[reach:reach + 8, 8:16] = own_ref[tiles]
+        to[reach:reach + 8, 16:24] = above(tiles)
         first = 0 if name == "k" else 7
         to[0:reach, 8:16] = x_low_ref[first:first + reach]
         to[reach + 8:2 * reach + 8, 8:16] = x_high_ref[first:first + reach]
@@ -154,18 +180,18 @@
         to, reach = (k0, 7) if name == "k" else (f0, 6)
         near_plane = reach - dx if side == "low" else reach + 7 + dx
         far_plane = reach - far if side == "low" else reach + 7 + far
-        below, above = y_low_ref[tile], y_high_ref[tile]
-        to[near_plane, 0:8] = below
-        to[near_plane, 16:24] = above
+        low, high = below(tile), above(tile)
+        to[near_plane, 0:8] = low
+        to[near_plane, 16:24] = high
         if far != dx:
-            to[far_plane, 0:8] = shifted(below, dx - 8, 0)
-            to[far_plane, 16:24] = shifted(above, 8 - dx, 0)
-
-
-def fine_kernel(own_ref, x_low_ref, x_high_ref, y_low_ref, y_high_ref,
+            to[far_plane, 0:8] = shifted(low, dx - 8, 0)
+            to[far_plane, 16:24] = shifted(high, 8 - dx, 0)
+
+
+def fine_kernel(core_ref, own_ref, x_low_ref, x_high_ref, sibling_ref, next_ref,
                 k0, f0, k1, f1, up_ref, down_ref, side_ref,
                 c0, diag0, g0, d0, e0, sums, zsums):
-    unpack(own_ref, x_low_ref, x_high_ref, y_low_ref, y_high_ref, k0, f0)
+    unpack(core_ref[0] == 0, own_ref, x_low_ref, x_high_ref, sibling_ref, next_ref, k0, f0)
 
     def setup(start):
         at = pl.ds(start, 2)
@@ -357,15 +383,13 @@
         blocks(4, planes2 + 4, size, left)
 
         flat = count3 * 2 * rows
-        f3 = jnp.zeros((flat, 128), F32)
-        k3 = jnp.zeros((flat, 128), F32)
-        row, lane = iota((128, 128), 0), iota((128, 128), 1)
-        for quarter in range(4):
-            fold = ones_where(lane == 32 * quarter + (row % 64) // 2)
-            f3 = f3 + dot(sums[pl.ds(quarter * count3, count3)].reshape(flat, 128), fold)
-            k3 = k3 + dot(sums[pl.ds(count_x + quarter * count3, count3)].reshape(flat, 128), fold)
-        f3 = f3.reshape(count3, *line)
-        k3 = k3.reshape(count3, *line)
+        row, lane = iota((512, 128), 0), iota((512, 128), 1)
+        fold = ones_where(lane == 32 * (row // 128) + (row % 64) // 2)
+        quarters = [jnp.concatenate([sums[pl.ds(first + quarter * count3, count3)].reshape(flat, 128)
+                                     for first in (0, count_x)], 0) for quarter in range(4)]
+        folded = dot(jnp.concatenate(quarters, 1), fold)
+        f3 = folded[0:flat].reshape(count3, *line)
+        k3 = folded[flat:].reshape(count3, *line)
         couplings, inverse, _ = coupling(k3, near3_inside(k3), (0, 1, 2, 3, 4, 5))
         for number in range(6):
             c3[number] = couplings[number]
@@ -386,6 +410,7 @@
             safe = jnp.clip(x3, 0, count_x - 1)
             plane = pltpu.roll(e3[safe % count3].reshape(2 * rows, 128), (128 - 32 * (safe // count3)) % 128, 1)
             parts.append(jnp.where(inside, plane, 0.0))
+        row, lane = iota((128, 128), 0), iota((128, 128), 1)
         unfold = ones_where((row < 32) & ((lane % 64) // 2 == row))
         up = dot(jnp.concatenate(parts, 0), unfold).reshape(5, *line)
         local = pl.ds(base, 10)
@@ -403,14 +428,16 @@
         row, lane = iota((128, 256), 0), iota((128, 256), 1)
         widen = ones_where(row == 64 * (lane // 128) + (lane % 128) // 2)
         wide = dot(found.reshape(6 * 2 * rows, 128), widen)
-        target, source = iota((16, 2 * rows), 0), iota((16, 2 * rows), 1)
+        target, source = iota((16, 4 * rows), 0), iota((16, 4 * rows), 1)
+        half, source = source // (2 * rows), source % (2 * rows)
         source = 2 * (source % rows) + source // rows
         inside = (target >= 2) & (target < 14) & (source == at_y - 1 + (target - 2) // 4)
-        first = ones_where(inside & ((target - 2) % 4 < 2))
-        other = ones_where(inside & ((target - 2) % 4 >= 2))
+        spread_rows = ones_where(inside & (((target - 2) % 4) // 2 == half))
+        both = [jnp.concatenate([wide[2 * rows * index:2 * rows * (index + 1), 128 * half:128 * half + 128]
+                                 for index in range(6)], 1) for half in range(2)]
+        near_e = dot_left(spread_rows, jnp.concatenate(both, 0))
         for index in range(6):
-            block = wide[index * 2 * rows:(index + 1) * 2 * rows]
-            near_ref[index] = dot(first, block[:, 0:128]) + dot(other, block[:, 128:256])
+            near_ref[index] = near_e[:, 128 * index:128 * index + 128]
 
     return coarse_kernel
 
@@ -444,9 +471,7 @@
     pass
 
 
-def post_kernel(near_ref, k_ref, f_ref, x_low_ref, x_high_ref, y_low_ref, y_high_ref, c0, diag0, g0, x0,
-                correction_ref, residual_ref,
-                k1, f1, c1, g1, x1, y1, d1, h1, wide, y0, d0, h0, v0):
+def prepare1_kernel(k_ref, f_ref, x_low_ref, x_high_ref, y_low_ref, y_high_ref, after_ref, c1, g1, x1, k1, f1, d1):
     row = iota((8, 128), 0)
 
     def join(low, middle, high):
@@ -485,6 +510,8 @@
 
     blocks(2, 14, 6, guess1)
 
+def post_kernel(near_ref, c1, g1, x1, c0, diag0, g0, x0, correction_ref, residual_ref,
+                y1, d1, h1, wide, y0, d0, h0, v0):
     up = near_ref[...]
     y1[2:14] = x1[2:14] + jnp.stack([up, up], 1).reshape(12, 16, 128)
     scaled = g1[3:13] - y1[3:13] + spread(c1, (pl.ds(3, 10),), near(y1, 3, 10))
@@ -560,20 +587,22 @@
         pack_x_kernel,
         out_shape=[jax.ShapeDtypeStruct((planes, *tile), F32) for planes in (13, 13, 16)],
         in_specs=[pl.BlockSpec(memory_space=pltpu.HBM)] * 2,
-        out_specs=[pl.BlockSpec(memory_space=pltpu.HBM)] * 3,
+        out_specs=[pl.BlockSpec(memory_space=pltpu.VMEM)] * 3,
         scratch_shapes=[pltpu.SemaphoreType.DMA((6,))],
-        compiler_params=pltpu.CompilerParams(vmem_limit_bytes=60 * MIB),
+        compiler_params=pltpu.CompilerParams(vmem_limit_bytes=4 * MIB),
         interpret=INTERPRET,
     )(k, f)
     x_low, x_high = both_sides(up, down, along_x)
-    packed, down = call(pack_y_kernel, 4, [(Y_TILES, *tile)] * 2, [], own, x_low, x_high)
-    y_low, y_high = both_sides(packed, down, along_y)
+    core = lax.axis_index("core").astype(jnp.int32).reshape(1)
+    packed, outer = call(pack_y_kernel, 4, [(Y_TILES, *tile)] * 2, [], core, own, x_low, x_high, scalars=1)
+    sibling = lax.ppermute(packed, "core", [(0, 1), (1, 0)])
+    after = lax.ppermute(outer, along_y, [pair for i in range(1, count_y - 1, 2) for pair in ((i, i + 1), (i + 1, i))])
 
     k0, f0, k1, f1, up, down, side = call(
         fine_kernel, 16,
         [(22, *full), (20, *full), (10, *full1), (8, *full1), (11, *tile1), (11, *tile1), (18, *tile1)],
         [(6, 20, *full)] + [(20, *full)] * 4 + [(18, *full), (18, 24, 128)],
-        packed, x_low, x_high, y_low, y_high)
+        core, packed, x_low, x_high, sibling, after, scalars=1)
     x_low, x_high = both_sides(up, down, along_x)
     y_low, y_high = both_sides(side, side, along_y)
     copies, = call(
@@ -601,6 +630,12 @@
     )(*waited)
     other = lax.ppermute(mine, "core", [(0, 1), (1, 0)])
 
+    prepared1 = call(
+        prepare1_kernel, 8,
+        [(6, 16, *full1)] + [(16, *full1)] * 2,
+        [(16, *full1)] * 3,
+        k1, f1, x_low, x_high, y_low, y_high, mine)
+
     place = jnp.stack([lax.axis_index("gx"), lax.axis_index(("chip", "core"))]).astype(jnp.int32)
     plane2 = (2, count_y // 2, 128)
     padded = (2 * count_x + 8, *plane2)
@@ -614,8 +649,8 @@
     correction, residual = call(
         post_kernel, 16,
         [f.shape, f.shape],
-        [(16, *full1)] * 2 + [(6, 16, *full1)] + [(16, *full1)] * 5 + [(8, *full1)] + [(16, *half)] * 4,
-        near_e, k1, f1, x_low, x_high, y_low, y_high, *prepared)
+        [(16, *full1)] * 3 + [(8, *full1)] + [(16, *half)] * 4,
+        near_e, *prepared1, *prepared)
     return correction, residual
 
 

time: 98.7 us -> 83.3 us (0.84)
  Pallas kernels: 28.5 us -> 16.8 us
  waiting for transfers between devices: 19.2 us -> 9.55 us
  starting transfers between devices: 46.7 us -> 51.9 us
    pallas_call x1, Pallas kernels: 11.6 us -> 0.47 us  [body(): pl.pallas_call(pack_x_kernel, out_shape=[jax.ShapeDtypeStruct((planes, *t...]
    ppermute x0 -> x2, starting transfers between devices: none -> 6.84 us  [the longest x1 4.92 us: body(): lax.ppermute(outer, along_y, [pair for i in range(1, count_y - 1, 2) for...]
    ppermute x4 -> x3, waiting for transfers between devices: 10.1 us -> 4.82 us  [both_sides(): high = lax.ppermute(down, axes, [(i + 1, i) for i in range(count - 1)])]
    all_to_all x1, waiting for transfers between devices: 6.21 us -> 1.68 us  [body(): mine = lax.all_to_all(copies, ('gx', 'chip'), 0, 0).reshape(-1, 128)]
    ppermute x4 -> x3, starting transfers between devices: 14.1 us -> 9.71 us  [both_sides(): low = lax.ppermute(up, axes, [(i, i + 1) for i in range(count - 1)])]
    ppermute x1, starting transfers between devices: 3.53 us -> 7.05 us  [body(): other = lax.ppermute(mine, 'core', [(0, 1), (1, 0)])]
    ppermute x0 -> x2, waiting for transfers between devices: none -> 1.76 us  [the longest x1 1.76 us: body(): lax.ppermute(outer, along_y, [pair for i in range(1, count_y - 1, 2) for...]
    ppermute x4 -> x3, waiting for transfers between devices: 1.5 us -> 0.39 us  [both_sides(): low = lax.ppermute(up, axes, [(i, i + 1) for i in range(count - 1)])]
  transfers between devices with their start and end apart: 10 -> 10, of which waited for: 7 -> 6; matrix products, arithmetic and copies ran while one was open for 0% -> 0% of each run, Pallas kernels for 2% -> 3%
where the time goes in v6:
time: 83.3 us; the launch traced here: 82.9 us
  starting transfers between devices  51.9 us (62%)
  Pallas kernels  16.8 us (20%)
  waiting for transfers between devices  9.55 us (11%)
  local copies, waits for them, and re-layouts  3.76 us (5%)
    all_to_all x1, starting transfers between devices, body(): mine = lax.all_to_all(copies, ('gx', 'chip'), 0, 0).reshape(-1, 128)  21.2 us
    pallas_call x7, Pallas kernels, call(): pl.pallas_call(kernel, out_shape=[jax.ShapeDtypeStruct(shape, F32) for sh...  16.3 us
    ppermute x3, starting transfers between devices, both_sides(): low = lax.ppermute(up, axes, [(i, i + 1) for i in range(count - 1)])  9.71 us
    ppermute x3, starting transfers between devices, both_sides(): high = lax.ppermute(down, axes, [(i + 1, i) for i in range(count - 1)])  7.14 us
    ppermute x1, starting transfers between devices, body(): other = lax.ppermute(mine, 'core', [(0, 1), (1, 0)])  7.05 us
    ppermute x1, starting transfers between devices, body(): lax.ppermute(outer, along_y, [pair for i in range(1, count_y - 1, 2) for...  4.92 us
    ppermute x3, waiting for transfers between devices, both_sides(): high = lax.ppermute(down, axes, [(i + 1, i) for i in range(count - 1)])  4.82 us
    unnamed x16, local copies, waits for them, and re-layouts  3.76 us
  transfers between devices with their start and end apart: 10, of which 6 were waited for; matrix products, arithmetic and copies ran while one was open for 0% of the time, Pallas kernels for 3%

profile of v6, /device:TPU:1, one launch (start us, length us, event | category | flops | bytes accessed | tf_op | source)
XLA Modules:
  0.0 82.9 jit_solution(14019615960385674837)
XLA Ops:
  0.6 0.0 copy-start.6
  0.6 0.8 %copy-done.6 = f32[8,8,256]{2,1,0:T(8,128)S(1)} copy-done((f32[8,8,256]{2,1,0:T(8,128)S(1)}, f32[8,8,256]{2,1,0:T(8,128)}, u32[]{:S(2)}) %copy-start.6) | copy-done | bytes 65560
  1.5 0.0 copy-start.7
  1.5 0.8 %copy-done.7 = f32[8,8,256]{2,1,0:T(8,128)S(1)} copy-done((f32[8,8,256]{2,1,0:T(8,128)S(1)}, f32[8,8,256]{2,1,0:T(8,128)}, u32[]{:S(2)}) %copy-start.7) | copy-done | bytes 65560
  2.3 0.5 shard_map.41
  2.8 4.8 %collective-permute-start = (f32[13,8,256]{2,1,0:T(8,128)S(1)}, f32[13,8,256]{2,1,0:T(8,128)S(1)}, u32[]{:S(2)}, u32[]{:S(2)}) collective-permute-start(f32[13,8,256]{2,1,0:T(8,128)S(1)} %get-tuple-element.22), channel_id=1, source_target_pairs={{0,16},{16,32},{32,48},{48,64},{64,80},{80,96},{96,112},{112,128},... | collective-permute-start | bytes 319496 | tf_op jit(solution)/shard_map/ppermute | solution.py:575
  7.6 1.3 %collective-permute-start.1 = (f32[13,8,256]{2,1,0:T(8,128)S(1)}, f32[13,8,256]{2,1,0:T(8,128)S(1)}, u32[]{:S(2)}, u32[]{:S(2)}) collective-permute-start(f32[13,8,256]{2,1,0:T(8,128)S(1)} %get-tuple-element.23), channel_id=1, source_target_pairs={{16,0},{32,16},{48,32},{64,48},{80,64},{96,80},{112,96},{128,112},... | collective-permute-start | bytes 319496 | tf_op jit(solution)/shard_map/ppermute | solution.py:576
  8.9 0.4 collective-permute-done.low_ref.x_low_ref
  9.3 4.4 %collective-permute-done.1.high_ref.x_high_ref = f32[13,8,256]{2,1,0:T(8,128)S(1)} collective-permute-done((f32[13,8,256]{2,1,0:T(8,128)S(1)}, f32[13,8,256]{2,1,0:T(8,128)S(1)}, u32[]{:S(2)}, u32[]{:S(2)}) %collective-permute-start.1) | collective-permute-done | bytes 106528 | tf_op jit(solution)/shard_map/ppermute | solution.py:576
  13.8 4.9 %collective-permute-start.3 = (f32[28,8,256]{2,1,0:T(8,128)S(1)}, f32[28,8,256]{2,1,0:T(8,128)S(1)}, u32[]{:S(2)}, u32[]{:S(2)}) collective-permute-start(f32[28,8,256]{2,1,0:T(8,128)S(1)} %get-tuple-element.25), channel_id=1, source_target_pairs={{1,2},{2,1},{3,4},{4,3},{5,6},{6,5},{7,8},{8,7},{9,10},{10,9},{11,... | collective-permute-start | bytes 688136 | tf_op jit(solution)/shard_map/ppermute | solution.py:599
  18.7 1.9 %collective-permute-start.2 = (f32[28,8,256]{2,1,0:T(8,128)S(1)}, f32[28,8,256]{2,1,0:T(8,128)S(1)}, u32[]{:S(2)}, u32[]{:S(2)}) collective-permute-start(f32[28,8,256]{2,1,0:T(8,128)S(1)} %get-tuple-element.24.own_ref), channel_id=1, source_target_pairs={{0,1},{1,0},{2,3},{3,2},{4,5},{5,4},{6,7},{7,6},{8,9},{9,8},{10,11... | collective-permute-start | bytes 688136 | tf_op jit(solution)/shard_map/ppermute | solution.py:598
  20.6 1.8 %collective-permute-done.3.next_ref = f32[28,8,256]{2,1,0:T(8,128)S(1)} collective-permute-done((f32[28,8,256]{2,1,0:T(8,128)S(1)}, f32[28,8,256]{2,1,0:T(8,128)S(1)}, u32[]{:S(2)}, u32[]{:S(2)}) %collective-permute-start.3) | collective-permute-done | bytes 229408 | tf_op jit(solution)/shard_map/ppermute | solution.py:599
  22.4 0.0 collective-permute-done.2.sibling_ref
  22.4 4.1 %shard_map.43 = (f32[22,24,256]{2,1,0:T(8,128)S(1)}, f32[20,24,256]{2,1,0:T(8,128)S(1)}, f32[10,16,128]{2,1,0:T(8,128)S(1)}, f32[8,16,128]{2,1,0:T(8,128)S(1)}, ...) custom-call(s32[1]{0:T(128)} %bitcast.2.core_ref, ...), custom_call_target="tpu_custom_call" | custom-call | tf_op jit(solution)/shard_map/pallas_call | solution.py:561
  26.5 1.5 %shard_map.44 = f32[256,4,128]{2,1,0:T(4,128)} custom-call(f32[10,16,128]{2,1,0:T(8,128)S(1)} %get-tuple-element.26.k1.k_ref, f32[8,16,128]{2,1,0:T(8,128)S(1)} %get-tuple-element.27.f1.f_ref), custom_call_target="tpu_custom_call" | custom-call | tf_op jit(solution)/shard_map/pallas_call | solution.py:561
  28.0 21.2 %all-to-all-start = ((f32[256,4,128]{2,1,0:T(4,128)}), f32[256,4,128]{2,1,0:T(4,128)S(1)}, u32[]{:S(2)}, u32[]{:S(2)}) async-start(f32[256,4,128]{2,1,0:T(4,128)} %shard_map.44), calls=%async_computation | async-start | bytes 1048576 | tf_op jit(solution)/shard_map/all_to_all | solution.py:620
  49.2 4.6 %collective-permute-start.7 = (f32[18,8,128]{2,1,0:T(8,128)}, f32[18,8,128]{2,1,0:T(8,128)S(1)}, u32[]{:S(2)}, u32[]{:S(2)}) collective-permute-start(f32[18,8,128]{2,1,0:T(8,128)} %get-tuple-element.30), channel_id=1, source_target_pairs={{1,0},{2,1},{3,2},{4,3},{5,4},{6,5},{7,6},{8,7},{9,8},{10,9},{11,1... | collective-permute-start | bytes 221192 | tf_op jit(solution)/shard_map/ppermute | solution.py:576
  53.7 1.9 %collective-permute-start.6 = (f32[18,8,128]{2,1,0:T(8,128)}, f32[18,8,128]{2,1,0:T(8,128)S(1)}, u32[]{:S(2)}, u32[]{:S(2)}) collective-permute-start(f32[18,8,128]{2,1,0:T(8,128)} %get-tuple-element.30), channel_id=1, source_target_pairs={{0,1},{1,2},{2,3},{3,4},{4,5},{5,6},{6,7},{7,8},{8,9},{9,10},{10,1... | collective-permute-start | bytes 221192 | tf_op jit(solution)/shard_map/ppermute | solution.py:575
  55.7 3.0 %collective-permute-start.4 = (f32[11,8,128]{2,1,0:T(8,128)}, f32[11,8,128]{2,1,0:T(8,128)S(1)}, u32[]{:S(2)}, u32[]{:S(2)}) collective-permute-start(f32[11,8,128]{2,1,0:T(8,128)} %get-tuple-element.28), channel_id=1, source_target_pairs={{0,16},{16,32},{32,48},{48,64},{64,80},{80,96},{96,112},{112,128},... | collective-permute-start | bytes 135176 | tf_op jit(solution)/shard_map/ppermute | solution.py:575
  58.6 1.3 %collective-permute-start.5 = (f32[11,8,128]{2,1,0:T(8,128)}, f32[11,8,128]{2,1,0:T(8,128)S(1)}, u32[]{:S(2)}, u32[]{:S(2)}) collective-permute-start(f32[11,8,128]{2,1,0:T(8,128)} %get-tuple-element.29), channel_id=1, source_target_pairs={{16,0},{32,16},{48,32},{64,48},{80,64},{96,80},{112,96},{128,112},... | collective-permute-start | bytes 135176 | tf_op jit(solution)/shard_map/ppermute | solution.py:576
  59.9 1.9 %shard_map.45 = (f32[6,16,16,256]{3,2,1,0:T(8,128)S(1)}, f32[16,16,256]{2,1,0:T(8,128)S(1)}, f32[16,16,256]{2,1,0:T(8,128)S(1)}, f32[16,16,256]{2,1,0:T(8,128)S(1)}) custom-call(f32[22,24,256]{2,1,0:T(8,128)S(1)} %get-tuple-element.31.k_ref, f32[20,24,256]{2,1,0:T(8,128)S(1)} %get-tuple-element.32.f_ref), custom_call_target="tpu_custom_call" | custom-call | tf_op jit(solution)/shard_map/pallas_call | solution.py:561
  61.8 0.0 copy-start
  61.8 0.7 copy-done
  62.5 0.0 copy-start.2
  62.5 0.7 copy-done.2
  63.2 0.0 copy-start.4
  63.2 0.7 copy-done.4
  63.9 0.0 collective-permute-done.4.refs_1_.x_low_ref
  63.9 0.4 collective-permute-done.5.refs_2_.x_high_ref
  64.3 0.0 collective-permute-done.7.refs_4_.y_high_ref
  64.3 0.0 collective-permute-done.6.refs_3_.y_low_ref
  64.3 1.7 %all-to-all-done = f32[256,4,128]{2,1,0:T(4,128)S(1)} async-done(((f32[256,4,128]{2,1,0:T(4,128)}), f32[256,4,128]{2,1,0:T(4,128)S(1)}, u32[]{:S(2)}, u32[]{:S(2)}) %all-to-all-start) | async-done | bytes 524320 | tf_op jit(solution)/shard_map/all_to_all | solution.py:620
  66.0 7.0 %collective-permute-start.8 = (f32[1024,128]{1,0:T(8,128)S(1)}, f32[1024,128]{1,0:T(8,128)S(1)}, u32[]{:S(2)}, u32[]{:S(2)}) collective-permute-start(f32[1024,128]{1,0:T(8,128)S(1)} %shard_map.46.mine_ref.after_ref), channel_id=1, source_target_pairs={{0,1},{1,0},{2,3},{3,2},{4,5},{5,4},{6,7},{7,6},{8,9},{9,8},{10,11... | collective-permute-start | bytes 1572872 | tf_op jit(solution)/shard_map/ppermute | solution.py:631
  73.1 0.1 pad_add_fusion.place_ref
  73.1 0.5 shard_map.48
  73.6 0.0 copy-start.1
  73.6 0.0 copy-start.3
  73.7 0.0 copy-start.5
  73.7 0.9 %collective-permute-done.8.other_ref = f32[1024,128]{1,0:T(8,128)S(1)} collective-permute-done((f32[1024,128]{1,0:T(8,128)S(1)}, f32[1024,128]{1,0:T(8,128)S(1)}, u32[]{:S(2)}, u32[]{:S(2)}) %collective-permute-start.8) | collective-permute-done | bytes 524320 | tf_op jit(solution)/shard_map/ppermute | solution.py:631
  74.6 6.0 %shard_map.47.near_ref = f32[6,16,128]{2,1,0:T(8,128)S(1)} custom-call(s32[2]{0:T(128)S(1)} %pad_add_fusion.place_ref, f32[1024,128]{1,0:T(8,128)S(1)} %shard_map.46.mine_ref.after_ref, f32[1024,128]{1,0:T(8,128)S(1)} %collective-permute-done.8.other_ref), custom_call_target="tpu_custom_call" | custom-call | flops 6000000000 | tf_op jit(solution)/shard_map/pallas_call | solution.py:561
  80.6 0.0 copy-done.1
  80.6 0.0 copy-done.3
  80.6 0.0 copy-done.5
  80.6 2.2 %shard_map.49 = (f32[8,8,256]{2,1,0:T(8,128)}, f32[8,8,256]{2,1,0:T(8,128)}) custom-call(f32[6,16,128]{2,1,0:T(8,128)S(1)} %shard_map.47.near_ref, f32[6,16,16,128]{3,2,1,0:T(8,128)S(1)} %get-tuple-element.34.c1, f32[16,16,128]{2,1,0:T(8,128)S(1)} %get-tuple-element.35.g1, f32[16,16,128]{2,1,0:T(8,128)S(1)} %get-tuple-element.36.x1, ...), custom_call_target="tpu_custom_call" | custom-call | tf_op jit(solution)/shard_map/pallas_call | solution.py:561
  (2 shorter events, 0.0 us)
Async XLA Ops:
  0.6 0.8 %copy-start.6 = (f32[8,8,256]{2,1,0:T(8,128)S(1)}, f32[8,8,256]{2,1,0:T(8,128)}, u32[]{:S(2)}) copy-start(f32[8,8,256]{2,1,0:T(8,128)} %k_ref.1) | copy-start | bytes 196612
  1.5 0.8 %copy-start.7 = (f32[8,8,256]{2,1,0:T(8,128)S(1)}, f32[8,8,256]{2,1,0:T(8,128)}, u32[]{:S(2)}) copy-start(f32[8,8,256]{2,1,0:T(8,128)} %f_ref.1) | copy-start | bytes 196612
  2.8 6.5 %collective-permute-start = (f32[13,8,256]{2,1,0:T(8,128)S(1)}, f32[13,8,256]{2,1,0:T(8,128)S(1)}, u32[]{:S(2)}, u32[]{:S(2)}) collective-permute-start(f32[13,8,256]{2,1,0:T(8,128)S(1)} %get-tuple-element.22), channel_id=1, source_target_pairs={{0,16},{16,32},{32,48},{48,64},{64,80},{80,96},{96,112},{112,128},... | collective-permute-start | bytes 319496 | tf_op jit(solution)/shard_map/ppermute | solution.py:575
  7.6 6.1 %collective-permute-start.1 = (f32[13,8,256]{2,1,0:T(8,128)S(1)}, f32[13,8,256]{2,1,0:T(8,128)S(1)}, u32[]{:S(2)}, u32[]{:S(2)}) collective-permute-start(f32[13,8,256]{2,1,0:T(8,128)S(1)} %get-tuple-element.23), channel_id=1, source_target_pairs={{16,0},{32,16},{48,32},{64,48},{80,64},{96,80},{112,96},{128,112},... | collective-permute-start | bytes 319496 | tf_op jit(solution)/shard_map/ppermute | solution.py:576
  13.8 8.6 %collective-permute-start.3 = (f32[28,8,256]{2,1,0:T(8,128)S(1)}, f32[28,8,256]{2,1,0:T(8,128)S(1)}, u32[]{:S(2)}, u32[]{:S(2)}) collective-permute-start(f32[28,8,256]{2,1,0:T(8,128)S(1)} %get-tuple-element.25), channel_id=1, source_target_pairs={{1,2},{2,1},{3,4},{4,3},{5,6},{6,5},{7,8},{8,7},{9,10},{10,9},{11,... | collective-permute-start | bytes 688136 | tf_op jit(solution)/shard_map/ppermute | solution.py:599
  18.7 3.7 %collective-permute-start.2 = (f32[28,8,256]{2,1,0:T(8,128)S(1)}, f32[28,8,256]{2,1,0:T(8,128)S(1)}, u32[]{:S(2)}, u32[]{:S(2)}) collective-permute-start(f32[28,8,256]{2,1,0:T(8,128)S(1)} %get-tuple-element.24.own_ref), channel_id=1, source_target_pairs={{0,1},{1,0},{2,3},{3,2},{4,5},{5,4},{6,7},{7,6},{8,9},{9,8},{10,11... | collective-permute-start | bytes 688136 | tf_op jit(solution)/shard_map/ppermute | solution.py:598
  28.0 38.0 %all-to-all-start = ((f32[256,4,128]{2,1,0:T(4,128)}), f32[256,4,128]{2,1,0:T(4,128)S(1)}, u32[]{:S(2)}, u32[]{:S(2)}) async-start(f32[256,4,128]{2,1,0:T(4,128)} %shard_map.44), calls=%async_computation | async-start | bytes 1048576 | tf_op jit(solution)/shard_map/all_to_all | solution.py:620
  49.2 15.1 %collective-permute-start.7 = (f32[18,8,128]{2,1,0:T(8,128)}, f32[18,8,128]{2,1,0:T(8,128)S(1)}, u32[]{:S(2)}, u32[]{:S(2)}) collective-permute-start(f32[18,8,128]{2,1,0:T(8,128)} %get-tuple-element.30), channel_id=1, source_target_pairs={{1,0},{2,1},{3,2},{4,3},{5,4},{6,5},{7,6},{8,7},{9,8},{10,9},{11,1... | collective-permute-start | bytes 221192 | tf_op jit(solution)/shard_map/ppermute | solution.py:576
  53.7 10.6 %collective-permute-start.6 = (f32[18,8,128]{2,1,0:T(8,128)}, f32[18,8,128]{2,1,0:T(8,128)S(1)}, u32[]{:S(2)}, u32[]{:S(2)}) collective-permute-start(f32[18,8,128]{2,1,0:T(8,128)} %get-tuple-element.30), channel_id=1, source_target_pairs={{0,1},{1,2},{2,3},{3,4},{4,5},{5,6},{6,7},{7,8},{8,9},{9,10},{10,1... | collective-permute-start | bytes 221192 | tf_op jit(solution)/shard_map/ppermute | solution.py:575
  55.7 8.2 %collective-permute-start.4 = (f32[11,8,128]{2,1,0:T(8,128)}, f32[11,8,128]{2,1,0:T(8,128)S(1)}, u32[]{:S(2)}, u32[]{:S(2)}) collective-permute-start(f32[11,8,128]{2,1,0:T(8,128)} %get-tuple-element.28), channel_id=1, source_target_pairs={{0,16},{16,32},{32,48},{48,64},{64,80},{80,96},{96,112},{112,128},... | collective-permute-start | bytes 135176 | tf_op jit(solution)/shard_map/ppermute | solution.py:575
  58.6 5.7 %collective-permute-start.5 = (f32[11,8,128]{2,1,0:T(8,128)}, f32[11,8,128]{2,1,0:T(8,128)S(1)}, u32[]{:S(2)}, u32[]{:S(2)}) collective-permute-start(f32[11,8,128]{2,1,0:T(8,128)} %get-tuple-element.29), channel_id=1, source_target_pairs={{16,0},{32,16},{48,32},{64,48},{80,64},{96,80},{112,96},{128,112},... | collective-permute-start | bytes 135176 | tf_op jit(solution)/shard_map/ppermute | solution.py:576
  61.8 0.7 copy-start
  62.5 0.7 copy-start.2
  63.2 0.7 copy-start.4
  66.0 8.6 %collective-permute-start.8 = (f32[1024,128]{1,0:T(8,128)S(1)}, f32[1024,128]{1,0:T(8,128)S(1)}, u32[]{:S(2)}, u32[]{:S(2)}) collective-permute-start(f32[1024,128]{1,0:T(8,128)S(1)} %shard_map.46.mine_ref.after_ref), channel_id=1, source_target_pairs={{0,1},{1,0},{2,3},{3,2},{4,5},{5,4},{6,7},{7,6},{8,9},{9,8},{10,11... | collective-permute-start | bytes 1572872 | tf_op jit(solution)/shard_map/ppermute | solution.py:631
  73.6 7.0 %copy-start.1 = (f32[16,16,256]{2,1,0:T(8,128)S(1)}, f32[16,16,256]{2,1,0:T(8,128)}, u32[]{:S(2)}) copy-start(f32[16,16,256]{2,1,0:T(8,128)} %copy-done) | copy-start | bytes 786436
  73.6 7.0 %copy-start.3 = (f32[16,16,256]{2,1,0:T(8,128)S(1)}, f32[16,16,256]{2,1,0:T(8,128)}, u32[]{:S(2)}) copy-start(f32[16,16,256]{2,1,0:T(8,128)} %copy-done.2) | copy-start | bytes 786436
  73.7 7.0 %copy-start.5 = (f32[16,16,256]{2,1,0:T(8,128)S(1)}, f32[16,16,256]{2,1,0:T(8,128)}, u32[]{:S(2)}) copy-start(f32[16,16,256]{2,1,0:T(8,128)} %copy-done.4) | copy-start | bytes 786436

commit v7 on v6

--- a/solution.py
+++ b/solution.py
@@ -118,8 +118,10 @@
 Y_TILES = 28
 
 
-def pack_x_kernel(k_ref, f_ref, up_ref, down_ref, own_ref, done):
-    pieces = ((k_ref, 1, up_ref, 0, 7), (f_ref, 2, up_ref, 7, 6), (k_ref, 0, down_ref, 0, 7), (f_ref, 0, down_ref, 7, 6),
+def pack_x_kernel(core_ref, k_ref, f_ref, one_ref, two_ref, own_ref, done):
+    core = core_ref[0]
+    pieces = ((k_ref, 1 - core, one_ref, 0, 7), (f_ref, 2 - 2 * core, one_ref, 7, 6),
+              (k_ref, core, two_ref, 0, 7), (f_ref, 2 * core, two_ref, 7, 6),
               (k_ref, 0, own_ref, 0, 8), (f_ref, 0, own_ref, 8, 8))
     copies = [pltpu.make_async_copy(ref.at[pl.ds(first, size)], to.at[pl.ds(place, size)], done.at[number])
               for number, (ref, first, to, place, size) in enumerate(pieces)]
@@ -129,6 +131,16 @@
         copy.wait()
 
 
+def chosen(first_core, one_ref, two_ref):
+    def low(at):
+        return jnp.where(first_core, one_ref[at], two_ref[at])
+
+    def high(at):
+        return jnp.where(first_core, two_ref[at], one_ref[at])
+
+    return low, high
+
+
 def pair_tiles():
     tile = 16
     for pairs in PAIRS:
@@ -138,41 +150,38 @@
                 tile += 1
 
 
-def halo_plane(name, side, dx, low_ref, high_ref):
+def halo_plane(name, side, dx, x_low, x_high):
     reach = 7 if name == "k" else 6
     base = 0 if name == "k" else 7
-    return low_ref[base + reach - dx] if side == "low" else high_ref[base + dx - 1]
-
-
-def pack_y_kernel(core_ref, own_ref, low_ref, high_ref, sibling_ref, next_ref):
+    return x_low(base + reach - dx) if side == "low" else x_high(base + dx - 1)
+
+
+def pack_y_kernel(core_ref, own_ref, x_one_ref, x_two_ref, sibling_ref, next_ref):
     first_core = core_ref[0] == 0
+    x_low, x_high = chosen(first_core, x_one_ref, x_two_ref)
     for ref in (sibling_ref, next_ref):
         ref[0:16] = own_ref[...]
     row = iota((8, own_ref.shape[2]), 0)
     for tile, name, side, dx, far in pair_tiles():
-        near_plane = halo_plane(name, side, dx, low_ref, high_ref)
-        far_plane = halo_plane(name, side, far, low_ref, high_ref)
+        near_plane = halo_plane(name, side, dx, x_low, x_high)
+        far_plane = halo_plane(name, side, far, x_low, x_high)
         up = jnp.where(row < dx, shifted(far_plane, 8 - dx, 0), near_plane)
         down = jnp.where(row >= 8 - dx, shifted(far_plane, dx - 8, 0), near_plane)
         sibling_ref[tile] = jnp.where(first_core, up, down)
         next_ref[tile] = jnp.where(first_core, down, up)
 
 
-def unpack(first_core, own_ref, x_low_ref, x_high_ref, sibling_ref, next_ref, k0, f0):
-    def below(tiles):
-        return jnp.where(first_core, next_ref[tiles], sibling_ref[tiles])
-
-    def above(tiles):
-        return jnp.where(first_core, sibling_ref[tiles], next_ref[tiles])
-
+def unpack(first_core, own_ref, x_one_ref, x_two_ref, sibling_ref, next_ref, k0, f0):
+    x_low, x_high = chosen(first_core, x_one_ref, x_two_ref)
+    below, above = chosen(first_core, next_ref, sibling_ref)
     for to, base, reach, name in ((k0, 0, 7, "k"), (f0, 8, 6, "f")):
         tiles = pl.ds(base, 8)
         to[reach:reach + 8, 0:8] = below(tiles)
         to[reach:reach + 8, 8:16] = own_ref[tiles]
         to[reach:reach + 8, 16:24] = above(tiles)
         first = 0 if name == "k" else 7
-        to[0:reach, 8:16] = x_low_ref[first:first + reach]
-        to[reach + 8:2 * reach + 8, 8:16] = x_high_ref[first:first + reach]
+        to[0:reach, 8:16] = x_low(pl.ds(first, reach))
+        to[reach + 8:2 * reach + 8, 8:16] = x_high(pl.ds(first, reach))
         for plane in (0, 2 * reach + 7):
             to[plane, 0:8] = jnp.zeros(own_ref.shape[1:], F32)
             to[plane, 16:24] = jnp.zeros(own_ref.shape[1:], F32)
@@ -188,10 +197,10 @@
             to[far_plane, 16:24] = shifted(high, 8 - dx, 0)
 
 
-def fine_kernel(core_ref, own_ref, x_low_ref, x_high_ref, sibling_ref, next_ref,
+def fine_kernel(core_ref, own_ref, x_one_ref, x_two_ref, sibling_ref, next_ref,
                 k0, f0, k1, f1, up_ref, down_ref, side_ref,
                 c0, diag0, g0, d0, e0, sums, zsums):
-    unpack(core_ref[0] == 0, own_ref, x_low_ref, x_high_ref, sibling_ref, next_ref, k0, f0)
+    unpack(core_ref[0] == 0, own_ref, x_one_ref, x_two_ref, sibling_ref, next_ref, k0, f0)
 
     def setup(start):
         at = pl.ds(start, 2)
@@ -266,10 +275,7 @@
              + folded[number, 8:9, 128:256] + folded[number, 9:10, 128:256] for number in range(4)]
     payload = jnp.concatenate(lines, 0)
 
-    def copy(start):
-        copies_ref[pl.ds(start, 8)] = jnp.broadcast_to(payload[None], (8, 4, 128))
-
-    blocks(0, copies_ref.shape[0], 8, copy)
+    copies_ref[...] = jnp.broadcast_to(payload[None], copies_ref.shape)
 
 
 def near2(ref, start, size):
@@ -321,7 +327,7 @@
 
 def make_coarse_kernel(count_x, count_y):
     planes2, rows, count3 = 2 * count_x, count_y // 2, count_x // 4
-    size = 8
+    size = 4
     line = (2, rows, 128)
 
     def coarse_kernel(place_ref, mine_ref, other_ref, near_ref,
@@ -583,18 +589,20 @@
     along_x, along_y = ("gx",), ("chip", "core")
     tile, full, half = f.shape[1:], (24, 256), (16, 256)
     tile1, full1 = (8, 128), (16, 128)
-    up, down, own = pl.pallas_call(
+    core = lax.axis_index("core").astype(jnp.int32).reshape(1)
+    one, two, own = pl.pallas_call(
         pack_x_kernel,
         out_shape=[jax.ShapeDtypeStruct((planes, *tile), F32) for planes in (13, 13, 16)],
-        in_specs=[pl.BlockSpec(memory_space=pltpu.HBM)] * 2,
+        in_specs=[pl.BlockSpec(memory_space=pltpu.SMEM)] + [pl.BlockSpec(memory_space=pltpu.HBM)] * 2,
         out_specs=[pl.BlockSpec(memory_space=pltpu.VMEM)] * 3,
         scratch_shapes=[pltpu.SemaphoreType.DMA((6,))],
         compiler_params=pltpu.CompilerParams(vmem_limit_bytes=4 * MIB),
         interpret=INTERPRET,
-    )(k, f)
-    x_low, x_high = both_sides(up, down, along_x)
-    core = lax.axis_index("core").astype(jnp.int32).reshape(1)
-    packed, outer = call(pack_y_kernel, 4, [(Y_TILES, *tile)] * 2, [], core, own, x_low, x_high, scalars=1)
+    )(core, k, f)
+    route = [(2 * i, 2 * i + 2) for i in range(count_x - 1)] + [(2 * i + 3, 2 * i + 1) for i in range(count_x - 1)]
+    one = lax.ppermute(one, ("gx", "core"), route)
+    two = lax.ppermute(two, ("gx", "core"), [(to, source) for source, to in route])
+    packed, outer = call(pack_y_kernel, 4, [(Y_TILES, *tile)] * 2, [], core, own, one, two, scalars=1)
     sibling = lax.ppermute(packed, "core", [(0, 1), (1, 0)])
     after = lax.ppermute(outer, along_y, [pair for i in range(1, count_y - 1, 2) for pair in ((i, i + 1), (i + 1, i))])
 
@@ -602,12 +610,12 @@
         fine_kernel, 16,
         [(22, *full), (20, *full), (10, *full1), (8, *full1), (11, *tile1), (11, *tile1), (18, *tile1)],
         [(6, 20, *full)] + [(20, *full)] * 4 + [(18, *full), (18, 24, 128)],
-        core, packed, x_low, x_high, sibling, after, scalars=1)
+        core, packed, one, two, sibling, after, scalars=1)
     x_low, x_high = both_sides(up, down, along_x)
     y_low, y_high = both_sides(side, side, along_y)
     copies, = call(
         next_kernel, 8,
-        [(count_x * chips, 4, 128)],
+        [(chips, 4, 128)],
         [(6, 8, *full1)] + [(8, *full1)] * 4 + [(4, *full1)],
         k1, f1)
 
@@ -617,7 +625,9 @@
         [(16, *half)],
         k0, f0)
 
-    mine = lax.all_to_all(copies, ("gx", "chip"), 0, 0).reshape(-1, 128)
+    line = lax.all_to_all(copies, "chip", 0, 0).reshape(-1, 128)
+    copies = jnp.broadcast_to(line[None], (count_x, *line.shape))
+    mine = lax.all_to_all(copies, "gx", 0, 0).reshape(-1, 128)
     waited = (mine, x_low, x_high, y_low, y_high, prepared[0])
     mine = pl.pallas_call(
         gate_kernel,

time: 83.3 us -> 86.7 us (1.041)
  the two profiles are of different devices: /device:TPU:1 before, /device:TPU:3 now
where the time goes in v7:
time: 86.7 us; the launch traced here: 86.2 us
  starting transfers between devices  39.7 us (46%)
  Pallas kernels  17.5 us (20%)
  blocking collectives  13.3 us (15%)
  waiting for transfers between devices  10 us (12%)
  local copies, waits for them, and re-layouts  4.63 us (5%)
  between operations  0.87 us (1%)
    pallas_call x7, Pallas kernels, call(): pl.pallas_call(kernel, out_shape=[jax.ShapeDtypeStruct(shape, F32) for sh...  17.1 us
    all_to_all x1, blocking collectives, body(): line = lax.all_to_all(copies, 'chip', 0, 0).reshape(-1, 128)  13.3 us
    ppermute x1, starting transfers between devices, body(): one = lax.ppermute(one, ('gx', 'core'), route)  10.6 us
    ppermute x2, starting transfers between devices, both_sides(): high = lax.ppermute(down, axes, [(i + 1, i) for i in range(count - 1)])  10.6 us
    ppermute x1, waiting for transfers between devices, body(): lax.ppermute(two, ('gx', 'core'), [(to, source) for source, to in route])  5.62 us
    ppermute x2, starting transfers between devices, both_sides(): low = lax.ppermute(up, axes, [(i, i + 1) for i in range(count - 1)])  5.23 us
    all_to_all x1, starting transfers between devices, body(): mine = lax.all_to_all(copies, 'gx', 0, 0).reshape(-1, 128)  4.78 us
    unnamed x16, local copies, waits for them, and re-layouts  3.76 us
  transfers between devices with their start and end apart: 10, of which 3 were waited for; matrix products, arithmetic and copies ran while one was open for 0% of the time, Pallas kernels for 3%

profile of v7, /device:TPU:3, one launch (start us, length us, event | category | flops | bytes accessed | tf_op | source)
XLA Modules:
  0.0 86.2 jit_solution(439408684547419715)
XLA Ops:
  0.6 0.0 copy-start.6
  0.6 0.8 copy-done.6
  1.5 0.0 copy-start.7
  1.5 0.8 copy-done.7
  2.3 0.5 shard_map.41
  2.8 10.6 %collective-permute-start = (f32[13,8,256]{2,1,0:T(8,128)S(1)}, f32[13,8,256]{2,1,0:T(8,128)S(1)}, u32[]{:S(2)}, u32[]{:S(2)}) collective-permute-start(f32[13,8,256]{2,1,0:T(8,128)S(1)} %get-tuple-element.22), channel_id=1, source_target_pairs={{0,16},{16,32},{32,48},{48,64},{64,80},{80,96},{96,112},{112,128},... | collective-permute-start | bytes 319496 | tf_op jit(solution)/shard_map/ppermute | solution.py:603
  13.4 1.9 %collective-permute-start.1 = (f32[13,8,256]{2,1,0:T(8,128)S(1)}, f32[13,8,256]{2,1,0:T(8,128)S(1)}, u32[]{:S(2)}, u32[]{:S(2)}) collective-permute-start(f32[13,8,256]{2,1,0:T(8,128)S(1)} %get-tuple-element.23), channel_id=1, source_target_pairs={{16,0},{32,16},{48,32},{64,48},{80,64},{96,80},{112,96},{128,112},... | collective-permute-start | bytes 319496 | tf_op jit(solution)/shard_map/ppermute | solution.py:604
  15.4 0.0 collective-permute-done.x_one_ref
  15.4 5.6 %collective-permute-done.1.x_two_ref = f32[13,8,256]{2,1,0:T(8,128)S(1)} collective-permute-done((f32[13,8,256]{2,1,0:T(8,128)S(1)}, f32[13,8,256]{2,1,0:T(8,128)S(1)}, u32[]{:S(2)}, u32[]{:S(2)}) %collective-permute-start.1) | collective-permute-done | bytes 106528 | tf_op jit(solution)/shard_map/ppermute | solution.py:604
  21.0 1.9 %collective-permute-start.3 = (f32[28,8,256]{2,1,0:T(8,128)S(1)}, f32[28,8,256]{2,1,0:T(8,128)S(1)}, u32[]{:S(2)}, u32[]{:S(2)}) collective-permute-start(f32[28,8,256]{2,1,0:T(8,128)S(1)} %get-tuple-element.25), channel_id=1, source_target_pairs={{1,2},{2,1},{3,4},{4,3},{5,6},{6,5},{7,8},{8,7},{9,10},{10,9},{11,... | collective-permute-start | bytes 688136 | tf_op jit(solution)/shard_map/ppermute | solution.py:607
  23.0 1.9 %collective-permute-start.2 = (f32[28,8,256]{2,1,0:T(8,128)S(1)}, f32[28,8,256]{2,1,0:T(8,128)S(1)}, u32[]{:S(2)}, u32[]{:S(2)}) collective-permute-start(f32[28,8,256]{2,1,0:T(8,128)S(1)} %get-tuple-element.24.own_ref), channel_id=1, source_target_pairs={{0,1},{1,0},{2,3},{3,2},{4,5},{5,4},{6,7},{7,6},{8,9},{9,8},{10,11... | collective-permute-start | bytes 688136 | tf_op jit(solution)/shard_map/ppermute | solution.py:606
  24.9 3.5 %collective-permute-done.3.next_ref = f32[28,8,256]{2,1,0:T(8,128)S(1)} collective-permute-done((f32[28,8,256]{2,1,0:T(8,128)S(1)}, f32[28,8,256]{2,1,0:T(8,128)S(1)}, u32[]{:S(2)}, u32[]{:S(2)}) %collective-permute-start.3) | collective-permute-done | bytes 229408 | tf_op jit(solution)/shard_map/ppermute | solution.py:607
  28.4 0.0 collective-permute-done.2.sibling_ref
  28.4 4.1 %shard_map.43 = (f32[22,24,256]{2,1,0:T(8,128)S(1)}, f32[20,24,256]{2,1,0:T(8,128)S(1)}, f32[10,16,128]{2,1,0:T(8,128)S(1)}, f32[8,16,128]{2,1,0:T(8,128)S(1)}, ...) custom-call(s32[1]{0:T(128)} %bitcast.2.core_ref, ...), custom_call_target="tpu_custom_call" | custom-call | tf_op jit(solution)/shard_map/pallas_call | solution.py:567
  32.5 0.5 shard_map.44
  33.1 13.3 %all_to_all.10 = f32[8,4,128]{2,1,0:T(4,128)S(1)} all-to-all(f32[8,4,128]{2,1,0:T(4,128)S(1)} %shard_map.44), channel_id=1, replica_groups=mesh['gx'=32,'chip'=8,'core'=2] {'chip'}, dimensions={0} | all-to-all | bytes 32768 | tf_op jit(solution)/shard_map/all_to_all | solution.py:628
  46.4 0.9 broadcast_in_dim.8
  47.2 4.8 %all-to-all-start.1 = ((f32[32,32,128]{2,1,0:T(8,128)}), f32[32,32,128]{2,1,0:T(8,128)S(1)}, u32[]{:S(2)}, u32[]{:S(2)}) async-start(f32[32,32,128]{2,1,0:T(8,128)} %broadcast_in_dim.8), calls=%async_computation.1 | async-start | bytes 1048576 | tf_op jit(solution)/shard_map/all_to_all | solution.py:630
  52.0 6.3 %collective-permute-start.7 = (f32[18,8,128]{2,1,0:T(8,128)}, f32[18,8,128]{2,1,0:T(8,128)S(1)}, u32[]{:S(2)}, u32[]{:S(2)}) collective-permute-start(f32[18,8,128]{2,1,0:T(8,128)} %get-tuple-element.30), channel_id=1, source_target_pairs={{1,0},{2,1},{3,2},{4,3},{5,4},{6,5},{7,6},{8,7},{9,8},{10,9},{11,1... | collective-permute-start | bytes 221192 | tf_op jit(solution)/shard_map/ppermute | solution.py:582
  58.3 2.1 %collective-permute-start.6 = (f32[18,8,128]{2,1,0:T(8,128)}, f32[18,8,128]{2,1,0:T(8,128)S(1)}, u32[]{:S(2)}, u32[]{:S(2)}) collective-permute-start(f32[18,8,128]{2,1,0:T(8,128)} %get-tuple-element.30), channel_id=1, source_target_pairs={{0,1},{1,2},{2,3},{3,4},{4,5},{5,6},{6,7},{7,8},{8,9},{9,10},{10,1... | collective-permute-start | bytes 221192 | tf_op jit(solution)/shard_map/ppermute | solution.py:581
  60.4 3.1 %collective-permute-start.4 = (f32[11,8,128]{2,1,0:T(8,128)}, f32[11,8,128]{2,1,0:T(8,128)S(1)}, u32[]{:S(2)}, u32[]{:S(2)}) collective-permute-start(f32[11,8,128]{2,1,0:T(8,128)} %get-tuple-element.28), channel_id=1, source_target_pairs={{0,16},{16,32},{32,48},{48,64},{64,80},{80,96},{96,112},{112,128},... | collective-permute-start | bytes 135176 | tf_op jit(solution)/shard_map/ppermute | solution.py:581
  63.5 4.3 %collective-permute-start.5 = (f32[11,8,128]{2,1,0:T(8,128)}, f32[11,8,128]{2,1,0:T(8,128)S(1)}, u32[]{:S(2)}, u32[]{:S(2)}) collective-permute-start(f32[11,8,128]{2,1,0:T(8,128)} %get-tuple-element.29), channel_id=1, source_target_pairs={{16,0},{32,16},{48,32},{64,48},{80,64},{96,80},{112,96},{128,112},... | collective-permute-start | bytes 135176 | tf_op jit(solution)/shard_map/ppermute | solution.py:582
  67.9 1.9 %shard_map.45 = (f32[6,16,16,256]{3,2,1,0:T(8,128)S(1)}, f32[16,16,256]{2,1,0:T(8,128)S(1)}, f32[16,16,256]{2,1,0:T(8,128)S(1)}, f32[16,16,256]{2,1,0:T(8,128)S(1)}) custom-call(f32[22,24,256]{2,1,0:T(8,128)S(1)} %get-tuple-element.31.k_ref, f32[20,24,256]{2,1,0:T(8,128)S(1)} %get-tuple-element.32.f_ref), custom_call_target="tpu_custom_call" | custom-call | tf_op jit(solution)/shard_map/pallas_call | solution.py:567
  69.7 0.0 copy-start
  69.7 0.7 copy-done
  70.4 0.0 copy-start.2
  70.4 0.7 copy-done.2
  71.1 0.0 copy-start.4
  71.1 0.7 copy-done.4
  71.8 0.0 collective-permute-done.4.refs_1_.x_low_ref
  71.8 0.0 collective-permute-done.5.refs_2_.x_high_ref
  71.8 0.0 collective-permute-done.7.refs_4_.y_high_ref
  71.8 0.0 collective-permute-done.6.refs_3_.y_low_ref
  71.8 0.0 all-to-all-done.1
  71.8 2.7 %collective-permute-start.8 = (f32[1024,128]{1,0:T(8,128)S(1)}, f32[1024,128]{1,0:T(8,128)S(1)}, u32[]{:S(2)}, u32[]{:S(2)}) collective-permute-start(f32[1024,128]{1,0:T(8,128)S(1)} %shard_map.46.mine_ref.after_ref), channel_id=1, source_target_pairs={{0,1},{1,0},{2,3},{3,2},{4,5},{5,4},{6,7},{7,6},{8,9},{9,8},{10,11... | collective-permute-start | bytes 1572872 | tf_op jit(solution)/shard_map/ppermute | solution.py:641
  74.6 0.1 pad_add_fusion.place_ref
  74.7 0.5 shard_map.48
  75.2 0.0 copy-start.1
  75.2 0.0 copy-start.3
  75.2 0.0 copy-start.5
  75.2 0.9 %collective-permute-done.8.other_ref = f32[1024,128]{1,0:T(8,128)S(1)} collective-permute-done((f32[1024,128]{1,0:T(8,128)S(1)}, f32[1024,128]{1,0:T(8,128)S(1)}, u32[]{:S(2)}, u32[]{:S(2)}) %collective-permute-start.8) | collective-permute-done | bytes 524320 | tf_op jit(solution)/shard_map/ppermute | solution.py:641
  76.1 7.8 %shard_map.47.near_ref = f32[6,16,128]{2,1,0:T(8,128)S(1)} custom-call(s32[2]{0:T(128)S(1)} %pad_add_fusion.place_ref, f32[1024,128]{1,0:T(8,128)S(1)} %shard_map.46.mine_ref.after_ref, f32[1024,128]{1,0:T(8,128)S(1)} %collective-permute-done.8.other_ref), custom_call_target="tpu_custom_call" | custom-call | flops 6000000000 | tf_op jit(solution)/shard_map/pallas_call | solution.py:567
  83.9 0.0 copy-done.1
  83.9 0.0 copy-done.3
  83.9 0.0 copy-done.5
  83.9 2.2 %shard_map.49 = (f32[8,8,256]{2,1,0:T(8,128)}, f32[8,8,256]{2,1,0:T(8,128)}) custom-call(f32[6,16,128]{2,1,0:T(8,128)S(1)} %shard_map.47.near_ref, f32[6,16,16,128]{3,2,1,0:T(8,128)S(1)} %get-tuple-element.34.c1, f32[16,16,128]{2,1,0:T(8,128)S(1)} %get-tuple-element.35.g1, f32[16,16,128]{2,1,0:T(8,128)S(1)} %get-tuple-element.36.x1, ...), custom_call_target="tpu_custom_call" | custom-call | tf_op jit(solution)/shard_map/pallas_call | solution.py:567
  (2 shorter events, 0.0 us)
Async XLA Ops:
  0.6 0.8 copy-start.6
  1.5 0.8 copy-start.7
  2.8 12.6 %collective-permute-start = (f32[13,8,256]{2,1,0:T(8,128)S(1)}, f32[13,8,256]{2,1,0:T(8,128)S(1)}, u32[]{:S(2)}, u32[]{:S(2)}) collective-permute-start(f32[13,8,256]{2,1,0:T(8,128)S(1)} %get-tuple-element.22), channel_id=1, source_target_pairs={{0,16},{16,32},{32,48},{48,64},{64,80},{80,96},{96,112},{112,128},... | collective-permute-start | bytes 319496 | tf_op jit(solution)/shard_map/ppermute | solution.py:603
  13.4 7.6 %collective-permute-start.1 = (f32[13,8,256]{2,1,0:T(8,128)S(1)}, f32[13,8,256]{2,1,0:T(8,128)S(1)}, u32[]{:S(2)}, u32[]{:S(2)}) collective-permute-start(f32[13,8,256]{2,1,0:T(8,128)S(1)} %get-tuple-element.23), channel_id=1, source_target_pairs={{16,0},{32,16},{48,32},{64,48},{80,64},{96,80},{112,96},{128,112},... | collective-permute-start | bytes 319496 | tf_op jit(solution)/shard_map/ppermute | solution.py:604
  21.0 7.3 %collective-permute-start.3 = (f32[28,8,256]{2,1,0:T(8,128)S(1)}, f32[28,8,256]{2,1,0:T(8,128)S(1)}, u32[]{:S(2)}, u32[]{:S(2)}) collective-permute-start(f32[28,8,256]{2,1,0:T(8,128)S(1)} %get-tuple-element.25), channel_id=1, source_target_pairs={{1,2},{2,1},{3,4},{4,3},{5,6},{6,5},{7,8},{8,7},{9,10},{10,9},{11,... | collective-permute-start | bytes 688136 | tf_op jit(solution)/shard_map/ppermute | solution.py:607
  23.0 5.4 %collective-permute-start.2 = (f32[28,8,256]{2,1,0:T(8,128)S(1)}, f32[28,8,256]{2,1,0:T(8,128)S(1)}, u32[]{:S(2)}, u32[]{:S(2)}) collective-permute-start(f32[28,8,256]{2,1,0:T(8,128)S(1)} %get-tuple-element.24.own_ref), channel_id=1, source_target_pairs={{0,1},{1,0},{2,3},{3,2},{4,5},{5,4},{6,7},{7,6},{8,9},{9,8},{10,11... | collective-permute-start | bytes 688136 | tf_op jit(solution)/shard_map/ppermute | solution.py:606
  47.2 24.6 %all-to-all-start.1 = ((f32[32,32,128]{2,1,0:T(8,128)}), f32[32,32,128]{2,1,0:T(8,128)S(1)}, u32[]{:S(2)}, u32[]{:S(2)}) async-start(f32[32,32,128]{2,1,0:T(8,128)} %broadcast_in_dim.8), calls=%async_computation.1 | async-start | bytes 1048576 | tf_op jit(solution)/shard_map/all_to_all | solution.py:630
  52.0 19.8 %collective-permute-start.7 = (f32[18,8,128]{2,1,0:T(8,128)}, f32[18,8,128]{2,1,0:T(8,128)S(1)}, u32[]{:S(2)}, u32[]{:S(2)}) collective-permute-start(f32[18,8,128]{2,1,0:T(8,128)} %get-tuple-element.30), channel_id=1, source_target_pairs={{1,0},{2,1},{3,2},{4,3},{5,4},{6,5},{7,6},{8,7},{9,8},{10,9},{11,1... | collective-permute-start | bytes 221192 | tf_op jit(solution)/shard_map/ppermute | solution.py:582
  58.3 13.5 %collective-permute-start.6 = (f32[18,8,128]{2,1,0:T(8,128)}, f32[18,8,128]{2,1,0:T(8,128)S(1)}, u32[]{:S(2)}, u32[]{:S(2)}) collective-permute-start(f32[18,8,128]{2,1,0:T(8,128)} %get-tuple-element.30), channel_id=1, source_target_pairs={{0,1},{1,2},{2,3},{3,4},{4,5},{5,6},{6,7},{7,8},{8,9},{9,10},{10,1... | collective-permute-start | bytes 221192 | tf_op jit(solution)/shard_map/ppermute | solution.py:581
  60.4 11.4 %collective-permute-start.4 = (f32[11,8,128]{2,1,0:T(8,128)}, f32[11,8,128]{2,1,0:T(8,128)S(1)}, u32[]{:S(2)}, u32[]{:S(2)}) collective-permute-start(f32[11,8,128]{2,1,0:T(8,128)} %get-tuple-element.28), channel_id=1, source_target_pairs={{0,16},{16,32},{32,48},{48,64},{64,80},{80,96},{96,112},{112,128},... | collective-permute-start | bytes 135176 | tf_op jit(solution)/shard_map/ppermute | solution.py:581
  63.5 8.3 %collective-permute-start.5 = (f32[11,8,128]{2,1,0:T(8,128)}, f32[11,8,128]{2,1,0:T(8,128)S(1)}, u32[]{:S(2)}, u32[]{:S(2)}) collective-permute-start(f32[11,8,128]{2,1,0:T(8,128)} %get-tuple-element.29), channel_id=1, source_target_pairs={{16,0},{32,16},{48,32},{64,48},{80,64},{96,80},{112,96},{128,112},... | collective-permute-start | bytes 135176 | tf_op jit(solution)/shard_map/ppermute | solution.py:582
  69.7 0.7 copy-start
  70.4 0.7 copy-start.2
  71.1 0.7 copy-start.4
  71.8 4.3 %collective-permute-start.8 = (f32[1024,128]{1,0:T(8,128)S(1)}, f32[1024,128]{1,0:T(8,128)S(1)}, u32[]{:S(2)}, u32[]{:S(2)}) collective-permute-start(f32[1024,128]{1,0:T(8,128)S(1)} %shard_map.46.mine_ref.after_ref), channel_id=1, source_target_pairs={{0,1},{1,0},{2,3},{3,2},{4,5},{5,4},{6,7},{7,6},{8,9},{9,8},{10,11... | collective-permute-start | bytes 1572872 | tf_op jit(solution)/shard_map/ppermute | solution.py:641
  75.2 8.7 %copy-start.1 = (f32[16,16,256]{2,1,0:T(8,128)S(1)}, f32[16,16,256]{2,1,0:T(8,128)}, u32[]{:S(2)}) copy-start(f32[16,16,256]{2,1,0:T(8,128)} %copy-done) | copy-start | bytes 786436
  75.2 8.7 %copy-start.3 = (f32[16,16,256]{2,1,0:T(8,128)S(1)}, f32[16,16,256]{2,1,0:T(8,128)}, u32[]{:S(2)}) copy-start(f32[16,16,256]{2,1,0:T(8,128)} %copy-done.2) | copy-start | bytes 786436
  75.2 8.7 %copy-start.5 = (f32[16,16,256]{2,1,0:T(8,128)S(1)}, f32[16,16,256]{2,1,0:T(8,128)}, u32[]{:S(2)}) copy-start(f32[16,16,256]{2,1,0:T(8,128)} %copy-done.4) | copy-start | bytes 786436

commit v8 on v7

--- a/solution.py
+++ b/solution.py
@@ -112,6 +112,27 @@
     for number in range(1, 6):
         total = total + pick(c_ref, number, where) * around[number]
     return total
+
+
+def face_sums(k_ref, start, size):
+    center = k_ref[pl.ds(start, size)]
+    around = near_inside(k_ref, start, size)
+    total = 6.0 * center
+    for value in around:
+        total = total + value
+    inside = center > 0.0
+    half_inverse = jnp.where(inside, 1.0 / jnp.where(inside, total, 1.0), 0.0)
+    return (center + around[1], center + around[3], jnp.where(around[5] > 0.0, center + around[5], 0.0), half_inverse)
+
+
+def spread_faces(w_ref, v_ref, start, size):
+    at = pl.ds(start, size)
+    here, along_y, along_z = v_ref[at], w_ref.at[1][at], w_ref.at[2][at]
+    total = w_ref.at[0][at] * v_ref[pl.ds(start + 1, size)]
+    total = total + w_ref.at[0][pl.ds(start - 1, size)] * v_ref[pl.ds(start - 1, size)]
+    total = total + along_y * shifted(here, 1, 1) + shifted(along_y * here, -1, 1)
+    total = total + along_z * shifted(here, 1, 2) + shifted(along_z * here, -1, 2)
+    return w_ref.at[3][at] * total
 
 
 PAIRS = ([("k", dx, 7 - dx) for dx in (1, 2, 3)], [("f", dx, 6 - dx) for dx in (1, 2, 3)])
@@ -203,8 +224,8 @@
     unpack(core_ref[0] == 0, own_ref, x_one_ref, x_two_ref, sibling_ref, next_ref, k0, f0)
 
     def setup(start):
-        at = pl.ds(start, 2)
-        couplings, inverse, diagonal = coupling(k0[pl.ds(start + 1, 2)], near_inside(k0, start + 1, 2), (4, 5))
+        at = pl.ds(start, 4)
+        couplings, inverse, diagonal = coupling(k0[pl.ds(start + 1, 4)], near_inside(k0, start + 1, 4), (4, 5))
         for number in range(6):
             c0.at[number][at] = couplings[number]
         diag0[at] = diagonal
@@ -212,23 +233,24 @@
         g0[at] = scaled
         d0[at] = FIRST * scaled
 
-    blocks(0, 20, 2, setup)
+    blocks(0, 20, 4, setup)
 
     def second(start):
-        at = pl.ds(start, 2)
+        at = pl.ds(start, 6)
         here = d0[at]
-        scaled = g0[at] - here + spread(c0, (at,), near(d0, start, 2))
+        scaled = g0[at] - here + spread(c0, (at,), near(d0, start, 6))
         g0[at] = scaled
         e0[at] = KEEP * here + ADD * scaled
 
-    blocks(1, 19, 2, second)
+    blocks(1, 19, 6, second)
 
     def left(start):
-        at = pl.ds(start, 2)
-        rest = diag0[at] * (g0[at] - e0[at] + spread(c0, (at,), near(e0, start, 2)))
+        at = pl.ds(start, 4)
+        rest = diag0[at] * (g0[at] - e0[at] + spread(c0, (at,), near(e0, start, 4)))
         sums[start // 2 - 1] = 0.5 * (rest[0] + rest[1])
-
-    blocks(2, 18, 2, left)
+        sums[start // 2] = 0.5 * (rest[2] + rest[3])
+
+    blocks(2, 18, 4, left)
     for index in range(10):
         sums[index + 8] = 0.125 * (k0[2 * index + 1] + k0[2 * index + 2])
     fold = ones_where(iota((256, 128), 0) // 2 == iota((256, 128), 1))
@@ -327,7 +349,7 @@
 
 def make_coarse_kernel(count_x, count_y):
     planes2, rows, count3 = 2 * count_x, count_y // 2, count_x // 4
-    size = 4
+    size = 16
     line = (2, rows, 128)
 
     def coarse_kernel(place_ref, mine_ref, other_ref, near_ref,
@@ -448,36 +470,35 @@
     return coarse_kernel
 
 
-def prepare_kernel(k_ref, f_ref, c0, diag0, g0, x0, d0):
+def prepare_kernel(k_ref, f_ref, after_ref, w0, g0, x0, d0):
+    def cut(value):
+        return shifted(value, 4, 1)[:, 0:16]
+
     def setup0(start):
-        def cut(value):
-            return shifted(value, 4, 1)[:, 0:16]
-
-        at = pl.ds(start, 2)
-        couplings, inverse, diagonal = coupling(k_ref[pl.ds(start + 3, 2)], near_inside(k_ref, start + 3, 2), (4, 5))
-        for number in range(6):
-            c0.at[number][at] = cut(couplings[number])
-        diag0[at] = cut(diagonal)
-        scaled = cut(inverse * f_ref[pl.ds(start + 2, 2)])
+        at = pl.ds(start, 4)
+        faces = face_sums(k_ref, start + 3, 4)
+        for number in range(4):
+            w0.at[number][at] = cut(faces[number])
+        scaled = cut(2.0 * faces[3] * f_ref[pl.ds(start + 2, 4)])
         g0[at] = scaled
         d0[at] = FIRST * scaled
 
-    blocks(0, 16, 2, setup0)
+    blocks(0, 16, 4, setup0)
 
     def guess0(start):
-        at = pl.ds(start, 2)
+        at = pl.ds(start, 7)
         here = d0[at]
-        scaled = g0[at] - here + spread(c0, (at,), near(d0, start, 2))
+        scaled = g0[at] - here + spread_faces(w0, d0, start, 7)
         x0[at] = (1.0 + KEEP) * here + ADD * scaled
 
-    blocks(1, 15, 2, guess0)
+    blocks(1, 15, 7, guess0)
 
 
 def gate_kernel(*refs):
     pass
 
 
-def prepare1_kernel(k_ref, f_ref, x_low_ref, x_high_ref, y_low_ref, y_high_ref, after_ref, c1, g1, x1, k1, f1, d1):
+def prepare1_kernel(k_ref, f_ref, x_low_ref, x_high_ref, y_low_ref, y_high_ref, after_ref, w1, g1, x1, k1, f1, d1):
     row = iota((8, 128), 0)
 
     def join(low, middle, high):
@@ -499,32 +520,29 @@
 
     def setup1(start):
         at = pl.ds(start, 7)
-        couplings, inverse, _ = coupling(k1[at], near_inside(k1, start, 7), (4, 5))
-        for number in range(6):
-            c1.at[number][at] = couplings[number]
-        scaled = inverse * f1[at]
+        faces = face_sums(k1, start, 7)
+        for number in range(4):
+            w1.at[number][at] = faces[number]
+        scaled = 2.0 * faces[3] * f1[at]
         g1[at] = scaled
         d1[at] = FIRST * scaled
 
     blocks(1, 15, 7, setup1)
-
-    def guess1(start):
-        at = pl.ds(start, 6)
-        here = d1[at]
-        scaled = g1[at] - here + spread(c1, (at,), near(d1, start, 6))
-        x1[at] = (1.0 + KEEP) * here + ADD * scaled
-
-    blocks(2, 14, 6, guess1)
-
-def post_kernel(near_ref, c1, g1, x1, c0, diag0, g0, x0, correction_ref, residual_ref,
+    at = pl.ds(2, 12)
+    here = d1[at]
+    scaled = g1[at] - here + spread_faces(w1, d1, 2, 12)
+    x1[at] = (1.0 + KEEP) * here + ADD * scaled
+
+
+def post_kernel(near_ref, w1, g1, x1, w0, g0, x0, correction_ref, residual_ref,
                 y1, d1, h1, wide, y0, d0, h0, v0):
     up = near_ref[...]
     y1[2:14] = x1[2:14] + jnp.stack([up, up], 1).reshape(12, 16, 128)
-    scaled = g1[3:13] - y1[3:13] + spread(c1, (pl.ds(3, 10),), near(y1, 3, 10))
+    scaled = g1[3:13] - y1[3:13] + spread_faces(w1, y1, 3, 10)
     h1[3:13] = scaled
     d1[3:13] = FIRST * scaled
     here = d1[4:12]
-    scaled = h1[4:12] - here + spread(c1, (pl.ds(4, 8),), near(d1, 4, 8))
+    scaled = h1[4:12] - here + spread_faces(w1, d1, 4, 8)
     found = y1[4:12] + (1.0 + KEEP) * here + ADD * scaled
     wide[:, pl.ds(0, 8, stride=2), :] = found[:, 4:12]
     wide[:, pl.ds(1, 8, stride=2), :] = found[:, 4:12]
@@ -535,30 +553,30 @@
         y0[index] = x0[index] + up[index // 2]
 
     def first0(start):
-        at = pl.ds(start, 3)
-        scaled = g0[at] - y0[at] + spread(c0, (at,), near(y0, start, 3))
+        at = pl.ds(start, 6)
+        scaled = g0[at] - y0[at] + spread_faces(w0, y0, start, 6)
         h0[at] = scaled
         d0[at] = FIRST * scaled
 
-    blocks(2, 14, 3, first0)
+    blocks(2, 14, 6, first0)
 
     def second0(start):
-        at = pl.ds(start, 2)
+        at = pl.ds(start, 5)
         here = d0[at]
-        scaled = h0[at] - here + spread(c0, (at,), near(d0, start, 2))
+        scaled = h0[at] - here + spread_faces(w0, d0, start, 5)
         h0[at] = scaled
         v0[at] = KEEP * here + ADD * scaled
 
-    blocks(3, 13, 2, second0)
+    blocks(3, 13, 5, second0)
 
     def last0(start):
-        at, to = pl.ds(start, 2), pl.ds(start - 4, 2)
+        at, to = pl.ds(start, 4), pl.ds(start - 4, 4)
         here = v0[at]
         correction_ref[to] = (y0[at] + d0[at] + here)[:, 4:12]
-        scaled = h0[at] - here + spread(c0, (at,), near(v0, start, 2))
-        residual_ref[to] = (diag0[at] * scaled)[:, 4:12]
-
-    blocks(4, 12, 2, last0)
+        scaled = h0[at] - here + spread_faces(w0, v0, start, 4)
+        residual_ref[to] = scaled[:, 4:12] * (0.5 / w0.at[3][at][:, 4:12])
+
+    blocks(4, 12, 4, last0)
 
 
 def call(kernel, limit, shapes, scratch, *operands, scalars=0, flops=0):
@@ -619,16 +637,10 @@
         [(6, 8, *full1)] + [(8, *full1)] * 4 + [(4, *full1)],
         k1, f1)
 
-    prepared = call(
-        prepare_kernel, 16,
-        [(6, 16, *half)] + [(16, *half)] * 3,
-        [(16, *half)],
-        k0, f0)
-
     line = lax.all_to_all(copies, "chip", 0, 0).reshape(-1, 128)
     copies = jnp.broadcast_to(line[None], (count_x, *line.shape))
     mine = lax.all_to_all(copies, "gx", 0, 0).reshape(-1, 128)
-    waited = (mine, x_low, x_high, y_low, y_high, prepared[0])
+    waited = (mine, x_low, x_high, y_low, y_high)
     mine = pl.pallas_call(
         gate_kernel,
         out_shape=jax.ShapeDtypeStruct(mine.shape, F32),
@@ -640,9 +652,14 @@
     )(*waited)
     other = lax.ppermute(mine, "core", [(0, 1), (1, 0)])
 
+    prepared = call(
+        prepare_kernel, 16,
+        [(4, 16, *half)] + [(16, *half)] * 2,
+        [(16, *half)],
+        k0, f0, mine)
     prepared1 = call(
         prepare1_kernel, 8,
-        [(6, 16, *full1)] + [(16, *full1)] * 2,
+        [(4, 16, *full1)] + [(16, *full1)] * 2,
         [(16, *full1)] * 3,
         k1, f1, x_low, x_high, y_low, y_high, mine)
 

time: 86.7 us -> 84.2 us (0.971)
  the two profiles are of different devices: /device:TPU:3 before, /device:TPU:1 now
where the time goes in v8:
time: 84.2 us; the launch traced here: 83.6 us
  starting transfers between devices  45.5 us (54%)
  Pallas kernels  12.2 us (14%)
  blocking collectives  11.5 us (14%)
  waiting for transfers between devices  11 us (13%)
  local copies, waits for them, and re-layouts  2.52 us (3%)
    all_to_all x1, starting transfers between devices, body(): mine = lax.all_to_all(copies, 'gx', 0, 0).reshape(-1, 128)  12.3 us
    pallas_call x7, Pallas kernels, call(): pl.pallas_call(kernel, out_shape=[jax.ShapeDtypeStruct(shape, F32) for sh...  11.8 us
    all_to_all x1, blocking collectives, body(): line = lax.all_to_all(copies, 'chip', 0, 0).reshape(-1, 128)  11.5 us
    ppermute x1, starting transfers between devices, body(): sibling = lax.ppermute(packed, 'core', [(0, 1), (1, 0)])  8.23 us
    ppermute x2, starting transfers between devices, both_sides(): low = lax.ppermute(up, axes, [(i, i + 1) for i in range(count - 1)])  8.19 us
    ppermute x1, starting transfers between devices, body(): lax.ppermute(two, ('gx', 'core'), [(to, source) for source, to in route])  5.46 us
    ppermute x1, waiting for transfers between devices, body(): lax.ppermute(outer, along_y, [pair for i in range(1, count_y - 1, 2) for...  5.4 us
    ppermute x1, starting transfers between devices, body(): other = lax.ppermute(mine, 'core', [(0, 1), (1, 0)])  4.97 us
  transfers between devices with their start and end apart: 10, of which 6 were waited for; matrix products, arithmetic and copies ran while one was open for 0% of the time, Pallas kernels for 2%

profile of v8, /device:TPU:1, one launch (start us, length us, event | category | flops | bytes accessed | tf_op | source)
XLA Modules:
  0.0 83.6 jit_solution(17024232128084227956)
XLA Ops:
  0.6 0.0 copy-start
  0.6 0.8 copy-done
  1.5 0.0 copy-start.1
  1.5 0.8 %copy-done.1 = f32[8,8,256]{2,1,0:T(8,128)S(1)} copy-done((f32[8,8,256]{2,1,0:T(8,128)S(1)}, f32[8,8,256]{2,1,0:T(8,128)}, u32[]{:S(2)}) %copy-start.1) | copy-done | bytes 65560
  2.3 0.5 shard_map.41
  2.8 1.3 %collective-permute-start = (f32[13,8,256]{2,1,0:T(8,128)S(1)}, f32[13,8,256]{2,1,0:T(8,128)S(1)}, u32[]{:S(2)}, u32[]{:S(2)}) collective-permute-start(f32[13,8,256]{2,1,0:T(8,128)S(1)} %get-tuple-element.21), channel_id=1, source_target_pairs={{0,16},{16,32},{32,48},{48,64},{64,80},{80,96},{96,112},{112,128},... | collective-permute-start | bytes 319496 | tf_op jit(solution)/shard_map/ppermute | solution.py:621
  4.1 5.5 %collective-permute-start.1 = (f32[13,8,256]{2,1,0:T(8,128)S(1)}, f32[13,8,256]{2,1,0:T(8,128)S(1)}, u32[]{:S(2)}, u32[]{:S(2)}) collective-permute-start(f32[13,8,256]{2,1,0:T(8,128)S(1)} %get-tuple-element.22), channel_id=1, source_target_pairs={{16,0},{32,16},{48,32},{64,48},{80,64},{96,80},{112,96},{128,112},... | collective-permute-start | bytes 319496 | tf_op jit(solution)/shard_map/ppermute | solution.py:622
  9.6 0.1 collective-permute-done.x_one_ref
  9.7 1.5 %collective-permute-done.1.x_two_ref = f32[13,8,256]{2,1,0:T(8,128)S(1)} collective-permute-done((f32[13,8,256]{2,1,0:T(8,128)S(1)}, f32[13,8,256]{2,1,0:T(8,128)S(1)}, u32[]{:S(2)}, u32[]{:S(2)}) %collective-permute-start.1) | collective-permute-done | bytes 106528 | tf_op jit(solution)/shard_map/ppermute | solution.py:622
  11.3 8.2 %collective-permute-start.2 = (f32[28,8,256]{2,1,0:T(8,128)S(1)}, f32[28,8,256]{2,1,0:T(8,128)S(1)}, u32[]{:S(2)}, u32[]{:S(2)}) collective-permute-start(f32[28,8,256]{2,1,0:T(8,128)S(1)} %get-tuple-element.23.own_ref), channel_id=1, source_target_pairs={{0,1},{1,0},{2,3},{3,2},{4,5},{5,4},{6,7},{7,6},{8,9},{9,8},{10,11... | collective-permute-start | bytes 688136 | tf_op jit(solution)/shard_map/ppermute | solution.py:624
  19.5 1.9 %collective-permute-start.3 = (f32[28,8,256]{2,1,0:T(8,128)S(1)}, f32[28,8,256]{2,1,0:T(8,128)S(1)}, u32[]{:S(2)}, u32[]{:S(2)}) collective-permute-start(f32[28,8,256]{2,1,0:T(8,128)S(1)} %get-tuple-element.24), channel_id=1, source_target_pairs={{1,2},{2,1},{3,4},{4,3},{5,6},{6,5},{7,8},{8,7},{9,10},{10,9},{11,... | collective-permute-start | bytes 688136 | tf_op jit(solution)/shard_map/ppermute | solution.py:625
  21.5 0.0 collective-permute-done.2.sibling_ref
  21.5 5.4 %collective-permute-done.3.next_ref = f32[28,8,256]{2,1,0:T(8,128)S(1)} collective-permute-done((f32[28,8,256]{2,1,0:T(8,128)S(1)}, f32[28,8,256]{2,1,0:T(8,128)S(1)}, u32[]{:S(2)}, u32[]{:S(2)}) %collective-permute-start.3) | collective-permute-done | bytes 229408 | tf_op jit(solution)/shard_map/ppermute | solution.py:625
  26.9 2.5 %shard_map.43 = (f32[22,24,256]{2,1,0:T(8,128)S(1)}, f32[20,24,256]{2,1,0:T(8,128)S(1)}, f32[10,16,128]{2,1,0:T(8,128)S(1)}, f32[8,16,128]{2,1,0:T(8,128)S(1)}, ...) custom-call(s32[1]{0:T(128)} %bitcast.2.core_ref, ...), custom_call_target="tpu_custom_call" | custom-call | tf_op jit(solution)/shard_map/pallas_call | solution.py:585
  29.3 0.5 shard_map.44
  29.9 11.5 %all_to_all.10 = f32[8,4,128]{2,1,0:T(4,128)S(1)} all-to-all(f32[8,4,128]{2,1,0:T(4,128)S(1)} %shard_map.44), channel_id=1, replica_groups=mesh['gx'=32,'chip'=8,'core'=2] {'chip'}, dimensions={0} | all-to-all | bytes 32768 | tf_op jit(solution)/shard_map/all_to_all | solution.py:640
  41.4 0.8 %broadcast_in_dim.8 = f32[32,32,128]{2,1,0:T(8,128)} broadcast(f32[32,128]{1,0:T(8,128)S(1)} %bitcast.6), dimensions={1,2} | broadcast | bytes 540672 | tf_op jit(solution)/shard_map/broadcast_in_dim | solution.py:641
  42.2 12.3 %all-to-all-start.1 = ((f32[32,32,128]{2,1,0:T(8,128)}), f32[32,32,128]{2,1,0:T(8,128)S(1)}, u32[]{:S(2)}, u32[]{:S(2)}) async-start(f32[32,32,128]{2,1,0:T(8,128)} %broadcast_in_dim.8), calls=%async_computation.1 | async-start | bytes 1048576 | tf_op jit(solution)/shard_map/all_to_all | solution.py:642
  54.5 4.8 %collective-permute-start.6 = (f32[18,8,128]{2,1,0:T(8,128)S(1)}, f32[18,8,128]{2,1,0:T(8,128)S(1)}, u32[]{:S(2)}, u32[]{:S(2)}) collective-permute-start(f32[18,8,128]{2,1,0:T(8,128)S(1)} %get-tuple-element.29), channel_id=1, source_target_pairs={{0,1},{1,2},{2,3},{3,4},{4,5},{5,6},{6,7},{7,8},{8,9},{9,10},{10,1... | collective-permute-start | bytes 221192 | tf_op jit(solution)/shard_map/ppermute | solution.py:599
  59.3 1.9 %collective-permute-start.7 = (f32[18,8,128]{2,1,0:T(8,128)S(1)}, f32[18,8,128]{2,1,0:T(8,128)S(1)}, u32[]{:S(2)}, u32[]{:S(2)}) collective-permute-start(f32[18,8,128]{2,1,0:T(8,128)S(1)} %get-tuple-element.29), channel_id=1, source_target_pairs={{1,0},{2,1},{3,2},{4,3},{5,4},{6,5},{7,6},{8,7},{9,8},{10,9},{11,1... | collective-permute-start | bytes 221192 | tf_op jit(solution)/shard_map/ppermute | solution.py:600
  61.2 3.4 %collective-permute-start.4 = (f32[11,8,128]{2,1,0:T(8,128)S(1)}, f32[11,8,128]{2,1,0:T(8,128)S(1)}, u32[]{:S(2)}, u32[]{:S(2)}) collective-permute-start(f32[11,8,128]{2,1,0:T(8,128)S(1)} %get-tuple-element.27), channel_id=1, source_target_pairs={{0,16},{16,32},{32,48},{48,64},{64,80},{80,96},{96,112},{112,128},... | collective-permute-start | bytes 135176 | tf_op jit(solution)/shard_map/ppermute | solution.py:599
  64.6 1.3 %collective-permute-start.5 = (f32[11,8,128]{2,1,0:T(8,128)S(1)}, f32[11,8,128]{2,1,0:T(8,128)S(1)}, u32[]{:S(2)}, u32[]{:S(2)}) collective-permute-start(f32[11,8,128]{2,1,0:T(8,128)S(1)} %get-tuple-element.28), channel_id=1, source_target_pairs={{16,0},{32,16},{48,32},{64,48},{80,64},{96,80},{112,96},{128,112},... | collective-permute-start | bytes 135176 | tf_op jit(solution)/shard_map/ppermute | solution.py:600
  65.9 1.3 %collective-permute-done.4.refs_1_.x_low_ref = f32[11,8,128]{2,1,0:T(8,128)S(1)} collective-permute-done((f32[11,8,128]{2,1,0:T(8,128)S(1)}, f32[11,8,128]{2,1,0:T(8,128)S(1)}, u32[]{:S(2)}, u32[]{:S(2)}) %collective-permute-start.4) | collective-permute-done | bytes 45088 | tf_op jit(solution)/shard_map/ppermute | solution.py:599
  67.3 2.5 %collective-permute-done.5.refs_2_.x_high_ref = f32[11,8,128]{2,1,0:T(8,128)S(1)} collective-permute-done((f32[11,8,128]{2,1,0:T(8,128)S(1)}, f32[11,8,128]{2,1,0:T(8,128)S(1)}, u32[]{:S(2)}, u32[]{:S(2)}) %collective-permute-start.5) | collective-permute-done | bytes 45088 | tf_op jit(solution)/shard_map/ppermute | solution.py:600
  69.7 0.0 collective-permute-done.6.refs_3_.y_low_ref
  69.7 0.0 collective-permute-done.7.refs_4_.y_high_ref
  69.7 0.0 all-to-all-done.1
  69.8 5.0 %collective-permute-start.8 = (f32[1024,128]{1,0:T(8,128)S(1)}, f32[1024,128]{1,0:T(8,128)S(1)}, u32[]{:S(2)}, u32[]{:S(2)}) collective-permute-start(f32[1024,128]{1,0:T(8,128)S(1)} %shard_map.45.mine_ref.after_ref), channel_id=1, source_target_pairs={{0,1},{1,0},{2,3},{3,2},{4,5},{5,4},{6,7},{7,6},{8,9},{9,8},{10,11... | collective-permute-start | bytes 1572872 | tf_op jit(solution)/shard_map/ppermute | solution.py:653
  74.7 0.1 pad_add_fusion.place_ref
  74.8 1.0 %shard_map.48 = (f32[4,16,16,256]{3,2,1,0:T(8,128)S(1)}, f32[16,16,256]{2,1,0:T(8,128)S(1)}, f32[16,16,256]{2,1,0:T(8,128)S(1)}) custom-call(f32[22,24,256]{2,1,0:T(8,128)S(1)} %get-tuple-element.33.k_ref, f32[20,24,256]{2,1,0:T(8,128)S(1)} %get-tuple-element.34.f_ref, f32[1024,128]{1,0:T(8,128)S(1)} %shard_map.45.mine_ref.after_ref), custom_call_target="tpu_custom_call" | custom-call | tf_op jit(solution)/shard_map/pallas_call | solution.py:585
  75.8 0.4 shard_map.47
  76.2 0.1 collective-permute-done.8.other_ref
  76.2 5.6 %shard_map.46.near_ref = f32[6,16,128]{2,1,0:T(8,128)S(1)} custom-call(s32[2]{0:T(128)S(1)} %pad_add_fusion.place_ref, f32[1024,128]{1,0:T(8,128)S(1)} %shard_map.45.mine_ref.after_ref, f32[1024,128]{1,0:T(8,128)S(1)} %collective-permute-done.8.other_ref), custom_call_target="tpu_custom_call" | custom-call | flops 6000000000 | tf_op jit(solution)/shard_map/pallas_call | solution.py:585
  81.8 1.8 %shard_map.49 = (f32[8,8,256]{2,1,0:T(8,128)}, f32[8,8,256]{2,1,0:T(8,128)}) custom-call(f32[6,16,128]{2,1,0:T(8,128)S(1)} %shard_map.46.near_ref, f32[4,16,16,128]{3,2,1,0:T(8,128)S(1)} %get-tuple-element.30.w1, f32[16,16,128]{2,1,0:T(8,128)S(1)} %get-tuple-element.31.g1, f32[16,16,128]{2,1,0:T(8,128)S(1)} %get-tuple-element.32.x1, ...), custom_call_target="tpu_custom_call" | custom-call | tf_op jit(solution)/shard_map/pallas_call | solution.py:585
  (2 shorter events, 0.0 us)
Async XLA Ops:
  0.6 0.8 %copy-start = (f32[8,8,256]{2,1,0:T(8,128)S(1)}, f32[8,8,256]{2,1,0:T(8,128)}, u32[]{:S(2)}) copy-start(f32[8,8,256]{2,1,0:T(8,128)} %k_ref.1) | copy-start | bytes 196612
  1.5 0.8 %copy-start.1 = (f32[8,8,256]{2,1,0:T(8,128)S(1)}, f32[8,8,256]{2,1,0:T(8,128)}, u32[]{:S(2)}) copy-start(f32[8,8,256]{2,1,0:T(8,128)} %f_ref.1) | copy-start | bytes 196612
  2.8 6.9 %collective-permute-start = (f32[13,8,256]{2,1,0:T(8,128)S(1)}, f32[13,8,256]{2,1,0:T(8,128)S(1)}, u32[]{:S(2)}, u32[]{:S(2)}) collective-permute-start(f32[13,8,256]{2,1,0:T(8,128)S(1)} %get-tuple-element.21), channel_id=1, source_target_pairs={{0,16},{16,32},{32,48},{48,64},{64,80},{80,96},{96,112},{112,128},... | collective-permute-start | bytes 319496 | tf_op jit(solution)/shard_map/ppermute | solution.py:621
  4.1 7.2 %collective-permute-start.1 = (f32[13,8,256]{2,1,0:T(8,128)S(1)}, f32[13,8,256]{2,1,0:T(8,128)S(1)}, u32[]{:S(2)}, u32[]{:S(2)}) collective-permute-start(f32[13,8,256]{2,1,0:T(8,128)S(1)} %get-tuple-element.22), channel_id=1, source_target_pairs={{16,0},{32,16},{48,32},{64,48},{80,64},{96,80},{112,96},{128,112},... | collective-permute-start | bytes 319496 | tf_op jit(solution)/shard_map/ppermute | solution.py:622
  11.3 10.2 %collective-permute-start.2 = (f32[28,8,256]{2,1,0:T(8,128)S(1)}, f32[28,8,256]{2,1,0:T(8,128)S(1)}, u32[]{:S(2)}, u32[]{:S(2)}) collective-permute-start(f32[28,8,256]{2,1,0:T(8,128)S(1)} %get-tuple-element.23.own_ref), channel_id=1, source_target_pairs={{0,1},{1,0},{2,3},{3,2},{4,5},{5,4},{6,7},{7,6},{8,9},{9,8},{10,11... | collective-permute-start | bytes 688136 | tf_op jit(solution)/shard_map/ppermute | solution.py:624
  19.5 7.3 %collective-permute-start.3 = (f32[28,8,256]{2,1,0:T(8,128)S(1)}, f32[28,8,256]{2,1,0:T(8,128)S(1)}, u32[]{:S(2)}, u32[]{:S(2)}) collective-permute-start(f32[28,8,256]{2,1,0:T(8,128)S(1)} %get-tuple-element.24), channel_id=1, source_target_pairs={{1,2},{2,1},{3,4},{4,3},{5,6},{6,5},{7,8},{8,7},{9,10},{10,9},{11,... | collective-permute-start | bytes 688136 | tf_op jit(solution)/shard_map/ppermute | solution.py:625
  42.2 27.5 %all-to-all-start.1 = ((f32[32,32,128]{2,1,0:T(8,128)}), f32[32,32,128]{2,1,0:T(8,128)S(1)}, u32[]{:S(2)}, u32[]{:S(2)}) async-start(f32[32,32,128]{2,1,0:T(8,128)} %broadcast_in_dim.8), calls=%async_computation.1 | async-start | bytes 1048576 | tf_op jit(solution)/shard_map/all_to_all | solution.py:642
  54.5 15.2 %collective-permute-start.6 = (f32[18,8,128]{2,1,0:T(8,128)S(1)}, f32[18,8,128]{2,1,0:T(8,128)S(1)}, u32[]{:S(2)}, u32[]{:S(2)}) collective-permute-start(f32[18,8,128]{2,1,0:T(8,128)S(1)} %get-tuple-element.29), channel_id=1, source_target_pairs={{0,1},{1,2},{2,3},{3,4},{4,5},{5,6},{6,7},{7,8},{8,9},{9,10},{10,1... | collective-permute-start | bytes 221192 | tf_op jit(solution)/shard_map/ppermute | solution.py:599
  59.3 10.4 %collective-permute-start.7 = (f32[18,8,128]{2,1,0:T(8,128)S(1)}, f32[18,8,128]{2,1,0:T(8,128)S(1)}, u32[]{:S(2)}, u32[]{:S(2)}) collective-permute-start(f32[18,8,128]{2,1,0:T(8,128)S(1)} %get-tuple-element.29), channel_id=1, source_target_pairs={{1,0},{2,1},{3,2},{4,3},{5,4},{6,5},{7,6},{8,7},{9,8},{10,9},{11,1... | collective-permute-start | bytes 221192 | tf_op jit(solution)/shard_map/ppermute | solution.py:600
  61.2 6.0 %collective-permute-start.4 = (f32[11,8,128]{2,1,0:T(8,128)S(1)}, f32[11,8,128]{2,1,0:T(8,128)S(1)}, u32[]{:S(2)}, u32[]{:S(2)}) collective-permute-start(f32[11,8,128]{2,1,0:T(8,128)S(1)} %get-tuple-element.27), channel_id=1, source_target_pairs={{0,16},{16,32},{32,48},{48,64},{64,80},{80,96},{96,112},{112,128},... | collective-permute-start | bytes 135176 | tf_op jit(solution)/shard_map/ppermute | solution.py:599
  64.6 5.1 %collective-permute-start.5 = (f32[11,8,128]{2,1,0:T(8,128)S(1)}, f32[11,8,128]{2,1,0:T(8,128)S(1)}, u32[]{:S(2)}, u32[]{:S(2)}) collective-permute-start(f32[11,8,128]{2,1,0:T(8,128)S(1)} %get-tuple-element.28), channel_id=1, source_target_pairs={{16,0},{32,16},{48,32},{64,48},{80,64},{96,80},{112,96},{128,112},... | collective-permute-start | bytes 135176 | tf_op jit(solution)/shard_map/ppermute | solution.py:600
  69.8 6.5 %collective-permute-start.8 = (f32[1024,128]{1,0:T(8,128)S(1)}, f32[1024,128]{1,0:T(8,128)S(1)}, u32[]{:S(2)}, u32[]{:S(2)}) collective-permute-start(f32[1024,128]{1,0:T(8,128)S(1)} %shard_map.45.mine_ref.after_ref), channel_id=1, source_target_pairs={{0,1},{1,0},{2,3},{3,2},{4,5},{5,4},{6,7},{7,6},{8,9},{9,8},{10,11... | collective-permute-start | bytes 1572872 | tf_op jit(solution)/shard_map/ppermute | solution.py:653

commit v9 on v8

--- a/solution.py
+++ b/solution.py
@@ -297,7 +297,11 @@
              + folded[number, 8:9, 128:256] + folded[number, 9:10, 128:256] for number in range(4)]
     payload = jnp.concatenate(lines, 0)
 
-    copies_ref[...] = jnp.broadcast_to(payload[None], copies_ref.shape)
+
+    def copy(start):
+        copies_ref[pl.ds(start, 8)] = jnp.broadcast_to(payload[None], (8, 4, 128))
+
+    blocks(0, copies_ref.shape[0], 8, copy)
 
 
 def near2(ref, start, size):
@@ -628,18 +632,16 @@
         fine_kernel, 16,
         [(22, *full), (20, *full), (10, *full1), (8, *full1), (11, *tile1), (11, *tile1), (18, *tile1)],
         [(6, 20, *full)] + [(20, *full)] * 4 + [(18, *full), (18, 24, 128)],
-        core, packed, one, two, sibling, after, scalars=1)
+        core, outer, one, two, sibling, after, scalars=1)
     x_low, x_high = both_sides(up, down, along_x)
     y_low, y_high = both_sides(side, side, along_y)
     copies, = call(
         next_kernel, 8,
-        [(chips, 4, 128)],
+        [(count_x * chips, 4, 128)],
         [(6, 8, *full1)] + [(8, *full1)] * 4 + [(4, *full1)],
         k1, f1)
 
-    line = lax.all_to_all(copies, "chip", 0, 0).reshape(-1, 128)
-    copies = jnp.broadcast_to(line[None], (count_x, *line.shape))
-    mine = lax.all_to_all(copies, "gx", 0, 0).reshape(-1, 128)
+    mine = lax.all_to_all(copies, ("gx", "chip"), 0, 0).reshape(-1, 128)
     waited = (mine, x_low, x_high, y_low, y_high)
     mine = pl.pallas_call(
         gate_kernel,

time: 84.2 us -> 80.7 us (0.958)
  blocking collectives: 11.5 us -> 0 us
  starting transfers between devices: 45.5 us -> 55 us
  waiting for transfers between devices: 11 us -> 9.53 us
  Pallas kernels: 12.2 us -> 13.2 us
  local copies, waits for them, and re-layouts: 2.52 us -> 1.67 us
    all_to_all x1 -> x0, blocking collectives: 11.5 us -> none  [body(): line = lax.all_to_all(copies, 'chip', 0, 0).reshape(-1, 128)]
    all_to_all x1, starting transfers between devices: 12.3 us -> 21.2 us  [body(): mine = lax.all_to_all(copies, ('gx', 'chip'), 0, 0).reshape(-1, 128)]
    ppermute x1, starting transfers between devices: 8.23 us -> 1.92 us  [body(): sibling = lax.ppermute(packed, 'core', [(0, 1), (1, 0)])]
    ppermute x1, starting transfers between devices: 1.92 us -> 7.38 us  [body(): lax.ppermute(outer, along_y, [pair for i in range(1, count_y - 1, 2) for...]
    ppermute x1, waiting for transfers between devices: 5.4 us -> 1.76 us  [body(): lax.ppermute(outer, along_y, [pair for i in range(1, count_y - 1, 2) for...]
    ppermute x1, starting transfers between devices: 4.97 us -> 7.05 us  [body(): other = lax.ppermute(mine, 'core', [(0, 1), (1, 0)])]
    all_to_all x1, waiting for transfers between devices: 0.01 us -> 2.03 us  [body(): mine = lax.all_to_all(copies, ('gx', 'chip'), 0, 0).reshape(-1, 128)]
    ppermute x2, waiting for transfers between devices: 2.47 us -> 3.66 us  [both_sides(): high = lax.ppermute(down, axes, [(i + 1, i) for i in range(count - 1)])]
  transfers between devices with their start and end apart: 10 -> 10, of which waited for: 6 -> 7; matrix products, arithmetic and copies ran while one was open for 0% -> 0% of each run, Pallas kernels for 2% -> 2%
where the time goes in v9:
time: 80.7 us; the launch traced here: 80.3 us
  starting transfers between devices  55 us (68%)
  Pallas kernels  13.2 us (16%)
  waiting for transfers between devices  9.53 us (12%)
  local copies, waits for them, and re-layouts  1.67 us (2%)
    all_to_all x1, starting transfers between devices, body(): mine = lax.all_to_all(copies, ('gx', 'chip'), 0, 0).reshape(-1, 128)  21.2 us
    pallas_call x7, Pallas kernels, call(): pl.pallas_call(kernel, out_shape=[jax.ShapeDtypeStruct(shape, F32) for sh...  12.7 us
    ppermute x2, starting transfers between devices, both_sides(): low = lax.ppermute(up, axes, [(i, i + 1) for i in range(count - 1)])  7.51 us
    ppermute x1, starting transfers between devices, body(): lax.ppermute(outer, along_y, [pair for i in range(1, count_y - 1, 2) for...  7.38 us
    ppermute x1, starting transfers between devices, body(): other = lax.ppermute(mine, 'core', [(0, 1), (1, 0)])  7.05 us
    ppermute x1, starting transfers between devices, body(): lax.ppermute(two, ('gx', 'core'), [(to, source) for source, to in route])  5.46 us
    ppermute x2, waiting for transfers between devices, both_sides(): high = lax.ppermute(down, axes, [(i + 1, i) for i in range(count - 1)])  3.66 us
    ppermute x2, starting transfers between devices, both_sides(): high = lax.ppermute(down, axes, [(i + 1, i) for i in range(count - 1)])  3.21 us
  transfers between devices with their start and end apart: 10, of which 7 were waited for; matrix products, arithmetic and copies ran while one was open for 0% of the time, Pallas kernels for 2%

profile of v9, /device:TPU:1, one launch (start us, length us, event | category | flops | bytes accessed | tf_op | source)
XLA Modules:
  0.0 80.3 jit_solution(1754706968191171653)
XLA Ops:
  0.6 0.0 copy-start
  0.6 0.8 %copy-done = f32[8,8,256]{2,1,0:T(8,128)S(1)} copy-done((f32[8,8,256]{2,1,0:T(8,128)S(1)}, f32[8,8,256]{2,1,0:T(8,128)}, u32[]{:S(2)}) %copy-start) | copy-done | bytes 65560
  1.5 0.0 copy-start.1
  1.5 0.8 %copy-done.1 = f32[8,8,256]{2,1,0:T(8,128)S(1)} copy-done((f32[8,8,256]{2,1,0:T(8,128)S(1)}, f32[8,8,256]{2,1,0:T(8,128)}, u32[]{:S(2)}) %copy-start.1) | copy-done | bytes 65560
  2.3 0.5 shard_map.41
  2.8 1.3 %collective-permute-start = (f32[13,8,256]{2,1,0:T(8,128)S(1)}, f32[13,8,256]{2,1,0:T(8,128)S(1)}, u32[]{:S(2)}, u32[]{:S(2)}) collective-permute-start(f32[13,8,256]{2,1,0:T(8,128)S(1)} %get-tuple-element.21), channel_id=1, source_target_pairs={{0,16},{16,32},{32,48},{48,64},{64,80},{80,96},{96,112},{112,128},... | collective-permute-start | bytes 319496 | tf_op jit(solution)/shard_map/ppermute | solution.py:625
  4.1 5.5 %collective-permute-start.1 = (f32[13,8,256]{2,1,0:T(8,128)S(1)}, f32[13,8,256]{2,1,0:T(8,128)S(1)}, u32[]{:S(2)}, u32[]{:S(2)}) collective-permute-start(f32[13,8,256]{2,1,0:T(8,128)S(1)} %get-tuple-element.22), channel_id=1, source_target_pairs={{16,0},{32,16},{48,32},{64,48},{80,64},{96,80},{112,96},{128,112},... | collective-permute-start | bytes 319496 | tf_op jit(solution)/shard_map/ppermute | solution.py:626
  9.6 0.1 collective-permute-done.x_one_ref
  9.7 1.5 %collective-permute-done.1.x_two_ref = f32[13,8,256]{2,1,0:T(8,128)S(1)} collective-permute-done((f32[13,8,256]{2,1,0:T(8,128)S(1)}, f32[13,8,256]{2,1,0:T(8,128)S(1)}, u32[]{:S(2)}, u32[]{:S(2)}) %collective-permute-start.1) | collective-permute-done | bytes 106528 | tf_op jit(solution)/shard_map/ppermute | solution.py:626
  11.3 7.4 %collective-permute-start.3 = (f32[28,8,256]{2,1,0:T(8,128)S(1)}, f32[28,8,256]{2,1,0:T(8,128)S(1)}, u32[]{:S(2)}, u32[]{:S(2)}) collective-permute-start(f32[28,8,256]{2,1,0:T(8,128)S(1)} %get-tuple-element.23.own_ref), channel_id=1, source_target_pairs={{1,2},{2,1},{3,4},{4,3},{5,6},{6,5},{7,8},{8,7},{9,10},{10,9},{11,... | collective-permute-start | bytes 688136 | tf_op jit(solution)/shard_map/ppermute | solution.py:629
  18.7 1.9 %collective-permute-start.2 = (f32[28,8,256]{2,1,0:T(8,128)S(1)}, f32[28,8,256]{2,1,0:T(8,128)S(1)}, u32[]{:S(2)}, u32[]{:S(2)}) collective-permute-start(f32[28,8,256]{2,1,0:T(8,128)S(1)} %get-tuple-element.24), channel_id=1, source_target_pairs={{0,1},{1,0},{2,3},{3,2},{4,5},{5,4},{6,7},{7,6},{8,9},{9,8},{10,11... | collective-permute-start | bytes 688136 | tf_op jit(solution)/shard_map/ppermute | solution.py:628
  20.6 1.8 %collective-permute-done.3.next_ref = f32[28,8,256]{2,1,0:T(8,128)S(1)} collective-permute-done((f32[28,8,256]{2,1,0:T(8,128)S(1)}, f32[28,8,256]{2,1,0:T(8,128)S(1)}, u32[]{:S(2)}, u32[]{:S(2)}) %collective-permute-start.3) | collective-permute-done | bytes 229408 | tf_op jit(solution)/shard_map/ppermute | solution.py:629
  22.4 0.0 collective-permute-done.2.sibling_ref
  22.4 2.5 %shard_map.43 = (f32[22,24,256]{2,1,0:T(8,128)S(1)}, f32[20,24,256]{2,1,0:T(8,128)S(1)}, f32[10,16,128]{2,1,0:T(8,128)S(1)}, f32[8,16,128]{2,1,0:T(8,128)S(1)}, ...) custom-call(s32[1]{0:T(128)} %bitcast.2.core_ref, ...), custom_call_target="tpu_custom_call" | custom-call | tf_op jit(solution)/shard_map/pallas_call | solution.py:589
  24.8 1.5 %shard_map.44 = f32[256,4,128]{2,1,0:T(4,128)} custom-call(f32[10,16,128]{2,1,0:T(8,128)S(1)} %get-tuple-element.25.k1.k_ref, f32[8,16,128]{2,1,0:T(8,128)S(1)} %get-tuple-element.26.f1.f_ref), custom_call_target="tpu_custom_call" | custom-call | tf_op jit(solution)/shard_map/pallas_call | solution.py:589
  26.3 21.2 %all-to-all-start = ((f32[256,4,128]{2,1,0:T(4,128)}), f32[256,4,128]{2,1,0:T(4,128)S(1)}, u32[]{:S(2)}, u32[]{:S(2)}) async-start(f32[256,4,128]{2,1,0:T(4,128)} %shard_map.44), calls=%async_computation | async-start | bytes 1048576 | tf_op jit(solution)/shard_map/all_to_all | solution.py:644
  47.5 4.4 %collective-permute-start.6 = (f32[18,8,128]{2,1,0:T(8,128)S(1)}, f32[18,8,128]{2,1,0:T(8,128)S(1)}, u32[]{:S(2)}, u32[]{:S(2)}) collective-permute-start(f32[18,8,128]{2,1,0:T(8,128)S(1)} %get-tuple-element.29), channel_id=1, source_target_pairs={{0,1},{1,2},{2,3},{3,4},{4,5},{5,6},{6,7},{7,8},{8,9},{9,10},{10,1... | collective-permute-start | bytes 221192 | tf_op jit(solution)/shard_map/ppermute | solution.py:603
  51.9 1.9 %collective-permute-start.7 = (f32[18,8,128]{2,1,0:T(8,128)S(1)}, f32[18,8,128]{2,1,0:T(8,128)S(1)}, u32[]{:S(2)}, u32[]{:S(2)}) collective-permute-start(f32[18,8,128]{2,1,0:T(8,128)S(1)} %get-tuple-element.29), channel_id=1, source_target_pairs={{1,0},{2,1},{3,2},{4,3},{5,4},{6,5},{7,6},{8,7},{9,8},{10,9},{11,1... | collective-permute-start | bytes 221192 | tf_op jit(solution)/shard_map/ppermute | solution.py:604
  53.9 3.1 %collective-permute-start.4 = (f32[11,8,128]{2,1,0:T(8,128)S(1)}, f32[11,8,128]{2,1,0:T(8,128)S(1)}, u32[]{:S(2)}, u32[]{:S(2)}) collective-permute-start(f32[11,8,128]{2,1,0:T(8,128)S(1)} %get-tuple-element.27), channel_id=1, source_target_pairs={{0,16},{16,32},{32,48},{48,64},{64,80},{80,96},{96,112},{112,128},... | collective-permute-start | bytes 135176 | tf_op jit(solution)/shard_map/ppermute | solution.py:603
  57.0 1.3 %collective-permute-start.5 = (f32[11,8,128]{2,1,0:T(8,128)S(1)}, f32[11,8,128]{2,1,0:T(8,128)S(1)}, u32[]{:S(2)}, u32[]{:S(2)}) collective-permute-start(f32[11,8,128]{2,1,0:T(8,128)S(1)} %get-tuple-element.28), channel_id=1, source_target_pairs={{16,0},{32,16},{48,32},{64,48},{80,64},{96,80},{112,96},{128,112},... | collective-permute-start | bytes 135176 | tf_op jit(solution)/shard_map/ppermute | solution.py:604
  58.3 0.3 collective-permute-done.4.refs_1_.x_low_ref
  58.6 3.7 %collective-permute-done.5.refs_2_.x_high_ref = f32[11,8,128]{2,1,0:T(8,128)S(1)} collective-permute-done((f32[11,8,128]{2,1,0:T(8,128)S(1)}, f32[11,8,128]{2,1,0:T(8,128)S(1)}, u32[]{:S(2)}, u32[]{:S(2)}) %collective-permute-start.5) | collective-permute-done | bytes 45088 | tf_op jit(solution)/shard_map/ppermute | solution.py:604
  62.2 0.0 collective-permute-done.6.refs_3_.y_low_ref
  62.2 0.0 collective-permute-done.7.refs_4_.y_high_ref
  62.2 2.0 %all-to-all-done = f32[256,4,128]{2,1,0:T(4,128)S(1)} async-done(((f32[256,4,128]{2,1,0:T(4,128)}), f32[256,4,128]{2,1,0:T(4,128)S(1)}, u32[]{:S(2)}, u32[]{:S(2)}) %all-to-all-start) | async-done | bytes 524320 | tf_op jit(solution)/shard_map/all_to_all | solution.py:644
  64.3 7.1 %collective-permute-start.8 = (f32[1024,128]{1,0:T(8,128)S(1)}, f32[1024,128]{1,0:T(8,128)S(1)}, u32[]{:S(2)}, u32[]{:S(2)}) collective-permute-start(f32[1024,128]{1,0:T(8,128)S(1)} %shard_map.45.mine_ref.after_ref), channel_id=1, source_target_pairs={{0,1},{1,0},{2,3},{3,2},{4,5},{5,4},{6,7},{7,6},{8,9},{9,8},{10,11... | collective-permute-start | bytes 1572872 | tf_op jit(solution)/shard_map/ppermute | solution.py:655
  71.3 0.1 pad_add_fusion.place_ref
  71.4 1.0 %shard_map.48 = (f32[4,16,16,256]{3,2,1,0:T(8,128)S(1)}, f32[16,16,256]{2,1,0:T(8,128)S(1)}, f32[16,16,256]{2,1,0:T(8,128)S(1)}) custom-call(f32[22,24,256]{2,1,0:T(8,128)S(1)} %get-tuple-element.33.k_ref, f32[20,24,256]{2,1,0:T(8,128)S(1)} %get-tuple-element.34.f_ref, f32[1024,128]{1,0:T(8,128)S(1)} %shard_map.45.mine_ref.after_ref), custom_call_target="tpu_custom_call" | custom-call | tf_op jit(solution)/shard_map/pallas_call | solution.py:589
  72.4 0.4 shard_map.47
  72.8 0.1 collective-permute-done.8.other_ref
  72.8 5.6 %shard_map.46.near_ref = f32[6,16,128]{2,1,0:T(8,128)S(1)} custom-call(s32[2]{0:T(128)S(1)} %pad_add_fusion.place_ref, f32[1024,128]{1,0:T(8,128)S(1)} %shard_map.45.mine_ref.after_ref, f32[1024,128]{1,0:T(8,128)S(1)} %collective-permute-done.8.other_ref), custom_call_target="tpu_custom_call" | custom-call | flops 6000000000 | tf_op jit(solution)/shard_map/pallas_call | solution.py:589
  78.4 1.8 %shard_map.49 = (f32[8,8,256]{2,1,0:T(8,128)}, f32[8,8,256]{2,1,0:T(8,128)}) custom-call(f32[6,16,128]{2,1,0:T(8,128)S(1)} %shard_map.46.near_ref, f32[4,16,16,128]{3,2,1,0:T(8,128)S(1)} %get-tuple-element.30.w1, f32[16,16,128]{2,1,0:T(8,128)S(1)} %get-tuple-element.31.g1, f32[16,16,128]{2,1,0:T(8,128)S(1)} %get-tuple-element.32.x1, ...), custom_call_target="tpu_custom_call" | custom-call | tf_op jit(solution)/shard_map/pallas_call | solution.py:589
  (2 shorter events, 0.0 us)
Async XLA Ops:
  0.6 0.8 %copy-start = (f32[8,8,256]{2,1,0:T(8,128)S(1)}, f32[8,8,256]{2,1,0:T(8,128)}, u32[]{:S(2)}) copy-start(f32[8,8,256]{2,1,0:T(8,128)} %k_ref.1) | copy-start | bytes 196612
  1.5 0.8 %copy-start.1 = (f32[8,8,256]{2,1,0:T(8,128)S(1)}, f32[8,8,256]{2,1,0:T(8,128)}, u32[]{:S(2)}) copy-start(f32[8,8,256]{2,1,0:T(8,128)} %f_ref.1) | copy-start | bytes 196612
  2.8 6.9 %collective-permute-start = (f32[13,8,256]{2,1,0:T(8,128)S(1)}, f32[13,8,256]{2,1,0:T(8,128)S(1)}, u32[]{:S(2)}, u32[]{:S(2)}) collective-permute-start(f32[13,8,256]{2,1,0:T(8,128)S(1)} %get-tuple-element.21), channel_id=1, source_target_pairs={{0,16},{16,32},{32,48},{48,64},{64,80},{80,96},{96,112},{112,128},... | collective-permute-start | bytes 319496 | tf_op jit(solution)/shard_map/ppermute | solution.py:625
  4.1 7.2 %collective-permute-start.1 = (f32[13,8,256]{2,1,0:T(8,128)S(1)}, f32[13,8,256]{2,1,0:T(8,128)S(1)}, u32[]{:S(2)}, u32[]{:S(2)}) collective-permute-start(f32[13,8,256]{2,1,0:T(8,128)S(1)} %get-tuple-element.22), channel_id=1, source_target_pairs={{16,0},{32,16},{48,32},{64,48},{80,64},{96,80},{112,96},{128,112},... | collective-permute-start | bytes 319496 | tf_op jit(solution)/shard_map/ppermute | solution.py:626
  11.3 11.1 %collective-permute-start.3 = (f32[28,8,256]{2,1,0:T(8,128)S(1)}, f32[28,8,256]{2,1,0:T(8,128)S(1)}, u32[]{:S(2)}, u32[]{:S(2)}) collective-permute-start(f32[28,8,256]{2,1,0:T(8,128)S(1)} %get-tuple-element.23.own_ref), channel_id=1, source_target_pairs={{1,2},{2,1},{3,4},{4,3},{5,6},{6,5},{7,8},{8,7},{9,10},{10,9},{11,... | collective-permute-start | bytes 688136 | tf_op jit(solution)/shard_map/ppermute | solution.py:629
  18.7 3.7 %collective-permute-start.2 = (f32[28,8,256]{2,1,0:T(8,128)S(1)}, f32[28,8,256]{2,1,0:T(8,128)S(1)}, u32[]{:S(2)}, u32[]{:S(2)}) collective-permute-start(f32[28,8,256]{2,1,0:T(8,128)S(1)} %get-tuple-element.24), channel_id=1, source_target_pairs={{0,1},{1,0},{2,3},{3,2},{4,5},{5,4},{6,7},{7,6},{8,9},{9,8},{10,11... | collective-permute-start | bytes 688136 | tf_op jit(solution)/shard_map/ppermute | solution.py:628
  26.3 37.9 %all-to-all-start = ((f32[256,4,128]{2,1,0:T(4,128)}), f32[256,4,128]{2,1,0:T(4,128)S(1)}, u32[]{:S(2)}, u32[]{:S(2)}) async-start(f32[256,4,128]{2,1,0:T(4,128)} %shard_map.44), calls=%async_computation | async-start | bytes 1048576 | tf_op jit(solution)/shard_map/all_to_all | solution.py:644
  47.5 14.7 %collective-permute-start.6 = (f32[18,8,128]{2,1,0:T(8,128)S(1)}, f32[18,8,128]{2,1,0:T(8,128)S(1)}, u32[]{:S(2)}, u32[]{:S(2)}) collective-permute-start(f32[18,8,128]{2,1,0:T(8,128)S(1)} %get-tuple-element.29), channel_id=1, source_target_pairs={{0,1},{1,2},{2,3},{3,4},{4,5},{5,6},{6,7},{7,8},{8,9},{9,10},{10,1... | collective-permute-start | bytes 221192 | tf_op jit(solution)/shard_map/ppermute | solution.py:603
  51.9 10.3 %collective-permute-start.7 = (f32[18,8,128]{2,1,0:T(8,128)S(1)}, f32[18,8,128]{2,1,0:T(8,128)S(1)}, u32[]{:S(2)}, u32[]{:S(2)}) collective-permute-start(f32[18,8,128]{2,1,0:T(8,128)S(1)} %get-tuple-element.29), channel_id=1, source_target_pairs={{1,0},{2,1},{3,2},{4,3},{5,4},{6,5},{7,6},{8,7},{9,8},{10,9},{11,1... | collective-permute-start | bytes 221192 | tf_op jit(solution)/shard_map/ppermute | solution.py:604
  53.9 4.7 %collective-permute-start.4 = (f32[11,8,128]{2,1,0:T(8,128)S(1)}, f32[11,8,128]{2,1,0:T(8,128)S(1)}, u32[]{:S(2)}, u32[]{:S(2)}) collective-permute-start(f32[11,8,128]{2,1,0:T(8,128)S(1)} %get-tuple-element.27), channel_id=1, source_target_pairs={{0,16},{16,32},{32,48},{48,64},{64,80},{80,96},{96,112},{112,128},... | collective-permute-start | bytes 135176 | tf_op jit(solution)/shard_map/ppermute | solution.py:603
  57.0 5.3 %collective-permute-start.5 = (f32[11,8,128]{2,1,0:T(8,128)S(1)}, f32[11,8,128]{2,1,0:T(8,128)S(1)}, u32[]{:S(2)}, u32[]{:S(2)}) collective-permute-start(f32[11,8,128]{2,1,0:T(8,128)S(1)} %get-tuple-element.28), channel_id=1, source_target_pairs={{16,0},{32,16},{48,32},{64,48},{80,64},{96,80},{112,96},{128,112},... | collective-permute-start | bytes 135176 | tf_op jit(solution)/shard_map/ppermute | solution.py:604
  64.3 8.6 %collective-permute-start.8 = (f32[1024,128]{1,0:T(8,128)S(1)}, f32[1024,128]{1,0:T(8,128)S(1)}, u32[]{:S(2)}, u32[]{:S(2)}) collective-permute-start(f32[1024,128]{1,0:T(8,128)S(1)} %shard_map.45.mine_ref.after_ref), channel_id=1, source_target_pairs={{0,1},{1,0},{2,3},{3,2},{4,5},{5,4},{6,7},{7,6},{8,9},{9,8},{10,11... | collective-permute-start | bytes 1572872 | tf_op jit(solution)/shard_map/ppermute | solution.py:655

commit v10 on v9

--- a/solution.py
+++ b/solution.py
@@ -353,7 +353,7 @@
 
 def make_coarse_kernel(count_x, count_y):
     planes2, rows, count3 = 2 * count_x, count_y // 2, count_x // 4
-    size = 16
+    size = 32
     line = (2, rows, 128)
 
     def coarse_kernel(place_ref, mine_ref, other_ref, near_ref,

time: 80.7 us -> 80.4 us (level)
  no operation moved by 1% of the time
where the time goes in v10:
time: 80.4 us; the launch traced here: 80 us
  starting transfers between devices  55 us (68%)
  Pallas kernels  12.9 us (16%)
  waiting for transfers between devices  9.53 us (12%)
  local copies, waits for them, and re-layouts  1.67 us (2%)
    all_to_all x1, starting transfers between devices, body(): mine = lax.all_to_all(copies, ('gx', 'chip'), 0, 0).reshape(-1, 128)  21.2 us
    pallas_call x7, Pallas kernels, call(): pl.pallas_call(kernel, out_shape=[jax.ShapeDtypeStruct(shape, F32) for sh...  12.4 us
    ppermute x2, starting transfers between devices, both_sides(): low = lax.ppermute(up, axes, [(i, i + 1) for i in range(count - 1)])  7.51 us
    ppermute x1, starting transfers between devices, body(): lax.ppermute(outer, along_y, [pair for i in range(1, count_y - 1, 2) for...  7.38 us
    ppermute x1, starting transfers between devices, body(): other = lax.ppermute(mine, 'core', [(0, 1), (1, 0)])  7.05 us
    ppermute x1, starting transfers between devices, body(): lax.ppermute(two, ('gx', 'core'), [(to, source) for source, to in route])  5.46 us
    ppermute x2, waiting for transfers between devices, both_sides(): high = lax.ppermute(down, axes, [(i + 1, i) for i in range(count - 1)])  3.66 us
    ppermute x2, starting transfers between devices, both_sides(): high = lax.ppermute(down, axes, [(i + 1, i) for i in range(count - 1)])  3.21 us
  transfers between devices with their start and end apart: 10, of which 7 were waited for; matrix products, arithmetic and copies ran while one was open for 0% of the time, Pallas kernels for 2%

profile of v10, /device:TPU:1, one launch (start us, length us, event | category | flops | bytes accessed | tf_op | source)
XLA Modules:
  0.0 80.0 jit_solution(10253342909245204640)
XLA Ops:
  0.6 0.0 copy-start
  0.6 0.8 %copy-done = f32[8,8,256]{2,1,0:T(8,128)S(1)} copy-done((f32[8,8,256]{2,1,0:T(8,128)S(1)}, f32[8,8,256]{2,1,0:T(8,128)}, u32[]{:S(2)}) %copy-start) | copy-done | bytes 65560
  1.5 0.0 copy-start.1
  1.5 0.8 %copy-done.1 = f32[8,8,256]{2,1,0:T(8,128)S(1)} copy-done((f32[8,8,256]{2,1,0:T(8,128)S(1)}, f32[8,8,256]{2,1,0:T(8,128)}, u32[]{:S(2)}) %copy-start.1) | copy-done | bytes 65560
  2.3 0.5 shard_map.41
  2.8 1.3 %collective-permute-start = (f32[13,8,256]{2,1,0:T(8,128)S(1)}, f32[13,8,256]{2,1,0:T(8,128)S(1)}, u32[]{:S(2)}, u32[]{:S(2)}) collective-permute-start(f32[13,8,256]{2,1,0:T(8,128)S(1)} %get-tuple-element.21), channel_id=1, source_target_pairs={{0,16},{16,32},{32,48},{48,64},{64,80},{80,96},{96,112},{112,128},... | collective-permute-start | bytes 319496 | tf_op jit(solution)/shard_map/ppermute | solution.py:625
  4.1 5.5 %collective-permute-start.1 = (f32[13,8,256]{2,1,0:T(8,128)S(1)}, f32[13,8,256]{2,1,0:T(8,128)S(1)}, u32[]{:S(2)}, u32[]{:S(2)}) collective-permute-start(f32[13,8,256]{2,1,0:T(8,128)S(1)} %get-tuple-element.22), channel_id=1, source_target_pairs={{16,0},{32,16},{48,32},{64,48},{80,64},{96,80},{112,96},{128,112},... | collective-permute-start | bytes 319496 | tf_op jit(solution)/shard_map/ppermute | solution.py:626
  9.6 0.1 collective-permute-done.x_one_ref
  9.7 1.5 %collective-permute-done.1.x_two_ref = f32[13,8,256]{2,1,0:T(8,128)S(1)} collective-permute-done((f32[13,8,256]{2,1,0:T(8,128)S(1)}, f32[13,8,256]{2,1,0:T(8,128)S(1)}, u32[]{:S(2)}, u32[]{:S(2)}) %collective-permute-start.1) | collective-permute-done | bytes 106528 | tf_op jit(solution)/shard_map/ppermute | solution.py:626
  11.3 7.4 %collective-permute-start.3 = (f32[28,8,256]{2,1,0:T(8,128)S(1)}, f32[28,8,256]{2,1,0:T(8,128)S(1)}, u32[]{:S(2)}, u32[]{:S(2)}) collective-permute-start(f32[28,8,256]{2,1,0:T(8,128)S(1)} %get-tuple-element.23.own_ref), channel_id=1, source_target_pairs={{1,2},{2,1},{3,4},{4,3},{5,6},{6,5},{7,8},{8,7},{9,10},{10,9},{11,... | collective-permute-start | bytes 688136 | tf_op jit(solution)/shard_map/ppermute | solution.py:629
  18.7 1.9 %collective-permute-start.2 = (f32[28,8,256]{2,1,0:T(8,128)S(1)}, f32[28,8,256]{2,1,0:T(8,128)S(1)}, u32[]{:S(2)}, u32[]{:S(2)}) collective-permute-start(f32[28,8,256]{2,1,0:T(8,128)S(1)} %get-tuple-element.24), channel_id=1, source_target_pairs={{0,1},{1,0},{2,3},{3,2},{4,5},{5,4},{6,7},{7,6},{8,9},{9,8},{10,11... | collective-permute-start | bytes 688136 | tf_op jit(solution)/shard_map/ppermute | solution.py:628
  20.6 1.8 %collective-permute-done.3.next_ref = f32[28,8,256]{2,1,0:T(8,128)S(1)} collective-permute-done((f32[28,8,256]{2,1,0:T(8,128)S(1)}, f32[28,8,256]{2,1,0:T(8,128)S(1)}, u32[]{:S(2)}, u32[]{:S(2)}) %collective-permute-start.3) | collective-permute-done | bytes 229408 | tf_op jit(solution)/shard_map/ppermute | solution.py:629
  22.4 0.0 collective-permute-done.2.sibling_ref
  22.4 2.5 %shard_map.43 = (f32[22,24,256]{2,1,0:T(8,128)S(1)}, f32[20,24,256]{2,1,0:T(8,128)S(1)}, f32[10,16,128]{2,1,0:T(8,128)S(1)}, f32[8,16,128]{2,1,0:T(8,128)S(1)}, ...) custom-call(s32[1]{0:T(128)} %bitcast.2.core_ref, ...), custom_call_target="tpu_custom_call" | custom-call | tf_op jit(solution)/shard_map/pallas_call | solution.py:589
  24.8 1.5 %shard_map.44 = f32[256,4,128]{2,1,0:T(4,128)} custom-call(f32[10,16,128]{2,1,0:T(8,128)S(1)} %get-tuple-element.25.k1.k_ref, f32[8,16,128]{2,1,0:T(8,128)S(1)} %get-tuple-element.26.f1.f_ref), custom_call_target="tpu_custom_call" | custom-call | tf_op jit(solution)/shard_map/pallas_call | solution.py:589
  26.3 21.2 %all-to-all-start = ((f32[256,4,128]{2,1,0:T(4,128)}), f32[256,4,128]{2,1,0:T(4,128)S(1)}, u32[]{:S(2)}, u32[]{:S(2)}) async-start(f32[256,4,128]{2,1,0:T(4,128)} %shard_map.44), calls=%async_computation | async-start | bytes 1048576 | tf_op jit(solution)/shard_map/all_to_all | solution.py:644
  47.5 4.4 %collective-permute-start.6 = (f32[18,8,128]{2,1,0:T(8,128)S(1)}, f32[18,8,128]{2,1,0:T(8,128)S(1)}, u32[]{:S(2)}, u32[]{:S(2)}) collective-permute-start(f32[18,8,128]{2,1,0:T(8,128)S(1)} %get-tuple-element.29), channel_id=1, source_target_pairs={{0,1},{1,2},{2,3},{3,4},{4,5},{5,6},{6,7},{7,8},{8,9},{9,10},{10,1... | collective-permute-start | bytes 221192 | tf_op jit(solution)/shard_map/ppermute | solution.py:603
  51.9 1.9 %collective-permute-start.7 = (f32[18,8,128]{2,1,0:T(8,128)S(1)}, f32[18,8,128]{2,1,0:T(8,128)S(1)}, u32[]{:S(2)}, u32[]{:S(2)}) collective-permute-start(f32[18,8,128]{2,1,0:T(8,128)S(1)} %get-tuple-element.29), channel_id=1, source_target_pairs={{1,0},{2,1},{3,2},{4,3},{5,4},{6,5},{7,6},{8,7},{9,8},{10,9},{11,1... | collective-permute-start | bytes 221192 | tf_op jit(solution)/shard_map/ppermute | solution.py:604
  53.9 3.1 %collective-permute-start.4 = (f32[11,8,128]{2,1,0:T(8,128)S(1)}, f32[11,8,128]{2,1,0:T(8,128)S(1)}, u32[]{:S(2)}, u32[]{:S(2)}) collective-permute-start(f32[11,8,128]{2,1,0:T(8,128)S(1)} %get-tuple-element.27), channel_id=1, source_target_pairs={{0,16},{16,32},{32,48},{48,64},{64,80},{80,96},{96,112},{112,128},... | collective-permute-start | bytes 135176 | tf_op jit(solution)/shard_map/ppermute | solution.py:603
  57.0 1.3 %collective-permute-start.5 = (f32[11,8,128]{2,1,0:T(8,128)S(1)}, f32[11,8,128]{2,1,0:T(8,128)S(1)}, u32[]{:S(2)}, u32[]{:S(2)}) collective-permute-start(f32[11,8,128]{2,1,0:T(8,128)S(1)} %get-tuple-element.28), channel_id=1, source_target_pairs={{16,0},{32,16},{48,32},{64,48},{80,64},{96,80},{112,96},{128,112},... | collective-permute-start | bytes 135176 | tf_op jit(solution)/shard_map/ppermute | solution.py:604
  58.3 0.3 collective-permute-done.4.refs_1_.x_low_ref
  58.6 3.7 %collective-permute-done.5.refs_2_.x_high_ref = f32[11,8,128]{2,1,0:T(8,128)S(1)} collective-permute-done((f32[11,8,128]{2,1,0:T(8,128)S(1)}, f32[11,8,128]{2,1,0:T(8,128)S(1)}, u32[]{:S(2)}, u32[]{:S(2)}) %collective-permute-start.5) | collective-permute-done | bytes 45088 | tf_op jit(solution)/shard_map/ppermute | solution.py:604
  62.2 0.0 collective-permute-done.6.refs_3_.y_low_ref
  62.2 0.0 collective-permute-done.7.refs_4_.y_high_ref
  62.2 2.0 %all-to-all-done = f32[256,4,128]{2,1,0:T(4,128)S(1)} async-done(((f32[256,4,128]{2,1,0:T(4,128)}), f32[256,4,128]{2,1,0:T(4,128)S(1)}, u32[]{:S(2)}, u32[]{:S(2)}) %all-to-all-start) | async-done | bytes 524320 | tf_op jit(solution)/shard_map/all_to_all | solution.py:644
  64.3 7.1 %collective-permute-start.8 = (f32[1024,128]{1,0:T(8,128)S(1)}, f32[1024,128]{1,0:T(8,128)S(1)}, u32[]{:S(2)}, u32[]{:S(2)}) collective-permute-start(f32[1024,128]{1,0:T(8,128)S(1)} %shard_map.45.mine_ref.after_ref), channel_id=1, source_target_pairs={{0,1},{1,0},{2,3},{3,2},{4,5},{5,4},{6,7},{7,6},{8,9},{9,8},{10,11... | collective-permute-start | bytes 1572872 | tf_op jit(solution)/shard_map/ppermute | solution.py:655
  71.3 0.1 pad_add_fusion.place_ref
  71.4 1.0 %shard_map.48 = (f32[4,16,16,256]{3,2,1,0:T(8,128)S(1)}, f32[16,16,256]{2,1,0:T(8,128)S(1)}, f32[16,16,256]{2,1,0:T(8,128)S(1)}) custom-call(f32[22,24,256]{2,1,0:T(8,128)S(1)} %get-tuple-element.33.k_ref, f32[20,24,256]{2,1,0:T(8,128)S(1)} %get-tuple-element.34.f_ref, f32[1024,128]{1,0:T(8,128)S(1)} %shard_map.45.mine_ref.after_ref), custom_call_target="tpu_custom_call" | custom-call | tf_op jit(solution)/shard_map/pallas_call | solution.py:589
  72.4 0.4 shard_map.47
  72.8 0.1 collective-permute-done.8.other_ref
  72.8 5.3 %shard_map.46.near_ref = f32[6,16,128]{2,1,0:T(8,128)S(1)} custom-call(s32[2]{0:T(128)S(1)} %pad_add_fusion.place_ref, f32[1024,128]{1,0:T(8,128)S(1)} %shard_map.45.mine_ref.after_ref, f32[1024,128]{1,0:T(8,128)S(1)} %collective-permute-done.8.other_ref), custom_call_target="tpu_custom_call" | custom-call | flops 6000000000 | tf_op jit(solution)/shard_map/pallas_call | solution.py:589
  78.2 1.8 %shard_map.49 = (f32[8,8,256]{2,1,0:T(8,128)}, f32[8,8,256]{2,1,0:T(8,128)}) custom-call(f32[6,16,128]{2,1,0:T(8,128)S(1)} %shard_map.46.near_ref, f32[4,16,16,128]{3,2,1,0:T(8,128)S(1)} %get-tuple-element.30.w1, f32[16,16,128]{2,1,0:T(8,128)S(1)} %get-tuple-element.31.g1, f32[16,16,128]{2,1,0:T(8,128)S(1)} %get-tuple-element.32.x1, ...), custom_call_target="tpu_custom_call" | custom-call | tf_op jit(solution)/shard_map/pallas_call | solution.py:589
  (2 shorter events, 0.0 us)
Async XLA Ops:
  0.6 0.8 %copy-start = (f32[8,8,256]{2,1,0:T(8,128)S(1)}, f32[8,8,256]{2,1,0:T(8,128)}, u32[]{:S(2)}) copy-start(f32[8,8,256]{2,1,0:T(8,128)} %k_ref.1) | copy-start | bytes 196612
  1.5 0.8 %copy-start.1 = (f32[8,8,256]{2,1,0:T(8,128)S(1)}, f32[8,8,256]{2,1,0:T(8,128)}, u32[]{:S(2)}) copy-start(f32[8,8,256]{2,1,0:T(8,128)} %f_ref.1) | copy-start | bytes 196612
  2.8 6.9 %collective-permute-start = (f32[13,8,256]{2,1,0:T(8,128)S(1)}, f32[13,8,256]{2,1,0:T(8,128)S(1)}, u32[]{:S(2)}, u32[]{:S(2)}) collective-permute-start(f32[13,8,256]{2,1,0:T(8,128)S(1)} %get-tuple-element.21), channel_id=1, source_target_pairs={{0,16},{16,32},{32,48},{48,64},{64,80},{80,96},{96,112},{112,128},... | collective-permute-start | bytes 319496 | tf_op jit(solution)/shard_map/ppermute | solution.py:625
  4.1 7.2 %collective-permute-start.1 = (f32[13,8,256]{2,1,0:T(8,128)S(1)}, f32[13,8,256]{2,1,0:T(8,128)S(1)}, u32[]{:S(2)}, u32[]{:S(2)}) collective-permute-start(f32[13,8,256]{2,1,0:T(8,128)S(1)} %get-tuple-element.22), channel_id=1, source_target_pairs={{16,0},{32,16},{48,32},{64,48},{80,64},{96,80},{112,96},{128,112},... | collective-permute-start | bytes 319496 | tf_op jit(solution)/shard_map/ppermute | solution.py:626
  11.3 11.1 %collective-permute-start.3 = (f32[28,8,256]{2,1,0:T(8,128)S(1)}, f32[28,8,256]{2,1,0:T(8,128)S(1)}, u32[]{:S(2)}, u32[]{:S(2)}) collective-permute-start(f32[28,8,256]{2,1,0:T(8,128)S(1)} %get-tuple-element.23.own_ref), channel_id=1, source_target_pairs={{1,2},{2,1},{3,4},{4,3},{5,6},{6,5},{7,8},{8,7},{9,10},{10,9},{11,... | collective-permute-start | bytes 688136 | tf_op jit(solution)/shard_map/ppermute | solution.py:629
  18.7 3.7 %collective-permute-start.2 = (f32[28,8,256]{2,1,0:T(8,128)S(1)}, f32[28,8,256]{2,1,0:T(8,128)S(1)}, u32[]{:S(2)}, u32[]{:S(2)}) collective-permute-start(f32[28,8,256]{2,1,0:T(8,128)S(1)} %get-tuple-element.24), channel_id=1, source_target_pairs={{0,1},{1,0},{2,3},{3,2},{4,5},{5,4},{6,7},{7,6},{8,9},{9,8},{10,11... | collective-permute-start | bytes 688136 | tf_op jit(solution)/shard_map/ppermute | solution.py:628
  26.3 37.9 %all-to-all-start = ((f32[256,4,128]{2,1,0:T(4,128)}), f32[256,4,128]{2,1,0:T(4,128)S(1)}, u32[]{:S(2)}, u32[]{:S(2)}) async-start(f32[256,4,128]{2,1,0:T(4,128)} %shard_map.44), calls=%async_computation | async-start | bytes 1048576 | tf_op jit(solution)/shard_map/all_to_all | solution.py:644
  47.5 14.7 %collective-permute-start.6 = (f32[18,8,128]{2,1,0:T(8,128)S(1)}, f32[18,8,128]{2,1,0:T(8,128)S(1)}, u32[]{:S(2)}, u32[]{:S(2)}) collective-permute-start(f32[18,8,128]{2,1,0:T(8,128)S(1)} %get-tuple-element.29), channel_id=1, source_target_pairs={{0,1},{1,2},{2,3},{3,4},{4,5},{5,6},{6,7},{7,8},{8,9},{9,10},{10,1... | collective-permute-start | bytes 221192 | tf_op jit(solution)/shard_map/ppermute | solution.py:603
  51.9 10.3 %collective-permute-start.7 = (f32[18,8,128]{2,1,0:T(8,128)S(1)}, f32[18,8,128]{2,1,0:T(8,128)S(1)}, u32[]{:S(2)}, u32[]{:S(2)}) collective-permute-start(f32[18,8,128]{2,1,0:T(8,128)S(1)} %get-tuple-element.29), channel_id=1, source_target_pairs={{1,0},{2,1},{3,2},{4,3},{5,4},{6,5},{7,6},{8,7},{9,8},{10,9},{11,1... | collective-permute-start | bytes 221192 | tf_op jit(solution)/shard_map/ppermute | solution.py:604
  53.9 4.7 %collective-permute-start.4 = (f32[11,8,128]{2,1,0:T(8,128)S(1)}, f32[11,8,128]{2,1,0:T(8,128)S(1)}, u32[]{:S(2)}, u32[]{:S(2)}) collective-permute-start(f32[11,8,128]{2,1,0:T(8,128)S(1)} %get-tuple-element.27), channel_id=1, source_target_pairs={{0,16},{16,32},{32,48},{48,64},{64,80},{80,96},{96,112},{112,128},... | collective-permute-start | bytes 135176 | tf_op jit(solution)/shard_map/ppermute | solution.py:603
  57.0 5.3 %collective-permute-start.5 = (f32[11,8,128]{2,1,0:T(8,128)S(1)}, f32[11,8,128]{2,1,0:T(8,128)S(1)}, u32[]{:S(2)}, u32[]{:S(2)}) collective-permute-start(f32[11,8,128]{2,1,0:T(8,128)S(1)} %get-tuple-element.28), channel_id=1, source_target_pairs={{16,0},{32,16},{48,32},{64,48},{80,64},{96,80},{112,96},{128,112},... | collective-permute-start | bytes 135176 | tf_op jit(solution)/shard_map/ppermute | solution.py:604
  64.3 8.6 %collective-permute-start.8 = (f32[1024,128]{1,0:T(8,128)S(1)}, f32[1024,128]{1,0:T(8,128)S(1)}, u32[]{:S(2)}, u32[]{:S(2)}) collective-permute-start(f32[1024,128]{1,0:T(8,128)S(1)} %shard_map.45.mine_ref.after_ref), channel_id=1, source_target_pairs={{0,1},{1,0},{2,3},{3,2},{4,5},{5,4},{6,7},{7,6},{8,9},{9,8},{10,11... | collective-permute-start | bytes 1572872 | tf_op jit(solution)/shard_map/ppermute | solution.py:655
